TPU v7x, 32 devices: a whole 2x2x4 slice. The times are simulated.
32 devices in a mesh: ctx: 8 (over y, x, core), dp: 4 (over z).
Axes of the slice: x: 2, y: 2, z: 4, core: 2. Of those that a mesh axis runs over, the one named last changes fastest.
Arguments:
- tokens: bfloat16 [4, 3072, 4096], P('dp', 'ctx'), may hold values from -6 to 6
- key_input: bfloat16 [4, 3072, 2048], P('dp', 'ctx'), may hold values from -6 to 6
- values: bfloat16 [4, 3072, 2048], P('dp', 'ctx'), may hold values from -6 to 6
- q_weight: bfloat16 [4096, 2048], P(('ctx', 'dp')), may hold values from -0.09375 to 0.09375
- q_spikes: int32 [4, 3072, 2048], P('dp', 'ctx'), may hold values 0 or 1
- k_spikes: int32 [4, 3072, 2048], P('dp', 'ctx'), may hold values 0 or 1
- cotangent: bfloat16 [4, 3072, 2048], P('dp', 'ctx'), may hold values from -6 to 6
Outputs:
- attended: bfloat16 [4, 3072, 2048], P('dp', 'ctx')
- grad_tokens: bfloat16 [4, 3072, 4096], P('dp', 'ctx')
- grad_keys: bfloat16 [4, 3072, 2048], P('dp', 'ctx')
- grad_values: bfloat16 [4, 3072, 2048], P('dp', 'ctx')
All inputs are finite; a program needn't handle non-finite values. No bound on the sum of `q_spikes` or of `k_spikes` on one device may be relied on, other than what follows from the above.
Results may differ from a plain program's by a relative error of at most 0.005.
Values may be sent and summed in bfloat16 or wider, within the bound.
No kernel may reach another device: no remote copies, remote signals or barrier semaphores. Data moves between devices by JAX's collectives and lax.ppermute only.
A program may use at most 256 MiB of HBM per device.

v0:
```python
import functools
import math

import jax
import jax.numpy as jnp
from jax import lax
from jax.experimental import pallas as pl
from jax.experimental.pallas import tpu as pltpu
from jax.sharding import Mesh, PartitionSpec as P

HEAD = 128
PIECE = 128
WIDE = 512
CTX = ("chip", "core")
SWAP = [(0, 1), (1, 0)]
f32, bf16 = jnp.float32, jnp.bfloat16
VMEM_LIMIT = 60 * 1024 * 1024


def nn(a, b):
    return lax.dot_general(a, b, (((1,), (0,)), ((), ())), preferred_element_type=f32)


def nt(a, b):
    return lax.dot_general(a, b, (((1,), (1,)), ((), ())), preferred_element_type=f32)


def tn(a, b):
    return lax.dot_general(a, b, (((0,), (0,)), ((), ())), preferred_element_type=f32)


def params(flops, moved):
    return dict(
        compiler_params=pltpu.CompilerParams(vmem_limit_bytes=VMEM_LIMIT),
        cost_estimate=pl.CostEstimate(flops=flops, bytes_accessed=moved, transcendentals=0),
    )


def columns(length):
    return pl.BlockSpec((length, WIDE), lambda j: (0, j))


def states():
    return pl.BlockSpec((WIDE, HEAD), lambda j: (j, 0))


def anywhere():
    return pl.BlockSpec(memory_space=pl.ANY)


def memory_kernel(key_ref, spike_ref, value_ref, after_ref, keys_ref, own_ref, sent_ref):
    del after_ref
    keys = key_ref[...] * spike_ref[...].astype(f32).astype(bf16)
    keys_ref[...] = keys
    for at in range(0, WIDE, HEAD):
        own = tn(keys[:, at : at + HEAD], value_ref[:, at : at + HEAD])
        own_ref[at : at + HEAD, :] = own
        sent_ref[at : at + HEAD, :] = own.astype(bf16)


def memory_call(key_input, k_spikes, values, after):
    length, total = values.shape
    return pl.pallas_call(
        memory_kernel,
        grid=(total // WIDE,),
        in_specs=[columns(length)] * 3 + [anywhere()],
        out_specs=[columns(length), states(), states()],
        out_shape=[
            jax.ShapeDtypeStruct((length, total), bf16),
            jax.ShapeDtypeStruct((total, HEAD), f32),
            jax.ShapeDtypeStruct((total, HEAD), bf16),
        ],
        name="own_memory",
        **params(2 * length * total * HEAD, 12 * length * total),
    )(key_input, k_spikes, values, after)


def tie_kernel(*refs):
    del refs


def tie(array, *others):
    return pl.pallas_call(
        tie_kernel,
        in_specs=[anywhere()] * (1 + len(others)),
        out_specs=anywhere(),
        out_shape=jax.ShapeDtypeStruct(array.shape, array.dtype),
        input_output_aliases={0: 0},
        name="tie",
        **params(0, 0),
    )(array, *others)


def keep_lower(square, flipped=False):
    row = lax.broadcasted_iota(jnp.int32, square.shape, 0)
    col = lax.broadcasted_iota(jnp.int32, square.shape, 1)
    return jnp.where((col >= row) if flipped else (col <= row), square, 0.0).astype(bf16)


def causal(a, b):
    length = a.shape[0]
    cut = length - HEAD
    top = keep_lower(nt(a[:cut], b[:cut]))
    whole = nt(a[cut:], b)
    bottom = jnp.concatenate([whole[:, :cut].astype(bf16), keep_lower(whole[:, cut:])], axis=1)
    return [(slice(0, cut), slice(0, cut), top), (slice(cut, length), slice(0, length), bottom)]


def causal_turned(a, b):
    length = a.shape[0]
    whole = nt(a[:HEAD], b)
    top = jnp.concatenate(
        [keep_lower(whole[:, :HEAD], True), whole[:, HEAD:].astype(bf16)], axis=1
    )
    bottom = keep_lower(nt(a[HEAD:], b[HEAD:]), True)
    return [
        (slice(0, HEAD), slice(0, length), top),
        (slice(HEAD, length), slice(HEAD, length), bottom),
    ]


def twice(array):
    return jnp.concatenate([array, array], axis=1)


def masked_kernel(factor, grad_ref, value_ref, keys_ref, spike_ref, high_ref, low_ref, out_ref):
    for head in range(0, WIDE, HEAD):
        part = slice(head, head + HEAD)
        grad, value, keys = grad_ref[:, part], value_ref[:, part], keys_ref[:, part]
        state = jnp.concatenate([high_ref[part, :], low_ref[part, :]], axis=1)
        for rows, cols, scores in causal(grad, value):
            made = nn(scores, keys[cols]) + nt(twice(grad[rows]), state)
            out_ref[rows, part] = (factor * made * spike_ref[rows, part].astype(f32)).astype(bf16)


def masked_call(factor, cotangent, values, keys, q_spikes, high, low):
    length, total = values.shape
    return pl.pallas_call(
        functools.partial(masked_kernel, factor),
        grid=(total // WIDE,),
        in_specs=[columns(length)] * 4 + [states()] * 2,
        out_specs=columns(length),
        out_shape=jax.ShapeDtypeStruct((length, total), bf16),
        name="masked_grad",
        **params(8 * length * total * length, 12 * length * total),
    )(cotangent, values, keys, q_spikes, high, low)


def rows_of(blocks):
    return sum(block.shape[0] for block in blocks)


def product(tokens, blocks):
    return nn(
        jnp.concatenate([ref[...] for ref in tokens], axis=1),
        jnp.concatenate([ref[...] for ref in blocks], axis=0),
    )


def project_kernel(number, size, has_sum, *refs):
    _, *refs = refs
    tokens, blocks = refs[:number], refs[number : number + size]
    rest = refs[number + size :]
    made = product(tokens, blocks)
    if has_sum:
        made = made + rest[0][...]
    rest[-1][...] = made


def token_specs(number, length):
    def one(piece):
        return pl.BlockSpec((length, PIECE), lambda j, places: (0, places[piece]))

    return [one(piece) for piece in range(number)]


def wide_spec(rows):
    return pl.BlockSpec((rows, WIDE), lambda j, places: (0, j))


def project_call(places, tokens, blocks, before):
    length = tokens.shape[0]
    total = blocks[0].shape[1]
    depth = rows_of(blocks)
    number = depth // PIECE
    extra = [] if before is None else [before]
    return pl.pallas_call(
        functools.partial(project_kernel, number, len(blocks), before is not None),
        grid_spec=pltpu.PrefetchScalarGridSpec(
            num_scalar_prefetch=1,
            grid=(total // WIDE,),
            in_specs=token_specs(number, length)
            + [wide_spec(block.shape[0]) for block in blocks]
            + [wide_spec(length)] * len(extra),
            out_specs=wide_spec(length),
        ),
        out_shape=jax.ShapeDtypeStruct((length, total), f32),
        input_output_aliases={} if before is None else {1 + number + len(blocks): 0},
        name="project",
        **params(2 * length * depth * total, depth * total * 2 + 8 * length * total),
    )(places, *[tokens] * number, *blocks, *extra)


def query_kernel(number, size, *refs):
    _, *refs = refs
    tokens, blocks = refs[:number], refs[number : number + size]
    sum_ref, spike_ref, grad_ref, query_ref, own_ref, sent_ref = refs[number + size :]
    made = product(tokens, blocks) + sum_ref[...]
    queries = (made * spike_ref[...].astype(f32)).astype(bf16)
    query_ref[...] = queries
    for at in range(0, WIDE, HEAD):
        own = tn(queries[:, at : at + HEAD], grad_ref[:, at : at + HEAD])
        own_ref[at : at + HEAD, :] = own
        sent_ref[at : at + HEAD, :] = own.astype(bf16)


def query_call(places, tokens, blocks, before, q_spikes, cotangent):
    length = tokens.shape[0]
    total = blocks[0].shape[1]
    depth = rows_of(blocks)
    number = depth // PIECE
    state_spec = pl.BlockSpec((WIDE, HEAD), lambda j, places: (j, 0))
    return pl.pallas_call(
        functools.partial(query_kernel, number, len(blocks)),
        grid_spec=pltpu.PrefetchScalarGridSpec(
            num_scalar_prefetch=1,
            grid=(total // WIDE,),
            in_specs=token_specs(number, length)
            + [wide_spec(block.shape[0]) for block in blocks]
            + [wide_spec(length)] * 3,
            out_specs=[wide_spec(length), state_spec, state_spec],
        ),
        out_shape=[
            jax.ShapeDtypeStruct((length, total), bf16),
            jax.ShapeDtypeStruct((total, HEAD), f32),
            jax.ShapeDtypeStruct((total, HEAD), bf16),
        ],
        name="queries",
        **params(2 * length * depth * total, depth * total * 2 + 12 * length * total),
    )(places, *[tokens] * number, *blocks, before, q_spikes, cotangent)


def back_kernel(number, size, has_before, places_ref, *refs):
    blocks, masked_ref = refs[:size], refs[size]
    out_ref, sum_ref, round_ref, sems = refs[size + (2 if has_before else 1) :]
    step = pl.program_id(0)
    made = nt(masked_ref[...], jnp.concatenate([ref[...] for ref in blocks], axis=0))

    @pl.when(step == 0)
    def _():
        sum_ref[...] = made

    @pl.when(step > 0)
    def _():
        sum_ref[...] += made

    @pl.when(step == pl.num_programs(0) - 1)
    def _():
        round_ref[...] = sum_ref[...].astype(bf16)
        copies = []
        for piece in range(number):
            place = pl.multiple_of(places_ref[piece] * PIECE, PIECE)
            copy = pltpu.make_async_copy(
                round_ref.at[:, pl.ds(piece * PIECE, PIECE)],
                out_ref.at[:, pl.ds(place, PIECE)],
                sems.at[piece],
            )
            copy.start()
            copies.append(copy)
        for copy in copies:
            copy.wait()


def back_call(places, blocks, masked, before, width):
    length, total = masked.shape
    depth = rows_of(blocks)
    number = depth // PIECE
    extra = [] if before is None else [before]
    return pl.pallas_call(
        functools.partial(back_kernel, number, len(blocks), before is not None),
        grid_spec=pltpu.PrefetchScalarGridSpec(
            num_scalar_prefetch=1,
            grid=(total // WIDE,),
            in_specs=[wide_spec(block.shape[0]) for block in blocks]
            + [wide_spec(length)]
            + [anywhere()] * len(extra),
            out_specs=anywhere(),
            scratch_shapes=[
                pltpu.VMEM((length, depth), f32),
                pltpu.VMEM((length, depth), bf16),
                pltpu.SemaphoreType.DMA((number,)),
            ],
        ),
        out_shape=jax.ShapeDtypeStruct((length, width), bf16),
        input_output_aliases={} if before is None else {2 + len(blocks): 0},
        name="grad_tokens",
        **params(2 * length * depth * total, depth * total * 2 + 4 * length * total),
    )(places, *blocks, masked, *extra)


def inner_kernel(
    factor, query_ref, keys_ref, value_ref, grad_ref, high_ref, low_ref, out_ref, key_ref, val_ref
):
    for head in range(0, WIDE, HEAD):
        part = slice(head, head + HEAD)
        query, keys = query_ref[:, part], keys_ref[:, part]
        value, grad = value_ref[:, part], grad_ref[:, part]
        state = [high_ref[part, :], low_ref[part, :]]
        for rows, cols, scores in causal(query, keys):
            made = nn(
                jnp.concatenate([scores, twice(query[rows])], axis=1),
                jnp.concatenate([value[cols], *state], axis=0),
            )
            out_ref[rows, part] = (factor * made).astype(bf16)
        for rows, cols, scores in causal_turned(keys, query):
            val_ref[rows, part] = nn(scores, grad[cols])
        for rows, cols, scores in causal_turned(value, grad):
            key_ref[rows, part] = nn(scores, query[cols])


def inner_call(factor, queries, keys, values, cotangent, high, low):
    length, total = values.shape
    return pl.pallas_call(
        functools.partial(inner_kernel, factor),
        grid=(total // WIDE,),
        in_specs=[columns(length)] * 4 + [states()] * 2,
        out_specs=[columns(length)] * 3,
        out_shape=[
            jax.ShapeDtypeStruct((length, total), bf16),
            jax.ShapeDtypeStruct((length, total), f32),
            jax.ShapeDtypeStruct((length, total), f32),
        ],
        name="inner",
        **params(16 * length * total * length, 18 * length * total),
    )(queries, keys, values, cotangent, high, low)


def outer_kernel(
    factor, key_ref, val_ref, keys_ref, value_ref, spike_ref, high_ref, low_ref, gk_ref, gv_ref
):
    for head in range(0, WIDE, HEAD):
        part = slice(head, head + HEAD)
        keys, value = keys_ref[:, part], value_ref[:, part]
        state = [high_ref[part, :], low_ref[part, :]]
        key_grad = key_ref[:, part] + nt(twice(value), jnp.concatenate(state, axis=1))
        gk_ref[:, part] = (factor * key_grad * spike_ref[:, part].astype(f32)).astype(bf16)
        value_grad = val_ref[:, part] + nn(twice(keys), jnp.concatenate(state, axis=0))
        gv_ref[:, part] = (factor * value_grad).astype(bf16)


def outer_call(factor, key_part, value_part, keys, values, k_spikes, high, low):
    length, total = values.shape
    return pl.pallas_call(
        functools.partial(outer_kernel, factor),
        grid=(total // WIDE,),
        in_specs=[columns(length)] * 5 + [states()] * 2,
        out_specs=[columns(length)] * 2,
        out_shape=[jax.ShapeDtypeStruct((length, total), bf16)] * 2,
        name="outer",
        **params(8 * length * total * HEAD, 20 * length * total),
    )(key_part, value_part, keys, values, k_spikes, high, low)


def halves(state):
    high = state.astype(bf16)
    return high, (state - high.astype(f32)).astype(bf16)


def scan_any(own, sent, count, reverse):
    place = lax.axis_index(CTX)
    total = own
    state = jnp.zeros_like(own)
    bits = count.bit_length() - 1
    for bit in range(bits):
        step = 1 << bit
        last = bit == bits - 1
        pairs = []
        for source in range(count):
            high = bool(source & step)
            if not last or high == reverse:
                pairs.append((source, source ^ step))
        got = lax.ppermute(sent, CTX, pairs).astype(f32)
        if last:
            state = state + got
        else:
            mine = ((place // step) % 2) == (0 if reverse else 1)
            state = state + jnp.where(mine, got, 0.0)
            total = total + got
            sent = total.astype(bf16)
    return state


def links(first, keep=lambda source, target: True):
    pairs = []
    for chip in range(4):
        for core in range(2):
            other = chip ^ (first if core == 0 else 3 - first)
            if keep((chip, core), other):
                pairs.append((chip * 2 + core, other * 2 + core))
    return pairs


def scan_four(own, sent, reverse):
    chip, core = lax.axis_index("chip"), lax.axis_index("core")
    low_bit = 1 - chip % 2 if reverse else chip % 2
    flip = 3 if reverse else 0
    half = own.shape[0] // 2
    sibling = lax.ppermute(sent, "core", SWAP)
    both = own + sibling.astype(f32)
    both = jnp.where(core == 0, both[:half], both[half:])

    def upward(source, target):
        at = source[0] ^ flip
        crossing = source[0] ^ target
        return crossing == 1 or not at & 2

    got = lax.ppermute(both.astype(bf16), CTX, links(1, upward)).astype(f32)
    first = jnp.where((core == 1) | (low_bit == 1), got, 0.0)
    message = got + jnp.where((core == 0) | (low_bit == 0), both, 0.0)
    more = lax.ppermute(message.astype(bf16), CTX, links(2, upward)).astype(f32)
    state = first + more
    other = lax.ppermute(state, "core", SWAP)
    whole = jnp.concatenate(
        [jnp.where(core == 0, state, other), jnp.where(core == 0, other, state)], axis=0
    )
    return whole + jnp.where(core == (0 if reverse else 1), sibling.astype(f32), 0.0)


def scan_sum(own, sent, chips, reverse):
    if chips == 4:
        return halves(scan_four(own, sent, reverse))
    return halves(scan_any(own, sent, chips * 2, reverse))


def gather_any(q_weight):
    whole = lax.all_gather(q_weight, ("chip", "core", "dp"), axis=0, tiled=True)
    cut = whole.shape[0] // (2 * PIECE) * PIECE
    number = whole.shape[0] // PIECE
    return [whole[:cut], whole[cut:]], jnp.arange(number, dtype=jnp.int32)


def place_of(chip, side, layer):
    return [(chip * 2 + side) * 4 + one for one in layer]


def crossed(side):
    return (0, 1 + side, 2 - side, 3)


def per_device(tokens, key_input, values, q_weight, q_spikes, k_spikes, cotangent):
    batches, length, width = tokens.shape
    assert batches == 1
    total = q_weight.shape[1]
    chips, spread = lax.axis_size("chip"), lax.axis_size("dp")
    factor = 3.0 / math.sqrt(HEAD * length * chips * 2)
    tokens, key_input, values, q_spikes, k_spikes, cotangent = (
        array.reshape(length, array.shape[2])
        for array in (tokens, key_input, values, q_spikes, k_spikes, cotangent)
    )
    special = chips == 4 and spread == 4

    def sibling(array):
        return lax.ppermute(array, "core", SWAP)

    if special:
        chip, core, layer = (lax.axis_index(name) for name in ("chip", "core", "dp"))
        layered = lax.all_gather(q_weight, "dp", axis=0)
        first = lax.ppermute(q_weight, CTX, links(1))
        second = lax.ppermute(q_weight, CTX, links(2))
        other = sibling(q_weight)
        after = other
    else:
        arrived, places = gather_any(q_weight)
        after = q_weight
    keys, own, sent = memory_call(key_input, k_spikes, values, after)
    high, low = scan_sum(own, sent, chips, False)
    masked = masked_call(factor, cotangent, values, keys, q_spikes, high, low)

    def products(places, blocks, partial, grad_tokens):
        return (
            project_call(places, tokens, blocks, partial),
            back_call(places, blocks, masked, grad_tokens, width),
        )

    if special:
        third = lax.ppermute(first, CTX, links(2))
        around = [(layer + turn) % 4 for turn in range(1, 4)]
        rest = jnp.concatenate(
            [lax.dynamic_index_in_dim(layered, one, 0, False) for one in around], axis=0
        )
        rest_first = lax.ppermute(rest, CTX, links(1))
        rest_second = lax.ppermute(rest, CTX, links(2))
        mine = [q_weight, first, second, third]
        early = mine + [other] + [sibling(one) for one in mine[1:]] + [rest, sibling(rest)]
        sides = (core, 1 - core)
        places = [
            place
            for side in sides
            for flip in crossed(side)
            for place in place_of(chip ^ flip, side, [layer])
        ]
        places += [place for side in sides for place in place_of(chip, side, around)]
        middle_places = [
            place
            for side in sides
            for flip in crossed(side)[1:3]
            for place in place_of(chip ^ flip, side, around)
        ]
        late_places = [place for side in sides for place in place_of(chip ^ 3, side, around)]
        places, middle_places, late_places = (
            jnp.stack(some).astype(jnp.int32) for some in (places, middle_places, late_places)
        )
        partial, grad_tokens = products(places, early, None, None)
        rest_first = tie(rest_first, partial, grad_tokens)
        rest_third = lax.ppermute(rest_first, CTX, links(2))
        mine = [rest_first, rest_second]
        partial, grad_tokens = products(
            middle_places, mine + [sibling(one) for one in mine], partial, grad_tokens
        )
        rest_third = tie(rest_third, partial, grad_tokens)
        late = [rest_third, sibling(rest_third)]
    else:
        half = places.shape[0] // 2
        partial, grad_tokens = products(places[:half], arrived[:1], None, None)
        late, late_places = arrived[1:], places[half:]
    queries, own, sent = query_call(late_places, tokens, late, partial, q_spikes, cotangent)
    adjoint = scan_sum(own, sent, chips, True)
    attended, key_part, value_part = inner_call(
        factor, queries, keys, values, cotangent, high, low
    )
    grad_tokens = back_call(late_places, late, masked, grad_tokens, width)
    grad_keys, grad_values = outer_call(
        factor, key_part, value_part, keys, values, k_spikes, *adjoint
    )
    return tuple(
        array.reshape(1, length, array.shape[1])
        for array in (attended, grad_tokens, grad_keys, grad_values)
    )


def solution(mesh):
    count, spread = mesh.shape["ctx"], mesh.shape["dp"]
    fine = Mesh(mesh.devices.reshape(count // 2, 2, spread), ("chip", "core", "dp"))
    block = P("dp", CTX, None)
    rows = P(("chip", "core", "dp"), None)
    in_specs = (block, block, block, rows, block, block, block)
    return jax.shard_map(
        per_device, mesh=fine, in_specs=in_specs, out_specs=(block,) * 4, check_vma=False
    )
```

profile of v0, /device:TPU:1, one launch (start us, length us, event | category | flops | bytes accessed | tf_op | source)
XLA Modules:
  0.0 195.9 jit_solution(17550686458656432903)
XLA Ops:
  8.0 2.1 %collective-permute-done.4.refs_19_.after_ref.refs_4_ = bf16[128,2048]{1,0:T(8,128)(2,1)S(1)} collective-permute-done((bf16[128,2048]{1,0:T(8,128)(2,1)}, bf16[128,2048]{1,0:T(8,128)(2,1)S(1)}, u32[]{:S(2)}, u32[]{:S(2)}) %collective-permute-start.4) | collective-permute-done | bytes 524320 | tf_op jit(solution)/shard_map/ppermute | solution.py:463
  10.9 5.1 %own_memory.1 = (bf16[384,2048]{1,0:T(8,128)(2,1)}, f32[2048,128]{1,0:T(8,128)}, bf16[2048,128]{1,0:T(8,128)(2,1)}) custom-call(bf16[384,2048]{1,0:T(8,128)(2,1)} %bitcast.93, s32[384,2048]{1,0:T(8,128)} %bitcast.88, bf16[384,2048]{1,0:T(8,128)(2,1)} %bitcast.82, bf16[128,2048]{1,0:T(8,128)(2,1)} %copy-done.6), custom_call_target="tpu_custom_call" | custom-call | flops 201326592 | bytes 9437184 | tf_op jit(solution)/shard_map/own_memory/pallas_call | solution.py:63
  16.1 2.0 %collective-permute-done.9 = bf16[2048,128]{1,0:T(8,128)(2,1)S(1)} collective-permute-done((bf16[2048,128]{1,0:T(8,128)(2,1)}, bf16[2048,128]{1,0:T(8,128)(2,1)S(1)}, u32[]{:S(2)}, u32[]{:S(2)}) %collective-permute-start.9) | collective-permute-done | bytes 524320 | tf_op jit(solution)/shard_map/ppermute | solution.py:408
  18.1 1.6 convert_add_fusion.1
  19.7 4.3 %collective-permute-start.10 = (bf16[1024,128]{1,0:T(8,128)(2,1)S(1)}, bf16[1024,128]{1,0:T(8,128)(2,1)S(1)}, u32[]{:S(2)}, u32[]{:S(2)}) collective-permute-start(bf16[1024,128]{1,0:T(8,128)(2,1)S(1)} %fusion.8), channel_id=1, source_target_pairs={{0,8},{4,20},{8,0},{12,28},{16,24},{24,16},{1,9},{5,21},{9,1},{13,... | collective-permute-start | bytes 786440 | tf_op jit(solution)/shard_map/ppermute | solution.py:417
  24.1 1.3 collective-permute-start.2
  25.4 1.9 collective-permute-done.10
  27.4 3.1 %collective-permute-start.11 = (bf16[1024,128]{1,0:T(8,128)(2,1)S(1)}, bf16[1024,128]{1,0:T(8,128)(2,1)S(1)}, u32[]{:S(2)}, u32[]{:S(2)}) collective-permute-start(bf16[1024,128]{1,0:T(8,128)(2,1)S(1)} %fusion.3), channel_id=1, source_target_pairs={{0,16},{4,12},{8,24},{12,4},{20,28},{28,20},{1,17},{5,13},{9,25},{... | collective-permute-start | bytes 786440 | tf_op jit(solution)/shard_map/ppermute | solution.py:420
  30.5 27.1 %all-gather.3.cloned.1.call-done = bf16[512,2048]{1,0:T(8,128)(2,1)} async-done(((bf16[128,2048]{1,0:T(8,128)(2,1)}), bf16[512,2048]{1,0:T(8,128)(2,1)}) %all-gather.3.cloned.1.call-update) | async-done | bytes 2097168 | tf_op jit(solution)/shard_map/all_gather | solution.py:467
  57.6 1.5 dynamic-slice_bitcast_fusion.2
  62.6 1.8 collective-permute-done.12
  67.0 1.3 broadcast_select_fusion.3
  68.3 3.9 %collective-permute-done.3.refs_18_.refs_3_ = bf16[128,2048]{1,0:T(8,128)(2,1)} collective-permute-done((bf16[128,2048]{1,0:T(8,128)(2,1)}, bf16[128,2048]{1,0:T(8,128)(2,1)}, u32[]{:S(2)}, u32[]{:S(2)}) %collective-permute-start.3) | collective-permute-done | bytes 524320 | tf_op jit(solution)/shard_map/ppermute | solution.py:486
  72.2 2.7 %collective-permute-start.6 = (bf16[128,2048]{1,0:T(8,128)(2,1)}, bf16[128,2048]{1,0:T(8,128)(2,1)S(1)}, u32[]{:S(2)}, u32[]{:S(2)}) collective-permute-start(bf16[128,2048]{1,0:T(8,128)(2,1)} %collective-permute-done.2.refs_17_.refs_2_), channel_id=1, source_target_pairs={{0,4},{4,0},{1,5},{5,1},{2,6},{6,2},{3,7},{7,3},{8,12},{12,8},{9,1... | collective-permute-start | bytes 1572872 | tf_op jit(solution)/shard_map/ppermute | solution.py:463
  76.1 7.4 %masked_grad.1.refs_10_.refs_4_.refs_2_ = bf16[384,2048]{1,0:T(8,128)(2,1)} custom-call(bf16[384,2048]{1,0:T(8,128)(2,1)} %bitcast.90, bf16[384,2048]{1,0:T(8,128)(2,1)} %bitcast.83, bf16[384,2048]{1,0:T(8,128)(2,1)} %get-tuple-element.15.keys_ref, s32[384,2048]{1,0:T(8,128)} %bitcast.86, bf16[2048,128]{1,0:T(8,128)(2,1)} %get-tuple-element.32.high_ref, ...), custom_call_target="tpu_custom_call" | custom-call | flops 2415919104 | bytes 9437184 | tf_op jit(solution)/shard_map/masked_grad/pallas_call | solution.py:138
  84.3 8.8 %grad_tokens.3.refs_2_.refs_5_ = bf16[384,4096]{1,0:T(8,128)(2,1)} custom-call(s32[14]{0:T(128)} %stack.126.refs_0_.places_ref, bf16[128,2048]{1,0:T(8,128)(2,1)} %refs_0_.1, bf16[128,2048]{1,0:T(8,128)(2,1)} %collective-permute-done.1.refs_16_.refs_1_, bf16[128,2048]{1,0:T(8,128)(2,1)} %collective-permute-done.2.refs_17_.refs_2_, ...), custom_call_target="tpu_custom_call" | custom-call | flops 2818572288 | bytes 10485760 | tf_op jit(solution)/shard_map/grad_tokens/pallas_call | solution.py:279
  93.1 8.6 %project.2.refs_1_.refs_17_ = f32[384,2048]{1,0:T(8,128)} custom-call(s32[14]{0:T(128)} %stack.126.refs_0_.places_ref, bf16[384,4096]{1,0:T(8,128)(2,1)} %bitcast.49, bf16[384,4096]{1,0:T(8,128)(2,1)} %bitcast.50, bf16[384,4096]{1,0:T(8,128)(2,1)} %bitcast.51, bf16[384,4096]{1,0:T(8,128)(2,1)} %bitcast.52, bf16[384,4096]{1,0:T(8,128)(2,1)} %bitcast.53, ...), custom_call_target="tpu_custom_call" | custom-call | flops 2818572288 | bytes 13631488 | tf_op jit(solution)/shard_map/project/pallas_call | solution.py:187
  106.6 2.4 %collective-permute-done.16.refs_16_.refs_3_ = bf16[384,2048]{1,0:T(8,128)(2,1)} collective-permute-done((bf16[384,2048]{1,0:T(8,128)(2,1)}, bf16[384,2048]{1,0:T(8,128)(2,1)}, u32[]{:S(2)}, u32[]{:S(2)}) %collective-permute-start.16) | collective-permute-done | bytes 1572896 | tf_op jit(solution)/shard_map/ppermute | solution.py:463
  109.0 8.0 %grad_tokens.4.refs_2_.refs_3_ = bf16[384,4096]{1,0:T(8,128)(2,1)} custom-call(s32[12]{0:T(128)} %stack.139.refs_0_.places_ref, bf16[384,2048]{1,0:T(8,128)(2,1)} %tie.2.refs_13_.refs_0_, bf16[384,2048]{1,0:T(8,128)(2,1)} %collective-permute-done.14.refs_14_.refs_1_, bf16[384,2048]{1,0:T(8,128)(2,1)} %copy-done.4, ...), custom_call_target="tpu_custom_call", output_to_operand_aliasing={{}: (6, {})} | custom-call | flops 2415919104 | bytes 9437184 | tf_op jit(solution)/shard_map/grad_tokens/pallas_call | solution.py:279
  116.9 8.6 %project.3.refs_1_.refs_9_ = f32[384,2048]{1,0:T(8,128)} custom-call(s32[12]{0:T(128)} %stack.139.refs_0_.places_ref, bf16[384,4096]{1,0:T(8,128)(2,1)} %bitcast.64, bf16[384,4096]{1,0:T(8,128)(2,1)} %bitcast.63, bf16[384,4096]{1,0:T(8,128)(2,1)} %bitcast.65, bf16[384,4096]{1,0:T(8,128)(2,1)} %bitcast.66, ...), custom_call_target="tpu_custom_call", output_to_operand_aliasing={{}: (17, {})} | custom-call | flops 2415919104 | bytes 12582912 | tf_op jit(solution)/shard_map/project/pallas_call | solution.py:187
  127.7 2.6 %collective-permute-done.17.refs_8_.refs_1_ = bf16[384,2048]{1,0:T(8,128)(2,1)S(1)} collective-permute-done((bf16[384,2048]{1,0:T(8,128)(2,1)}, bf16[384,2048]{1,0:T(8,128)(2,1)S(1)}, u32[]{:S(2)}, u32[]{:S(2)}) %collective-permute-start.17) | collective-permute-done | bytes 1572896 | tf_op jit(solution)/shard_map/ppermute | solution.py:463
  131.5 8.4 %queries.1 = (bf16[384,2048]{1,0:T(8,128)(2,1)}, f32[2048,128]{1,0:T(8,128)}, bf16[2048,128]{1,0:T(8,128)(2,1)}) custom-call(s32[6]{0:T(128)} %stack.111.refs_0_.places_ref, bf16[384,4096]{1,0:T(8,128)(2,1)} %bitcast.75, bf16[384,4096]{1,0:T(8,128)(2,1)} %bitcast.76, bf16[384,4096]{1,0:T(8,128)(2,1)} %bitcast.77, bf16[384,4096]{1,0:T(8,128)(2,1)} %bitcast.78, ...), custom_call_target="tpu_custom_call" | custom-call | flops 1207959552 | bytes 12582912 | tf_op jit(solution)/shard_map/queries/pallas_call | solution.py:223
  140.3 1.7 collective-permute-done.18
  142.0 1.3 convert_add_fusion
  143.4 1.3 collective-permute-start.19
  144.7 6.9 %collective-permute-done.19 = bf16[1024,128]{1,0:T(8,128)(2,1)S(1)} collective-permute-done((bf16[1024,128]{1,0:T(8,128)(2,1)S(1)}, bf16[1024,128]{1,0:T(8,128)(2,1)S(1)}, u32[]{:S(2)}, u32[]{:S(2)}) %collective-permute-start.19) | collective-permute-done | bytes 262176 | tf_op jit(solution)/shard_map/ppermute | solution.py:417
  151.7 3.3 %collective-permute-start.20 = (bf16[1024,128]{1,0:T(8,128)(2,1)S(1)}, bf16[1024,128]{1,0:T(8,128)(2,1)S(1)}, u32[]{:S(2)}, u32[]{:S(2)}) collective-permute-start(bf16[1024,128]{1,0:T(8,128)(2,1)S(1)} %fusion.5), channel_id=1, source_target_pairs={{4,12},{12,4},{16,0},{20,28},{24,8},{28,20},{5,13},{13,5},{17,1},{... | collective-permute-start | bytes 786440 | tf_op jit(solution)/shard_map/ppermute | solution.py:420
  155.0 4.1 %collective-permute-done.20 = bf16[1024,128]{1,0:T(8,128)(2,1)S(1)} collective-permute-done((bf16[1024,128]{1,0:T(8,128)(2,1)S(1)}, bf16[1024,128]{1,0:T(8,128)(2,1)S(1)}, u32[]{:S(2)}, u32[]{:S(2)}) %collective-permute-start.20) | collective-permute-done | bytes 262176 | tf_op jit(solution)/shard_map/ppermute | solution.py:420
  159.1 1.9 collective-permute-start.21
  161.0 6.0 %grad_tokens.5 = bf16[384,4096]{1,0:T(8,128)(2,1)} custom-call(s32[6]{0:T(128)} %stack.111.refs_0_.places_ref, bf16[384,2048]{1,0:T(8,128)(2,1)} %tie.3.refs_7_.refs_0_, bf16[384,2048]{1,0:T(8,128)(2,1)} %copy-done.3, bf16[384,2048]{1,0:T(8,128)(2,1)} %masked_grad.1.refs_10_.refs_4_.refs_2_, ...), custom_call_target="tpu_custom_call", output_to_operand_aliasing={{}: (4, {})} | custom-call | flops 1207959552 | bytes 6291456 | tf_op jit(solution)/shard_map/grad_tokens/pallas_call | solution.py:279
  167.0 13.1 %inner.1 = (bf16[384,2048]{1,0:T(8,128)(2,1)}, f32[384,2048]{1,0:T(8,128)}, f32[384,2048]{1,0:T(8,128)}) custom-call(bf16[384,2048]{1,0:T(8,128)(2,1)} %get-tuple-element.18.query_ref, bf16[384,2048]{1,0:T(8,128)(2,1)} %get-tuple-element.15.keys_ref, bf16[384,2048]{1,0:T(8,128)(2,1)} %bitcast.84, bf16[384,2048]{1,0:T(8,128)(2,1)} %bitcast.92, ...), custom_call_target="tpu_custom_call" | custom-call | flops 4831838208 | bytes 14155776 | tf_op jit(solution)/shard_map/inner/pallas_call | solution.py:323
  181.4 7.6 %outer.1 = (bf16[384,2048]{1,0:T(8,128)(2,1)}, bf16[384,2048]{1,0:T(8,128)(2,1)}) custom-call(f32[384,2048]{1,0:T(8,128)} %get-tuple-element.20.key_ref, f32[384,2048]{1,0:T(8,128)} %get-tuple-element.21.val_ref, bf16[384,2048]{1,0:T(8,128)(2,1)} %get-tuple-element.15.keys_ref, bf16[384,2048]{1,0:T(8,128)(2,1)} %bitcast.85, s32[384,2048]{1,0:T(8,128)} %bitcast.89, ...), custom_call_target="tpu_custom_call" | custom-call | flops 805306368 | bytes 15728640 | tf_op jit(solution)/shard_map/outer/pallas_call | solution.py:353
  (68 shorter events, 20.2 us)
Async XLA Ops:
  7.2 50.5 %all-gather.3.cloned.1.call-start = ((), (), s32[]{:S(2)}) async-start(), calls=%async_computation | async-start | bytes 2621440 | tf_op jit(solution)/shard_map/all_gather | solution.py:467
  7.9 2.2 %collective-permute-start.4 = (bf16[128,2048]{1,0:T(8,128)(2,1)}, bf16[128,2048]{1,0:T(8,128)(2,1)S(1)}, u32[]{:S(2)}, u32[]{:S(2)}) collective-permute-start(bf16[128,2048]{1,0:T(8,128)(2,1)} %refs_0_.1), channel_id=1, source_target_pairs={{0,4},{4,0},{1,5},{5,1},{2,6},{6,2},{3,7},{7,3},{8,12},{12,8},{9,1... | collective-permute-start | bytes 1572872 | tf_op jit(solution)/shard_map/ppermute | solution.py:463
  16.0 2.1 %collective-permute-start.9 = (bf16[2048,128]{1,0:T(8,128)(2,1)}, bf16[2048,128]{1,0:T(8,128)(2,1)S(1)}, u32[]{:S(2)}, u32[]{:S(2)}) collective-permute-start(bf16[2048,128]{1,0:T(8,128)(2,1)} %get-tuple-element.17), channel_id=1, source_target_pairs={{0,4},{4,0},{1,5},{5,1},{2,6},{6,2},{3,7},{7,3},{8,12},{12,8},{9,1... | collective-permute-start | bytes 1572872 | tf_op jit(solution)/shard_map/ppermute | solution.py:408
  18.1 1.6 copy-start.9
  18.1 6.0 %copy-start.5 = (bf16[128,2048]{1,0:T(8,128)(2,1)S(1)}, bf16[128,2048]{1,0:T(8,128)(2,1)}, u32[]{:S(2)}) copy-start(bf16[128,2048]{1,0:T(8,128)(2,1)} %refs_0_.1) | copy-start | bytes 1572868
  19.7 7.6 %collective-permute-start.10 = (bf16[1024,128]{1,0:T(8,128)(2,1)S(1)}, bf16[1024,128]{1,0:T(8,128)(2,1)S(1)}, u32[]{:S(2)}, u32[]{:S(2)}) collective-permute-start(bf16[1024,128]{1,0:T(8,128)(2,1)S(1)} %fusion.8), channel_id=1, source_target_pairs={{0,8},{4,20},{8,0},{12,28},{16,24},{24,16},{1,9},{5,21},{9,1},{13,... | collective-permute-start | bytes 786440 | tf_op jit(solution)/shard_map/ppermute | solution.py:417
  24.0 36.1 %collective-permute-start.1 = (bf16[128,2048]{1,0:T(8,128)(2,1)S(1)}, bf16[128,2048]{1,0:T(8,128)(2,1)}, u32[]{:S(2)}, u32[]{:S(2)}) collective-permute-start(bf16[128,2048]{1,0:T(8,128)(2,1)S(1)} %copy-done.5), channel_id=1, source_target_pairs={{0,8},{4,20},{8,0},{12,28},{16,24},{20,4},{24,16},{28,12},{1,9},{5... | collective-permute-start | bytes 1572872 | tf_op jit(solution)/shard_map/ppermute | solution.py:468
  24.1 38.0 %collective-permute-start.2 = (bf16[128,2048]{1,0:T(8,128)(2,1)S(1)}, bf16[128,2048]{1,0:T(8,128)(2,1)}, u32[]{:S(2)}, u32[]{:S(2)}) collective-permute-start(bf16[128,2048]{1,0:T(8,128)(2,1)S(1)} %copy-done.5), channel_id=1, source_target_pairs={{0,16},{4,12},{8,24},{12,4},{16,0},{20,28},{24,8},{28,20},{1,17},{... | collective-permute-start | bytes 1572872 | tf_op jit(solution)/shard_map/ppermute | solution.py:469
  27.4 32.5 %collective-permute-start.11 = (bf16[1024,128]{1,0:T(8,128)(2,1)S(1)}, bf16[1024,128]{1,0:T(8,128)(2,1)S(1)}, u32[]{:S(2)}, u32[]{:S(2)}) collective-permute-start(bf16[1024,128]{1,0:T(8,128)(2,1)S(1)} %fusion.3), channel_id=1, source_target_pairs={{0,16},{4,12},{8,24},{12,4},{20,28},{28,20},{1,17},{5,13},{9,25},{... | collective-permute-start | bytes 786440 | tf_op jit(solution)/shard_map/ppermute | solution.py:420
  59.2 9.1 %copy-start = (bf16[384,2048]{1,0:T(8,128)(2,1)}, bf16[384,2048]{1,0:T(8,128)(2,1)S(1)}, u32[]{:S(2)}) copy-start(bf16[384,2048]{1,0:T(8,128)(2,1)S(1)} %pad_maximum_fusion.refs_23_.refs_8_) | copy-start | bytes 4718596
  59.2 24.3 %collective-permute-start.8 = (bf16[384,2048]{1,0:T(8,128)(2,1)S(1)}, bf16[384,2048]{1,0:T(8,128)(2,1)}, u32[]{:S(2)}, u32[]{:S(2)}) collective-permute-start(bf16[384,2048]{1,0:T(8,128)(2,1)S(1)} %pad_maximum_fusion.refs_23_.refs_8_), channel_id=1, source_target_pairs={{0,4},{4,0},{1,5},{5,1},{2,6},{6,2},{3,7},{7,3},{8,12},{12,8},{9,1... | collective-permute-start | bytes 4718600 | tf_op jit(solution)/shard_map/ppermute | solution.py:463
  60.0 2.5 %copy-start.8 = (f32[1024,128]{1,0:T(8,128)}, f32[1024,128]{1,0:T(8,128)S(1)}, u32[]{:S(2)}) copy-start(f32[1024,128]{1,0:T(8,128)S(1)} %fusion.2) | copy-start | bytes 1572868
  60.0 4.3 %collective-permute-start.12 = (f32[1024,128]{1,0:T(8,128)S(1)}, f32[1024,128]{1,0:T(8,128)S(1)}, u32[]{:S(2)}, u32[]{:S(2)}) collective-permute-start(f32[1024,128]{1,0:T(8,128)S(1)} %fusion.2), channel_id=1, source_target_pairs={{0,4},{4,0},{1,5},{5,1},{2,6},{6,2},{3,7},{7,3},{8,12},{12,8},{9,1... | collective-permute-start | bytes 1572872 | tf_op jit(solution)/shard_map/ppermute | solution.py:422
  60.1 12.1 %collective-permute-start.3 = (bf16[128,2048]{1,0:T(8,128)(2,1)}, bf16[128,2048]{1,0:T(8,128)(2,1)}, u32[]{:S(2)}, u32[]{:S(2)}) collective-permute-start(bf16[128,2048]{1,0:T(8,128)(2,1)} %collective-permute-done.1.refs_16_.refs_1_), channel_id=1, source_target_pairs={{0,16},{4,12},{8,24},{12,4},{16,0},{20,28},{24,8},{28,20},{1,17},{... | collective-permute-start | bytes 1572872 | tf_op jit(solution)/shard_map/ppermute | solution.py:486
  61.4 13.6 %collective-permute-start.5 = (bf16[128,2048]{1,0:T(8,128)(2,1)}, bf16[128,2048]{1,0:T(8,128)(2,1)}, u32[]{:S(2)}, u32[]{:S(2)}) collective-permute-start(bf16[128,2048]{1,0:T(8,128)(2,1)} %collective-permute-done.1.refs_16_.refs_1_), channel_id=1, source_target_pairs={{0,4},{4,0},{1,5},{5,1},{2,6},{6,2},{3,7},{7,3},{8,12},{12,8},{9,1... | collective-permute-start | bytes 1572872 | tf_op jit(solution)/shard_map/ppermute | solution.py:463
  62.1 39.6 %collective-permute-start = (bf16[384,2048]{1,0:T(8,128)(2,1)S(1)}, bf16[384,2048]{1,0:T(8,128)(2,1)S(1)}, u32[]{:S(2)}, u32[]{:S(2)}) collective-permute-start(bf16[384,2048]{1,0:T(8,128)(2,1)S(1)} %pad_maximum_fusion.refs_23_.refs_8_), channel_id=1, source_target_pairs={{0,8},{4,20},{8,0},{12,28},{16,24},{20,4},{24,16},{28,12},{1,9},{5... | collective-permute-start | bytes 4718600 | tf_op jit(solution)/shard_map/ppermute | solution.py:491
  65.2 38.2 %collective-permute-start.14 = (bf16[384,2048]{1,0:T(8,128)(2,1)S(1)}, bf16[384,2048]{1,0:T(8,128)(2,1)}, u32[]{:S(2)}, u32[]{:S(2)}) collective-permute-start(bf16[384,2048]{1,0:T(8,128)(2,1)S(1)} %pad_maximum_fusion.refs_23_.refs_8_), channel_id=1, source_target_pairs={{0,16},{4,12},{8,24},{12,4},{16,0},{20,28},{24,8},{28,20},{1,17},{... | collective-permute-start | bytes 4718600 | tf_op jit(solution)/shard_map/ppermute | solution.py:492
  67.0 8.0 %copy-start.10 = (bf16[2048,128]{1,0:T(8,128)(2,1)S(1)}, bf16[2048,128]{1,0:T(8,128)(2,1)}, u32[]{:S(2)}) copy-start(bf16[2048,128]{1,0:T(8,128)(2,1)} %copy-done.9) | copy-start | bytes 1572868
  72.2 11.3 %collective-permute-start.6 = (bf16[128,2048]{1,0:T(8,128)(2,1)}, bf16[128,2048]{1,0:T(8,128)(2,1)S(1)}, u32[]{:S(2)}, u32[]{:S(2)}) collective-permute-start(bf16[128,2048]{1,0:T(8,128)(2,1)} %collective-permute-done.2.refs_17_.refs_2_), channel_id=1, source_target_pairs={{0,4},{4,0},{1,5},{5,1},{2,6},{6,2},{3,7},{7,3},{8,12},{12,8},{9,1... | collective-permute-start | bytes 1572872 | tf_op jit(solution)/shard_map/ppermute | solution.py:463
  75.0 8.5 %collective-permute-start.7 = (bf16[128,2048]{1,0:T(8,128)(2,1)}, bf16[128,2048]{1,0:T(8,128)(2,1)}, u32[]{:S(2)}, u32[]{:S(2)}) collective-permute-start(bf16[128,2048]{1,0:T(8,128)(2,1)} %collective-permute-done.3.refs_18_.refs_3_), channel_id=1, source_target_pairs={{0,4},{4,0},{1,5},{5,1},{2,6},{6,2},{3,7},{7,3},{8,12},{12,8},{9,1... | collective-permute-start | bytes 1572872 | tf_op jit(solution)/shard_map/ppermute | solution.py:463
  101.7 1.1 copy-start.1
  102.8 3.8 %collective-permute-start.15 = (bf16[384,2048]{1,0:T(8,128)(2,1)}, bf16[384,2048]{1,0:T(8,128)(2,1)S(1)}, u32[]{:S(2)}, u32[]{:S(2)}) collective-permute-start(bf16[384,2048]{1,0:T(8,128)(2,1)} %tie.2.refs_13_.refs_0_), channel_id=1, source_target_pairs={{0,4},{4,0},{1,5},{5,1},{2,6},{6,2},{3,7},{7,3},{8,12},{12,8},{9,1... | collective-permute-start | bytes 4718600 | tf_op jit(solution)/shard_map/ppermute | solution.py:463
  103.3 5.6 %collective-permute-start.16 = (bf16[384,2048]{1,0:T(8,128)(2,1)}, bf16[384,2048]{1,0:T(8,128)(2,1)}, u32[]{:S(2)}, u32[]{:S(2)}) collective-permute-start(bf16[384,2048]{1,0:T(8,128)(2,1)} %collective-permute-done.14.refs_14_.refs_1_), channel_id=1, source_target_pairs={{0,4},{4,0},{1,5},{5,1},{2,6},{6,2},{3,7},{7,3},{8,12},{12,8},{9,1... | collective-permute-start | bytes 4718600 | tf_op jit(solution)/shard_map/ppermute | solution.py:463
  103.8 21.7 %collective-permute-start.13 = (bf16[384,2048]{1,0:T(8,128)(2,1)}, bf16[384,2048]{1,0:T(8,128)(2,1)S(1)}, u32[]{:S(2)}, u32[]{:S(2)}) collective-permute-start(bf16[384,2048]{1,0:T(8,128)(2,1)} %tie.2.refs_13_.refs_0_), channel_id=1, source_target_pairs={{0,16},{4,12},{8,24},{12,4},{16,0},{20,28},{24,8},{28,20},{1,17},{... | collective-permute-start | bytes 4718600 | tf_op jit(solution)/shard_map/ppermute | solution.py:515
  106.6 2.4 %copy-start.4 = (bf16[384,2048]{1,0:T(8,128)(2,1)}, bf16[384,2048]{1,0:T(8,128)(2,1)S(1)}, u32[]{:S(2)}) copy-start(bf16[384,2048]{1,0:T(8,128)(2,1)S(1)} %collective-permute-done.15.refs_15_.refs_2_) | copy-start | bytes 4718596
  125.6 1.1 copy-start.2
  126.7 3.6 %collective-permute-start.17 = (bf16[384,2048]{1,0:T(8,128)(2,1)}, bf16[384,2048]{1,0:T(8,128)(2,1)S(1)}, u32[]{:S(2)}, u32[]{:S(2)}) collective-permute-start(bf16[384,2048]{1,0:T(8,128)(2,1)} %tie.3.refs_7_.refs_0_), channel_id=1, source_target_pairs={{0,4},{4,0},{1,5},{5,1},{2,6},{6,2},{3,7},{7,3},{8,12},{12,8},{9,1... | collective-permute-start | bytes 4718600 | tf_op jit(solution)/shard_map/ppermute | solution.py:463
  130.3 1.1 copy-start.3
  139.9 2.2 %collective-permute-start.18 = (bf16[2048,128]{1,0:T(8,128)(2,1)}, bf16[2048,128]{1,0:T(8,128)(2,1)S(1)}, u32[]{:S(2)}, u32[]{:S(2)}) collective-permute-start(bf16[2048,128]{1,0:T(8,128)(2,1)} %get-tuple-element.23), channel_id=1, source_target_pairs={{0,4},{4,0},{1,5},{5,1},{2,6},{6,2},{3,7},{7,3},{8,12},{12,8},{9,1... | collective-permute-start | bytes 1572872 | tf_op jit(solution)/shard_map/ppermute | solution.py:408
  143.4 8.2 %collective-permute-start.19 = (bf16[1024,128]{1,0:T(8,128)(2,1)S(1)}, bf16[1024,128]{1,0:T(8,128)(2,1)S(1)}, u32[]{:S(2)}, u32[]{:S(2)}) collective-permute-start(bf16[1024,128]{1,0:T(8,128)(2,1)S(1)} %fusion.9), channel_id=1, source_target_pairs={{0,8},{8,0},{16,24},{20,4},{24,16},{28,12},{1,9},{9,1},{17,25},{21... | collective-permute-start | bytes 786440 | tf_op jit(solution)/shard_map/ppermute | solution.py:417
  151.7 7.4 %collective-permute-start.20 = (bf16[1024,128]{1,0:T(8,128)(2,1)S(1)}, bf16[1024,128]{1,0:T(8,128)(2,1)S(1)}, u32[]{:S(2)}, u32[]{:S(2)}) collective-permute-start(bf16[1024,128]{1,0:T(8,128)(2,1)S(1)} %fusion.5), channel_id=1, source_target_pairs={{4,12},{12,4},{16,0},{20,28},{24,8},{28,20},{5,13},{13,5},{17,1},{... | collective-permute-start | bytes 786440 | tf_op jit(solution)/shard_map/ppermute | solution.py:420
  159.1 21.0 %collective-permute-start.21 = (f32[1024,128]{1,0:T(8,128)S(1)}, f32[1024,128]{1,0:T(8,128)S(1)}, u32[]{:S(2)}, u32[]{:S(2)}) collective-permute-start(f32[1024,128]{1,0:T(8,128)S(1)} %fusion.4), channel_id=1, source_target_pairs={{0,4},{4,0},{1,5},{5,1},{2,6},{6,2},{3,7},{7,3},{8,12},{12,8},{9,1... | collective-permute-start | bytes 1572872 | tf_op jit(solution)/shard_map/ppermute | solution.py:422
  (3 other events, 2.4 us)
Sparse Core Ops, SparseCore 0:
  9.6 48.0 all-gather.2
where the time goes:
time: 197 us; the launch traced here: 196 us
  Pallas kernels  81.5 us (41%)
  waiting for transfers between devices  58.1 us (29%)
  starting transfers between devices  25.6 us (13%)
  between operations  14.3 us (7%)
  local copies, waits for them, and re-layouts  9.17 us (5%)
  other arithmetic  7.25 us (4%)
    all_gather x1, waiting for transfers between devices, per_device(): layered = lax.all_gather(q_weight, 'dp', axis=0)  27.1 us
    pallas_call x3, Pallas kernels, back_call(): pl.pallas_call(functools.partial(back_kernel, number, len(blocks), before...  22.7 us
    pallas_call x2, Pallas kernels, project_call(): pl.pallas_call(functools.partial(project_kernel, number, len(blocks), bef...  17.2 us
    pallas_call x1, Pallas kernels, inner_call(): pl.pallas_call(functools.partial(inner_kernel, factor), grid=(total // WI...  13.1 us
    ppermute x2, waiting for transfers between devices, scan_four(): got = lax.ppermute(both.astype(bf16), CTX, links(1, upward)).astype(f32)  8.77 us
    pallas_call x1, Pallas kernels, query_call(): pl.pallas_call(functools.partial(query_kernel, number, len(blocks)), grid...  8.38 us
    ppermute x8, waiting for transfers between devices, sibling(): return lax.ppermute(array, 'core', SWAP)  7.98 us
    pallas_call x1, Pallas kernels, outer_call(): pl.pallas_call(functools.partial(outer_kernel, factor), grid=(total // WI...  7.62 us
  transfers between devices with their start and end apart: 23, of which 12 were waited for; matrix products, arithmetic and copies ran while one was open for 4% of the time, Pallas kernels for 33%

commit v1 on v0

v1 whole, which is shorter than its diff:
```python
import functools
import math

import jax
import jax.numpy as jnp
from jax import lax
from jax.experimental import pallas as pl
from jax.experimental.pallas import tpu as pltpu
from jax.sharding import Mesh, PartitionSpec as P

HEAD = 128
PIECE = 128
WIDE = 512
CTX = ("chip", "core")
SWAP = [(0, 1), (1, 0)]
f32, bf16 = jnp.float32, jnp.bfloat16
VMEM_LIMIT = 26 * 1024 * 1024


def nn(a, b):
    return lax.dot_general(a, b, (((1,), (0,)), ((), ())), preferred_element_type=f32)


def nt(a, b):
    return lax.dot_general(a, b, (((1,), (1,)), ((), ())), preferred_element_type=f32)


def tn(a, b):
    return lax.dot_general(a, b, (((0,), (0,)), ((), ())), preferred_element_type=f32)


def params(flops, moved):
    return dict(
        compiler_params=pltpu.CompilerParams(vmem_limit_bytes=VMEM_LIMIT),
        cost_estimate=pl.CostEstimate(flops=flops, bytes_accessed=moved, transcendentals=0),
    )


def columns(length):
    return pl.BlockSpec((length, WIDE), lambda j: (0, j))


def states():
    return pl.BlockSpec((WIDE, HEAD), lambda j: (j, 0))


def anywhere():
    return pl.BlockSpec(memory_space=pl.ANY)


def memory_kernel(key_ref, spike_ref, value_ref, after_ref, keys_ref, own_ref, sent_ref):
    del after_ref
    keys = key_ref[...] * spike_ref[...].astype(f32).astype(bf16)
    keys_ref[...] = keys
    for at in range(0, WIDE, HEAD):
        own = tn(keys[:, at : at + HEAD], value_ref[:, at : at + HEAD])
        own_ref[at : at + HEAD, :] = own
        sent_ref[at : at + HEAD, :] = own.astype(bf16)


def memory_call(key_input, k_spikes, values, after):
    length, total = values.shape
    return pl.pallas_call(
        memory_kernel,
        grid=(total // WIDE,),
        in_specs=[columns(length)] * 3 + [anywhere()],
        out_specs=[columns(length), states(), states()],
        out_shape=[
            jax.ShapeDtypeStruct((length, total), bf16),
            jax.ShapeDtypeStruct((total, HEAD), f32),
            jax.ShapeDtypeStruct((total, HEAD), bf16),
        ],
        name="own_memory",
        **params(2 * length * total * HEAD, 12 * length * total),
    )(key_input, k_spikes, values, after)


def tie_kernel(*refs):
    del refs


def tie(array, *others):
    return pl.pallas_call(
        tie_kernel,
        in_specs=[anywhere()] * (1 + len(others)),
        out_specs=anywhere(),
        out_shape=jax.ShapeDtypeStruct(array.shape, array.dtype),
        input_output_aliases={0: 0},
        name="tie",
        **params(0, 0),
    )(array, *others)


def keep_lower(square, flipped=False):
    row = lax.broadcasted_iota(jnp.int32, square.shape, 0)
    col = lax.broadcasted_iota(jnp.int32, square.shape, 1)
    return jnp.where((col >= row) if flipped else (col <= row), square, 0.0).astype(bf16)


def causal(a, b):
    length = a.shape[0]
    cut = length - HEAD
    top = keep_lower(nt(a[:cut], b[:cut]))
    whole = nt(a[cut:], b)
    bottom = jnp.concatenate([whole[:, :cut].astype(bf16), keep_lower(whole[:, cut:])], axis=1)
    return [(slice(0, cut), slice(0, cut), top), (slice(cut, length), slice(0, length), bottom)]


def causal_turned(a, b):
    length = a.shape[0]
    whole = nt(a[:HEAD], b)
    top = jnp.concatenate(
        [keep_lower(whole[:, :HEAD], True), whole[:, HEAD:].astype(bf16)], axis=1
    )
    bottom = keep_lower(nt(a[HEAD:], b[HEAD:]), True)
    return [
        (slice(0, HEAD), slice(0, length), top),
        (slice(HEAD, length), slice(HEAD, length), bottom),
    ]


def twice(array):
    return jnp.concatenate([array, array], axis=1)


def masked_kernel(factor, grad_ref, value_ref, keys_ref, spike_ref, high_ref, low_ref, out_ref):
    for head in range(0, WIDE, HEAD):
        part = slice(head, head + HEAD)
        grad, value, keys = grad_ref[:, part], value_ref[:, part], keys_ref[:, part]
        state = jnp.concatenate([high_ref[part, :], low_ref[part, :]], axis=1)
        for rows, cols, scores in causal(grad, value):
            made = nn(scores, keys[cols]) + nt(twice(grad[rows]), state)
            out_ref[rows, part] = (factor * made * spike_ref[rows, part].astype(f32)).astype(bf16)


def masked_call(factor, cotangent, values, keys, q_spikes, high, low):
    length, total = values.shape
    return pl.pallas_call(
        functools.partial(masked_kernel, factor),
        grid=(total // WIDE,),
        in_specs=[columns(length)] * 4 + [states()] * 2,
        out_specs=columns(length),
        out_shape=jax.ShapeDtypeStruct((length, total), bf16),
        name="masked_grad",
        **params(8 * length * total * length, 12 * length * total),
    )(cotangent, values, keys, q_spikes, high, low)


class Copies:
    def __init__(self, sems):
        self.sems = sems
        self.used = 0

    def start(self, source, target):
        copy = pltpu.make_async_copy(source, target, self.sems.at[self.used])
        self.used += 1
        copy.start()
        return copy


def rows_of(blocks):
    return sum(block.shape[0] for block in blocks)


def spans(blocks):
    at = 0
    for block in blocks:
        yield block, at, block.shape[0]
        at += block.shape[0]


def load_rows(copies, blocks, w_ref):
    bring = []
    for block, at, rows in spans(blocks):
        copy = copies.start(block, w_ref.at[pl.ds(at, rows), :])
        bring += [copy] * (rows // PIECE)
    return bring


def load_tokens(copies, places_ref, tokens_ref, some_ref):
    bring = []
    for piece in range(some_ref.shape[1] // PIECE):
        place = pl.multiple_of(places_ref[piece] * PIECE, PIECE)
        bring.append(
            copies.start(
                tokens_ref.at[:, pl.ds(place, PIECE)], some_ref.at[:, pl.ds(piece * PIECE, PIECE)]
            )
        )
    return bring


def wait_once(copies, done):
    for copy in copies:
        if not any(copy is one for one in done):
            copy.wait()
            done.append(copy)


def back_part(copies, places_ref, masked, w_ref, bring, done, out_ref, round_ref):
    going = []
    for at in range(0, w_ref.shape[0], 2 * PIECE):
        wait_once(bring[at // PIECE : at // PIECE + 2], done)
        both = slice(at, at + 2 * PIECE)
        round_ref[:, both] = nt(masked[...], w_ref[both, :]).astype(bf16)
        for piece in (at // PIECE, at // PIECE + 1):
            place = pl.multiple_of(places_ref[piece] * PIECE, PIECE)
            going.append(
                copies.start(
                    round_ref.at[:, pl.ds(piece * PIECE, PIECE)],
                    out_ref.at[:, pl.ds(place, PIECE)],
                )
            )
    return going


def products_kernel(size, has_before, places_ref, tokens_ref, masked_ref, *refs):
    blocks = refs[:size]
    refs = refs[size:]
    if has_before:
        before_ref, _, *refs = refs
    sum_out, back_out, w_ref, some_ref, masked, sum_ref, round_ref, sems = refs
    copies = Copies(sems)
    mask_copy = copies.start(masked_ref, masked)
    bring = load_rows(copies, blocks, w_ref)
    token_copies = load_tokens(copies, places_ref, tokens_ref, some_ref)
    if has_before:
        token_copies.append(copies.start(before_ref, sum_ref))
    mask_copy.wait()
    done = []
    going = back_part(copies, places_ref, masked, w_ref, bring, done, back_out, round_ref)
    wait_once(token_copies, done)
    for at in range(0, w_ref.shape[1], WIDE):
        part = slice(at, at + WIDE)
        made = nn(some_ref[...], w_ref[:, part])
        if has_before:
            made = made + sum_ref[:, part]
        sum_ref[:, part] = made
        here = pl.ds(at, WIDE)
        going.append(copies.start(sum_ref.at[:, here], sum_out.at[:, here]))
    for copy in going:
        copy.wait()


def smem():
    return pl.BlockSpec(memory_space=pltpu.SMEM)


def products_call(places, tokens, blocks, masked, before):
    length, width = tokens.shape
    total = masked.shape[1]
    depth = rows_of(blocks)
    number = depth // PIECE
    extra = [] if before is None else list(before)
    return pl.pallas_call(
        functools.partial(products_kernel, len(blocks), before is not None),
        in_specs=[smem()] + [anywhere()] * (2 + len(blocks) + len(extra)),
        out_specs=[anywhere()] * 2,
        out_shape=[
            jax.ShapeDtypeStruct((length, total), f32),
            jax.ShapeDtypeStruct((length, width), bf16),
        ],
        scratch_shapes=[
            pltpu.VMEM((depth, total), bf16),
            pltpu.VMEM((length, depth), bf16),
            pltpu.VMEM((length, total), bf16),
            pltpu.VMEM((length, total), f32),
            pltpu.VMEM((length, depth), bf16),
            pltpu.SemaphoreType.DMA((len(blocks) + 2 * number + total // WIDE + 2,)),
        ],
        input_output_aliases={3 + len(blocks) + at: at for at in range(len(extra))},
        name="products",
        **params(4 * length * depth * total, depth * total * 2 + 8 * length * total),
    )(places, tokens, masked, *blocks, *extra)


def back_kernel(size, places_ref, masked_ref, *refs):
    blocks = refs[:size]
    _, back_out, w_ref, masked, round_ref, sems = refs[size:]
    copies = Copies(sems)
    mask_copy = copies.start(masked_ref, masked)
    bring = load_rows(copies, blocks, w_ref)
    mask_copy.wait()
    for copy in back_part(copies, places_ref, masked, w_ref, bring, [], back_out, round_ref):
        copy.wait()


def back_call(places, blocks, masked, before):
    length, total = masked.shape
    depth = rows_of(blocks)
    number = depth // PIECE
    return pl.pallas_call(
        functools.partial(back_kernel, len(blocks)),
        in_specs=[smem()] + [anywhere()] * (2 + len(blocks)),
        out_specs=anywhere(),
        out_shape=jax.ShapeDtypeStruct(before.shape, bf16),
        scratch_shapes=[
            pltpu.VMEM((depth, total), bf16),
            pltpu.VMEM((length, total), bf16),
            pltpu.VMEM((length, depth), bf16),
            pltpu.SemaphoreType.DMA((len(blocks) + number + 1,)),
        ],
        input_output_aliases={2 + len(blocks): 0},
        name="grad_tokens",
        **params(2 * length * depth * total, depth * total * 2 + 4 * length * total),
    )(places, masked, *blocks, before)


def query_kernel(size, places_ref, tokens_ref, before_ref, spike_ref, grad_ref, *refs):
    blocks = refs[:size]
    refs = refs[size:]
    query_out, own_out, sent_out, w_ref, some_ref, sum_ref, spikes, grads, *refs = refs
    queries, own_ref, sent_ref, sems = refs
    copies = Copies(sems)
    wide = range(0, w_ref.shape[1], WIDE)
    bring = load_tokens(copies, places_ref, tokens_ref, some_ref)
    bring += load_rows(copies, blocks, w_ref)
    inputs = ((before_ref, sum_ref), (spike_ref, spikes), (grad_ref, grads))
    parts = [
        [copies.start(here.at[:, pl.ds(at, WIDE)], there.at[:, pl.ds(at, WIDE)])
         for here, there in inputs]
        for at in wide
    ]
    wait_once(bring, [])
    going = []
    for at, part_copies in zip(wide, parts):
        part = slice(at, at + WIDE)
        made = nn(some_ref[...], w_ref[:, part])
        for copy in part_copies:
            copy.wait()
        made = ((made + sum_ref[:, part]) * spikes[:, part].astype(f32)).astype(bf16)
        queries[:, part] = made
        going.append(
            copies.start(queries.at[:, pl.ds(at, WIDE)], query_out.at[:, pl.ds(at, WIDE)])
        )
        for head in range(0, WIDE, HEAD):
            own = tn(made[:, head : head + HEAD], grads[:, at + head : at + head + HEAD])
            own_ref[at + head : at + head + HEAD, :] = own
            sent_ref[at + head : at + head + HEAD, :] = own.astype(bf16)
    going.append(copies.start(sent_ref, sent_out))
    going.append(copies.start(own_ref, own_out))
    for copy in going:
        copy.wait()


def query_call(places, tokens, blocks, before, q_spikes, cotangent):
    length = tokens.shape[0]
    total = blocks[0].shape[1]
    depth = rows_of(blocks)
    number = depth // PIECE
    steps = total // WIDE
    return pl.pallas_call(
        functools.partial(query_kernel, len(blocks)),
        in_specs=[smem()] + [anywhere()] * (4 + len(blocks)),
        out_specs=[anywhere()] * 3,
        out_shape=[
            jax.ShapeDtypeStruct((length, total), bf16),
            jax.ShapeDtypeStruct((total, HEAD), f32),
            jax.ShapeDtypeStruct((total, HEAD), bf16),
        ],
        scratch_shapes=[
            pltpu.VMEM((depth, total), bf16),
            pltpu.VMEM((length, depth), bf16),
            pltpu.VMEM((length, total), f32),
            pltpu.VMEM((length, total), jnp.int32),
            pltpu.VMEM((length, total), bf16),
            pltpu.VMEM((length, total), bf16),
            pltpu.VMEM((total, HEAD), f32),
            pltpu.VMEM((total, HEAD), bf16),
            pltpu.SemaphoreType.DMA((len(blocks) + number + 4 * steps + 2,)),
        ],
        name="queries",
        **params(2 * length * depth * total, depth * total * 2 + 12 * length * total),
    )(places, tokens, before, q_spikes, cotangent, *blocks)


def attend_kernel(factor, query_ref, keys_ref, value_ref, high_ref, low_ref, out_ref):
    for head in range(0, WIDE, HEAD):
        part = slice(head, head + HEAD)
        query, keys, value = query_ref[:, part], keys_ref[:, part], value_ref[:, part]
        state = [high_ref[part, :], low_ref[part, :]]
        for rows, cols, scores in causal(query, keys):
            made = nn(
                jnp.concatenate([scores, twice(query[rows])], axis=1),
                jnp.concatenate([value[cols], *state], axis=0),
            )
            out_ref[rows, part] = (factor * made).astype(bf16)


def attend_call(factor, queries, keys, values, high, low):
    length, total = values.shape
    return pl.pallas_call(
        functools.partial(attend_kernel, factor),
        grid=(total // WIDE,),
        in_specs=[columns(length)] * 3 + [states()] * 2,
        out_specs=columns(length),
        out_shape=jax.ShapeDtypeStruct((length, total), bf16),
        name="attended",
        **params(8 * length * total * length, 8 * length * total),
    )(queries, keys, values, high, low)


def inner_kernel(query_ref, keys_ref, value_ref, grad_ref, key_ref, val_ref):
    for head in range(0, WIDE, HEAD):
        part = slice(head, head + HEAD)
        query, keys = query_ref[:, part], keys_ref[:, part]
        value, grad = value_ref[:, part], grad_ref[:, part]
        for rows, cols, scores in causal_turned(keys, query):
            val_ref[rows, part] = nn(scores, grad[cols])
        for rows, cols, scores in causal_turned(value, grad):
            key_ref[rows, part] = nn(scores, query[cols])


def inner_call(queries, keys, values, cotangent):
    length, total = values.shape
    return pl.pallas_call(
        inner_kernel,
        grid=(total // WIDE,),
        in_specs=[columns(length)] * 4,
        out_specs=[columns(length)] * 2,
        out_shape=[jax.ShapeDtypeStruct((length, total), f32)] * 2,
        name="inner",
        **params(12 * length * total * length, 16 * length * total),
    )(queries, keys, values, cotangent)


def outer_kernel(
    factor, key_ref, val_ref, keys_ref, value_ref, spike_ref, high_ref, low_ref, gk_ref, gv_ref
):
    for head in range(0, WIDE, HEAD):
        part = slice(head, head + HEAD)
        keys, value = keys_ref[:, part], value_ref[:, part]
        state = [high_ref[part, :], low_ref[part, :]]
        key_grad = key_ref[:, part] + nt(twice(value), jnp.concatenate(state, axis=1))
        gk_ref[:, part] = (factor * key_grad * spike_ref[:, part].astype(f32)).astype(bf16)
        value_grad = val_ref[:, part] + nn(twice(keys), jnp.concatenate(state, axis=0))
        gv_ref[:, part] = (factor * value_grad).astype(bf16)


def outer_call(factor, key_part, value_part, keys, values, k_spikes, high, low):
    length, total = values.shape
    return pl.pallas_call(
        functools.partial(outer_kernel, factor),
        grid=(total // WIDE,),
        in_specs=[columns(length)] * 5 + [states()] * 2,
        out_specs=[columns(length)] * 2,
        out_shape=[jax.ShapeDtypeStruct((length, total), bf16)] * 2,
        name="outer",
        **params(8 * length * total * HEAD, 20 * length * total),
    )(key_part, value_part, keys, values, k_spikes, high, low)


def halves(state):
    high = state.astype(bf16)
    return high, (state - high.astype(f32)).astype(bf16)


def scan_any(own, sent, count, reverse):
    place = lax.axis_index(CTX)
    total = own
    state = jnp.zeros_like(own)
    bits = count.bit_length() - 1
    for bit in range(bits):
        step = 1 << bit
        last = bit == bits - 1
        pairs = []
        for source in range(count):
            high = bool(source & step)
            if not last or high == reverse:
                pairs.append((source, source ^ step))
        got = lax.ppermute(sent, CTX, pairs).astype(f32)
        if last:
            state = state + got
        else:
            mine = ((place // step) % 2) == (0 if reverse else 1)
            state = state + jnp.where(mine, got, 0.0)
            total = total + got
            sent = total.astype(bf16)
    return state


def links(first, keep=lambda source, target: True):
    pairs = []
    for chip in range(4):
        for core in range(2):
            other = chip ^ (first if core == 0 else 3 - first)
            if keep((chip, core), other):
                pairs.append((chip * 2 + core, other * 2 + core))
    return pairs


def scan_four(own, sent, reverse, beside=()):
    chip, core = lax.axis_index("chip"), lax.axis_index("core")
    low_bit = 1 - chip % 2 if reverse else chip % 2
    flip = 3 if reverse else 0
    half = own.shape[0] // 2
    sibling = lax.ppermute(sent, "core", SWAP)
    both = own + sibling.astype(f32)
    both = jnp.where(core == 0, both[:half], both[half:])

    def upward(source, target):
        at = source[0] ^ flip
        crossing = source[0] ^ target
        return crossing == 1 or not at & 2

    got = lax.ppermute(both.astype(bf16), CTX, links(1, upward)).astype(f32)
    first = jnp.where((core == 1) | (low_bit == 1), got, 0.0)
    message = (got + jnp.where((core == 0) | (low_bit == 0), both, 0.0)).astype(bf16)
    if beside:
        message = tie(message, beside[0])
    more = lax.ppermute(message, CTX, links(2, upward)).astype(f32)
    state = first + more
    if beside:
        state = tie(state, beside[1])
    other = lax.ppermute(state, "core", SWAP)
    whole = jnp.concatenate(
        [jnp.where(core == 0, state, other), jnp.where(core == 0, other, state)], axis=0
    )
    return whole + jnp.where(core == (0 if reverse else 1), sibling.astype(f32), 0.0)


def scan_sum(own, sent, chips, reverse, beside=()):
    if chips == 4:
        return halves(scan_four(own, sent, reverse, beside))
    return halves(scan_any(own, sent, chips * 2, reverse))


def gather_any(q_weight):
    whole = lax.all_gather(q_weight, ("chip", "core", "dp"), axis=0, tiled=True)
    cut = whole.shape[0] // (2 * PIECE) * PIECE
    number = whole.shape[0] // PIECE
    return [whole[:cut], whole[cut:]], jnp.arange(number, dtype=jnp.int32)


def crossed(side):
    return (0, 1 + side, 2 - side, 3)


def per_device(tokens, key_input, values, q_weight, q_spikes, k_spikes, cotangent):
    batches, length, width = tokens.shape
    assert batches == 1
    total = q_weight.shape[1]
    chips, spread = lax.axis_size("chip"), lax.axis_size("dp")
    factor = 3.0 / math.sqrt(HEAD * length * chips * 2)
    tokens, key_input, values, q_spikes, k_spikes, cotangent = (
        array.reshape(length, array.shape[2])
        for array in (tokens, key_input, values, q_spikes, k_spikes, cotangent)
    )
    special = chips == 4 and spread == 4

    def sibling(array):
        return lax.ppermute(array, "core", SWAP)

    def along(array, pairs):
        return lax.ppermute(array, "dp", pairs)

    def cross(array):
        return lax.ppermute(array, CTX, links(1)), lax.ppermute(array, CTX, links(2))

    def onward(array):
        return lax.ppermute(array, CTX, links(2))

    if special:
        chip, core, layer = (lax.axis_index(name) for name in ("chip", "core", "dp"))
        within = (layer == 1) | (layer == 2)
        ends = [(0, 1), (1, 0), (2, 3), (3, 2)]
        middle = [(1, 2), (2, 1)]
        outward = [(1, 0), (2, 3)]
        near = along(q_weight, ends)
        mid = along(q_weight, middle)
        first, second = cross(q_weight)
        after = sibling(q_weight)
    else:
        arrived, places = gather_any(q_weight)
        after = q_weight
    keys, own, sent = memory_call(key_input, k_spikes, values, after)
    high, low = scan_sum(own, sent, chips, False)
    masked = masked_call(factor, cotangent, values, keys, q_spikes, high, low)

    if special:

        def numbers(sides, flips, layers):
            return jnp.stack(
                [
                    ((chip ^ crossed(side)[flip]) * 2 + side) * spread + one
                    for side in sides
                    for flip in flips
                    for one in layers
                ]
            ).astype(jnp.int32)

        sides = (core, 1 - core)
        two = jnp.where(layer < 2, 2, 1)
        three = jnp.where(layer < 2, 3, 0)
        far = along(near, middle)
        near_first, near_second = cross(near)
        mid_out = along(mid, outward)
        third = onward(first)
        far_out = along(far, outward)
        rest = jnp.concatenate(
            [jnp.where(within, mid, mid_out), jnp.where(within, far, far_out)], axis=0
        )
        near_third = onward(near_first)
        mine = [q_weight, first, second, third]
        early = mine + [after] + [sibling(one) for one in mine[1:]]
        mine = [near, near_first, near_second, near_third]
        early += mine + [sibling(one) for one in mine]
        early_places = jnp.concatenate(
            [numbers(sides, range(4), [layer]), numbers(sides, range(4), [layer ^ 1])]
        )
        rest_first, rest_second = cross(rest)
        done = products_call(early_places, tokens, early, masked, None)
        rest_first = tie(rest_first, *done)
        rest_third = onward(rest_first)
        mine = [rest, rest_first, rest_second]
        done = products_call(
            numbers(sides, range(3), [two, three]),
            tokens,
            mine + [sibling(one) for one in mine],
            masked,
            done,
        )
        rest_third = tie(rest_third, *done)
        late = [rest_third, sibling(rest_third)]
        late_places = numbers(sides, [3], [two, three])
    else:
        half = places.shape[0] // 2
        done = products_call(places[:half], tokens, arrived[:1], masked, None)
        late, late_places = arrived[1:], places[half:]
    partial, grad_tokens = done
    queries, own, sent = query_call(late_places, tokens, late, partial, q_spikes, cotangent)
    attended = attend_call(factor, queries, keys, values, high, low)
    key_part, value_part = inner_call(queries, keys, values, cotangent)
    adjoint = scan_sum(own, sent, chips, True, (attended, key_part))
    grad_tokens = back_call(late_places, late, masked, grad_tokens)
    grad_keys, grad_values = outer_call(
        factor, key_part, value_part, keys, values, k_spikes, *adjoint
    )
    return tuple(
        array.reshape(1, length, array.shape[1])
        for array in (attended, grad_tokens, grad_keys, grad_values)
    )


def solution(mesh):
    count, spread = mesh.shape["ctx"], mesh.shape["dp"]
    fine = Mesh(mesh.devices.reshape(count // 2, 2, spread), ("chip", "core", "dp"))
    block = P("dp", CTX, None)
    rows = P(("chip", "core", "dp"), None)
    in_specs = (block, block, block, rows, block, block, block)
    return jax.shard_map(
        per_device, mesh=fine, in_specs=in_specs, out_specs=(block,) * 4, check_vma=False
    )
```

time: 197 us -> 179 us (0.909)
  the two profiles are of different devices: /device:TPU:1 before, /device:TPU:12 now
where the time goes in v1:
time: 179 us; the launch traced here: 178 us
  Pallas kernels  61.2 us (34%)
  waiting for transfers between devices  46 us (26%)
  starting transfers between devices  31.5 us (18%)
  local copies, waits for them, and re-layouts  25.5 us (14%)
  other arithmetic  12.5 us (7%)
    pallas_call x2, Pallas kernels, products_call(): pl.pallas_call(functools.partial(products_kernel, len(blocks), before is...  25.8 us
    unnamed x82, local copies, waits for them, and re-layouts  25.4 us
    ppermute x3, waiting for transfers between devices, onward(): return lax.ppermute(array, CTX, links(2))  16.5 us
    ppermute x5, starting transfers between devices, along(): return lax.ppermute(array, 'dp', pairs)  11.7 us
    ppermute x5, waiting for transfers between devices, along(): return lax.ppermute(array, 'dp', pairs)  11 us
    ppermute x12, waiting for transfers between devices, sibling(): return lax.ppermute(array, 'core', SWAP)  9.16 us
    pallas_call x1, Pallas kernels, inner_call(): pl.pallas_call(inner_kernel, grid=(total // WIDE,), in_specs=[columns(len...  7.9 us
    ppermute x2, starting transfers between devices, scan_four(): got = lax.ppermute(both.astype(bf16), CTX, links(1, upward)).astype(f32)  6.82 us
  transfers between devices with their start and end apart: 34, of which 14 were waited for; matrix products, arithmetic and copies ran while one was open for 6% of the time, Pallas kernels for 29%

profile of v1, /device:TPU:12, one launch (start us, length us, event | category | flops | bytes accessed | tf_op | source)
XLA Modules:
  0.0 178.0 jit_solution(15695228726590861963)
XLA Ops:
  4.4 1.9 %copy-done.7 = s32[1,384,2048]{2,1,0:T(8,128)S(1)} copy-done((s32[1,384,2048]{2,1,0:T(8,128)S(1)}, s32[1,384,2048]{2,1,0:T(8,128)}, u32[]{:S(2)}) %copy-start.7) | copy-done | bytes 3145752
  7.7 2.7 %own_memory.1 = (bf16[384,2048]{1,0:T(8,128)(2,1)S(1)}, f32[2048,128]{1,0:T(8,128)S(1)}, bf16[2048,128]{1,0:T(8,128)(2,1)}) custom-call(bf16[384,2048]{1,0:T(8,128)(2,1)S(1)} %bitcast.59, s32[384,2048]{1,0:T(8,128)S(1)} %bitcast.50, bf16[384,2048]{1,0:T(8,128)(2,1)S(1)} %bitcast.43, bf16[128,2048]{1,0:T(8,128)(2,1)S(1)} %collective-permute-done.after_ref.refs_4_), custom_call_target="tpu_custom_call" | custom-call | flops 201326592 | bytes 9437184 | tf_op jit(solution)/shard_map/own_memory/pallas_call | solution.py:63
  10.5 3.5 %collective-permute-start.5 = (bf16[128,2048]{1,0:T(8,128)(2,1)S(1)}, bf16[128,2048]{1,0:T(8,128)(2,1)}, u32[]{:S(2)}, u32[]{:S(2)}) collective-permute-start(bf16[128,2048]{1,0:T(8,128)(2,1)S(1)} %copy-done.31), channel_id=1, source_target_pairs={{1,2},{2,1},{5,6},{6,5},{9,10},{10,9},{13,14},{14,13},{17,18},{18,... | collective-permute-start | bytes 1572872 | tf_op jit(solution)/shard_map/ppermute | solution.py:554
  15.4 3.5 %collective-permute-start.8 = (bf16[128,2048]{1,0:T(8,128)(2,1)}, bf16[128,2048]{1,0:T(8,128)(2,1)}, u32[]{:S(2)}, u32[]{:S(2)}) collective-permute-start(bf16[128,2048]{1,0:T(8,128)(2,1)} %collective-permute-done.7.refs_8_), channel_id=1, source_target_pairs={{1,2},{2,1},{5,6},{6,5},{9,10},{10,9},{13,14},{14,13},{17,18},{18,... | collective-permute-start | bytes 1572872 | tf_op jit(solution)/shard_map/ppermute | solution.py:554
  18.9 2.1 %convert_add_fusion.1 = f32[2048,128]{1,0:T(8,128)} fusion(f32[2048,128]{1,0:T(8,128)S(1)} %get-tuple-element.19, bf16[2048,128]{1,0:T(8,128)(2,1)} %collective-permute-done.1), kind=kLoop, calls=%fused_computation.3 | loop fusion | flops 524288 | bytes 2621440 | tf_op jit(solution)/shard_map/add | solution.py:497
  22.2 3.4 %collective-permute-start.2 = (bf16[1024,128]{1,0:T(8,128)(2,1)S(1)}, bf16[1024,128]{1,0:T(8,128)(2,1)S(1)}, u32[]{:S(2)}, u32[]{:S(2)}) collective-permute-start(bf16[1024,128]{1,0:T(8,128)(2,1)S(1)} %fusion.8), channel_id=1, source_target_pairs={{0,8},{4,20},{8,0},{12,28},{16,24},{24,16},{1,9},{5,21},{9,1},{13,... | collective-permute-start | bytes 786440 | tf_op jit(solution)/shard_map/ppermute | solution.py:505
  27.3 2.1 %collective-permute-start.6 = (bf16[128,2048]{1,0:T(8,128)(2,1)}, bf16[128,2048]{1,0:T(8,128)(2,1)}, u32[]{:S(2)}, u32[]{:S(2)}) collective-permute-start(bf16[128,2048]{1,0:T(8,128)(2,1)} %collective-permute-done.5), channel_id=1, source_target_pairs={{1,0},{2,3},{5,4},{6,7},{9,8},{10,11},{13,12},{14,15},{17,16},{18,... | collective-permute-start | bytes 1572872 | tf_op jit(solution)/shard_map/ppermute | solution.py:554
  29.4 8.6 %collective-permute-done.8 = bf16[128,2048]{1,0:T(8,128)(2,1)} collective-permute-done((bf16[128,2048]{1,0:T(8,128)(2,1)}, bf16[128,2048]{1,0:T(8,128)(2,1)}, u32[]{:S(2)}, u32[]{:S(2)}) %collective-permute-start.8) | collective-permute-done | bytes 524320 | tf_op jit(solution)/shard_map/ppermute | solution.py:554
  38.0 2.1 %collective-permute-start.9 = (bf16[128,2048]{1,0:T(8,128)(2,1)}, bf16[128,2048]{1,0:T(8,128)(2,1)}, u32[]{:S(2)}, u32[]{:S(2)}) collective-permute-start(bf16[128,2048]{1,0:T(8,128)(2,1)} %collective-permute-done.8), channel_id=1, source_target_pairs={{1,0},{2,3},{5,4},{6,7},{9,8},{10,11},{13,12},{14,15},{17,16},{18,... | collective-permute-start | bytes 1572872 | tf_op jit(solution)/shard_map/ppermute | solution.py:554
  40.1 2.0 %fusion.3 = bf16[1024,128]{1,0:T(8,128)(2,1)} fusion(bf16[1024,128]{1,0:T(8,128)(2,1)S(1)} %collective-permute-done.2, pred[]{:T(512)S(6)} %or.16, f32[2048,128]{1,0:T(8,128)} %convert_add_fusion.1, pred[]{:T(512)S(6)} %eq.19), kind=kLoop, calls=%fused_computation.14 | loop fusion | flops 655360 | bytes 1572866 | tf_op jit(solution)/shard_map/convert_element_type | solution.py:507
  43.4 3.4 %collective-permute-start.12 = (bf16[128,2048]{1,0:T(8,128)(2,1)S(1)}, bf16[128,2048]{1,0:T(8,128)(2,1)S(1)}, u32[]{:S(2)}, u32[]{:S(2)}) collective-permute-start(bf16[128,2048]{1,0:T(8,128)(2,1)S(1)} %copy-done.31), channel_id=1, source_target_pairs={{0,16},{4,12},{8,24},{12,4},{16,0},{20,28},{24,8},{28,20},{1,17},{... | collective-permute-start | bytes 1572872 | tf_op jit(solution)/shard_map/ppermute | solution.py:557
  46.9 3.7 %collective-permute-done.3 = bf16[1024,128]{1,0:T(8,128)(2,1)} collective-permute-done((bf16[1024,128]{1,0:T(8,128)(2,1)}, bf16[1024,128]{1,0:T(8,128)(2,1)}, u32[]{:S(2)}, u32[]{:S(2)}) %collective-permute-start.3) | collective-permute-done | bytes 262176 | tf_op jit(solution)/shard_map/ppermute | solution.py:510
  57.2 10.2 %collective-permute-done.13.refs_3_ = bf16[128,2048]{1,0:T(8,128)(2,1)S(1)} collective-permute-done((bf16[128,2048]{1,0:T(8,128)(2,1)S(1)}, bf16[128,2048]{1,0:T(8,128)(2,1)S(1)}, u32[]{:S(2)}, u32[]{:S(2)}) %collective-permute-start.13) | collective-permute-done | bytes 524320 | tf_op jit(solution)/shard_map/ppermute | solution.py:560
  70.9 2.1 %collective-permute-done.18.refs_10_ = bf16[128,2048]{1,0:T(8,128)(2,1)S(1)} collective-permute-done((bf16[128,2048]{1,0:T(8,128)(2,1)}, bf16[128,2048]{1,0:T(8,128)(2,1)S(1)}, u32[]{:S(2)}, u32[]{:S(2)}) %collective-permute-start.18) | collective-permute-done | bytes 524320 | tf_op jit(solution)/shard_map/ppermute | solution.py:557
  74.5 6.3 %collective-permute-done.19.refs_11_ = bf16[128,2048]{1,0:T(8,128)(2,1)S(1)} collective-permute-done((bf16[128,2048]{1,0:T(8,128)(2,1)S(1)}, bf16[128,2048]{1,0:T(8,128)(2,1)S(1)}, u32[]{:S(2)}, u32[]{:S(2)}) %collective-permute-start.19) | collective-permute-done | bytes 524320 | tf_op jit(solution)/shard_map/ppermute | solution.py:560
  82.2 4.9 %masked_grad.1.masked_ref = bf16[384,2048]{1,0:T(8,128)(2,1)S(1)} custom-call(bf16[384,2048]{1,0:T(8,128)(2,1)S(1)} %bitcast.52, bf16[384,2048]{1,0:T(8,128)(2,1)S(1)} %bitcast.44, bf16[384,2048]{1,0:T(8,128)(2,1)S(1)} %get-tuple-element.18.keys_ref, s32[384,2048]{1,0:T(8,128)S(1)} %bitcast.48, bf16[2048,128]{1,0:T(8,128)(2,1)S(1)} %get-tuple-element.35.high_ref, ...), custom_call_target="tpu_custom_call" | custom-call | flops 2415919104 | bytes 9437184 | tf_op jit(solution)/shard_map/masked_grad/pallas_call | solution.py:138
  87.9 14.3 %products.2 = (f32[384,2048]{1,0:T(8,128)S(1)}, bf16[384,4096]{1,0:T(8,128)(2,1)}) custom-call(s32[16]{0:T(128)S(1)} %concatenate.14.places_ref, bf16[384,4096]{1,0:T(8,128)(2,1)S(1)} %bitcast.55, bf16[384,2048]{1,0:T(8,128)(2,1)S(1)} %masked_grad.1.masked_ref, bf16[128,2048]{1,0:T(8,128)(2,1)S(1)} %copy-done.32, bf16[128,2048]{1,0:T(8,128)(2,1)S(1)} %copy-done.34, ...), custom_call_target="tpu_custom_call" | custom-call | flops 6442450944 | bytes 14680064 | tf_op jit(solution)/shard_map/products/pallas_call | solution.py:254
  102.2 1.9 %copy-done = bf16[384,4096]{1,0:T(8,128)(2,1)S(1)} copy-done((bf16[384,4096]{1,0:T(8,128)(2,1)S(1)}, bf16[384,4096]{1,0:T(8,128)(2,1)}, u32[]{:S(2)}) %copy-start) | copy-done | bytes 3145752
  104.7 2.4 %collective-permute-done.26.refs_4_ = bf16[256,2048]{1,0:T(8,128)(2,1)} collective-permute-done((bf16[256,2048]{1,0:T(8,128)(2,1)}, bf16[256,2048]{1,0:T(8,128)(2,1)}, u32[]{:S(2)}, u32[]{:S(2)}) %collective-permute-start.26) | collective-permute-done | bytes 1048608 | tf_op jit(solution)/shard_map/ppermute | solution.py:551
  110.0 1.9 %copy-done.18 = bf16[1,384,4096]{2,1,0:T(8,128)(2,1)S(1)} copy-done((bf16[1,384,4096]{2,1,0:T(8,128)(2,1)S(1)}, bf16[1,384,4096]{2,1,0:T(8,128)(2,1)}, u32[]{:S(2)}) %copy-start.18) | copy-done | bytes 3145752
  111.9 11.5 %products.3 = (f32[384,2048]{1,0:T(8,128)S(1)}, bf16[384,4096]{1,0:T(8,128)(2,1)}) custom-call(s32[12]{0:T(128)S(1)} %stack.119.places_ref, bf16[384,4096]{1,0:T(8,128)(2,1)S(1)} %bitcast.56, bf16[384,2048]{1,0:T(8,128)(2,1)S(1)} %copy-done.13, bf16[256,2048]{1,0:T(8,128)(2,1)} %pad_maximum_fusion.refs_0_, ...), custom_call_target="tpu_custom_call", output_to_operand_aliasing={{0}: (9, {}), {1}: (10, {})} | custom-call | flops 4831838208 | bytes 12582912 | tf_op jit(solution)/shard_map/products/pallas_call | solution.py:254
  123.5 1.9 %copy-done.1 = bf16[384,4096]{1,0:T(8,128)(2,1)S(1)} copy-done((bf16[384,4096]{1,0:T(8,128)(2,1)S(1)}, bf16[384,4096]{1,0:T(8,128)(2,1)}, u32[]{:S(2)}) %copy-start.1) | copy-done | bytes 3145752
  125.5 2.8 %collective-permute-done.29.refs_1_ = bf16[256,2048]{1,0:T(8,128)(2,1)} collective-permute-done((bf16[256,2048]{1,0:T(8,128)(2,1)}, bf16[256,2048]{1,0:T(8,128)(2,1)}, u32[]{:S(2)}, u32[]{:S(2)}) %collective-permute-start.29) | collective-permute-done | bytes 1048608 | tf_op jit(solution)/shard_map/ppermute | solution.py:551
  128.3 1.9 %copy-done.6 = s32[1,384,2048]{2,1,0:T(8,128)S(1)} copy-done((s32[1,384,2048]{2,1,0:T(8,128)S(1)}, s32[1,384,2048]{2,1,0:T(8,128)}, u32[]{:S(2)}) %copy-start.6) | copy-done | bytes 3145752
  131.6 1.9 %copy-done.19 = bf16[1,384,4096]{2,1,0:T(8,128)(2,1)S(1)} copy-done((bf16[1,384,4096]{2,1,0:T(8,128)(2,1)S(1)}, bf16[1,384,4096]{2,1,0:T(8,128)(2,1)}, u32[]{:S(2)}) %copy-start.19) | copy-done | bytes 3145752
  133.5 5.6 %queries.1 = (bf16[384,2048]{1,0:T(8,128)(2,1)S(1)}, f32[2048,128]{1,0:T(8,128)S(1)}, bf16[2048,128]{1,0:T(8,128)(2,1)S(1)}) custom-call(s32[4]{0:T(128)S(1)} %pad_add_fusion.places_ref, bf16[384,4096]{1,0:T(8,128)(2,1)S(1)} %bitcast.57, f32[384,2048]{1,0:T(8,128)S(1)} %get-tuple-element.23.refs_1_.before_ref, s32[384,2048]{1,0:T(8,128)S(1)} %bitcast.49, ...), custom_call_target="tpu_custom_call" | custom-call | flops 805306368 | bytes 11534336 | tf_op jit(solution)/shard_map/queries/pallas_call | solution.py:351
  139.3 1.8 collective-permute-done.30
  142.4 3.4 %collective-permute-start.31 = (bf16[1024,128]{1,0:T(8,128)(2,1)}, bf16[1024,128]{1,0:T(8,128)(2,1)S(1)}, u32[]{:S(2)}, u32[]{:S(2)}) collective-permute-start(bf16[1024,128]{1,0:T(8,128)(2,1)} %fusion.9), channel_id=1, source_target_pairs={{0,8},{8,0},{16,24},{20,4},{24,16},{28,12},{1,9},{9,1},{17,25},{21... | collective-permute-start | bytes 786440 | tf_op jit(solution)/shard_map/ppermute | solution.py:505
  149.3 5.5 %attended.1.refs_1_ = bf16[384,2048]{1,0:T(8,128)(2,1)} custom-call(bf16[384,2048]{1,0:T(8,128)(2,1)S(1)} %copy-done.29, bf16[384,2048]{1,0:T(8,128)(2,1)S(1)} %copy-done.16, bf16[384,2048]{1,0:T(8,128)(2,1)S(1)} %bitcast.45, bf16[2048,128]{1,0:T(8,128)(2,1)S(1)} %copy-done.23, bf16[2048,128]{1,0:T(8,128)(2,1)S(1)} %copy-done.21), custom_call_target="tpu_custom_call" | custom-call | flops 2415919104 | bytes 6291456 | tf_op jit(solution)/shard_map/attended/pallas_call | solution.py:391
  157.9 7.9 %inner.1 = (f32[384,2048]{1,0:T(8,128)S(1)}, f32[384,2048]{1,0:T(8,128)S(1)}) custom-call(bf16[384,2048]{1,0:T(8,128)(2,1)S(1)} %copy-done.30, bf16[384,2048]{1,0:T(8,128)(2,1)S(1)} %copy-done.16, bf16[384,2048]{1,0:T(8,128)(2,1)S(1)} %bitcast.46, bf16[384,2048]{1,0:T(8,128)(2,1)S(1)} %bitcast.54), custom_call_target="tpu_custom_call" | custom-call | flops 3623878656 | bytes 12582912 | tf_op jit(solution)/shard_map/inner/pallas_call | solution.py:415
  167.3 4.6 %grad_tokens.1 = bf16[384,4096]{1,0:T(8,128)(2,1)} custom-call(s32[4]{0:T(128)S(1)} %pad_add_fusion.places_ref, bf16[384,2048]{1,0:T(8,128)(2,1)S(1)} %copy-done.14, bf16[256,2048]{1,0:T(8,128)(2,1)} %tie.5.refs_0_, bf16[256,2048]{1,0:T(8,128)(2,1)} %collective-permute-done.29.refs_1_, ...), custom_call_target="tpu_custom_call", output_to_operand_aliasing={{}: (4, {})} | custom-call | flops 805306368 | bytes 5242880 | tf_op jit(solution)/shard_map/grad_tokens/pallas_call | solution.py:291
  173.8 4.2 %outer.1 = (bf16[384,2048]{1,0:T(8,128)(2,1)}, bf16[384,2048]{1,0:T(8,128)(2,1)}) custom-call(f32[384,2048]{1,0:T(8,128)S(1)} %get-tuple-element.26.refs_1_.key_ref, f32[384,2048]{1,0:T(8,128)S(1)} %get-tuple-element.27.val_ref, bf16[384,2048]{1,0:T(8,128)(2,1)S(1)} %copy-done.16, bf16[384,2048]{1,0:T(8,128)(2,1)S(1)} %bitcast.47, s32[384,2048]{1,0:T(8,128)S(1)} %bitcast.51, ...), custom_call_target="tpu_custom_call" | custom-call | flops 805306368 | bytes 15728640 | tf_op jit(solution)/shard_map/outer/pallas_call | solution.py:441
  (149 shorter events, 40.9 us)
Async XLA Ops:
  0.7 14.7 %collective-permute-start.7 = (bf16[128,2048]{1,0:T(8,128)(2,1)}, bf16[128,2048]{1,0:T(8,128)(2,1)}, u32[]{:S(2)}, u32[]{:S(2)}) collective-permute-start(bf16[128,2048]{1,0:T(8,128)(2,1)} %refs_0_.1), channel_id=1, source_target_pairs={{0,1},{1,0},{2,3},{3,2},{4,5},{5,4},{6,7},{7,6},{8,9},{9,8},{10,11... | collective-permute-start | bytes 1572872 | tf_op jit(solution)/shard_map/ppermute | solution.py:554
  10.4 8.5 %collective-permute-start.1 = (bf16[2048,128]{1,0:T(8,128)(2,1)}, bf16[2048,128]{1,0:T(8,128)(2,1)}, u32[]{:S(2)}, u32[]{:S(2)}) collective-permute-start(bf16[2048,128]{1,0:T(8,128)(2,1)} %get-tuple-element.20), channel_id=1, source_target_pairs={{0,4},{4,0},{1,5},{5,1},{2,6},{6,2},{3,7},{7,3},{8,12},{12,8},{9,1... | collective-permute-start | bytes 1572872 | tf_op jit(solution)/shard_map/ppermute | solution.py:496
  10.5 16.7 %collective-permute-start.5 = (bf16[128,2048]{1,0:T(8,128)(2,1)S(1)}, bf16[128,2048]{1,0:T(8,128)(2,1)}, u32[]{:S(2)}, u32[]{:S(2)}) collective-permute-start(bf16[128,2048]{1,0:T(8,128)(2,1)S(1)} %copy-done.31), channel_id=1, source_target_pairs={{1,2},{2,1},{5,6},{6,5},{9,10},{10,9},{13,14},{14,13},{17,18},{18,... | collective-permute-start | bytes 1572872 | tf_op jit(solution)/shard_map/ppermute | solution.py:554
  15.4 22.6 %collective-permute-start.8 = (bf16[128,2048]{1,0:T(8,128)(2,1)}, bf16[128,2048]{1,0:T(8,128)(2,1)}, u32[]{:S(2)}, u32[]{:S(2)}) collective-permute-start(bf16[128,2048]{1,0:T(8,128)(2,1)} %collective-permute-done.7.refs_8_), channel_id=1, source_target_pairs={{1,2},{2,1},{5,6},{6,5},{9,10},{10,9},{13,14},{14,13},{17,18},{18,... | collective-permute-start | bytes 1572872 | tf_op jit(solution)/shard_map/ppermute | solution.py:554
  22.2 17.9 %collective-permute-start.2 = (bf16[1024,128]{1,0:T(8,128)(2,1)S(1)}, bf16[1024,128]{1,0:T(8,128)(2,1)S(1)}, u32[]{:S(2)}, u32[]{:S(2)}) collective-permute-start(bf16[1024,128]{1,0:T(8,128)(2,1)S(1)} %fusion.8), channel_id=1, source_target_pairs={{0,8},{4,20},{8,0},{12,28},{16,24},{24,16},{1,9},{5,21},{9,1},{13,... | collective-permute-start | bytes 786440 | tf_op jit(solution)/shard_map/ppermute | solution.py:505
  25.6 21.2 %collective-permute-start.11 = (bf16[128,2048]{1,0:T(8,128)(2,1)S(1)}, bf16[128,2048]{1,0:T(8,128)(2,1)S(1)}, u32[]{:S(2)}, u32[]{:S(2)}) collective-permute-start(bf16[128,2048]{1,0:T(8,128)(2,1)S(1)} %copy-done.31), channel_id=1, source_target_pairs={{0,8},{4,20},{8,0},{12,28},{16,24},{20,4},{24,16},{28,12},{1,9},{5... | collective-permute-start | bytes 1572872 | tf_op jit(solution)/shard_map/ppermute | solution.py:557
  27.3 24.4 %collective-permute-start.6 = (bf16[128,2048]{1,0:T(8,128)(2,1)}, bf16[128,2048]{1,0:T(8,128)(2,1)}, u32[]{:S(2)}, u32[]{:S(2)}) collective-permute-start(bf16[128,2048]{1,0:T(8,128)(2,1)} %collective-permute-done.5), channel_id=1, source_target_pairs={{1,0},{2,3},{5,4},{6,7},{9,8},{10,11},{13,12},{14,15},{17,16},{18,... | collective-permute-start | bytes 1572872 | tf_op jit(solution)/shard_map/ppermute | solution.py:554
  38.0 15.3 %collective-permute-start.9 = (bf16[128,2048]{1,0:T(8,128)(2,1)}, bf16[128,2048]{1,0:T(8,128)(2,1)}, u32[]{:S(2)}, u32[]{:S(2)}) collective-permute-start(bf16[128,2048]{1,0:T(8,128)(2,1)} %collective-permute-done.8), channel_id=1, source_target_pairs={{1,0},{2,3},{5,4},{6,7},{9,8},{10,11},{13,12},{14,15},{17,16},{18,... | collective-permute-start | bytes 1572872 | tf_op jit(solution)/shard_map/ppermute | solution.py:554
  42.1 8.6 %collective-permute-start.3 = (bf16[1024,128]{1,0:T(8,128)(2,1)}, bf16[1024,128]{1,0:T(8,128)(2,1)}, u32[]{:S(2)}, u32[]{:S(2)}) collective-permute-start(bf16[1024,128]{1,0:T(8,128)(2,1)} %fusion.3), channel_id=1, source_target_pairs={{0,16},{4,12},{8,24},{12,4},{20,28},{28,20},{1,17},{5,13},{9,25},{... | collective-permute-start | bytes 786440 | tf_op jit(solution)/shard_map/ppermute | solution.py:510
  43.4 13.8 %collective-permute-start.12 = (bf16[128,2048]{1,0:T(8,128)(2,1)S(1)}, bf16[128,2048]{1,0:T(8,128)(2,1)S(1)}, u32[]{:S(2)}, u32[]{:S(2)}) collective-permute-start(bf16[128,2048]{1,0:T(8,128)(2,1)S(1)} %copy-done.31), channel_id=1, source_target_pairs={{0,16},{4,12},{8,24},{12,4},{16,0},{20,28},{24,8},{28,20},{1,17},{... | collective-permute-start | bytes 1572872 | tf_op jit(solution)/shard_map/ppermute | solution.py:557
  46.9 20.5 %collective-permute-start.13 = (bf16[128,2048]{1,0:T(8,128)(2,1)S(1)}, bf16[128,2048]{1,0:T(8,128)(2,1)S(1)}, u32[]{:S(2)}, u32[]{:S(2)}) collective-permute-start(bf16[128,2048]{1,0:T(8,128)(2,1)S(1)} %collective-permute-done.11.refs_1_), channel_id=1, source_target_pairs={{0,16},{4,12},{8,24},{12,4},{16,0},{20,28},{24,8},{28,20},{1,17},{... | collective-permute-start | bytes 1572872 | tf_op jit(solution)/shard_map/ppermute | solution.py:560
  50.7 16.8 %collective-permute-start.14 = (bf16[128,2048]{1,0:T(8,128)(2,1)S(1)}, bf16[128,2048]{1,0:T(8,128)(2,1)S(1)}, u32[]{:S(2)}, u32[]{:S(2)}) collective-permute-start(bf16[128,2048]{1,0:T(8,128)(2,1)S(1)} %collective-permute-done.11.refs_1_), channel_id=1, source_target_pairs={{0,4},{4,0},{1,5},{5,1},{2,6},{6,2},{3,7},{7,3},{8,12},{12,8},{9,1... | collective-permute-start | bytes 1572872 | tf_op jit(solution)/shard_map/ppermute | solution.py:551
  51.7 16.2 %collective-permute-start.17 = (bf16[128,2048]{1,0:T(8,128)(2,1)}, bf16[128,2048]{1,0:T(8,128)(2,1)S(1)}, u32[]{:S(2)}, u32[]{:S(2)}) collective-permute-start(bf16[128,2048]{1,0:T(8,128)(2,1)} %collective-permute-done.7.refs_8_), channel_id=1, source_target_pairs={{0,8},{4,20},{8,0},{12,28},{16,24},{20,4},{24,16},{28,12},{1,9},{5... | collective-permute-start | bytes 1572872 | tf_op jit(solution)/shard_map/ppermute | solution.py:557
  53.3 14.7 %collective-permute-start.4 = (f32[1024,128]{1,0:T(8,128)S(1)}, f32[1024,128]{1,0:T(8,128)S(1)}, u32[]{:S(2)}, u32[]{:S(2)}) collective-permute-start(f32[1024,128]{1,0:T(8,128)S(1)} %fusion.2), channel_id=1, source_target_pairs={{0,4},{4,0},{1,5},{5,1},{2,6},{6,2},{3,7},{7,3},{8,12},{12,8},{9,1... | collective-permute-start | bytes 1572872 | tf_op jit(solution)/shard_map/ppermute | solution.py:514
  57.2 15.8 %collective-permute-start.18 = (bf16[128,2048]{1,0:T(8,128)(2,1)}, bf16[128,2048]{1,0:T(8,128)(2,1)S(1)}, u32[]{:S(2)}, u32[]{:S(2)}) collective-permute-start(bf16[128,2048]{1,0:T(8,128)(2,1)} %collective-permute-done.7.refs_8_), channel_id=1, source_target_pairs={{0,16},{4,12},{8,24},{12,4},{16,0},{20,28},{24,8},{28,20},{1,17},{... | collective-permute-start | bytes 1572872 | tf_op jit(solution)/shard_map/ppermute | solution.py:557
  67.4 5.6 %collective-permute-start.20 = (bf16[128,2048]{1,0:T(8,128)(2,1)}, bf16[128,2048]{1,0:T(8,128)(2,1)S(1)}, u32[]{:S(2)}, u32[]{:S(2)}) collective-permute-start(bf16[128,2048]{1,0:T(8,128)(2,1)} %collective-permute-done.7.refs_8_), channel_id=1, source_target_pairs={{0,4},{4,0},{1,5},{5,1},{2,6},{6,2},{3,7},{7,3},{8,12},{12,8},{9,1... | collective-permute-start | bytes 1572872 | tf_op jit(solution)/shard_map/ppermute | solution.py:551
  67.4 2.7 %collective-permute-start.15 = (bf16[128,2048]{1,0:T(8,128)(2,1)S(1)}, bf16[128,2048]{1,0:T(8,128)(2,1)S(1)}, u32[]{:S(2)}, u32[]{:S(2)}) collective-permute-start(bf16[128,2048]{1,0:T(8,128)(2,1)S(1)} %collective-permute-done.12.refs_2_), channel_id=1, source_target_pairs={{0,4},{4,0},{1,5},{5,1},{2,6},{6,2},{3,7},{7,3},{8,12},{12,8},{9,1... | collective-permute-start | bytes 1572872 | tf_op jit(solution)/shard_map/ppermute | solution.py:551
  67.9 6.6 %collective-permute-start.16 = (bf16[128,2048]{1,0:T(8,128)(2,1)S(1)}, bf16[128,2048]{1,0:T(8,128)(2,1)S(1)}, u32[]{:S(2)}, u32[]{:S(2)}) collective-permute-start(bf16[128,2048]{1,0:T(8,128)(2,1)S(1)} %collective-permute-done.13.refs_3_), channel_id=1, source_target_pairs={{0,4},{4,0},{1,5},{5,1},{2,6},{6,2},{3,7},{7,3},{8,12},{12,8},{9,1... | collective-permute-start | bytes 1572872 | tf_op jit(solution)/shard_map/ppermute | solution.py:551
  68.0 12.9 %collective-permute-start.19 = (bf16[128,2048]{1,0:T(8,128)(2,1)S(1)}, bf16[128,2048]{1,0:T(8,128)(2,1)S(1)}, u32[]{:S(2)}, u32[]{:S(2)}) collective-permute-start(bf16[128,2048]{1,0:T(8,128)(2,1)S(1)} %collective-permute-done.17.refs_9_), channel_id=1, source_target_pairs={{0,16},{4,12},{8,24},{12,4},{16,0},{20,28},{24,8},{28,20},{1,17},{... | collective-permute-start | bytes 1572872 | tf_op jit(solution)/shard_map/ppermute | solution.py:560
  70.1 17.2 %collective-permute-start.21 = (bf16[128,2048]{1,0:T(8,128)(2,1)S(1)}, bf16[128,2048]{1,0:T(8,128)(2,1)S(1)}, u32[]{:S(2)}, u32[]{:S(2)}) collective-permute-start(bf16[128,2048]{1,0:T(8,128)(2,1)S(1)} %collective-permute-done.17.refs_9_), channel_id=1, source_target_pairs={{0,4},{4,0},{1,5},{5,1},{2,6},{6,2},{3,7},{7,3},{8,12},{12,8},{9,1... | collective-permute-start | bytes 1572872 | tf_op jit(solution)/shard_map/ppermute | solution.py:551
  73.0 14.8 %collective-permute-start.22 = (bf16[128,2048]{1,0:T(8,128)(2,1)S(1)}, bf16[128,2048]{1,0:T(8,128)(2,1)S(1)}, u32[]{:S(2)}, u32[]{:S(2)}) collective-permute-start(bf16[128,2048]{1,0:T(8,128)(2,1)S(1)} %collective-permute-done.18.refs_10_), channel_id=1, source_target_pairs={{0,4},{4,0},{1,5},{5,1},{2,6},{6,2},{3,7},{7,3},{8,12},{12,8},{9,1... | collective-permute-start | bytes 1572872 | tf_op jit(solution)/shard_map/ppermute | solution.py:551
  73.0 29.2 %collective-permute-start.10 = (bf16[256,2048]{1,0:T(8,128)(2,1)}, bf16[256,2048]{1,0:T(8,128)(2,1)}, u32[]{:S(2)}, u32[]{:S(2)}) collective-permute-start(bf16[256,2048]{1,0:T(8,128)(2,1)} %pad_maximum_fusion.refs_0_), channel_id=1, source_target_pairs={{0,8},{4,20},{8,0},{12,28},{16,24},{20,4},{24,16},{28,12},{1,9},{5... | collective-permute-start | bytes 3145736 | tf_op jit(solution)/shard_map/ppermute | solution.py:557
  74.5 29.6 %collective-permute-start.24 = (bf16[256,2048]{1,0:T(8,128)(2,1)}, bf16[256,2048]{1,0:T(8,128)(2,1)}, u32[]{:S(2)}, u32[]{:S(2)}) collective-permute-start(bf16[256,2048]{1,0:T(8,128)(2,1)} %pad_maximum_fusion.refs_0_), channel_id=1, source_target_pairs={{0,16},{4,12},{8,24},{12,4},{16,0},{20,28},{24,8},{28,20},{1,17},{... | collective-permute-start | bytes 3145736 | tf_op jit(solution)/shard_map/ppermute | solution.py:557
  80.9 6.9 %collective-permute-start.23 = (bf16[128,2048]{1,0:T(8,128)(2,1)S(1)}, bf16[128,2048]{1,0:T(8,128)(2,1)S(1)}, u32[]{:S(2)}, u32[]{:S(2)}) collective-permute-start(bf16[128,2048]{1,0:T(8,128)(2,1)S(1)} %collective-permute-done.19.refs_11_), channel_id=1, source_target_pairs={{0,4},{4,0},{1,5},{5,1},{2,6},{6,2},{3,7},{7,3},{8,12},{12,8},{9,1... | collective-permute-start | bytes 1572872 | tf_op jit(solution)/shard_map/ppermute | solution.py:551
  87.2 17.5 %collective-permute-start.25 = (bf16[256,2048]{1,0:T(8,128)(2,1)}, bf16[256,2048]{1,0:T(8,128)(2,1)}, u32[]{:S(2)}, u32[]{:S(2)}) collective-permute-start(bf16[256,2048]{1,0:T(8,128)(2,1)} %pad_maximum_fusion.refs_0_), channel_id=1, source_target_pairs={{0,4},{4,0},{1,5},{5,1},{2,6},{6,2},{3,7},{7,3},{8,12},{12,8},{9,1... | collective-permute-start | bytes 3145736 | tf_op jit(solution)/shard_map/ppermute | solution.py:551
  104.1 3.0 %collective-permute-start.26 = (bf16[256,2048]{1,0:T(8,128)(2,1)}, bf16[256,2048]{1,0:T(8,128)(2,1)}, u32[]{:S(2)}, u32[]{:S(2)}) collective-permute-start(bf16[256,2048]{1,0:T(8,128)(2,1)} %tie.4.refs_1_), channel_id=1, source_target_pairs={{0,4},{4,0},{1,5},{5,1},{2,6},{6,2},{3,7},{7,3},{8,12},{12,8},{9,1... | collective-permute-start | bytes 3145736 | tf_op jit(solution)/shard_map/ppermute | solution.py:551
  104.1 4.5 %collective-permute-start.27 = (bf16[256,2048]{1,0:T(8,128)(2,1)}, bf16[256,2048]{1,0:T(8,128)(2,1)}, u32[]{:S(2)}, u32[]{:S(2)}) collective-permute-start(bf16[256,2048]{1,0:T(8,128)(2,1)} %collective-permute-done.24.refs_2_), channel_id=1, source_target_pairs={{0,4},{4,0},{1,5},{5,1},{2,6},{6,2},{3,7},{7,3},{8,12},{12,8},{9,1... | collective-permute-start | bytes 3145736 | tf_op jit(solution)/shard_map/ppermute | solution.py:551
  104.6 18.8 %collective-permute-start.28 = (bf16[256,2048]{1,0:T(8,128)(2,1)}, bf16[256,2048]{1,0:T(8,128)(2,1)}, u32[]{:S(2)}, u32[]{:S(2)}) collective-permute-start(bf16[256,2048]{1,0:T(8,128)(2,1)} %tie.4.refs_1_), channel_id=1, source_target_pairs={{0,16},{4,12},{8,24},{12,4},{16,0},{20,28},{24,8},{28,20},{1,17},{... | collective-permute-start | bytes 3145736 | tf_op jit(solution)/shard_map/ppermute | solution.py:560
  125.3 3.0 %collective-permute-start.29 = (bf16[256,2048]{1,0:T(8,128)(2,1)}, bf16[256,2048]{1,0:T(8,128)(2,1)}, u32[]{:S(2)}, u32[]{:S(2)}) collective-permute-start(bf16[256,2048]{1,0:T(8,128)(2,1)} %tie.5.refs_0_), channel_id=1, source_target_pairs={{0,4},{4,0},{1,5},{5,1},{2,6},{6,2},{3,7},{7,3},{8,12},{12,8},{9,1... | collective-permute-start | bytes 3145736 | tf_op jit(solution)/shard_map/ppermute | solution.py:551
  142.4 12.4 %collective-permute-start.31 = (bf16[1024,128]{1,0:T(8,128)(2,1)}, bf16[1024,128]{1,0:T(8,128)(2,1)S(1)}, u32[]{:S(2)}, u32[]{:S(2)}) collective-permute-start(bf16[1024,128]{1,0:T(8,128)(2,1)} %fusion.9), channel_id=1, source_target_pairs={{0,8},{8,0},{16,24},{20,4},{24,16},{28,12},{1,9},{9,1},{17,25},{21... | collective-permute-start | bytes 786440 | tf_op jit(solution)/shard_map/ppermute | solution.py:505
  156.4 9.4 %collective-permute-start.32 = (bf16[1024,128]{1,0:T(8,128)(2,1)S(1)}, bf16[1024,128]{1,0:T(8,128)(2,1)S(1)}, u32[]{:S(2)}, u32[]{:S(2)}) collective-permute-start(bf16[1024,128]{1,0:T(8,128)(2,1)S(1)} %tie.6), channel_id=1, source_target_pairs={{4,12},{12,4},{16,0},{20,28},{24,8},{28,20},{5,13},{13,5},{17,1},{... | collective-permute-start | bytes 786440 | tf_op jit(solution)/shard_map/ppermute | solution.py:510
  165.9 6.0 %collective-permute-start.33 = (f32[1024,128]{1,0:T(8,128)S(1)}, f32[1024,128]{1,0:T(8,128)S(1)}, u32[]{:S(2)}, u32[]{:S(2)}) collective-permute-start(f32[1024,128]{1,0:T(8,128)S(1)} %tie.7), channel_id=1, source_target_pairs={{0,4},{4,0},{1,5},{5,1},{2,6},{6,2},{3,7},{7,3},{8,12},{12,8},{9,1... | collective-permute-start | bytes 1572872 | tf_op jit(solution)/shard_map/ppermute | solution.py:514
  (43 other events, 265.5 us)

commit v2 on v1

--- a/solution.py
+++ b/solution.py
@@ -11,10 +11,11 @@
 HEAD = 128
 PIECE = 128
 WIDE = 512
+PAIR = 256
 CTX = ("chip", "core")
 SWAP = [(0, 1), (1, 0)]
 f32, bf16 = jnp.float32, jnp.bfloat16
-VMEM_LIMIT = 26 * 1024 * 1024
+VMEM_LIMIT = 60 * 1024 * 1024
 
 
 def nn(a, b):
@@ -36,23 +37,36 @@
     )
 
 
-def columns(length):
-    return pl.BlockSpec((length, WIDE), lambda j: (0, j))
-
-
-def states():
-    return pl.BlockSpec((WIDE, HEAD), lambda j: (j, 0))
+def columns(length, wide=WIDE):
+    return pl.BlockSpec((length, wide), lambda j: (0, j))
+
+
+def states(wide=WIDE):
+    return pl.BlockSpec((wide, HEAD), lambda j: (j, 0))
+
+
+MARK = jax.ShapeDtypeStruct((8, HEAD), f32)
+
+
+def mark_spec():
+    return pl.BlockSpec((8, HEAD), lambda *at: (0, 0))
+
+
+def set_mark(mark_ref):
+    mark_ref[...] = jnp.zeros_like(mark_ref)
 
 
 def anywhere():
     return pl.BlockSpec(memory_space=pl.ANY)
 
 
-def memory_kernel(key_ref, spike_ref, value_ref, after_ref, keys_ref, own_ref, sent_ref):
+def memory_kernel(key_ref, spike_ref, value_ref, after_ref, keys_ref, mask_ref, own_ref, sent_ref):
     del after_ref
-    keys = key_ref[...] * spike_ref[...].astype(f32).astype(bf16)
+    mask = spike_ref[...].astype(f32).astype(bf16)
+    keys = key_ref[...] * mask
     keys_ref[...] = keys
-    for at in range(0, WIDE, HEAD):
+    mask_ref[...] = mask
+    for at in range(0, PAIR, HEAD):
         own = tn(keys[:, at : at + HEAD], value_ref[:, at : at + HEAD])
         own_ref[at : at + HEAD, :] = own
         sent_ref[at : at + HEAD, :] = own.astype(bf16)
@@ -62,33 +76,35 @@
     length, total = values.shape
     return pl.pallas_call(
         memory_kernel,
-        grid=(total // WIDE,),
-        in_specs=[columns(length)] * 3 + [anywhere()],
-        out_specs=[columns(length), states(), states()],
+        grid=(total // PAIR,),
+        in_specs=[columns(length, PAIR)] * 3 + [anywhere()],
+        out_specs=[columns(length, PAIR)] * 2 + [states(PAIR)] * 2,
         out_shape=[
+            jax.ShapeDtypeStruct((length, total), bf16),
             jax.ShapeDtypeStruct((length, total), bf16),
             jax.ShapeDtypeStruct((total, HEAD), f32),
             jax.ShapeDtypeStruct((total, HEAD), bf16),
         ],
         name="own_memory",
-        **params(2 * length * total * HEAD, 12 * length * total),
+        **params(0, 0),
     )(key_input, k_spikes, values, after)
 
 
-def tie_kernel(*refs):
+def join_kernel(*refs):
     del refs
 
 
-def tie(array, *others):
-    return pl.pallas_call(
-        tie_kernel,
-        in_specs=[anywhere()] * (1 + len(others)),
-        out_specs=anywhere(),
-        out_shape=jax.ShapeDtypeStruct(array.shape, array.dtype),
-        input_output_aliases={0: 0},
-        name="tie",
+def join(arrays, others=()):
+    number = len(arrays)
+    return pl.pallas_call(
+        join_kernel,
+        in_specs=[anywhere()] * (number + len(others)),
+        out_specs=[anywhere()] * number,
+        out_shape=[jax.ShapeDtypeStruct(one.shape, one.dtype) for one in arrays],
+        input_output_aliases={at: at for at in range(number)},
+        name="join",
         **params(0, 0),
-    )(array, *others)
+    )(*arrays, *others)
 
 
 def keep_lower(square, flipped=False):
@@ -123,7 +139,11 @@
     return jnp.concatenate([array, array], axis=1)
 
 
-def masked_kernel(factor, grad_ref, value_ref, keys_ref, spike_ref, high_ref, low_ref, out_ref):
+def masked_kernel(
+    factor, grad_ref, value_ref, keys_ref, spike_ref, high_ref, low_ref, out_ref, mask_ref, mark_ref
+):
+    set_mark(mark_ref)
+    mask_ref[...] = spike_ref[...].astype(f32).astype(bf16)
     for head in range(0, WIDE, HEAD):
         part = slice(head, head + HEAD)
         grad, value, keys = grad_ref[:, part], value_ref[:, part], keys_ref[:, part]
@@ -139,8 +159,8 @@
         functools.partial(masked_kernel, factor),
         grid=(total // WIDE,),
         in_specs=[columns(length)] * 4 + [states()] * 2,
-        out_specs=columns(length),
-        out_shape=jax.ShapeDtypeStruct((length, total), bf16),
+        out_specs=[columns(length)] * 2 + [mark_spec()],
+        out_shape=[jax.ShapeDtypeStruct((length, total), bf16)] * 2 + [MARK],
         name="masked_grad",
         **params(8 * length * total * length, 12 * length * total),
     )(cotangent, values, keys, q_spikes, high, low)
@@ -218,7 +238,8 @@
     refs = refs[size:]
     if has_before:
         before_ref, _, *refs = refs
-    sum_out, back_out, w_ref, some_ref, masked, sum_ref, round_ref, sems = refs
+    sum_out, back_out, mark_ref, w_ref, some_ref, masked, sum_ref, round_ref, sems = refs
+    set_mark(mark_ref)
     copies = Copies(sems)
     mask_copy = copies.start(masked_ref, masked)
     bring = load_rows(copies, blocks, w_ref)
@@ -254,10 +275,11 @@
     return pl.pallas_call(
         functools.partial(products_kernel, len(blocks), before is not None),
         in_specs=[smem()] + [anywhere()] * (2 + len(blocks) + len(extra)),
-        out_specs=[anywhere()] * 2,
+        out_specs=[anywhere()] * 2 + [pl.BlockSpec(memory_space=pltpu.VMEM)],
         out_shape=[
             jax.ShapeDtypeStruct((length, total), f32),
             jax.ShapeDtypeStruct((length, width), bf16),
+            MARK,
         ],
         scratch_shapes=[
             pltpu.VMEM((depth, total), bf16),
@@ -361,7 +383,7 @@
             pltpu.VMEM((depth, total), bf16),
             pltpu.VMEM((length, depth), bf16),
             pltpu.VMEM((length, total), f32),
-            pltpu.VMEM((length, total), jnp.int32),
+            pltpu.VMEM((length, total), bf16),
             pltpu.VMEM((length, total), bf16),
             pltpu.VMEM((length, total), bf16),
             pltpu.VMEM((total, HEAD), f32),
@@ -373,7 +395,8 @@
     )(places, tokens, before, q_spikes, cotangent, *blocks)
 
 
-def attend_kernel(factor, query_ref, keys_ref, value_ref, high_ref, low_ref, out_ref):
+def attend_kernel(factor, query_ref, keys_ref, value_ref, high_ref, low_ref, out_ref, mark_ref):
+    set_mark(mark_ref)
     for head in range(0, WIDE, HEAD):
         part = slice(head, head + HEAD)
         query, keys, value = query_ref[:, part], keys_ref[:, part], value_ref[:, part]
@@ -392,14 +415,15 @@
         functools.partial(attend_kernel, factor),
         grid=(total // WIDE,),
         in_specs=[columns(length)] * 3 + [states()] * 2,
-        out_specs=columns(length),
-        out_shape=jax.ShapeDtypeStruct((length, total), bf16),
+        out_specs=[columns(length), mark_spec()],
+        out_shape=[jax.ShapeDtypeStruct((length, total), bf16), MARK],
         name="attended",
         **params(8 * length * total * length, 8 * length * total),
     )(queries, keys, values, high, low)
 
 
-def inner_kernel(query_ref, keys_ref, value_ref, grad_ref, key_ref, val_ref):
+def inner_kernel(query_ref, keys_ref, value_ref, grad_ref, key_ref, val_ref, mark_ref):
+    set_mark(mark_ref)
     for head in range(0, WIDE, HEAD):
         part = slice(head, head + HEAD)
         query, keys = query_ref[:, part], keys_ref[:, part]
@@ -416,37 +440,37 @@
         inner_kernel,
         grid=(total // WIDE,),
         in_specs=[columns(length)] * 4,
-        out_specs=[columns(length)] * 2,
-        out_shape=[jax.ShapeDtypeStruct((length, total), f32)] * 2,
+        out_specs=[columns(length)] * 2 + [mark_spec()],
+        out_shape=[jax.ShapeDtypeStruct((length, total), f32)] * 2 + [MARK],
         name="inner",
         **params(12 * length * total * length, 16 * length * total),
     )(queries, keys, values, cotangent)
 
 
 def outer_kernel(
-    factor, key_ref, val_ref, keys_ref, value_ref, spike_ref, high_ref, low_ref, gk_ref, gv_ref
+    factor, key_ref, val_ref, keys_ref, value_ref, mask_ref, high_ref, low_ref, gk_ref, gv_ref
 ):
-    for head in range(0, WIDE, HEAD):
+    for head in range(0, PAIR, HEAD):
         part = slice(head, head + HEAD)
         keys, value = keys_ref[:, part], value_ref[:, part]
         state = [high_ref[part, :], low_ref[part, :]]
         key_grad = key_ref[:, part] + nt(twice(value), jnp.concatenate(state, axis=1))
-        gk_ref[:, part] = (factor * key_grad * spike_ref[:, part].astype(f32)).astype(bf16)
+        gk_ref[:, part] = (factor * key_grad * mask_ref[:, part].astype(f32)).astype(bf16)
         value_grad = val_ref[:, part] + nn(twice(keys), jnp.concatenate(state, axis=0))
         gv_ref[:, part] = (factor * value_grad).astype(bf16)
 
 
-def outer_call(factor, key_part, value_part, keys, values, k_spikes, high, low):
+def outer_call(factor, key_part, value_part, keys, values, k_mask, high, low):
     length, total = values.shape
     return pl.pallas_call(
         functools.partial(outer_kernel, factor),
-        grid=(total // WIDE,),
-        in_specs=[columns(length)] * 5 + [states()] * 2,
-        out_specs=[columns(length)] * 2,
+        grid=(total // PAIR,),
+        in_specs=[columns(length, PAIR)] * 5 + [states(PAIR)] * 2,
+        out_specs=[columns(length, PAIR)] * 2,
         out_shape=[jax.ShapeDtypeStruct((length, total), bf16)] * 2,
         name="outer",
         **params(8 * length * total * HEAD, 20 * length * total),
-    )(key_part, value_part, keys, values, k_spikes, high, low)
+    )(key_part, value_part, keys, values, k_mask, high, low)
 
 
 def halves(state):
@@ -506,11 +530,11 @@
     first = jnp.where((core == 1) | (low_bit == 1), got, 0.0)
     message = (got + jnp.where((core == 0) | (low_bit == 0), both, 0.0)).astype(bf16)
     if beside:
-        message = tie(message, beside[0])
+        message, = join([message], beside[:1])
     more = lax.ppermute(message, CTX, links(2, upward)).astype(f32)
     state = first + more
     if beside:
-        state = tie(state, beside[1])
+        state, = join([state], beside[1:])
     other = lax.ppermute(state, "core", SWAP)
     whole = jnp.concatenate(
         [jnp.where(core == 0, state, other), jnp.where(core == 0, other, state)], axis=0
@@ -567,73 +591,77 @@
         outward = [(1, 0), (2, 3)]
         near = along(q_weight, ends)
         mid = along(q_weight, middle)
-        first, second = cross(q_weight)
-        after = sibling(q_weight)
+        first_0, second_0 = cross(q_weight)
+        other_0 = sibling(q_weight)
+        after = other_0
     else:
         arrived, places = gather_any(q_weight)
         after = q_weight
-    keys, own, sent = memory_call(key_input, k_spikes, values, after)
+    keys, k_mask, own, sent = memory_call(key_input, k_spikes, values, after)
     high, low = scan_sum(own, sent, chips, False)
-    masked = masked_call(factor, cotangent, values, keys, q_spikes, high, low)
+    masked, q_mask, masked_mark = masked_call(
+        factor, cotangent, values, keys, q_spikes, high, low
+    )
 
     if special:
 
-        def numbers(sides, flips, layers):
+        def numbers(sides, layers):
             return jnp.stack(
                 [
-                    ((chip ^ crossed(side)[flip]) * 2 + side) * spread + one
+                    ((chip ^ flip) * 2 + side) * spread + one
+                    for one in layers
                     for side in sides
-                    for flip in flips
-                    for one in layers
+                    for flip in crossed(side)
                 ]
             ).astype(jnp.int32)
 
         sides = (core, 1 - core)
-        two = jnp.where(layer < 2, 2, 1)
-        three = jnp.where(layer < 2, 3, 0)
+        levels = [layer, layer ^ 1, jnp.where(layer < 2, 2, 1), jnp.where(layer < 2, 3, 0)]
+        near, mid, first_0, second_0 = join([near, mid, first_0, second_0])
+        third_0 = onward(first_0)
+        first_1, second_1 = cross(near)
         far = along(near, middle)
-        near_first, near_second = cross(near)
         mid_out = along(mid, outward)
-        third = onward(first)
+        third_0, first_1, second_1, far, mid_out = join(
+            [third_0, first_1, second_1, far, mid_out]
+        )
+        third_1 = onward(first_1)
+        next_layer = jnp.where(within, mid, mid_out)
+        first_2, second_2 = cross(next_layer)
         far_out = along(far, outward)
-        rest = jnp.concatenate(
-            [jnp.where(within, mid, mid_out), jnp.where(within, far, far_out)], axis=0
+        third_1, first_2, second_2, far_out = join(
+            [third_1, first_2, second_2, far_out], [masked_mark]
         )
-        near_third = onward(near_first)
-        mine = [q_weight, first, second, third]
-        early = mine + [after] + [sibling(one) for one in mine[1:]]
-        mine = [near, near_first, near_second, near_third]
-        early += mine + [sibling(one) for one in mine]
-        early_places = jnp.concatenate(
-            [numbers(sides, range(4), [layer]), numbers(sides, range(4), [layer ^ 1])]
-        )
-        rest_first, rest_second = cross(rest)
-        done = products_call(early_places, tokens, early, masked, None)
-        rest_first = tie(rest_first, *done)
-        rest_third = onward(rest_first)
-        mine = [rest, rest_first, rest_second]
-        done = products_call(
-            numbers(sides, range(3), [two, three]),
-            tokens,
-            mine + [sibling(one) for one in mine],
-            masked,
-            done,
-        )
-        rest_third = tie(rest_third, *done)
-        late = [rest_third, sibling(rest_third)]
-        late_places = numbers(sides, [3], [two, three])
+        third_2 = onward(first_2)
+        last_layer = jnp.where(within, far, far_out)
+        first_3, second_3 = cross(last_layer)
+
+        def whole(*mine):
+            return list(mine) + [sibling(one) for one in mine]
+
+        early = [q_weight, first_0, second_0, third_0, other_0]
+        early += [sibling(one) for one in early[1:4]]
+        early += whole(near, first_1, second_1, third_1)
+        *done, mark = products_call(numbers(sides, levels[:2]), tokens, early, masked, None)
+        third_2, first_3, second_3 = join([third_2, first_3, second_3], [mark])
+        third_3 = onward(first_3)
+        middle_blocks = whole(next_layer, first_2, second_2, third_2)
+        *done, mark = products_call(numbers(sides, levels[2:3]), tokens, middle_blocks, masked, done)
+        third_3, = join([third_3], [mark])
+        late = whole(last_layer, first_3, second_3, third_3)
+        late_places = numbers(sides, levels[3:])
     else:
         half = places.shape[0] // 2
-        done = products_call(places[:half], tokens, arrived[:1], masked, None)
+        *done, _ = products_call(places[:half], tokens, arrived[:1], masked, None)
         late, late_places = arrived[1:], places[half:]
     partial, grad_tokens = done
-    queries, own, sent = query_call(late_places, tokens, late, partial, q_spikes, cotangent)
-    attended = attend_call(factor, queries, keys, values, high, low)
-    key_part, value_part = inner_call(queries, keys, values, cotangent)
-    adjoint = scan_sum(own, sent, chips, True, (attended, key_part))
+    queries, own, sent = query_call(late_places, tokens, late, partial, q_mask, cotangent)
+    attended, attended_mark = attend_call(factor, queries, keys, values, high, low)
+    key_part, value_part, inner_mark = inner_call(queries, keys, values, cotangent)
+    adjoint = scan_sum(own, sent, chips, True, (attended_mark, inner_mark))
     grad_tokens = back_call(late_places, late, masked, grad_tokens)
     grad_keys, grad_values = outer_call(
-        factor, key_part, value_part, keys, values, k_spikes, *adjoint
+        factor, key_part, value_part, keys, values, k_mask, *adjoint
     )
     return tuple(
         array.reshape(1, length, array.shape[1])

time: 179 us -> 186 us (1.039)
  the two profiles are of different devices: /device:TPU:12 before, /device:TPU:1 now
where the time goes in v2:
time: 186 us; the launch traced here: 184 us
  Pallas kernels  82.5 us (44%)
  starting transfers between devices  54 us (29%)
  waiting for transfers between devices  25.8 us (14%)
  other arithmetic  12 us (6%)
  local copies, waits for them, and re-layouts  8.49 us (5%)
    pallas_call x2, Pallas kernels, products_call(): pl.pallas_call(functools.partial(products_kernel, len(blocks), before is...  25.7 us
    ppermute x16, starting transfers between devices, sibling(): return lax.ppermute(array, 'core', SWAP)  19.3 us
    pallas_call x1, Pallas kernels, inner_call(): pl.pallas_call(inner_kernel, grid=(total // WIDE,), in_specs=[columns(len...  9.37 us
    ppermute x4, waiting for transfers between devices, onward(): return lax.ppermute(array, CTX, links(2))  9.15 us
    pallas_call x1, Pallas kernels, outer_call(): pl.pallas_call(functools.partial(outer_kernel, factor), grid=(total // PA...  9.05 us
    pallas_call x1, Pallas kernels, query_call(): pl.pallas_call(functools.partial(query_kernel, len(blocks)), in_specs=[sm...  8.88 us
    pallas_call x1, Pallas kernels, masked_call(): pl.pallas_call(functools.partial(masked_kernel, factor), grid=(total // W...  7.8 us
    pallas_call x1, Pallas kernels, memory_call(): pl.pallas_call(memory_kernel, grid=(total // PAIR,), in_specs=[columns(le...  7.55 us
  transfers between devices with their start and end apart: 41, of which 11 were waited for; matrix products, arithmetic and copies ran while one was open for 4% of the time, Pallas kernels for 31%

profile of v2, /device:TPU:1, one launch (start us, length us, event | category | flops | bytes accessed | tf_op | source)
XLA Modules:
  0.0 184.0 jit_solution(17125273334253118440)
XLA Ops:
  0.8 2.1 %collective-permute-done.after_ref.refs_4_ = bf16[128,2048]{1,0:T(8,128)(2,1)S(1)} collective-permute-done((bf16[128,2048]{1,0:T(8,128)(2,1)}, bf16[128,2048]{1,0:T(8,128)(2,1)S(1)}, u32[]{:S(2)}, u32[]{:S(2)}) %collective-permute-start) | collective-permute-done | bytes 524320 | tf_op jit(solution)/shard_map/ppermute | solution.py:575
  3.6 7.6 %own_memory.1 = (bf16[384,2048]{1,0:T(8,128)(2,1)}, bf16[384,2048]{1,0:T(8,128)(2,1)}, f32[2048,128]{1,0:T(8,128)}, bf16[2048,128]{1,0:T(8,128)(2,1)}) custom-call(bf16[384,2048]{1,0:T(8,128)(2,1)} %bitcast.52, s32[384,2048]{1,0:T(8,128)} %bitcast.51, bf16[384,2048]{1,0:T(8,128)(2,1)} %bitcast.46, bf16[128,2048]{1,0:T(8,128)(2,1)} %copy-done.26), custom_call_target="tpu_custom_call" | custom-call | tf_op jit(solution)/shard_map/own_memory/pallas_call | solution.py:77
  11.3 2.0 %collective-permute-done.1 = bf16[2048,128]{1,0:T(8,128)(2,1)S(1)} collective-permute-done((bf16[2048,128]{1,0:T(8,128)(2,1)}, bf16[2048,128]{1,0:T(8,128)(2,1)S(1)}, u32[]{:S(2)}, u32[]{:S(2)}) %collective-permute-start.1) | collective-permute-done | bytes 524320 | tf_op jit(solution)/shard_map/ppermute | solution.py:520
  13.3 1.3 convert_add_fusion.1
  15.4 4.3 %collective-permute-start.2 = (bf16[1024,128]{1,0:T(8,128)(2,1)}, bf16[1024,128]{1,0:T(8,128)(2,1)S(1)}, u32[]{:S(2)}, u32[]{:S(2)}) collective-permute-start(bf16[1024,128]{1,0:T(8,128)(2,1)} %fusion.8), channel_id=1, source_target_pairs={{0,8},{4,20},{8,0},{12,28},{16,24},{24,16},{1,9},{5,21},{9,1},{13,... | collective-permute-start | bytes 786440 | tf_op jit(solution)/shard_map/ppermute | solution.py:529
  19.6 1.4 collective-permute-start.5
  23.3 3.1 %collective-permute-start.3 = (bf16[1024,128]{1,0:T(8,128)(2,1)S(1)}, bf16[1024,128]{1,0:T(8,128)(2,1)S(1)}, u32[]{:S(2)}, u32[]{:S(2)}) collective-permute-start(bf16[1024,128]{1,0:T(8,128)(2,1)S(1)} %fusion.3), channel_id=1, source_target_pairs={{0,16},{4,12},{8,24},{12,4},{20,28},{28,20},{1,17},{5,13},{9,25},{... | collective-permute-start | bytes 786440 | tf_op jit(solution)/shard_map/ppermute | solution.py:534
  26.5 6.4 %collective-permute-done.5.refs_0_ = bf16[128,2048]{1,0:T(8,128)(2,1)S(1)} collective-permute-done((bf16[128,2048]{1,0:T(8,128)(2,1)}, bf16[128,2048]{1,0:T(8,128)(2,1)S(1)}, u32[]{:S(2)}, u32[]{:S(2)}) %collective-permute-start.5) | collective-permute-done | bytes 524320 | tf_op jit(solution)/shard_map/ppermute | solution.py:578
  35.1 2.2 %collective-permute-start.9 = (bf16[128,2048]{1,0:T(8,128)(2,1)}, bf16[128,2048]{1,0:T(8,128)(2,1)S(1)}, u32[]{:S(2)}, u32[]{:S(2)}) collective-permute-start(bf16[128,2048]{1,0:T(8,128)(2,1)} %get-tuple-element.48.refs_1_), channel_id=1, source_target_pairs={{0,16},{4,12},{8,24},{12,4},{16,0},{20,28},{24,8},{28,20},{1,17},{... | collective-permute-start | bytes 1572872 | tf_op jit(solution)/shard_map/ppermute | solution.py:584
  42.4 3.6 %collective-permute-done.9.refs_0_ = bf16[128,2048]{1,0:T(8,128)(2,1)S(1)} collective-permute-done((bf16[128,2048]{1,0:T(8,128)(2,1)}, bf16[128,2048]{1,0:T(8,128)(2,1)S(1)}, u32[]{:S(2)}, u32[]{:S(2)}) %collective-permute-start.9) | collective-permute-done | bytes 524320 | tf_op jit(solution)/shard_map/ppermute | solution.py:584
  45.9 5.9 %collective-permute-start.4 = (f32[1024,128]{1,0:T(8,128)S(1)}, f32[1024,128]{1,0:T(8,128)}, u32[]{:S(2)}, u32[]{:S(2)}) collective-permute-start(f32[1024,128]{1,0:T(8,128)S(1)} %fusion.2), channel_id=1, source_target_pairs={{0,4},{4,0},{1,5},{5,1},{2,6},{6,2},{3,7},{7,3},{8,12},{12,8},{9,1... | collective-permute-start | bytes 1572872 | tf_op jit(solution)/shard_map/ppermute | solution.py:538
  51.9 3.3 %collective-permute-start.21 = (bf16[128,2048]{1,0:T(8,128)(2,1)}, bf16[128,2048]{1,0:T(8,128)(2,1)}, u32[]{:S(2)}, u32[]{:S(2)}) collective-permute-start(bf16[128,2048]{1,0:T(8,128)(2,1)} %get-tuple-element.48.refs_1_), channel_id=1, source_target_pairs={{0,4},{4,0},{1,5},{5,1},{2,6},{6,2},{3,7},{7,3},{8,12},{12,8},{9,1... | collective-permute-start | bytes 1572872 | tf_op jit(solution)/shard_map/ppermute | solution.py:575
  55.8 1.8 collective-permute-start.22
  60.4 1.3 collective-permute-start.15
  61.7 1.4 collective-permute-start.16
  64.2 5.6 %collective-permute-done.14.refs_0_ = bf16[128,2048]{1,0:T(8,128)(2,1)S(1)} collective-permute-done((bf16[128,2048]{1,0:T(8,128)(2,1)}, bf16[128,2048]{1,0:T(8,128)(2,1)S(1)}, u32[]{:S(2)}, u32[]{:S(2)}) %collective-permute-start.14) | collective-permute-done | bytes 524320 | tf_op jit(solution)/shard_map/ppermute | solution.py:584
  73.1 7.8 %masked_grad.1 = (bf16[384,2048]{1,0:T(8,128)(2,1)}, bf16[384,2048]{1,0:T(8,128)(2,1)}, f32[8,128]{1,0:T(8,128)}) custom-call(bf16[384,2048]{1,0:T(8,128)(2,1)} %bitcast.53, bf16[384,2048]{1,0:T(8,128)(2,1)} %bitcast.47, bf16[384,2048]{1,0:T(8,128)(2,1)} %get-tuple-element.43.keys_ref, s32[384,2048]{1,0:T(8,128)} %bitcast.56, ...), custom_call_target="tpu_custom_call" | custom-call | flops 2415919104 | bytes 9437184 | tf_op jit(solution)/shard_map/masked_grad/pallas_call | solution.py:158
  81.0 5.1 %collective-permute-start.24 = (bf16[128,2048]{1,0:T(8,128)(2,1)S(1)}, bf16[128,2048]{1,0:T(8,128)(2,1)}, u32[]{:S(2)}, u32[]{:S(2)}) collective-permute-start(bf16[128,2048]{1,0:T(8,128)(2,1)S(1)} %copy-done.23), channel_id=1, source_target_pairs={{0,4},{4,0},{1,5},{5,1},{2,6},{6,2},{3,7},{7,3},{8,12},{12,8},{9,1... | collective-permute-start | bytes 1572872 | tf_op jit(solution)/shard_map/ppermute | solution.py:575
  86.1 3.3 %collective-permute-start.23 = (bf16[128,2048]{1,0:T(8,128)(2,1)S(1)}, bf16[128,2048]{1,0:T(8,128)(2,1)}, u32[]{:S(2)}, u32[]{:S(2)}) collective-permute-start(bf16[128,2048]{1,0:T(8,128)(2,1)S(1)} %copy-done.21), channel_id=1, source_target_pairs={{0,4},{4,0},{1,5},{5,1},{2,6},{6,2},{3,7},{7,3},{8,12},{12,8},{9,1... | collective-permute-start | bytes 1572872 | tf_op jit(solution)/shard_map/ppermute | solution.py:575
  92.6 3.0 %collective-permute-start.19 = (bf16[128,2048]{1,0:T(8,128)(2,1)S(1)}, bf16[128,2048]{1,0:T(8,128)(2,1)S(1)}, u32[]{:S(2)}, u32[]{:S(2)}) collective-permute-start(bf16[128,2048]{1,0:T(8,128)(2,1)S(1)} %broadcast_select_fusion.refs_0_), channel_id=1, source_target_pairs={{0,8},{4,20},{8,0},{12,28},{16,24},{20,4},{24,16},{28,12},{1,9},{5... | collective-permute-start | bytes 1572872 | tf_op jit(solution)/shard_map/ppermute | solution.py:581
  95.6 1.5 collective-permute-start.18
  97.1 15.7 %products.2 = (f32[384,2048]{1,0:T(8,128)}, bf16[384,4096]{1,0:T(8,128)(2,1)}, f32[8,128]{1,0:T(8,128)}) custom-call(s32[16]{0:T(128)} %stack.139.places_ref, bf16[384,4096]{1,0:T(8,128)(2,1)} %bitcast.42, bf16[384,2048]{1,0:T(8,128)(2,1)} %get-tuple-element.46.masked_ref, bf16[128,2048]{1,0:T(8,128)(2,1)} %refs_0_.1, ...), custom_call_target="tpu_custom_call" | custom-call | flops 6442450944 | bytes 14680064 | tf_op jit(solution)/shard_map/products/pallas_call | solution.py:275
  115.9 2.1 %collective-permute-start.33 = (bf16[128,2048]{1,0:T(8,128)(2,1)S(1)}, bf16[128,2048]{1,0:T(8,128)(2,1)S(1)}, u32[]{:S(2)}, u32[]{:S(2)}) collective-permute-start(bf16[128,2048]{1,0:T(8,128)(2,1)S(1)} %broadcast_select_fusion.refs_0_), channel_id=1, source_target_pairs={{0,4},{4,0},{1,5},{5,1},{2,6},{6,2},{3,7},{7,3},{8,12},{12,8},{9,1... | collective-permute-start | bytes 1572872 | tf_op jit(solution)/shard_map/ppermute | solution.py:575
  118.6 9.9 %products.3 = (f32[384,2048]{1,0:T(8,128)}, bf16[384,4096]{1,0:T(8,128)(2,1)}, f32[8,128]{1,0:T(8,128)}) custom-call(s32[8]{0:T(128)} %stack.122.places_ref, bf16[384,4096]{1,0:T(8,128)(2,1)} %bitcast.43, bf16[384,2048]{1,0:T(8,128)(2,1)} %get-tuple-element.46.masked_ref, ...), custom_call_target="tpu_custom_call", output_to_operand_aliasing={{0}: (11, {}), {1}: (12, {})} | custom-call | flops 3221225472 | bytes 10485760 | tf_op jit(solution)/shard_map/products/pallas_call | solution.py:275
  132.2 8.9 %queries.1 = (bf16[384,2048]{1,0:T(8,128)(2,1)}, f32[2048,128]{1,0:T(8,128)}, bf16[2048,128]{1,0:T(8,128)(2,1)}) custom-call(s32[8]{0:T(128)} %stack.113.places_ref, bf16[384,4096]{1,0:T(8,128)(2,1)} %bitcast.44, f32[384,2048]{1,0:T(8,128)} %get-tuple-element.65.before_ref, bf16[384,2048]{1,0:T(8,128)(2,1)} %get-tuple-element.66.spike_ref, ...), custom_call_target="tpu_custom_call" | custom-call | flops 1610612736 | bytes 13631488 | tf_op jit(solution)/shard_map/queries/pallas_call | solution.py:373
  141.4 1.9 %collective-permute-done.37 = bf16[2048,128]{1,0:T(8,128)(2,1)S(1)} collective-permute-done((bf16[2048,128]{1,0:T(8,128)(2,1)}, bf16[2048,128]{1,0:T(8,128)(2,1)S(1)}, u32[]{:S(2)}, u32[]{:S(2)}) %collective-permute-start.37) | collective-permute-done | bytes 524320 | tf_op jit(solution)/shard_map/ppermute | solution.py:520
  143.3 1.3 convert_add_fusion
  146.0 6.9 %attended.1 = (bf16[384,2048]{1,0:T(8,128)(2,1)}, f32[8,128]{1,0:T(8,128)}) custom-call(bf16[384,2048]{1,0:T(8,128)(2,1)} %get-tuple-element.70.query_ref, bf16[384,2048]{1,0:T(8,128)(2,1)} %get-tuple-element.43.keys_ref, bf16[384,2048]{1,0:T(8,128)(2,1)} %bitcast.48, bf16[2048,128]{1,0:T(8,128)(2,1)} %get-tuple-element.85.high_ref, ...), custom_call_target="tpu_custom_call" | custom-call | flops 2415919104 | bytes 6291456 | tf_op jit(solution)/shard_map/attended/pallas_call | solution.py:414
  153.7 1.9 %collective-permute-start.39 = (bf16[1024,128]{1,0:T(8,128)(2,1)}, bf16[1024,128]{1,0:T(8,128)(2,1)S(1)}, u32[]{:S(2)}, u32[]{:S(2)}) collective-permute-start(bf16[1024,128]{1,0:T(8,128)(2,1)} %join.12), channel_id=1, source_target_pairs={{4,12},{12,4},{16,0},{20,28},{24,8},{28,20},{5,13},{13,5},{17,1},{... | collective-permute-start | bytes 786440 | tf_op jit(solution)/shard_map/ppermute | solution.py:534
  155.6 9.4 %inner.1 = (f32[384,2048]{1,0:T(8,128)}, f32[384,2048]{1,0:T(8,128)}, f32[8,128]{1,0:T(8,128)}) custom-call(bf16[384,2048]{1,0:T(8,128)(2,1)} %get-tuple-element.70.query_ref, bf16[384,2048]{1,0:T(8,128)(2,1)} %get-tuple-element.43.keys_ref, bf16[384,2048]{1,0:T(8,128)(2,1)} %bitcast.49, bf16[384,2048]{1,0:T(8,128)(2,1)} %bitcast.55), custom_call_target="tpu_custom_call" | custom-call | flops 3623878656 | bytes 12582912 | tf_op jit(solution)/shard_map/inner/pallas_call | solution.py:439
  166.3 7.3 %grad_tokens.1 = bf16[384,4096]{1,0:T(8,128)(2,1)} custom-call(s32[8]{0:T(128)} %stack.113.places_ref, bf16[384,2048]{1,0:T(8,128)(2,1)} %get-tuple-element.46.masked_ref, bf16[128,2048]{1,0:T(8,128)(2,1)} %copy-done.3, bf16[128,2048]{1,0:T(8,128)(2,1)} %get-tuple-element.67.refs_1_, ...), custom_call_target="tpu_custom_call", output_to_operand_aliasing={{}: (10, {})} | custom-call | flops 1610612736 | bytes 7340032 | tf_op jit(solution)/shard_map/grad_tokens/pallas_call | solution.py:313
  174.9 9.1 %outer.1 = (bf16[384,2048]{1,0:T(8,128)(2,1)}, bf16[384,2048]{1,0:T(8,128)(2,1)}) custom-call(f32[384,2048]{1,0:T(8,128)} %get-tuple-element.73.key_ref, f32[384,2048]{1,0:T(8,128)} %get-tuple-element.74.val_ref, bf16[384,2048]{1,0:T(8,128)(2,1)} %get-tuple-element.43.keys_ref, bf16[384,2048]{1,0:T(8,128)(2,1)} %bitcast.50, ...), custom_call_target="tpu_custom_call" | custom-call | flops 805306368 | bytes 15728640 | tf_op jit(solution)/shard_map/outer/pallas_call | solution.py:465
  (139 shorter events, 34.7 us)
Async XLA Ops:
  15.4 7.9 %collective-permute-start.2 = (bf16[1024,128]{1,0:T(8,128)(2,1)}, bf16[1024,128]{1,0:T(8,128)(2,1)S(1)}, u32[]{:S(2)}, u32[]{:S(2)}) collective-permute-start(bf16[1024,128]{1,0:T(8,128)(2,1)} %fusion.8), channel_id=1, source_target_pairs={{0,8},{4,20},{8,0},{12,28},{16,24},{24,16},{1,9},{5,21},{9,1},{13,... | collective-permute-start | bytes 786440 | tf_op jit(solution)/shard_map/ppermute | solution.py:529
  19.6 13.2 %collective-permute-start.5 = (bf16[128,2048]{1,0:T(8,128)(2,1)}, bf16[128,2048]{1,0:T(8,128)(2,1)S(1)}, u32[]{:S(2)}, u32[]{:S(2)}) collective-permute-start(bf16[128,2048]{1,0:T(8,128)(2,1)} %refs_0_.1), channel_id=1, source_target_pairs={{0,1},{1,0},{2,3},{3,2},{4,5},{5,4},{6,7},{7,6},{8,9},{9,8},{10,11... | collective-permute-start | bytes 1572872 | tf_op jit(solution)/shard_map/ppermute | solution.py:578
  21.0 11.9 %collective-permute-start.6 = (bf16[128,2048]{1,0:T(8,128)(2,1)}, bf16[128,2048]{1,0:T(8,128)(2,1)S(1)}, u32[]{:S(2)}, u32[]{:S(2)}) collective-permute-start(bf16[128,2048]{1,0:T(8,128)(2,1)} %refs_0_.1), channel_id=1, source_target_pairs={{1,2},{2,1},{5,6},{6,5},{9,10},{10,9},{13,14},{14,13},{17,18},{18,... | collective-permute-start | bytes 1572872 | tf_op jit(solution)/shard_map/ppermute | solution.py:578
  21.7 12.4 %collective-permute-start.7 = (bf16[128,2048]{1,0:T(8,128)(2,1)}, bf16[128,2048]{1,0:T(8,128)(2,1)S(1)}, u32[]{:S(2)}, u32[]{:S(2)}) collective-permute-start(bf16[128,2048]{1,0:T(8,128)(2,1)} %refs_0_.1), channel_id=1, source_target_pairs={{0,8},{4,20},{8,0},{12,28},{16,24},{20,4},{24,16},{28,12},{1,9},{5... | collective-permute-start | bytes 1572872 | tf_op jit(solution)/shard_map/ppermute | solution.py:581
  21.8 13.4 %collective-permute-start.8 = (bf16[128,2048]{1,0:T(8,128)(2,1)}, bf16[128,2048]{1,0:T(8,128)(2,1)}, u32[]{:S(2)}, u32[]{:S(2)}) collective-permute-start(bf16[128,2048]{1,0:T(8,128)(2,1)} %refs_0_.1), channel_id=1, source_target_pairs={{0,16},{4,12},{8,24},{12,4},{16,0},{20,28},{24,8},{28,20},{1,17},{... | collective-permute-start | bytes 1572872 | tf_op jit(solution)/shard_map/ppermute | solution.py:581
  23.3 16.0 %collective-permute-start.3 = (bf16[1024,128]{1,0:T(8,128)(2,1)S(1)}, bf16[1024,128]{1,0:T(8,128)(2,1)S(1)}, u32[]{:S(2)}, u32[]{:S(2)}) collective-permute-start(bf16[1024,128]{1,0:T(8,128)(2,1)S(1)} %fusion.3), channel_id=1, source_target_pairs={{0,16},{4,12},{8,24},{12,4},{20,28},{28,20},{1,17},{5,13},{9,25},{... | collective-permute-start | bytes 786440 | tf_op jit(solution)/shard_map/ppermute | solution.py:534
  35.1 10.8 %collective-permute-start.9 = (bf16[128,2048]{1,0:T(8,128)(2,1)}, bf16[128,2048]{1,0:T(8,128)(2,1)S(1)}, u32[]{:S(2)}, u32[]{:S(2)}) collective-permute-start(bf16[128,2048]{1,0:T(8,128)(2,1)} %get-tuple-element.48.refs_1_), channel_id=1, source_target_pairs={{0,16},{4,12},{8,24},{12,4},{16,0},{20,28},{24,8},{28,20},{1,17},{... | collective-permute-start | bytes 1572872 | tf_op jit(solution)/shard_map/ppermute | solution.py:584
  37.3 14.6 %collective-permute-start.10 = (bf16[128,2048]{1,0:T(8,128)(2,1)}, bf16[128,2048]{1,0:T(8,128)(2,1)}, u32[]{:S(2)}, u32[]{:S(2)}) collective-permute-start(bf16[128,2048]{1,0:T(8,128)(2,1)} %get-tuple-element.49.refs_8_), channel_id=1, source_target_pairs={{0,8},{4,20},{8,0},{12,28},{16,24},{20,4},{24,16},{28,12},{1,9},{5... | collective-permute-start | bytes 1572872 | tf_op jit(solution)/shard_map/ppermute | solution.py:581
  38.6 17.2 %collective-permute-start.11 = (bf16[128,2048]{1,0:T(8,128)(2,1)}, bf16[128,2048]{1,0:T(8,128)(2,1)}, u32[]{:S(2)}, u32[]{:S(2)}) collective-permute-start(bf16[128,2048]{1,0:T(8,128)(2,1)} %get-tuple-element.49.refs_8_), channel_id=1, source_target_pairs={{0,16},{4,12},{8,24},{12,4},{16,0},{20,28},{24,8},{28,20},{1,17},{... | collective-permute-start | bytes 1572872 | tf_op jit(solution)/shard_map/ppermute | solution.py:581
  38.6 19.0 %collective-permute-start.12 = (bf16[128,2048]{1,0:T(8,128)(2,1)}, bf16[128,2048]{1,0:T(8,128)(2,1)S(1)}, u32[]{:S(2)}, u32[]{:S(2)}) collective-permute-start(bf16[128,2048]{1,0:T(8,128)(2,1)} %get-tuple-element.49.refs_8_), channel_id=1, source_target_pairs={{1,2},{2,1},{5,6},{6,5},{9,10},{10,9},{13,14},{14,13},{17,18},{18,... | collective-permute-start | bytes 1572872 | tf_op jit(solution)/shard_map/ppermute | solution.py:578
  40.0 17.6 %collective-permute-start.13 = (bf16[128,2048]{1,0:T(8,128)(2,1)}, bf16[128,2048]{1,0:T(8,128)(2,1)S(1)}, u32[]{:S(2)}, u32[]{:S(2)}) collective-permute-start(bf16[128,2048]{1,0:T(8,128)(2,1)} %get-tuple-element.47), channel_id=1, source_target_pairs={{1,0},{2,3},{5,4},{6,7},{9,8},{10,11},{13,12},{14,15},{17,16},{18,... | collective-permute-start | bytes 1572872 | tf_op jit(solution)/shard_map/ppermute | solution.py:578
  45.9 15.8 %collective-permute-start.4 = (f32[1024,128]{1,0:T(8,128)S(1)}, f32[1024,128]{1,0:T(8,128)}, u32[]{:S(2)}, u32[]{:S(2)}) collective-permute-start(f32[1024,128]{1,0:T(8,128)S(1)} %fusion.2), channel_id=1, source_target_pairs={{0,4},{4,0},{1,5},{5,1},{2,6},{6,2},{3,7},{7,3},{8,12},{12,8},{9,1... | collective-permute-start | bytes 1572872 | tf_op jit(solution)/shard_map/ppermute | solution.py:538
  51.9 37.6 %collective-permute-start.21 = (bf16[128,2048]{1,0:T(8,128)(2,1)}, bf16[128,2048]{1,0:T(8,128)(2,1)}, u32[]{:S(2)}, u32[]{:S(2)}) collective-permute-start(bf16[128,2048]{1,0:T(8,128)(2,1)} %get-tuple-element.48.refs_1_), channel_id=1, source_target_pairs={{0,4},{4,0},{1,5},{5,1},{2,6},{6,2},{3,7},{7,3},{8,12},{12,8},{9,1... | collective-permute-start | bytes 1572872 | tf_op jit(solution)/shard_map/ppermute | solution.py:575
  55.8 34.5 %collective-permute-start.22 = (bf16[128,2048]{1,0:T(8,128)(2,1)}, bf16[128,2048]{1,0:T(8,128)(2,1)}, u32[]{:S(2)}, u32[]{:S(2)}) collective-permute-start(bf16[128,2048]{1,0:T(8,128)(2,1)} %get-tuple-element.57.refs_2_), channel_id=1, source_target_pairs={{0,4},{4,0},{1,5},{5,1},{2,6},{6,2},{3,7},{7,3},{8,12},{12,8},{9,1... | collective-permute-start | bytes 1572872 | tf_op jit(solution)/shard_map/ppermute | solution.py:575
  59.2 10.7 %collective-permute-start.14 = (bf16[128,2048]{1,0:T(8,128)(2,1)}, bf16[128,2048]{1,0:T(8,128)(2,1)S(1)}, u32[]{:S(2)}, u32[]{:S(2)}) collective-permute-start(bf16[128,2048]{1,0:T(8,128)(2,1)} %get-tuple-element.51.refs_9_), channel_id=1, source_target_pairs={{0,16},{4,12},{8,24},{12,4},{16,0},{20,28},{24,8},{28,20},{1,17},{... | collective-permute-start | bytes 1572872 | tf_op jit(solution)/shard_map/ppermute | solution.py:584
  60.4 20.5 %collective-permute-start.15 = (bf16[128,2048]{1,0:T(8,128)(2,1)S(1)}, bf16[128,2048]{1,0:T(8,128)(2,1)S(1)}, u32[]{:S(2)}, u32[]{:S(2)}) collective-permute-start(bf16[128,2048]{1,0:T(8,128)(2,1)S(1)} %broadcast_select_fusion.1.refs_0_), channel_id=1, source_target_pairs={{0,8},{4,20},{8,0},{12,28},{16,24},{20,4},{24,16},{28,12},{1,9},{5... | collective-permute-start | bytes 1572872 | tf_op jit(solution)/shard_map/ppermute | solution.py:581
  61.7 24.3 %collective-permute-start.16 = (bf16[128,2048]{1,0:T(8,128)(2,1)S(1)}, bf16[128,2048]{1,0:T(8,128)(2,1)}, u32[]{:S(2)}, u32[]{:S(2)}) collective-permute-start(bf16[128,2048]{1,0:T(8,128)(2,1)S(1)} %broadcast_select_fusion.1.refs_0_), channel_id=1, source_target_pairs={{0,16},{4,12},{8,24},{12,4},{16,0},{20,28},{24,8},{28,20},{1,17},{... | collective-permute-start | bytes 1572872 | tf_op jit(solution)/shard_map/ppermute | solution.py:581
  70.6 15.5 %collective-permute-start.17 = (bf16[128,2048]{1,0:T(8,128)(2,1)S(1)}, bf16[128,2048]{1,0:T(8,128)(2,1)S(1)}, u32[]{:S(2)}, u32[]{:S(2)}) collective-permute-start(bf16[128,2048]{1,0:T(8,128)(2,1)S(1)} %copy-done.8), channel_id=1, source_target_pairs={{1,0},{2,3},{5,4},{6,7},{9,8},{10,11},{13,12},{14,15},{17,16},{18,... | collective-permute-start | bytes 1572872 | tf_op jit(solution)/shard_map/ppermute | solution.py:578
  81.0 11.1 %collective-permute-start.24 = (bf16[128,2048]{1,0:T(8,128)(2,1)S(1)}, bf16[128,2048]{1,0:T(8,128)(2,1)}, u32[]{:S(2)}, u32[]{:S(2)}) collective-permute-start(bf16[128,2048]{1,0:T(8,128)(2,1)S(1)} %copy-done.23), channel_id=1, source_target_pairs={{0,4},{4,0},{1,5},{5,1},{2,6},{6,2},{3,7},{7,3},{8,12},{12,8},{9,1... | collective-permute-start | bytes 1572872 | tf_op jit(solution)/shard_map/ppermute | solution.py:575
  86.0 9.6 %collective-permute-start.25 = (bf16[128,2048]{1,0:T(8,128)(2,1)}, bf16[128,2048]{1,0:T(8,128)(2,1)}, u32[]{:S(2)}, u32[]{:S(2)}) collective-permute-start(bf16[128,2048]{1,0:T(8,128)(2,1)} %get-tuple-element.51.refs_9_), channel_id=1, source_target_pairs={{0,4},{4,0},{1,5},{5,1},{2,6},{6,2},{3,7},{7,3},{8,12},{12,8},{9,1... | collective-permute-start | bytes 1572872 | tf_op jit(solution)/shard_map/ppermute | solution.py:575
  92.1 23.8 %collective-permute-start.28 = (bf16[128,2048]{1,0:T(8,128)(2,1)S(1)}, bf16[128,2048]{1,0:T(8,128)(2,1)S(1)}, u32[]{:S(2)}, u32[]{:S(2)}) collective-permute-start(bf16[128,2048]{1,0:T(8,128)(2,1)S(1)} %broadcast_select_fusion.1.refs_0_), channel_id=1, source_target_pairs={{0,4},{4,0},{1,5},{5,1},{2,6},{6,2},{3,7},{7,3},{8,12},{12,8},{9,1... | collective-permute-start | bytes 1572872 | tf_op jit(solution)/shard_map/ppermute | solution.py:575
  92.6 21.5 %collective-permute-start.19 = (bf16[128,2048]{1,0:T(8,128)(2,1)S(1)}, bf16[128,2048]{1,0:T(8,128)(2,1)S(1)}, u32[]{:S(2)}, u32[]{:S(2)}) collective-permute-start(bf16[128,2048]{1,0:T(8,128)(2,1)S(1)} %broadcast_select_fusion.refs_0_), channel_id=1, source_target_pairs={{0,8},{4,20},{8,0},{12,28},{16,24},{20,4},{24,16},{28,12},{1,9},{5... | collective-permute-start | bytes 1572872 | tf_op jit(solution)/shard_map/ppermute | solution.py:581
  95.6 18.5 %collective-permute-start.20 = (bf16[128,2048]{1,0:T(8,128)(2,1)S(1)}, bf16[128,2048]{1,0:T(8,128)(2,1)S(1)}, u32[]{:S(2)}, u32[]{:S(2)}) collective-permute-start(bf16[128,2048]{1,0:T(8,128)(2,1)S(1)} %broadcast_select_fusion.refs_0_), channel_id=1, source_target_pairs={{0,16},{4,12},{8,24},{12,4},{16,0},{20,28},{24,8},{28,20},{1,17},{... | collective-permute-start | bytes 1572872 | tf_op jit(solution)/shard_map/ppermute | solution.py:581
  95.6 17.2 %collective-permute-start.18 = (bf16[128,2048]{1,0:T(8,128)(2,1)S(1)}, bf16[128,2048]{1,0:T(8,128)(2,1)S(1)}, u32[]{:S(2)}, u32[]{:S(2)}) collective-permute-start(bf16[128,2048]{1,0:T(8,128)(2,1)S(1)} %copy-done.11), channel_id=1, source_target_pairs={{0,16},{4,12},{8,24},{12,4},{16,0},{20,28},{24,8},{28,20},{1,17},{... | collective-permute-start | bytes 1572872 | tf_op jit(solution)/shard_map/ppermute | solution.py:584
  97.1 20.9 %collective-permute-start.29 = (bf16[128,2048]{1,0:T(8,128)(2,1)S(1)}, bf16[128,2048]{1,0:T(8,128)(2,1)}, u32[]{:S(2)}, u32[]{:S(2)}) collective-permute-start(bf16[128,2048]{1,0:T(8,128)(2,1)S(1)} %copy-done.11), channel_id=1, source_target_pairs={{0,4},{4,0},{1,5},{5,1},{2,6},{6,2},{3,7},{7,3},{8,12},{12,8},{9,1... | collective-permute-start | bytes 1572872 | tf_op jit(solution)/shard_map/ppermute | solution.py:575
  115.2 13.2 %collective-permute-start.32 = (bf16[128,2048]{1,0:T(8,128)(2,1)}, bf16[128,2048]{1,0:T(8,128)(2,1)S(1)}, u32[]{:S(2)}, u32[]{:S(2)}) collective-permute-start(bf16[128,2048]{1,0:T(8,128)(2,1)} %get-tuple-element.67.refs_1_), channel_id=1, source_target_pairs={{0,16},{4,12},{8,24},{12,4},{16,0},{20,28},{24,8},{28,20},{1,17},{... | collective-permute-start | bytes 1572872 | tf_op jit(solution)/shard_map/ppermute | solution.py:584
  115.9 14.3 %collective-permute-start.33 = (bf16[128,2048]{1,0:T(8,128)(2,1)S(1)}, bf16[128,2048]{1,0:T(8,128)(2,1)S(1)}, u32[]{:S(2)}, u32[]{:S(2)}) collective-permute-start(bf16[128,2048]{1,0:T(8,128)(2,1)S(1)} %broadcast_select_fusion.refs_0_), channel_id=1, source_target_pairs={{0,4},{4,0},{1,5},{5,1},{2,6},{6,2},{3,7},{7,3},{8,12},{12,8},{9,1... | collective-permute-start | bytes 1572872 | tf_op jit(solution)/shard_map/ppermute | solution.py:575
  118.0 12.1 %collective-permute-start.34 = (bf16[128,2048]{1,0:T(8,128)(2,1)}, bf16[128,2048]{1,0:T(8,128)(2,1)S(1)}, u32[]{:S(2)}, u32[]{:S(2)}) collective-permute-start(bf16[128,2048]{1,0:T(8,128)(2,1)} %get-tuple-element.67.refs_1_), channel_id=1, source_target_pairs={{0,4},{4,0},{1,5},{5,1},{2,6},{6,2},{3,7},{7,3},{8,12},{12,8},{9,1... | collective-permute-start | bytes 1572872 | tf_op jit(solution)/shard_map/ppermute | solution.py:575
  118.1 12.1 %collective-permute-start.35 = (bf16[128,2048]{1,0:T(8,128)(2,1)}, bf16[128,2048]{1,0:T(8,128)(2,1)S(1)}, u32[]{:S(2)}, u32[]{:S(2)}) collective-permute-start(bf16[128,2048]{1,0:T(8,128)(2,1)} %get-tuple-element.68.refs_2_), channel_id=1, source_target_pairs={{0,4},{4,0},{1,5},{5,1},{2,6},{6,2},{3,7},{7,3},{8,12},{12,8},{9,1... | collective-permute-start | bytes 1572872 | tf_op jit(solution)/shard_map/ppermute | solution.py:575
  144.7 8.2 %collective-permute-start.38 = (bf16[1024,128]{1,0:T(8,128)(2,1)S(1)}, bf16[1024,128]{1,0:T(8,128)(2,1)S(1)}, u32[]{:S(2)}, u32[]{:S(2)}) collective-permute-start(bf16[1024,128]{1,0:T(8,128)(2,1)S(1)} %fusion.9), channel_id=1, source_target_pairs={{0,8},{8,0},{16,24},{20,4},{24,16},{28,12},{1,9},{9,1},{17,25},{21... | collective-permute-start | bytes 786440 | tf_op jit(solution)/shard_map/ppermute | solution.py:529
  153.7 11.3 %collective-permute-start.39 = (bf16[1024,128]{1,0:T(8,128)(2,1)}, bf16[1024,128]{1,0:T(8,128)(2,1)S(1)}, u32[]{:S(2)}, u32[]{:S(2)}) collective-permute-start(bf16[1024,128]{1,0:T(8,128)(2,1)} %join.12), channel_id=1, source_target_pairs={{4,12},{12,4},{16,0},{20,28},{24,8},{28,20},{5,13},{13,5},{17,1},{... | collective-permute-start | bytes 786440 | tf_op jit(solution)/shard_map/ppermute | solution.py:534
  165.9 7.7 %collective-permute-start.40 = (f32[1024,128]{1,0:T(8,128)}, f32[1024,128]{1,0:T(8,128)S(1)}, u32[]{:S(2)}, u32[]{:S(2)}) collective-permute-start(f32[1024,128]{1,0:T(8,128)} %join.13), channel_id=1, source_target_pairs={{0,4},{4,0},{1,5},{5,1},{2,6},{6,2},{3,7},{7,3},{8,12},{12,8},{9,1... | collective-permute-start | bytes 1572872 | tf_op jit(solution)/shard_map/ppermute | solution.py:538
  (37 other events, 198.8 us)

commit v3 on v2

v3 whole, which is shorter than its diff:
```python
import functools
import math

import jax
import jax.numpy as jnp
from jax import lax
from jax.experimental import pallas as pl
from jax.experimental.pallas import tpu as pltpu
from jax.sharding import Mesh, PartitionSpec as P

HEAD = 128
PIECE = 128
WIDE = 512
CTX = ("chip", "core")
SWAP = [(0, 1), (1, 0)]
f32, bf16 = jnp.float32, jnp.bfloat16
VMEM_LIMIT = 26 * 1024 * 1024


def nn(a, b):
    return lax.dot_general(a, b, (((1,), (0,)), ((), ())), preferred_element_type=f32)


def nt(a, b):
    return lax.dot_general(a, b, (((1,), (1,)), ((), ())), preferred_element_type=f32)


def tn(a, b):
    return lax.dot_general(a, b, (((0,), (0,)), ((), ())), preferred_element_type=f32)


def params(flops, moved):
    return dict(
        compiler_params=pltpu.CompilerParams(vmem_limit_bytes=VMEM_LIMIT),
        cost_estimate=pl.CostEstimate(flops=flops, bytes_accessed=moved, transcendentals=0),
    )


MARK = jax.ShapeDtypeStruct((8, HEAD), f32)


def set_mark(mark_ref):
    mark_ref[...] = jnp.zeros_like(mark_ref)


def fast(array):
    return pltpu.with_memory_space_constraint(array, pltpu.VMEM)


def slow(array):
    return pltpu.with_memory_space_constraint(array, pltpu.HBM)


def specs(places):
    spaces = dict(V=pltpu.VMEM, H=pltpu.HBM, S=pltpu.SMEM, A=pl.ANY)
    return [pl.BlockSpec(memory_space=spaces[place]) for place in places]


def kernel_call(body, places, args, out_places, outs, name, cost, scratch=(), aliases=None):
    holds = dict(V=fast, H=slow)
    made = pl.pallas_call(
        body,
        in_specs=specs(places),
        out_specs=specs(out_places),
        out_shape=[
            pltpu.VMEM(shape, dtype) if place == "V" else jax.ShapeDtypeStruct(shape, dtype)
            for place, (shape, dtype) in zip(out_places, outs)
        ],
        scratch_shapes=list(scratch),
        input_output_aliases=aliases or {},
        name=name,
        **params(*cost),
    )
    return made(
        *[holds[place](one) if place in holds else one for place, one in zip(places, args)]
    )


class Copies:
    def __init__(self, sems):
        self.sems = sems
        self.used = 0

    def start(self, source, target):
        copy = pltpu.make_async_copy(source, target, self.sems.at[self.used])
        self.used += 1
        copy.start()
        return copy


def columns(at, wide=None):
    return (slice(None), pl.ds(at, wide or WIDE))


def groups(total, body):
    @pl.loop(0, total // WIDE)
    def _(group):
        body(group, pl.multiple_of(group * WIDE, WIDE))


def heads(at):
    return [pl.ds(pl.multiple_of(at + head, HEAD), HEAD) for head in range(0, WIDE, HEAD)]


def memory_kernel(
    key_ref, spike_ref, value_ref, keys_ref, mask_ref, values_ref, own_ref, sent_ref, mark_ref,
    key_in, spike_in, sems,
):
    set_mark(mark_ref)
    copies = Copies(sems)
    wide = range(0, keys_ref.shape[1], WIDE)
    pairs = ((key_ref, key_in), (spike_ref, spike_in), (value_ref, values_ref))
    parts = [
        [copies.start(here.at[columns(at)], there.at[columns(at)]) for here, there in pairs]
        for at in wide
    ]
    for at, part in zip(wide, parts):
        for copy in part:
            copy.wait()
        cols = slice(at, at + WIDE)
        mask = spike_in[:, cols].astype(f32).astype(bf16)
        keys = key_in[:, cols] * mask
        keys_ref[:, cols] = keys
        mask_ref[:, cols] = mask
        for head in range(0, WIDE, HEAD):
            here = slice(at + head, at + head + HEAD)
            own = tn(keys[:, head : head + HEAD], values_ref[:, here])
            own_ref[here, :] = own
            sent_ref[here, :] = own.astype(bf16)


def memory_call(key_input, k_spikes, values):
    length, total = values.shape
    block, state = (length, total), (total, HEAD)
    return kernel_call(
        memory_kernel,
        "HHH",
        (key_input, k_spikes, values),
        "VVVVVV",
        [(block, bf16)] * 3 + [(state, f32), (state, bf16), (MARK.shape, f32)],
        "own_memory",
        (2 * length * total * HEAD, 12 * length * total),
        [
            pltpu.VMEM(block, bf16),
            pltpu.VMEM(block, jnp.int32),
            pltpu.SemaphoreType.DMA((3 * total // WIDE,)),
        ],
    )


def join_kernel(*refs):
    del refs


def join(arrays, others=()):
    number = len(arrays)
    return kernel_call(
        join_kernel,
        ["H"] * number + ["A"] * len(others),
        (*arrays, *others),
        ["H"] * number,
        [(one.shape, one.dtype) for one in arrays],
        "join",
        (0, 0),
        aliases={at: at for at in range(number)},
    )


def keep_lower(square, flipped=False):
    row = lax.broadcasted_iota(jnp.int32, square.shape, 0)
    col = lax.broadcasted_iota(jnp.int32, square.shape, 1)
    return jnp.where((col >= row) if flipped else (col <= row), square, 0.0).astype(bf16)


def causal(a, b):
    length = a.shape[0]
    cut = length - HEAD
    top = keep_lower(nt(a[:cut], b[:cut]))
    whole = nt(a[cut:], b)
    bottom = jnp.concatenate([whole[:, :cut].astype(bf16), keep_lower(whole[:, cut:])], axis=1)
    return [(slice(0, cut), slice(0, cut), top), (slice(cut, length), slice(0, length), bottom)]


def causal_turned(a, b):
    length = a.shape[0]
    whole = nt(a[:HEAD], b)
    top = jnp.concatenate(
        [keep_lower(whole[:, :HEAD], True), whole[:, HEAD:].astype(bf16)], axis=1
    )
    bottom = keep_lower(nt(a[HEAD:], b[HEAD:]), True)
    return [
        (slice(0, HEAD), slice(0, length), top),
        (slice(HEAD, length), slice(HEAD, length), bottom),
    ]


def twice(array):
    return jnp.concatenate([array, array], axis=1)


def masked_kernel(
    factor, grad_ref, spike_ref, value_ref, keys_ref, high_ref, low_ref,
    out_ref, mask_ref, grads_ref, mark_ref, spike_in, sems,
):
    set_mark(mark_ref)
    total = out_ref.shape[1]

    def copies(group, at):
        return [
            pltpu.make_async_copy(grad_ref.at[columns(at)], grads_ref.at[columns(at)], sems.at[0, group]),
            pltpu.make_async_copy(spike_ref.at[columns(at)], spike_in.at[columns(at)], sems.at[1, group]),
        ]

    for group in range(total // WIDE):
        for copy in copies(group, group * WIDE):
            copy.start()

    def work(group, at):
        for copy in copies(group, at):
            copy.wait()
        for part in heads(at):
            mask = spike_in[:, part].astype(f32)
            mask_ref[:, part] = mask.astype(bf16)
            grad, value, keys = grads_ref[:, part], value_ref[:, part], keys_ref[:, part]
            state = jnp.concatenate([high_ref[part, :], low_ref[part, :]], axis=1)
            for rows, cols, scores in causal(grad, value):
                made = nn(scores, keys[cols]) + nt(twice(grad[rows]), state)
                out_ref[rows, part] = (factor * made * mask[rows]).astype(bf16)

    groups(total, work)


def masked_call(factor, cotangent, q_spikes, values, keys, high, low):
    length, total = values.shape
    block = (length, total)
    return kernel_call(
        functools.partial(masked_kernel, factor),
        "HHVVVV",
        (cotangent, q_spikes, values, keys, high, low),
        "VVVV",
        [(block, bf16)] * 3 + [(MARK.shape, f32)],
        "masked_grad",
        (8 * length * total * length, 12 * length * total),
        [pltpu.VMEM(block, jnp.int32), pltpu.SemaphoreType.DMA((2, total // WIDE))],
    )


def rows_of(blocks):
    return sum(block.shape[0] for block in blocks)


def spans(blocks):
    at = 0
    for block in blocks:
        yield block, at, block.shape[0]
        at += block.shape[0]


def load_rows(copies, blocks, w_ref):
    bring = []
    for block, at, rows in spans(blocks):
        copy = copies.start(block, w_ref.at[pl.ds(at, rows), :])
        bring += [copy] * (rows // PIECE)
    return bring


def load_tokens(copies, places_ref, tokens_ref, some_ref):
    bring = []
    for piece in range(some_ref.shape[1] // PIECE):
        place = pl.multiple_of(places_ref[piece] * PIECE, PIECE)
        bring.append(
            copies.start(
                tokens_ref.at[:, pl.ds(place, PIECE)], some_ref.at[:, pl.ds(piece * PIECE, PIECE)]
            )
        )
    return bring


def wait_once(copies, done):
    for copy in copies:
        if not any(copy is one for one in done):
            copy.wait()
            done.append(copy)


def back_part(copies, places_ref, masked, w_ref, bring, done, out_ref, round_ref):
    going = []
    for at in range(0, w_ref.shape[0], 2 * PIECE):
        wait_once(bring[at // PIECE : at // PIECE + 2], done)
        both = slice(at, at + 2 * PIECE)
        round_ref[:, both] = nt(masked[...], w_ref[both, :]).astype(bf16)
        for piece in (at // PIECE, at // PIECE + 1):
            place = pl.multiple_of(places_ref[piece] * PIECE, PIECE)
            going.append(
                copies.start(
                    round_ref.at[:, pl.ds(piece * PIECE, PIECE)],
                    out_ref.at[:, pl.ds(place, PIECE)],
                )
            )
    return going


def products_kernel(size, has_before, places_ref, tokens_ref, masked, *refs):
    blocks = refs[:size]
    refs = refs[size:]
    if has_before:
        before_ref, _, *refs = refs
    sum_ref, back_out, mark_ref, w_ref, some_ref, round_ref, sems = refs
    set_mark(mark_ref)
    copies = Copies(sems)
    bring = load_rows(copies, blocks, w_ref)
    token_copies = load_tokens(copies, places_ref, tokens_ref, some_ref)
    done = []
    going = back_part(copies, places_ref, masked, w_ref, bring, done, back_out, round_ref)
    wait_once(token_copies, done)
    for at in range(0, w_ref.shape[1], WIDE):
        part = slice(at, at + WIDE)
        made = nn(some_ref[...], w_ref[:, part])
        if has_before:
            made = made + before_ref[:, part]
        sum_ref[:, part] = made
    for copy in going:
        copy.wait()


def products_call(places, tokens, blocks, masked, before):
    length, width = tokens.shape
    total = masked.shape[1]
    depth = rows_of(blocks)
    number = depth // PIECE
    extra = [] if before is None else list(before)
    return kernel_call(
        functools.partial(products_kernel, len(blocks), before is not None),
        "SHV" + "H" * len(blocks) + "VH"[: len(extra)],
        (places, tokens, masked, *blocks, *extra),
        "VHV",
        [((length, total), f32), ((length, width), bf16), (MARK.shape, f32)],
        "products",
        (4 * length * depth * total, depth * total * 2 + 8 * length * total),
        [
            pltpu.VMEM((depth, total), bf16),
            pltpu.VMEM((length, depth), bf16),
            pltpu.VMEM((length, depth), bf16),
            pltpu.SemaphoreType.DMA((len(blocks) + 2 * number,)),
        ],
        {3 + len(blocks) + at: at for at in range(len(extra))},
    )


def back_kernel(size, places_ref, masked, *refs):
    blocks = refs[:size]
    _, back_out, w_ref, round_ref, sems = refs[size:]
    copies = Copies(sems)
    bring = load_rows(copies, blocks, w_ref)
    for copy in back_part(copies, places_ref, masked, w_ref, bring, [], back_out, round_ref):
        copy.wait()


def back_call(places, blocks, masked, before):
    length, total = masked.shape
    depth = rows_of(blocks)
    number = depth // PIECE
    return kernel_call(
        functools.partial(back_kernel, len(blocks)),
        "SV" + "H" * len(blocks) + "H",
        (places, masked, *blocks, before),
        "H",
        [(before.shape, bf16)],
        "grad_tokens",
        (2 * length * depth * total, depth * total * 2 + 4 * length * total),
        [
            pltpu.VMEM((depth, total), bf16),
            pltpu.VMEM((length, depth), bf16),
            pltpu.SemaphoreType.DMA((len(blocks) + number,)),
        ],
        {2 + len(blocks): 0},
    )[0]


def query_kernel(size, places_ref, tokens_ref, sum_ref, mask_ref, grad_ref, *refs):
    blocks = refs[:size]
    queries, own_ref, sent_ref, w_ref, some_ref, sems = refs[size:]
    copies = Copies(sems)
    bring = load_tokens(copies, places_ref, tokens_ref, some_ref)
    bring += load_rows(copies, blocks, w_ref)
    wait_once(bring, [])
    for at in range(0, w_ref.shape[1], WIDE):
        part = slice(at, at + WIDE)
        made = nn(some_ref[...], w_ref[:, part]) + sum_ref[:, part]
        made = (made * mask_ref[:, part].astype(f32)).astype(bf16)
        queries[:, part] = made
        for head in range(0, WIDE, HEAD):
            here = slice(at + head, at + head + HEAD)
            own = tn(made[:, head : head + HEAD], grad_ref[:, here])
            own_ref[here, :] = own
            sent_ref[here, :] = own.astype(bf16)


def query_call(places, tokens, blocks, before, q_mask, cotangent):
    length = tokens.shape[0]
    total = blocks[0].shape[1]
    depth = rows_of(blocks)
    number = depth // PIECE
    return kernel_call(
        functools.partial(query_kernel, len(blocks)),
        "SHVVV" + "H" * len(blocks),
        (places, tokens, before, q_mask, cotangent, *blocks),
        "VVV",
        [((length, total), bf16), ((total, HEAD), f32), ((total, HEAD), bf16)],
        "queries",
        (2 * length * depth * total, depth * total * 2 + 12 * length * total),
        [
            pltpu.VMEM((depth, total), bf16),
            pltpu.VMEM((length, depth), bf16),
            pltpu.SemaphoreType.DMA((len(blocks) + number,)),
        ],
    )


def out_copy(here, there, sems, group, at):
    return pltpu.make_async_copy(here.at[columns(at)], there.at[columns(at)], sems.at[group])


def attend_kernel(
    factor, query_ref, keys_ref, value_ref, high_ref, low_ref, out_ref, mark_ref, made_ref, sems
):
    set_mark(mark_ref)
    total = query_ref.shape[1]

    def work(group, at):
        for part in heads(at):
            query, keys, value = query_ref[:, part], keys_ref[:, part], value_ref[:, part]
            state = [high_ref[part, :], low_ref[part, :]]
            for rows, cols, scores in causal(query, keys):
                made = nn(
                    jnp.concatenate([scores, twice(query[rows])], axis=1),
                    jnp.concatenate([value[cols], *state], axis=0),
                )
                made_ref[rows, part] = (factor * made).astype(bf16)
        out_copy(made_ref, out_ref, sems, group, at).start()

    groups(total, work)
    for group in range(total // WIDE):
        out_copy(made_ref, out_ref, sems, group, group * WIDE).wait()


def attend_call(factor, queries, keys, values, high, low):
    length, total = values.shape
    return kernel_call(
        functools.partial(attend_kernel, factor),
        "VVVVV",
        (queries, keys, values, high, low),
        "HV",
        [((length, total), bf16), (MARK.shape, f32)],
        "attended",
        (8 * length * total * length, 8 * length * total),
        [pltpu.VMEM((length, total), bf16), pltpu.SemaphoreType.DMA((total // WIDE,))],
    )


def inner_kernel(query_ref, keys_ref, value_ref, grad_ref, key_ref, val_ref, mark_ref):
    set_mark(mark_ref)

    def work(group, at):
        for part in heads(at):
            query, keys = query_ref[:, part], keys_ref[:, part]
            value, grad = value_ref[:, part], grad_ref[:, part]
            for rows, cols, scores in causal_turned(keys, query):
                val_ref[rows, part] = nn(scores, grad[cols])
            for rows, cols, scores in causal_turned(value, grad):
                key_ref[rows, part] = nn(scores, query[cols])

    groups(query_ref.shape[1], work)


def inner_call(queries, keys, values, cotangent):
    length, total = values.shape
    block = (length, total)
    return kernel_call(
        inner_kernel,
        "VVVV",
        (queries, keys, values, cotangent),
        "VVV",
        [(block, f32), (block, f32), (MARK.shape, f32)],
        "inner",
        (12 * length * total * length, 16 * length * total),
    )


def outer_kernel(
    factor, key_ref, val_ref, keys_ref, value_ref, mask_ref, high_ref, low_ref,
    key_out, val_out, key_made, val_made, key_sems, val_sems,
):
    total = keys_ref.shape[1]

    def work(group, at):
        for part in heads(at):
            keys, value = keys_ref[:, part], value_ref[:, part]
            state = [high_ref[part, :], low_ref[part, :]]
            key_grad = key_ref[:, part] + nt(twice(value), jnp.concatenate(state, axis=1))
            key_made[:, part] = (factor * key_grad * mask_ref[:, part].astype(f32)).astype(bf16)
            value_grad = val_ref[:, part] + nn(twice(keys), jnp.concatenate(state, axis=0))
            val_made[:, part] = (factor * value_grad).astype(bf16)
        out_copy(key_made, key_out, key_sems, group, at).start()
        out_copy(val_made, val_out, val_sems, group, at).start()

    groups(total, work)
    for group in range(total // WIDE):
        out_copy(key_made, key_out, key_sems, group, group * WIDE).wait()
        out_copy(val_made, val_out, val_sems, group, group * WIDE).wait()


def outer_call(factor, key_part, value_part, keys, values, k_mask, high, low):
    length, total = values.shape
    block = (length, total)
    return kernel_call(
        functools.partial(outer_kernel, factor),
        "VVVVVVV",
        (key_part, value_part, keys, values, k_mask, high, low),
        "HH",
        [(block, bf16)] * 2,
        "outer",
        (8 * length * total * HEAD, 20 * length * total),
        [pltpu.VMEM(block, bf16)] * 2 + [pltpu.SemaphoreType.DMA((total // WIDE,))] * 2,
    )


def halves(state):
    high = state.astype(bf16)
    return high, (state - high.astype(f32)).astype(bf16)


def scan_any(own, sent, count, reverse):
    place = lax.axis_index(CTX)
    total = own
    state = jnp.zeros_like(own)
    bits = count.bit_length() - 1
    for bit in range(bits):
        step = 1 << bit
        last = bit == bits - 1
        pairs = []
        for source in range(count):
            high = bool(source & step)
            if not last or high == reverse:
                pairs.append((source, source ^ step))
        got = lax.ppermute(sent, CTX, pairs).astype(f32)
        if last:
            state = state + got
        else:
            mine = ((place // step) % 2) == (0 if reverse else 1)
            state = state + jnp.where(mine, got, 0.0)
            total = total + got
            sent = total.astype(bf16)
    return state


def links(first, keep=lambda source, target: True):
    pairs = []
    for chip in range(4):
        for core in range(2):
            other = chip ^ (first if core == 0 else 3 - first)
            if keep((chip, core), other):
                pairs.append((chip * 2 + core, other * 2 + core))
    return pairs


def scan_first(own, sent, reverse):
    chip, core = lax.axis_index("chip"), lax.axis_index("core")
    low_bit = 1 - chip % 2 if reverse else chip % 2
    half = own.shape[0] // 2
    sibling = lax.ppermute(sent, "core", SWAP)
    both = own + sibling.astype(f32)
    both = jnp.where(core == 0, both[:half], both[half:])
    got = lax.ppermute(both.astype(bf16), CTX, links(1, upward(reverse))).astype(f32)
    first = jnp.where((core == 1) | (low_bit == 1), got, 0.0)
    message = (got + jnp.where((core == 0) | (low_bit == 0), both, 0.0)).astype(bf16)
    return message, first, sibling


def upward(reverse):
    flip = 3 if reverse else 0

    def keep(source, target):
        at = source[0] ^ flip
        return source[0] ^ target == 1 or not at & 2

    return keep


def scan_second(message, first, sibling, reverse, others=()):
    core = lax.axis_index("core")
    more = lax.ppermute(message, CTX, links(2, upward(reverse))).astype(f32)
    state = first + more
    if others:
        state, = join([state], others)
    other = lax.ppermute(state, "core", SWAP)
    whole = jnp.concatenate(
        [jnp.where(core == 0, state, other), jnp.where(core == 0, other, state)], axis=0
    )
    return halves(whole + jnp.where(core == (0 if reverse else 1), sibling.astype(f32), 0.0))


def gather_any(q_weight):
    whole = lax.all_gather(q_weight, ("chip", "core", "dp"), axis=0, tiled=True)
    cut = whole.shape[0] // (2 * PIECE) * PIECE
    number = whole.shape[0] // PIECE
    return [whole[:cut], whole[cut:]], jnp.arange(number, dtype=jnp.int32)


def crossed(side):
    return (0, 1 + side, 2 - side, 3)


def per_device(tokens, key_input, values, q_weight, q_spikes, k_spikes, cotangent):
    batches, length, width = tokens.shape
    assert batches == 1
    total = q_weight.shape[1]
    chips, spread = lax.axis_size("chip"), lax.axis_size("dp")
    factor = 3.0 / math.sqrt(HEAD * length * chips * 2)
    tokens, key_input, values, q_spikes, k_spikes, cotangent = (
        array.reshape(length, array.shape[2])
        for array in (tokens, key_input, values, q_spikes, k_spikes, cotangent)
    )
    special = chips == 4 and spread == 4

    def sibling(array):
        return lax.ppermute(array, "core", SWAP)

    def along(array, pairs):
        return lax.ppermute(array, "dp", pairs)

    def cross(array):
        return lax.ppermute(array, CTX, links(1)), lax.ppermute(array, CTX, links(2))

    def onward(array):
        return lax.ppermute(array, CTX, links(2))

    keys, k_mask, values, own, sent, own_mark = memory_call(key_input, k_spikes, values)
    if special:
        chip, core, layer = (lax.axis_index(name) for name in ("chip", "core", "dp"))
        within = (layer == 1) | (layer == 2)
        ends = [(0, 1), (1, 0), (2, 3), (3, 2)]
        middle = [(1, 2), (2, 1)]
        outward = [(1, 0), (2, 3)]
        near = along(q_weight, ends)
        mid = along(q_weight, middle)
        first_0, second_0 = cross(q_weight)
        other_0 = sibling(q_weight)
        near, mid, first_0, second_0, sent = join([near, mid, first_0, second_0, sent])
        message, *rest = scan_first(own, sent, False)
    else:
        arrived, places = gather_any(q_weight)
        high, low = halves(scan_any(own, sent, chips * 2, False))

    if special:

        def numbers(sides, layers):
            return jnp.stack(
                [
                    ((chip ^ flip) * 2 + side) * spread + one
                    for one in layers
                    for side in sides
                    for flip in crossed(side)
                ]
            ).astype(jnp.int32)

        sides = (core, 1 - core)
        levels = [layer, layer ^ 1, jnp.where(layer < 2, 2, 1), jnp.where(layer < 2, 3, 0)]
        third_0 = onward(first_0)
        first_1, second_1 = cross(near)
        far = along(near, middle)
        mid_out = along(mid, outward)
        third_0, first_1, second_1, far, mid_out, message = join(
            [third_0, first_1, second_1, far, mid_out, message]
        )
        third_1 = onward(first_1)
        next_layer = jnp.where(within, mid, mid_out)
        first_2, second_2 = cross(next_layer)
        far_out = along(far, outward)
        high, low = scan_second(message, *rest, False)
        masked, q_mask, cotangent, mark = masked_call(
            factor, cotangent, q_spikes, values, keys, high, low
        )
        third_1, first_2, second_2, far_out = join(
            [third_1, first_2, second_2, far_out], [mark]
        )
        third_2 = onward(first_2)
        last_layer = jnp.where(within, far, far_out)
        first_3, second_3 = cross(last_layer)

        def whole(*mine):
            return list(mine) + [sibling(one) for one in mine]

        blocks = [q_weight, first_0, second_0, third_0, other_0]
        blocks += [sibling(one) for one in blocks[1:4]]
        *done, _ = products_call(numbers(sides, levels[:1]), tokens, blocks, masked, None)
        blocks = whole(near, first_1, second_1, third_1)
        *done, mark = products_call(numbers(sides, levels[1:2]), tokens, blocks, masked, done)
        third_2, first_3, second_3 = join([third_2, first_3, second_3], [mark])
        third_3 = onward(first_3)
        blocks = whole(next_layer, first_2, second_2, third_2)
        *done, mark = products_call(numbers(sides, levels[2:3]), tokens, blocks, masked, done)
        third_3, = join([third_3], [mark])
        late = whole(last_layer, first_3, second_3, third_3)
        late_places = numbers(sides, levels[3:])
    else:
        masked, q_mask, cotangent, _ = masked_call(
            factor, cotangent, q_spikes, values, keys, high, low
        )
        half = places.shape[0] // 2
        *done, _ = products_call(places[:half], tokens, arrived[:1], masked, None)
        late, late_places = arrived[1:], places[half:]
    partial, grad_tokens = done
    queries, own, sent = query_call(late_places, tokens, late, partial, q_mask, cotangent)
    attended, attended_mark = attend_call(factor, queries, keys, values, high, low)
    key_part, value_part, inner_mark = inner_call(queries, keys, values, cotangent)
    if special:
        message, *rest = scan_first(own, sent, True)
        message, = join([message], [attended_mark])
        adjoint = scan_second(message, *rest, True, [inner_mark])
    else:
        adjoint = halves(scan_any(own, sent, chips * 2, True))
    grad_tokens = back_call(late_places, late, masked, grad_tokens)
    grad_keys, grad_values = outer_call(
        factor, key_part, value_part, keys, values, k_mask, *adjoint
    )
    return tuple(
        array.reshape(1, length, array.shape[1])
        for array in (attended, grad_tokens, grad_keys, grad_values)
    )


def solution(mesh):
    count, spread = mesh.shape["ctx"], mesh.shape["dp"]
    fine = Mesh(mesh.devices.reshape(count // 2, 2, spread), ("chip", "core", "dp"))
    block = P("dp", CTX, None)
    rows = P(("chip", "core", "dp"), None)
    in_specs = (block, block, block, rows, block, block, block)
    return jax.shard_map(
        per_device, mesh=fine, in_specs=in_specs, out_specs=(block,) * 4, check_vma=False
    )
```

time: 186 us -> 177 us (0.952)
  Pallas kernels: 82.5 us -> 62 us
  starting transfers between devices: 54 us -> 37 us
  waiting for transfers between devices: 25.8 us -> 41.8 us
  local copies, waits for them, and re-layouts: 8.49 us -> 17.9 us
  other arithmetic: 12 us -> 14 us
    pallas_call x16 -> x17, Pallas kernels: 82.5 us -> 62 us  [kernel_call(): made(*[holds[place](one) if place in holds else one for place, one in zip...]
    ppermute x4, waiting for transfers between devices: 1.17 us -> 13.4 us  [cross(): lax.ppermute(array, CTX, links(1))]
    unnamed x56 -> x88, local copies, waits for them, and re-layouts: 6.51 us -> 17.6 us
    ppermute x16, starting transfers between devices: 19.3 us -> 9.11 us  [sibling(): return lax.ppermute(array, 'core', SWAP)]
    ppermute x8, starting transfers between devices: 17.4 us -> 10.2 us  [the longest x2 5.26 us: scan_second(): more = lax.ppermute(message, CTX, links(2, upward(reverse))).astype(f32)]
    ppermute x5, waiting for transfers between devices: 6.44 us -> 1.67 us  [along(): return lax.ppermute(array, 'dp', pairs)]
    ppermute x8, waiting for transfers between devices: 4.1 us -> 7.85 us  [the longest x2 4.02 us: scan_second(): more = lax.ppermute(message, CTX, links(2, upward(reverse))).astype(f32)]
    ppermute x4, waiting for transfers between devices: 9.15 us -> 12.7 us  [onward(): return lax.ppermute(array, CTX, links(2))]
  transfers between devices with their start and end apart: 41 -> 41, of which waited for: 11 -> 12; matrix products, arithmetic and copies ran while one was open for 4% -> 6% of each run, Pallas kernels for 31% -> 30%
where the time goes in v3:
time: 177 us; the launch traced here: 174 us
  Pallas kernels  62 us (35%)
  waiting for transfers between devices  41.8 us (24%)
  starting transfers between devices  37 us (21%)
  local copies, waits for them, and re-layouts  17.9 us (10%)
  other arithmetic  14 us (8%)
    pallas_call x17, Pallas kernels, kernel_call(): made(*[holds[place](one) if place in holds else one for place, one in zip...  62 us
    unnamed x88, local copies, waits for them, and re-layouts  17.6 us
    ppermute x4, waiting for transfers between devices, cross(): lax.ppermute(array, CTX, links(1))  13.4 us
    ppermute x4, waiting for transfers between devices, onward(): return lax.ppermute(array, CTX, links(2))  12.7 us
    ppermute x16, starting transfers between devices, sibling(): return lax.ppermute(array, 'core', SWAP)  9.11 us
    ppermute x5, starting transfers between devices, along(): return lax.ppermute(array, 'dp', pairs)  7.69 us
    ppermute x2, starting transfers between devices, scan_second(): more = lax.ppermute(message, CTX, links(2, upward(reverse))).astype(f32)  5.26 us
    ppermute x4, starting transfers between devices, cross(): lax.ppermute(array, CTX, links(2))  4.96 us
  transfers between devices with their start and end apart: 41, of which 12 were waited for; matrix products, arithmetic and copies ran while one was open for 6% of the time, Pallas kernels for 30%

profile of v3, /device:TPU:1, one launch (start us, length us, event | category | flops | bytes accessed | tf_op | source)
XLA Modules:
  0.0 174.2 jit_solution(17739729177108305791)
XLA Ops:
  0.6 2.2 %collective-permute-start = (bf16[128,2048]{1,0:T(8,128)(2,1)}, bf16[128,2048]{1,0:T(8,128)(2,1)}, u32[]{:S(2)}, u32[]{:S(2)}) collective-permute-start(bf16[128,2048]{1,0:T(8,128)(2,1)} %refs_0_.1), channel_id=1, source_target_pairs={{0,1},{1,0},{2,3},{3,2},{4,5},{5,4},{6,7},{7,6},{8,9},{9,8},{10,11... | collective-permute-start | bytes 1572872 | tf_op jit(solution)/shard_map/ppermute | solution.py:630
  6.7 3.5 %own_memory.1 = (bf16[384,2048]{1,0:T(8,128)(2,1)S(1)}, bf16[384,2048]{1,0:T(8,128)(2,1)S(1)}, bf16[384,2048]{1,0:T(8,128)(2,1)S(1)}, f32[2048,128]{1,0:T(8,128)...) custom-call(bf16[384,2048]{1,0:T(8,128)(2,1)} %bitcast.48, s32[384,2048]{1,0:T(8,128)} %bitcast.47, ...), custom_call_target="tpu_custom_call" | custom-call | flops 201326592 | bytes 9437184 | tf_op jit(solution)/shard_map/own_memory/pallas_call | solution.py:74
  13.1 1.7 collective-permute-done.refs_0_
  15.6 4.0 %collective-permute-done.3.refs_3_ = bf16[128,2048]{1,0:T(8,128)(2,1)S(1)} collective-permute-done((bf16[128,2048]{1,0:T(8,128)(2,1)}, bf16[128,2048]{1,0:T(8,128)(2,1)S(1)}, u32[]{:S(2)}, u32[]{:S(2)}) %collective-permute-start.3) | collective-permute-done | bytes 524320 | tf_op jit(solution)/shard_map/ppermute | solution.py:633
  21.0 1.9 %collective-permute-done.4 = bf16[2048,128]{1,0:T(8,128)(2,1)} collective-permute-done((bf16[2048,128]{1,0:T(8,128)(2,1)}, bf16[2048,128]{1,0:T(8,128)(2,1)}, u32[]{:S(2)}, u32[]{:S(2)}) %collective-permute-start.4) | collective-permute-done | bytes 524320 | tf_op jit(solution)/shard_map/ppermute | solution.py:571
  22.9 1.4 convert_add_fusion.1
  25.3 2.1 %collective-permute-start.5 = (bf16[1024,128]{1,0:T(8,128)(2,1)S(1)}, bf16[1024,128]{1,0:T(8,128)(2,1)S(1)}, u32[]{:S(2)}, u32[]{:S(2)}) collective-permute-start(bf16[1024,128]{1,0:T(8,128)(2,1)S(1)} %fusion.8), channel_id=1, source_target_pairs={{0,8},{4,20},{8,0},{12,28},{16,24},{24,16},{1,9},{5,21},{9,1},{13,... | collective-permute-start | bytes 786440 | tf_op jit(solution)/shard_map/ppermute | solution.py:574
  28.8 1.5 collective-permute-start.9
  32.1 2.0 %fusion.3.refs_5_ = bf16[1024,128]{1,0:T(8,128)(2,1)} fusion(bf16[1024,128]{1,0:T(8,128)(2,1)S(1)} %collective-permute-done.5, pred[]{:T(512)S(6)} %or.16, f32[2048,128]{1,0:T(8,128)} %copy-done.23, pred[]{:T(512)S(6)} %eq.19), kind=kLoop, calls=%fused_computation.13 | loop fusion | flops 655360 | bytes 1572866 | tf_op jit(solution)/shard_map/convert_element_type | solution.py:576
  34.1 7.6 %collective-permute-done.7.refs_1_ = bf16[128,2048]{1,0:T(8,128)(2,1)} collective-permute-done((bf16[128,2048]{1,0:T(8,128)(2,1)}, bf16[128,2048]{1,0:T(8,128)(2,1)}, u32[]{:S(2)}, u32[]{:S(2)}) %collective-permute-start.7) | collective-permute-done | bytes 524320 | tf_op jit(solution)/shard_map/ppermute | solution.py:633
  41.7 8.3 %collective-permute-done.6.refs_0_ = bf16[128,2048]{1,0:T(8,128)(2,1)} collective-permute-done((bf16[128,2048]{1,0:T(8,128)(2,1)}, bf16[128,2048]{1,0:T(8,128)(2,1)}, u32[]{:S(2)}, u32[]{:S(2)}) %collective-permute-start.6) | collective-permute-done | bytes 524320 | tf_op jit(solution)/shard_map/ppermute | solution.py:636
  50.0 3.1 %collective-permute-start.11 = (bf16[1024,128]{1,0:T(8,128)(2,1)}, bf16[1024,128]{1,0:T(8,128)(2,1)}, u32[]{:S(2)}, u32[]{:S(2)}) collective-permute-start(bf16[1024,128]{1,0:T(8,128)(2,1)} %get-tuple-element.57), channel_id=1, source_target_pairs={{0,16},{4,12},{8,24},{12,4},{20,28},{28,20},{1,17},{5,13},{9,25},{... | collective-permute-start | bytes 786440 | tf_op jit(solution)/shard_map/ppermute | solution.py:592
  53.4 4.0 %collective-permute-done.11 = bf16[1024,128]{1,0:T(8,128)(2,1)} collective-permute-done((bf16[1024,128]{1,0:T(8,128)(2,1)}, bf16[1024,128]{1,0:T(8,128)(2,1)}, u32[]{:S(2)}, u32[]{:S(2)}) %collective-permute-start.11) | collective-permute-done | bytes 262176 | tf_op jit(solution)/shard_map/ppermute | solution.py:592
  57.5 1.8 %fusion.2 = f32[1024,128]{1,0:T(8,128)} fusion(bf16[1024,128]{1,0:T(8,128)(2,1)S(1)} %collective-permute-done.5, bf16[1024,128]{1,0:T(8,128)(2,1)} %collective-permute-done.11, pred[]{:T(512)S(6)} %or.15), kind=kLoop, calls=%fused_computation.12 | loop fusion | flops 524288 | bytes 1048577 | tf_op jit(solution)/shard_map/add | solution.py:593
  59.3 1.9 %broadcast_select_fusion.1.refs_0_ = bf16[128,2048]{1,0:T(8,128)(2,1)} fusion(bf16[128,2048]{1,0:T(8,128)(2,1)} %get-tuple-element.56, bf16[128,2048]{1,0:T(8,128)(2,1)} %get-tuple-element.59, pred[]{:T(512)S(6)} %or.17), kind=kLoop, calls=%fused_computation.19 | loop fusion | flops 262144 | bytes 1572865 | tf_op jit(solution)/shard_map/jit(_where)/select_n | solution.py:677
  61.2 1.7 collective-permute-start.14
  68.1 5.0 %collective-permute-done.14.refs_1_ = bf16[128,2048]{1,0:T(8,128)(2,1)} collective-permute-done((bf16[128,2048]{1,0:T(8,128)(2,1)}, bf16[128,2048]{1,0:T(8,128)(2,1)}, u32[]{:S(2)}, u32[]{:S(2)}) %collective-permute-start.14) | collective-permute-done | bytes 524320 | tf_op jit(solution)/shard_map/ppermute | solution.py:633
  73.1 2.8 %collective-permute-start.26 = (bf16[128,2048]{1,0:T(8,128)(2,1)S(1)}, bf16[128,2048]{1,0:T(8,128)(2,1)S(1)}, u32[]{:S(2)}, u32[]{:S(2)}) collective-permute-start(bf16[128,2048]{1,0:T(8,128)(2,1)S(1)} %copy-done.40), channel_id=1, source_target_pairs={{0,4},{4,0},{1,5},{5,1},{2,6},{6,2},{3,7},{7,3},{8,12},{12,8},{9,1... | collective-permute-start | bytes 1572872 | tf_op jit(solution)/shard_map/ppermute | solution.py:627
  77.2 4.4 %collective-permute-done.13.refs_0_ = bf16[128,2048]{1,0:T(8,128)(2,1)S(1)} collective-permute-done((bf16[128,2048]{1,0:T(8,128)(2,1)}, bf16[128,2048]{1,0:T(8,128)(2,1)S(1)}, u32[]{:S(2)}, u32[]{:S(2)}) %collective-permute-start.13) | collective-permute-done | bytes 524320 | tf_op jit(solution)/shard_map/ppermute | solution.py:636
  82.1 5.8 %masked_grad.1 = (bf16[384,2048]{1,0:T(8,128)(2,1)S(1)}, bf16[384,2048]{1,0:T(8,128)(2,1)S(1)}, bf16[384,2048]{1,0:T(8,128)(2,1)S(1)}, f32[8,128]{1,0:T(8,128)S(1)}) custom-call(bf16[384,2048]{1,0:T(8,128)(2,1)} %bitcast.51, s32[384,2048]{1,0:T(8,128)} %bitcast.50, bf16[384,2048]{1,0:T(8,128)(2,1)S(1)} %get-tuple-element.49.value_ref, ...), custom_call_target="tpu_custom_call" | custom-call | flops 2415919104 | bytes 9437184 | tf_op jit(solution)/shard_map/masked_grad/pallas_call | solution.py:74
  89.7 1.5 broadcast_select_fusion.refs_0_
  93.9 8.3 %products.3 = (f32[384,2048]{1,0:T(8,128)S(1)}, bf16[384,4096]{1,0:T(8,128)(2,1)}, f32[8,128]{1,0:T(8,128)}) custom-call(s32[8]{0:T(128)S(1)} %stack.143.places_ref, bf16[384,4096]{1,0:T(8,128)(2,1)} %bitcast.42, bf16[384,2048]{1,0:T(8,128)(2,1)S(1)} %get-tuple-element.58.masked, bf16[128,2048]{1,0:T(8,128)(2,1)} %refs_0_.1, ...), custom_call_target="tpu_custom_call" | custom-call | flops 3221225472 | bytes 10485760 | tf_op jit(solution)/shard_map/products/pallas_call | solution.py:74
  104.3 8.0 %products.4 = (f32[384,2048]{1,0:T(8,128)S(1)}, bf16[384,4096]{1,0:T(8,128)(2,1)}, f32[8,128]{1,0:T(8,128)S(1)}) custom-call(s32[8]{0:T(128)S(1)} %stack.134.places_ref, bf16[384,4096]{1,0:T(8,128)(2,1)} %bitcast.43, bf16[384,2048]{1,0:T(8,128)(2,1)S(1)} %get-tuple-element.58.masked, ...), custom_call_target="tpu_custom_call", output_to_operand_aliasing={{0}: (11, {}), {1}: (12, {})} | custom-call | flops 3221225472 | bytes 10485760 | tf_op jit(solution)/shard_map/products/pallas_call | solution.py:74
  117.5 8.0 %products.5 = (f32[384,2048]{1,0:T(8,128)S(1)}, bf16[384,4096]{1,0:T(8,128)(2,1)}, f32[8,128]{1,0:T(8,128)S(1)}) custom-call(s32[8]{0:T(128)S(1)} %stack.125.places_ref, bf16[384,4096]{1,0:T(8,128)(2,1)} %bitcast.44, bf16[384,2048]{1,0:T(8,128)(2,1)S(1)} %copy-done.1, ...), custom_call_target="tpu_custom_call", output_to_operand_aliasing={{0}: (11, {}), {1}: (12, {})} | custom-call | flops 3221225472 | bytes 10485760 | tf_op jit(solution)/shard_map/products/pallas_call | solution.py:74
  125.8 2.1 %collective-permute-done.36.refs_7_ = bf16[128,2048]{1,0:T(8,128)(2,1)} collective-permute-done((bf16[128,2048]{1,0:T(8,128)(2,1)}, bf16[128,2048]{1,0:T(8,128)(2,1)}, u32[]{:S(2)}, u32[]{:S(2)}) %collective-permute-start.36) | collective-permute-done | bytes 524320 | tf_op jit(solution)/shard_map/ppermute | solution.py:627
  130.7 6.4 %queries.1 = (bf16[384,2048]{1,0:T(8,128)(2,1)S(1)}, f32[2048,128]{1,0:T(8,128)S(1)}, bf16[2048,128]{1,0:T(8,128)(2,1)S(1)}) custom-call(s32[8]{0:T(128)S(1)} %stack.116.places_ref, bf16[384,4096]{1,0:T(8,128)(2,1)} %bitcast.45, f32[384,2048]{1,0:T(8,128)S(1)} %get-tuple-element.76.sum_ref, bf16[384,2048]{1,0:T(8,128)(2,1)S(1)} %copy-done.13, ...), custom_call_target="tpu_custom_call" | custom-call | flops 1610612736 | bytes 13631488 | tf_op jit(solution)/shard_map/queries/pallas_call | solution.py:74
  137.3 1.8 %collective-permute-done.37 = bf16[2048,128]{1,0:T(8,128)(2,1)S(1)} collective-permute-done((bf16[2048,128]{1,0:T(8,128)(2,1)S(1)}, bf16[2048,128]{1,0:T(8,128)(2,1)S(1)}, u32[]{:S(2)}, u32[]{:S(2)}) %collective-permute-start.37) | collective-permute-done | bytes 524320 | tf_op jit(solution)/shard_map/ppermute | solution.py:571
  145.7 5.1 %attended.1 = (bf16[384,2048]{1,0:T(8,128)(2,1)}, f32[8,128]{1,0:T(8,128)S(1)}) custom-call(bf16[384,2048]{1,0:T(8,128)(2,1)S(1)} %copy-done.21, bf16[384,2048]{1,0:T(8,128)(2,1)S(1)} %copy-done.4, bf16[384,2048]{1,0:T(8,128)(2,1)S(1)} %copy-done.8, bf16[2048,128]{1,0:T(8,128)(2,1)S(1)} %copy-done.19, bf16[2048,128]{1,0:T(8,128)(2,1)S(1)} %copy-done.17), custom_call_target="tpu_custom_call" | custom-call | flops 2415919104 | bytes 6291456 | tf_op jit(solution)/shard_map/attended/pallas_call | solution.py:74
  151.7 2.2 %collective-permute-start.39 = (bf16[1024,128]{1,0:T(8,128)(2,1)}, bf16[1024,128]{1,0:T(8,128)(2,1)S(1)}, u32[]{:S(2)}, u32[]{:S(2)}) collective-permute-start(bf16[1024,128]{1,0:T(8,128)(2,1)} %join.12), channel_id=1, source_target_pairs={{4,12},{12,4},{16,0},{20,28},{24,8},{28,20},{5,13},{13,5},{17,1},{... | collective-permute-start | bytes 786440 | tf_op jit(solution)/shard_map/ppermute | solution.py:592
  153.9 6.9 %inner.1 = (f32[384,2048]{1,0:T(8,128)S(1)}, f32[384,2048]{1,0:T(8,128)S(1)}, f32[8,128]{1,0:T(8,128)S(1)}) custom-call(bf16[384,2048]{1,0:T(8,128)(2,1)S(1)} %copy-done.22, bf16[384,2048]{1,0:T(8,128)(2,1)S(1)} %copy-done.4, bf16[384,2048]{1,0:T(8,128)(2,1)S(1)} %copy-done.8, bf16[384,2048]{1,0:T(8,128)(2,1)S(1)} %copy-done.11), custom_call_target="tpu_custom_call" | custom-call | flops 3623878656 | bytes 12582912 | tf_op jit(solution)/shard_map/inner/pallas_call | solution.py:74
  162.3 6.5 %grad_tokens.1 = bf16[384,4096]{1,0:T(8,128)(2,1)} custom-call(s32[8]{0:T(128)S(1)} %stack.116.places_ref, bf16[384,2048]{1,0:T(8,128)(2,1)S(1)} %copy-done.2, bf16[128,2048]{1,0:T(8,128)(2,1)} %copy-done.29, bf16[128,2048]{1,0:T(8,128)(2,1)} %get-tuple-element.79.refs_1_, ...), custom_call_target="tpu_custom_call", output_to_operand_aliasing={{}: (10, {})} | custom-call | flops 1610612736 | bytes 7340032 | tf_op jit(solution)/shard_map/grad_tokens/pallas_call | solution.py:74
  170.5 3.5 %outer.1 = (bf16[384,2048]{1,0:T(8,128)(2,1)}, bf16[384,2048]{1,0:T(8,128)(2,1)}) custom-call(f32[384,2048]{1,0:T(8,128)S(1)} %get-tuple-element.85.key_ref, f32[384,2048]{1,0:T(8,128)S(1)} %get-tuple-element.86.val_ref, bf16[384,2048]{1,0:T(8,128)(2,1)S(1)} %copy-done.4, bf16[384,2048]{1,0:T(8,128)(2,1)S(1)} %copy-done.8, bf16[384,2048]{1,0:T(8,128)(2,1)S(1)} %copy-done.6, ...), custom_call_target="tpu_custom_call" | custom-call | flops 805306368 | bytes 15728640 | tf_op jit(solution)/shard_map/outer/pallas_call | solution.py:74
  (173 shorter events, 45.8 us)
Async XLA Ops:
  0.6 14.2 %collective-permute-start = (bf16[128,2048]{1,0:T(8,128)(2,1)}, bf16[128,2048]{1,0:T(8,128)(2,1)}, u32[]{:S(2)}, u32[]{:S(2)}) collective-permute-start(bf16[128,2048]{1,0:T(8,128)(2,1)} %refs_0_.1), channel_id=1, source_target_pairs={{0,1},{1,0},{2,3},{3,2},{4,5},{5,4},{6,7},{7,6},{8,9},{9,8},{10,11... | collective-permute-start | bytes 1572872 | tf_op jit(solution)/shard_map/ppermute | solution.py:630
  2.8 12.0 %collective-permute-start.1 = (bf16[128,2048]{1,0:T(8,128)(2,1)}, bf16[128,2048]{1,0:T(8,128)(2,1)}, u32[]{:S(2)}, u32[]{:S(2)}) collective-permute-start(bf16[128,2048]{1,0:T(8,128)(2,1)} %refs_0_.1), channel_id=1, source_target_pairs={{1,2},{2,1},{5,6},{6,5},{9,10},{10,9},{13,14},{14,13},{17,18},{18,... | collective-permute-start | bytes 1572872 | tf_op jit(solution)/shard_map/ppermute | solution.py:630
  4.3 11.3 %collective-permute-start.2 = (bf16[128,2048]{1,0:T(8,128)(2,1)}, bf16[128,2048]{1,0:T(8,128)(2,1)}, u32[]{:S(2)}, u32[]{:S(2)}) collective-permute-start(bf16[128,2048]{1,0:T(8,128)(2,1)} %refs_0_.1), channel_id=1, source_target_pairs={{0,8},{4,20},{8,0},{12,28},{16,24},{20,4},{24,16},{28,12},{1,9},{5... | collective-permute-start | bytes 1572872 | tf_op jit(solution)/shard_map/ppermute | solution.py:633
  5.5 14.1 %collective-permute-start.3 = (bf16[128,2048]{1,0:T(8,128)(2,1)}, bf16[128,2048]{1,0:T(8,128)(2,1)S(1)}, u32[]{:S(2)}, u32[]{:S(2)}) collective-permute-start(bf16[128,2048]{1,0:T(8,128)(2,1)} %refs_0_.1), channel_id=1, source_target_pairs={{0,16},{4,12},{8,24},{12,4},{16,0},{20,28},{24,8},{28,20},{1,17},{... | collective-permute-start | bytes 1572872 | tf_op jit(solution)/shard_map/ppermute | solution.py:633
  27.5 14.2 %collective-permute-start.7 = (bf16[128,2048]{1,0:T(8,128)(2,1)}, bf16[128,2048]{1,0:T(8,128)(2,1)}, u32[]{:S(2)}, u32[]{:S(2)}) collective-permute-start(bf16[128,2048]{1,0:T(8,128)(2,1)} %get-tuple-element.55.refs_0_), channel_id=1, source_target_pairs={{0,8},{4,20},{8,0},{12,28},{16,24},{20,4},{24,16},{28,12},{1,9},{5... | collective-permute-start | bytes 1572872 | tf_op jit(solution)/shard_map/ppermute | solution.py:633
  27.6 14.1 %collective-permute-start.8 = (bf16[128,2048]{1,0:T(8,128)(2,1)}, bf16[128,2048]{1,0:T(8,128)(2,1)}, u32[]{:S(2)}, u32[]{:S(2)}) collective-permute-start(bf16[128,2048]{1,0:T(8,128)(2,1)} %get-tuple-element.55.refs_0_), channel_id=1, source_target_pairs={{0,16},{4,12},{8,24},{12,4},{16,0},{20,28},{24,8},{28,20},{1,17},{... | collective-permute-start | bytes 1572872 | tf_op jit(solution)/shard_map/ppermute | solution.py:633
  28.8 12.9 %collective-permute-start.9 = (bf16[128,2048]{1,0:T(8,128)(2,1)}, bf16[128,2048]{1,0:T(8,128)(2,1)}, u32[]{:S(2)}, u32[]{:S(2)}) collective-permute-start(bf16[128,2048]{1,0:T(8,128)(2,1)} %get-tuple-element.55.refs_0_), channel_id=1, source_target_pairs={{1,2},{2,1},{5,6},{6,5},{9,10},{10,9},{13,14},{14,13},{17,18},{18,... | collective-permute-start | bytes 1572872 | tf_op jit(solution)/shard_map/ppermute | solution.py:630
  30.3 19.7 %collective-permute-start.6 = (bf16[128,2048]{1,0:T(8,128)(2,1)}, bf16[128,2048]{1,0:T(8,128)(2,1)}, u32[]{:S(2)}, u32[]{:S(2)}) collective-permute-start(bf16[128,2048]{1,0:T(8,128)(2,1)} %get-tuple-element.54.refs_1_), channel_id=1, source_target_pairs={{0,16},{4,12},{8,24},{12,4},{16,0},{20,28},{24,8},{28,20},{1,17},{... | collective-permute-start | bytes 1572872 | tf_op jit(solution)/shard_map/ppermute | solution.py:636
  30.8 19.3 %collective-permute-start.10 = (bf16[128,2048]{1,0:T(8,128)(2,1)}, bf16[128,2048]{1,0:T(8,128)(2,1)}, u32[]{:S(2)}, u32[]{:S(2)}) collective-permute-start(bf16[128,2048]{1,0:T(8,128)(2,1)} %get-tuple-element.56), channel_id=1, source_target_pairs={{1,0},{2,3},{5,4},{6,7},{9,8},{10,11},{13,12},{14,15},{17,16},{18,... | collective-permute-start | bytes 1572872 | tf_op jit(solution)/shard_map/ppermute | solution.py:630
  53.1 14.0 %collective-permute-start.24 = (bf16[128,2048]{1,0:T(8,128)(2,1)}, bf16[128,2048]{1,0:T(8,128)(2,1)}, u32[]{:S(2)}, u32[]{:S(2)}) collective-permute-start(bf16[128,2048]{1,0:T(8,128)(2,1)} %refs_0_.1), channel_id=1, source_target_pairs={{0,4},{4,0},{1,5},{5,1},{2,6},{6,2},{3,7},{7,3},{8,12},{12,8},{9,1... | collective-permute-start | bytes 1572872 | tf_op jit(solution)/shard_map/ppermute | solution.py:627
  61.2 11.9 %collective-permute-start.14 = (bf16[128,2048]{1,0:T(8,128)(2,1)}, bf16[128,2048]{1,0:T(8,128)(2,1)}, u32[]{:S(2)}, u32[]{:S(2)}) collective-permute-start(bf16[128,2048]{1,0:T(8,128)(2,1)} %broadcast_select_fusion.1.refs_0_), channel_id=1, source_target_pairs={{0,8},{4,20},{8,0},{12,28},{16,24},{20,4},{24,16},{28,12},{1,9},{5... | collective-permute-start | bytes 1572872 | tf_op jit(solution)/shard_map/ppermute | solution.py:633
  63.0 14.1 %collective-permute-start.15 = (bf16[128,2048]{1,0:T(8,128)(2,1)}, bf16[128,2048]{1,0:T(8,128)(2,1)}, u32[]{:S(2)}, u32[]{:S(2)}) collective-permute-start(bf16[128,2048]{1,0:T(8,128)(2,1)} %broadcast_select_fusion.1.refs_0_), channel_id=1, source_target_pairs={{0,16},{4,12},{8,24},{12,4},{16,0},{20,28},{24,8},{28,20},{1,17},{... | collective-permute-start | bytes 1572872 | tf_op jit(solution)/shard_map/ppermute | solution.py:633
  64.3 17.3 %collective-permute-start.13 = (bf16[128,2048]{1,0:T(8,128)(2,1)}, bf16[128,2048]{1,0:T(8,128)(2,1)S(1)}, u32[]{:S(2)}, u32[]{:S(2)}) collective-permute-start(bf16[128,2048]{1,0:T(8,128)(2,1)} %get-tuple-element.60.refs_1_), channel_id=1, source_target_pairs={{0,16},{4,12},{8,24},{12,4},{16,0},{20,28},{24,8},{28,20},{1,17},{... | collective-permute-start | bytes 1572872 | tf_op jit(solution)/shard_map/ppermute | solution.py:636
  64.5 17.1 %collective-permute-start.16 = (bf16[128,2048]{1,0:T(8,128)(2,1)}, bf16[128,2048]{1,0:T(8,128)(2,1)S(1)}, u32[]{:S(2)}, u32[]{:S(2)}) collective-permute-start(bf16[128,2048]{1,0:T(8,128)(2,1)} %get-tuple-element.61), channel_id=1, source_target_pairs={{1,0},{2,3},{5,4},{6,7},{9,8},{10,11},{13,12},{14,15},{17,16},{18,... | collective-permute-start | bytes 1572872 | tf_op jit(solution)/shard_map/ppermute | solution.py:630
  67.1 22.0 %collective-permute-start.25 = (bf16[128,2048]{1,0:T(8,128)(2,1)}, bf16[128,2048]{1,0:T(8,128)(2,1)S(1)}, u32[]{:S(2)}, u32[]{:S(2)}) collective-permute-start(bf16[128,2048]{1,0:T(8,128)(2,1)} %get-tuple-element.54.refs_1_), channel_id=1, source_target_pairs={{0,4},{4,0},{1,5},{5,1},{2,6},{6,2},{3,7},{7,3},{8,12},{12,8},{9,1... | collective-permute-start | bytes 1572872 | tf_op jit(solution)/shard_map/ppermute | solution.py:627
  73.1 16.3 %collective-permute-start.26 = (bf16[128,2048]{1,0:T(8,128)(2,1)S(1)}, bf16[128,2048]{1,0:T(8,128)(2,1)S(1)}, u32[]{:S(2)}, u32[]{:S(2)}) collective-permute-start(bf16[128,2048]{1,0:T(8,128)(2,1)S(1)} %copy-done.40), channel_id=1, source_target_pairs={{0,4},{4,0},{1,5},{5,1},{2,6},{6,2},{3,7},{7,3},{8,12},{12,8},{9,1... | collective-permute-start | bytes 1572872 | tf_op jit(solution)/shard_map/ppermute | solution.py:627
  77.2 14.1 %collective-permute-start.20 = (bf16[128,2048]{1,0:T(8,128)(2,1)}, bf16[128,2048]{1,0:T(8,128)(2,1)S(1)}, u32[]{:S(2)}, u32[]{:S(2)}) collective-permute-start(bf16[128,2048]{1,0:T(8,128)(2,1)} %get-tuple-element.55.refs_0_), channel_id=1, source_target_pairs={{0,4},{4,0},{1,5},{5,1},{2,6},{6,2},{3,7},{7,3},{8,12},{12,8},{9,1... | collective-permute-start | bytes 1572872 | tf_op jit(solution)/shard_map/ppermute | solution.py:627
  81.6 12.0 %collective-permute-start.21 = (bf16[128,2048]{1,0:T(8,128)(2,1)}, bf16[128,2048]{1,0:T(8,128)(2,1)S(1)}, u32[]{:S(2)}, u32[]{:S(2)}) collective-permute-start(bf16[128,2048]{1,0:T(8,128)(2,1)} %get-tuple-element.60.refs_1_), channel_id=1, source_target_pairs={{0,4},{4,0},{1,5},{5,1},{2,6},{6,2},{3,7},{7,3},{8,12},{12,8},{9,1... | collective-permute-start | bytes 1572872 | tf_op jit(solution)/shard_map/ppermute | solution.py:627
  81.6 10.7 %collective-permute-start.27 = (bf16[128,2048]{1,0:T(8,128)(2,1)}, bf16[128,2048]{1,0:T(8,128)(2,1)S(1)}, u32[]{:S(2)}, u32[]{:S(2)}) collective-permute-start(bf16[128,2048]{1,0:T(8,128)(2,1)} %get-tuple-element.69.refs_3_), channel_id=1, source_target_pairs={{0,4},{4,0},{1,5},{5,1},{2,6},{6,2},{3,7},{7,3},{8,12},{12,8},{9,1... | collective-permute-start | bytes 1572872 | tf_op jit(solution)/shard_map/ppermute | solution.py:627
  89.1 13.1 %collective-permute-start.22 = (bf16[128,2048]{1,0:T(8,128)(2,1)}, bf16[128,2048]{1,0:T(8,128)(2,1)S(1)}, u32[]{:S(2)}, u32[]{:S(2)}) collective-permute-start(bf16[128,2048]{1,0:T(8,128)(2,1)} %get-tuple-element.66.refs_2_), channel_id=1, source_target_pairs={{0,4},{4,0},{1,5},{5,1},{2,6},{6,2},{3,7},{7,3},{8,12},{12,8},{9,1... | collective-permute-start | bytes 1572872 | tf_op jit(solution)/shard_map/ppermute | solution.py:627
  89.4 14.1 %collective-permute-start.23 = (bf16[128,2048]{1,0:T(8,128)(2,1)}, bf16[128,2048]{1,0:T(8,128)(2,1)S(1)}, u32[]{:S(2)}, u32[]{:S(2)}) collective-permute-start(bf16[128,2048]{1,0:T(8,128)(2,1)} %get-tuple-element.67.refs_3_), channel_id=1, source_target_pairs={{0,4},{4,0},{1,5},{5,1},{2,6},{6,2},{3,7},{7,3},{8,12},{12,8},{9,1... | collective-permute-start | bytes 1572872 | tf_op jit(solution)/shard_map/ppermute | solution.py:627
  91.2 21.1 %collective-permute-start.18 = (bf16[128,2048]{1,0:T(8,128)(2,1)S(1)}, bf16[128,2048]{1,0:T(8,128)(2,1)S(1)}, u32[]{:S(2)}, u32[]{:S(2)}) collective-permute-start(bf16[128,2048]{1,0:T(8,128)(2,1)S(1)} %broadcast_select_fusion.refs_0_), channel_id=1, source_target_pairs={{0,8},{4,20},{8,0},{12,28},{16,24},{20,4},{24,16},{28,12},{1,9},{5... | collective-permute-start | bytes 1572872 | tf_op jit(solution)/shard_map/ppermute | solution.py:633
  92.4 20.1 %collective-permute-start.19 = (bf16[128,2048]{1,0:T(8,128)(2,1)S(1)}, bf16[128,2048]{1,0:T(8,128)(2,1)S(1)}, u32[]{:S(2)}, u32[]{:S(2)}) collective-permute-start(bf16[128,2048]{1,0:T(8,128)(2,1)S(1)} %broadcast_select_fusion.refs_0_), channel_id=1, source_target_pairs={{0,16},{4,12},{8,24},{12,4},{16,0},{20,28},{24,8},{28,20},{1,17},{... | collective-permute-start | bytes 1572872 | tf_op jit(solution)/shard_map/ppermute | solution.py:633
  93.6 18.9 %collective-permute-start.17 = (bf16[128,2048]{1,0:T(8,128)(2,1)}, bf16[128,2048]{1,0:T(8,128)(2,1)S(1)}, u32[]{:S(2)}, u32[]{:S(2)}) collective-permute-start(bf16[128,2048]{1,0:T(8,128)(2,1)} %get-tuple-element.63.refs_1_), channel_id=1, source_target_pairs={{0,16},{4,12},{8,24},{12,4},{16,0},{20,28},{24,8},{28,20},{1,17},{... | collective-permute-start | bytes 1572872 | tf_op jit(solution)/shard_map/ppermute | solution.py:636
  102.2 12.0 %collective-permute-start.28 = (bf16[128,2048]{1,0:T(8,128)(2,1)}, bf16[128,2048]{1,0:T(8,128)(2,1)}, u32[]{:S(2)}, u32[]{:S(2)}) collective-permute-start(bf16[128,2048]{1,0:T(8,128)(2,1)} %broadcast_select_fusion.1.refs_0_), channel_id=1, source_target_pairs={{0,4},{4,0},{1,5},{5,1},{2,6},{6,2},{3,7},{7,3},{8,12},{12,8},{9,1... | collective-permute-start | bytes 1572872 | tf_op jit(solution)/shard_map/ppermute | solution.py:627
  103.5 12.1 %collective-permute-start.29 = (bf16[128,2048]{1,0:T(8,128)(2,1)}, bf16[128,2048]{1,0:T(8,128)(2,1)}, u32[]{:S(2)}, u32[]{:S(2)}) collective-permute-start(bf16[128,2048]{1,0:T(8,128)(2,1)} %get-tuple-element.63.refs_1_), channel_id=1, source_target_pairs={{0,4},{4,0},{1,5},{5,1},{2,6},{6,2},{3,7},{7,3},{8,12},{12,8},{9,1... | collective-permute-start | bytes 1572872 | tf_op jit(solution)/shard_map/ppermute | solution.py:627
  113.9 11.7 %collective-permute-start.32 = (bf16[128,2048]{1,0:T(8,128)(2,1)}, bf16[128,2048]{1,0:T(8,128)(2,1)}, u32[]{:S(2)}, u32[]{:S(2)}) collective-permute-start(bf16[128,2048]{1,0:T(8,128)(2,1)} %get-tuple-element.79.refs_1_), channel_id=1, source_target_pairs={{0,16},{4,12},{8,24},{12,4},{16,0},{20,28},{24,8},{28,20},{1,17},{... | collective-permute-start | bytes 1572872 | tf_op jit(solution)/shard_map/ppermute | solution.py:636
  114.2 11.6 %collective-permute-start.33 = (bf16[128,2048]{1,0:T(8,128)(2,1)}, bf16[128,2048]{1,0:T(8,128)(2,1)}, u32[]{:S(2)}, u32[]{:S(2)}) collective-permute-start(bf16[128,2048]{1,0:T(8,128)(2,1)} %copy-done.29), channel_id=1, source_target_pairs={{0,4},{4,0},{1,5},{5,1},{2,6},{6,2},{3,7},{7,3},{8,12},{12,8},{9,1... | collective-permute-start | bytes 1572872 | tf_op jit(solution)/shard_map/ppermute | solution.py:627
  115.6 10.2 %collective-permute-start.34 = (bf16[128,2048]{1,0:T(8,128)(2,1)}, bf16[128,2048]{1,0:T(8,128)(2,1)}, u32[]{:S(2)}, u32[]{:S(2)}) collective-permute-start(bf16[128,2048]{1,0:T(8,128)(2,1)} %get-tuple-element.79.refs_1_), channel_id=1, source_target_pairs={{0,4},{4,0},{1,5},{5,1},{2,6},{6,2},{3,7},{7,3},{8,12},{12,8},{9,1... | collective-permute-start | bytes 1572872 | tf_op jit(solution)/shard_map/ppermute | solution.py:627
  115.7 10.1 %collective-permute-start.35 = (bf16[128,2048]{1,0:T(8,128)(2,1)}, bf16[128,2048]{1,0:T(8,128)(2,1)}, u32[]{:S(2)}, u32[]{:S(2)}) collective-permute-start(bf16[128,2048]{1,0:T(8,128)(2,1)} %get-tuple-element.80.refs_2_), channel_id=1, source_target_pairs={{0,4},{4,0},{1,5},{5,1},{2,6},{6,2},{3,7},{7,3},{8,12},{12,8},{9,1... | collective-permute-start | bytes 1572872 | tf_op jit(solution)/shard_map/ppermute | solution.py:627
  140.9 9.9 %collective-permute-start.38 = (bf16[1024,128]{1,0:T(8,128)(2,1)}, bf16[1024,128]{1,0:T(8,128)(2,1)S(1)}, u32[]{:S(2)}, u32[]{:S(2)}) collective-permute-start(bf16[1024,128]{1,0:T(8,128)(2,1)} %fusion.9), channel_id=1, source_target_pairs={{0,8},{8,0},{16,24},{20,4},{24,16},{28,12},{1,9},{9,1},{17,25},{21... | collective-permute-start | bytes 786440 | tf_op jit(solution)/shard_map/ppermute | solution.py:574
  151.7 9.1 %collective-permute-start.39 = (bf16[1024,128]{1,0:T(8,128)(2,1)}, bf16[1024,128]{1,0:T(8,128)(2,1)S(1)}, u32[]{:S(2)}, u32[]{:S(2)}) collective-permute-start(bf16[1024,128]{1,0:T(8,128)(2,1)} %join.12), channel_id=1, source_target_pairs={{4,12},{12,4},{16,0},{20,28},{24,8},{28,20},{5,13},{13,5},{17,1},{... | collective-permute-start | bytes 786440 | tf_op jit(solution)/shard_map/ppermute | solution.py:592
  (53 other events, 336.6 us)

commit v4 on v3

--- a/solution.py
+++ b/solution.py
@@ -156,9 +156,9 @@
     number = len(arrays)
     return kernel_call(
         join_kernel,
-        ["H"] * number + ["A"] * len(others),
-        (*arrays, *others),
-        ["H"] * number,
+        ["A"] * (number + len(others)),
+        (*[fast(one) for one in arrays], *others),
+        ["A"] * number,
         [(one.shape, one.dtype) for one in arrays],
         "join",
         (0, 0),
@@ -249,19 +249,12 @@
     return sum(block.shape[0] for block in blocks)
 
 
-def spans(blocks):
+def back_blocks(blocks):
     at = 0
     for block in blocks:
-        yield block, at, block.shape[0]
-        at += block.shape[0]
-
-
-def load_rows(copies, blocks, w_ref):
-    bring = []
-    for block, at, rows in spans(blocks):
-        copy = copies.start(block, w_ref.at[pl.ds(at, rows), :])
-        bring += [copy] * (rows // PIECE)
-    return bring
+        for row in range(0, block.shape[0], PIECE):
+            yield at, block[row : row + PIECE, :]
+            at += 1
 
 
 def load_tokens(copies, places_ref, tokens_ref, some_ref):
@@ -276,20 +269,14 @@
     return bring
 
 
-def wait_once(copies, done):
-    for copy in copies:
-        if not any(copy is one for one in done):
-            copy.wait()
-            done.append(copy)
-
-
-def back_part(copies, places_ref, masked, w_ref, bring, done, out_ref, round_ref):
+def back_part(copies, places_ref, masked, blocks, out_ref, round_ref):
     going = []
-    for at in range(0, w_ref.shape[0], 2 * PIECE):
-        wait_once(bring[at // PIECE : at // PIECE + 2], done)
-        both = slice(at, at + 2 * PIECE)
-        round_ref[:, both] = nt(masked[...], w_ref[both, :]).astype(bf16)
-        for piece in (at // PIECE, at // PIECE + 1):
+    pieces = list(back_blocks(blocks))
+    for (first, upper), (second, lower) in zip(pieces[::2], pieces[1::2]):
+        both = slice(first * PIECE, (second + 1) * PIECE)
+        made = nt(masked[...], jnp.concatenate([upper, lower], axis=0))
+        round_ref[:, both] = made.astype(bf16)
+        for piece in (first, second):
             place = pl.multiple_of(places_ref[piece] * PIECE, PIECE)
             going.append(
                 copies.start(
@@ -300,93 +287,91 @@
     return going
 
 
-def products_kernel(size, has_before, places_ref, tokens_ref, masked, *refs):
-    blocks = refs[:size]
-    refs = refs[size:]
-    if has_before:
-        before_ref, _, *refs = refs
-    sum_ref, back_out, mark_ref, w_ref, some_ref, round_ref, sems = refs
+def products_kernel(size, project, back, has_sum, has_back, places_ref, *refs):
+    blocks, refs = refs[:size], list(refs[size:])
+    tokens_ref = refs.pop(0) if project else None
+    before_ref = refs.pop(0) if has_sum else None
+    masked = refs.pop(0) if back else None
+    if has_back:
+        refs.pop(0)
+    sum_ref = refs.pop(0) if project else None
+    back_out = refs.pop(0) if back else None
+    mark_ref = refs.pop(0)
+    sems = refs.pop()
     set_mark(mark_ref)
     copies = Copies(sems)
-    bring = load_rows(copies, blocks, w_ref)
-    token_copies = load_tokens(copies, places_ref, tokens_ref, some_ref)
-    done = []
-    going = back_part(copies, places_ref, masked, w_ref, bring, done, back_out, round_ref)
-    wait_once(token_copies, done)
-    for at in range(0, w_ref.shape[1], WIDE):
-        part = slice(at, at + WIDE)
-        made = nn(some_ref[...], w_ref[:, part])
-        if has_before:
-            made = made + before_ref[:, part]
-        sum_ref[:, part] = made
+    going = []
+    if project:
+        some_ref = refs.pop(0)
+        bring = load_tokens(copies, places_ref, tokens_ref, some_ref)
+    if back:
+        going = back_part(copies, places_ref, masked, blocks, back_out, refs.pop(0))
+    if project:
+        for copy in bring:
+            copy.wait()
+        for at in range(0, sum_ref.shape[1], WIDE):
+            part = slice(at, at + WIDE)
+            made = nn(some_ref[...], jnp.concatenate([block[:, part] for block in blocks], axis=0))
+            if has_sum:
+                made = made + before_ref[:, part]
+            sum_ref[:, part] = made
     for copy in going:
         copy.wait()
 
 
-def products_call(places, tokens, blocks, masked, before):
+def products_call(places, blocks, tokens, partial=None, masked=None, grad=None, project=True):
     length, width = tokens.shape
-    total = masked.shape[1]
+    total = blocks[0].shape[1]
     depth = rows_of(blocks)
     number = depth // PIECE
-    extra = [] if before is None else list(before)
-    return kernel_call(
-        functools.partial(products_kernel, len(blocks), before is not None),
-        "SHV" + "H" * len(blocks) + "VH"[: len(extra)],
-        (places, tokens, masked, *blocks, *extra),
-        "VHV",
-        [((length, total), f32), ((length, width), bf16), (MARK.shape, f32)],
-        "products",
-        (4 * length * depth * total, depth * total * 2 + 8 * length * total),
-        [
-            pltpu.VMEM((depth, total), bf16),
-            pltpu.VMEM((length, depth), bf16),
-            pltpu.VMEM((length, depth), bf16),
-            pltpu.SemaphoreType.DMA((len(blocks) + 2 * number,)),
-        ],
-        {3 + len(blocks) + at: at for at in range(len(extra))},
-    )
-
-
-def back_kernel(size, places_ref, masked, *refs):
-    blocks = refs[:size]
-    _, back_out, w_ref, round_ref, sems = refs[size:]
-    copies = Copies(sems)
-    bring = load_rows(copies, blocks, w_ref)
-    for copy in back_part(copies, places_ref, masked, w_ref, bring, [], back_out, round_ref):
-        copy.wait()
-
-
-def back_call(places, blocks, masked, before):
-    length, total = masked.shape
-    depth = rows_of(blocks)
-    number = depth // PIECE
-    return kernel_call(
-        functools.partial(back_kernel, len(blocks)),
-        "SV" + "H" * len(blocks) + "H",
-        (places, masked, *blocks, before),
-        "H",
-        [(before.shape, bf16)],
-        "grad_tokens",
-        (2 * length * depth * total, depth * total * 2 + 4 * length * total),
-        [
-            pltpu.VMEM((depth, total), bf16),
-            pltpu.VMEM((length, depth), bf16),
-            pltpu.SemaphoreType.DMA((len(blocks) + number,)),
-        ],
-        {2 + len(blocks): 0},
-    )[0]
+    back = masked is not None
+    places_in, args = "S" + "V" * len(blocks), [places, *blocks]
+    places_out, outs = "", []
+    scratch, aliases = [], {}
+    if project:
+        places_in, args = places_in + "H", args + [tokens]
+        if partial is not None:
+            aliases[len(args)] = 0
+            places_in, args = places_in + "V", args + [partial]
+        places_out, outs = "V", [((length, total), f32)]
+        scratch.append(pltpu.VMEM((length, depth), bf16))
+    if back:
+        places_in, args = places_in + "V", args + [masked]
+        if grad is not None:
+            aliases[len(args)] = len(outs)
+            places_in, args = places_in + "H", args + [grad]
+        places_out, outs = places_out + "H", outs + [((length, width), bf16)]
+        scratch.append(pltpu.VMEM((length, depth), bf16))
+    made = kernel_call(
+        functools.partial(
+            products_kernel, len(blocks), project, back, partial is not None, grad is not None
+        ),
+        places_in,
+        args,
+        places_out + "V",
+        outs + [(MARK.shape, f32)],
+        "products" if project and back else "project" if project else "grad_tokens",
+        (2 * (project + back) * length * depth * total, 0),
+        scratch + [pltpu.SemaphoreType.DMA((2 * number,))],
+        aliases,
+    )
+    made = list(made)
+    partial = made.pop(0) if project else partial
+    grad = made.pop(0) if back else grad
+    return partial, grad, made[0]
 
 
 def query_kernel(size, places_ref, tokens_ref, sum_ref, mask_ref, grad_ref, *refs):
     blocks = refs[:size]
-    queries, own_ref, sent_ref, w_ref, some_ref, sems = refs[size:]
+    queries, own_ref, sent_ref, some_ref, sems = refs[size:]
     copies = Copies(sems)
     bring = load_tokens(copies, places_ref, tokens_ref, some_ref)
-    bring += load_rows(copies, blocks, w_ref)
-    wait_once(bring, [])
-    for at in range(0, w_ref.shape[1], WIDE):
+    for copy in bring:
+        copy.wait()
+    for at in range(0, queries.shape[1], WIDE):
         part = slice(at, at + WIDE)
-        made = nn(some_ref[...], w_ref[:, part]) + sum_ref[:, part]
+        made = nn(some_ref[...], jnp.concatenate([block[:, part] for block in blocks], axis=0))
+        made = made + sum_ref[:, part]
         made = (made * mask_ref[:, part].astype(f32)).astype(bf16)
         queries[:, part] = made
         for head in range(0, WIDE, HEAD):
@@ -403,17 +388,13 @@
     number = depth // PIECE
     return kernel_call(
         functools.partial(query_kernel, len(blocks)),
-        "SHVVV" + "H" * len(blocks),
+        "SHVVV" + "V" * len(blocks),
         (places, tokens, before, q_mask, cotangent, *blocks),
         "VVV",
         [((length, total), bf16), ((total, HEAD), f32), ((total, HEAD), bf16)],
         "queries",
-        (2 * length * depth * total, depth * total * 2 + 12 * length * total),
-        [
-            pltpu.VMEM((depth, total), bf16),
-            pltpu.VMEM((length, depth), bf16),
-            pltpu.SemaphoreType.DMA((len(blocks) + number,)),
-        ],
+        (2 * length * depth * total, 0),
+        [pltpu.VMEM((length, depth), bf16), pltpu.SemaphoreType.DMA((number,))],
     )
 
 
@@ -670,19 +651,19 @@
         first_1, second_1 = cross(near)
         far = along(near, middle)
         mid_out = along(mid, outward)
-        third_0, first_1, second_1, far, mid_out, message = join(
-            [third_0, first_1, second_1, far, mid_out, message]
+        third_0, first_1, second_1, far, mid_out = join(
+            [third_0, first_1, second_1, far, mid_out]
         )
         third_1 = onward(first_1)
         next_layer = jnp.where(within, mid, mid_out)
         first_2, second_2 = cross(next_layer)
         far_out = along(far, outward)
-        high, low = scan_second(message, *rest, False)
-        masked, q_mask, cotangent, mark = masked_call(
-            factor, cotangent, q_spikes, values, keys, high, low
-        )
+        own_blocks = [q_weight, first_0, second_0, third_0, other_0]
+        own_blocks += [sibling(one) for one in own_blocks[1:4]]
+        own_places = numbers(sides, levels[:1])
+        partial, _, own_mark = products_call(own_places, own_blocks, tokens)
         third_1, first_2, second_2, far_out = join(
-            [third_1, first_2, second_2, far_out], [mark]
+            [third_1, first_2, second_2, far_out], [own_mark]
         )
         third_2 = onward(first_2)
         last_layer = jnp.where(within, far, far_out)
@@ -691,15 +672,23 @@
         def whole(*mine):
             return list(mine) + [sibling(one) for one in mine]
 
-        blocks = [q_weight, first_0, second_0, third_0, other_0]
-        blocks += [sibling(one) for one in blocks[1:4]]
-        *done, _ = products_call(numbers(sides, levels[:1]), tokens, blocks, masked, None)
+        high, low = scan_second(message, *rest, False)
+        masked, q_mask, cotangent, _ = masked_call(
+            factor, cotangent, q_spikes, values, keys, high, low
+        )
+        _, grad, mark_0 = products_call(
+            own_places, own_blocks, tokens, masked=masked, project=False
+        )
         blocks = whole(near, first_1, second_1, third_1)
-        *done, mark = products_call(numbers(sides, levels[1:2]), tokens, blocks, masked, done)
-        third_2, first_3, second_3 = join([third_2, first_3, second_3], [mark])
+        partial, grad, mark_1 = products_call(
+            numbers(sides, levels[1:2]), blocks, tokens, partial, masked, grad
+        )
+        third_2, first_3, second_3 = join([third_2, first_3, second_3], [mark_0, mark_1])
         third_3 = onward(first_3)
         blocks = whole(next_layer, first_2, second_2, third_2)
-        *done, mark = products_call(numbers(sides, levels[2:3]), tokens, blocks, masked, done)
+        partial, grad, mark = products_call(
+            numbers(sides, levels[2:3]), blocks, tokens, partial, masked, grad
+        )
         third_3, = join([third_3], [mark])
         late = whole(last_layer, first_3, second_3, third_3)
         late_places = numbers(sides, levels[3:])
@@ -708,9 +697,8 @@
             factor, cotangent, q_spikes, values, keys, high, low
         )
         half = places.shape[0] // 2
-        *done, _ = products_call(places[:half], tokens, arrived[:1], masked, None)
+        partial, grad, _ = products_call(places[:half], arrived[:1], tokens, masked=masked)
         late, late_places = arrived[1:], places[half:]
-    partial, grad_tokens = done
     queries, own, sent = query_call(late_places, tokens, late, partial, q_mask, cotangent)
     attended, attended_mark = attend_call(factor, queries, keys, values, high, low)
     key_part, value_part, inner_mark = inner_call(queries, keys, values, cotangent)
@@ -720,7 +708,9 @@
         adjoint = scan_second(message, *rest, True, [inner_mark])
     else:
         adjoint = halves(scan_any(own, sent, chips * 2, True))
-    grad_tokens = back_call(late_places, late, masked, grad_tokens)
+    _, grad_tokens, _ = products_call(
+        late_places, late, tokens, masked=masked, grad=grad, project=False
+    )
     grad_keys, grad_values = outer_call(
         factor, key_part, value_part, keys, values, k_mask, *adjoint
     )

time: 177 us -> 158 us (0.89)
  the two profiles are of different devices: /device:TPU:1 before, /device:TPU:12 now
where the time goes in v4:
time: 158 us; the launch traced here: 157 us
  Pallas kernels  55.5 us (35%)
  starting transfers between devices  41.4 us (26%)
  local copies, waits for them, and re-layouts  30.5 us (19%)
  waiting for transfers between devices  19.3 us (12%)
  other arithmetic  8.21 us (5%)
  between operations  1.65 us (1%)
    pallas_call x18, Pallas kernels, kernel_call(): made(*[holds[place](one) if place in holds else one for place, one in zip...  55.5 us
    unnamed x126, local copies, waits for them, and re-layouts  30.2 us
    ppermute x5, starting transfers between devices, along(): return lax.ppermute(array, 'dp', pairs)  10.7 us
    ppermute x4, waiting for transfers between devices, cross(): lax.ppermute(array, CTX, links(1))  6.62 us
    ppermute x4, starting transfers between devices, cross(): lax.ppermute(array, CTX, links(1))  6.54 us
    ppermute x2, starting transfers between devices, scan_first(): lax.ppermute(both.astype(bf16), CTX, links(1, upward(reverse))).astype(f32)  6.41 us
    ppermute x4, starting transfers between devices, cross(): lax.ppermute(array, CTX, links(2))  6.13 us
    ppermute x5, waiting for transfers between devices, along(): return lax.ppermute(array, 'dp', pairs)  4.91 us
  transfers between devices with their start and end apart: 41, of which 9 were waited for; matrix products, arithmetic and copies ran while one was open for 5% of the time, Pallas kernels for 29%

profile of v4, /device:TPU:12, one launch (start us, length us, event | category | flops | bytes accessed | tf_op | source)
XLA Modules:
  0.0 156.5 jit_solution(17989062182817835218)
XLA Ops:
  1.1 4.6 %collective-permute-start.1 = (bf16[128,2048]{1,0:T(8,128)(2,1)}, bf16[128,2048]{1,0:T(8,128)(2,1)S(1)}, u32[]{:S(2)}, u32[]{:S(2)}) collective-permute-start(bf16[128,2048]{1,0:T(8,128)(2,1)} %refs_0_.3), channel_id=1, source_target_pairs={{1,2},{2,1},{5,6},{6,5},{9,10},{10,9},{13,14},{14,13},{17,18},{18,... | collective-permute-start | bytes 1572872 | tf_op jit(solution)/shard_map/ppermute | solution.py:611
  5.8 1.6 collective-permute-start.2
  7.8 3.5 %own_memory.1 = (bf16[384,2048]{1,0:T(8,128)(2,1)S(1)}, bf16[384,2048]{1,0:T(8,128)(2,1)S(1)}, bf16[384,2048]{1,0:T(8,128)(2,1)S(1)}, f32[2048,128]{1,0:T(8,128)...) custom-call(bf16[384,2048]{1,0:T(8,128)(2,1)} %bitcast.48, s32[384,2048]{1,0:T(8,128)} %bitcast.47, ...), custom_call_target="tpu_custom_call" | custom-call | flops 201326592 | bytes 9437184 | tf_op jit(solution)/shard_map/own_memory/pallas_call | solution.py:74
  14.6 3.0 %collective-permute-done.1.refs_1_ = bf16[128,2048]{1,0:T(8,128)(2,1)S(1)} collective-permute-done((bf16[128,2048]{1,0:T(8,128)(2,1)}, bf16[128,2048]{1,0:T(8,128)(2,1)S(1)}, u32[]{:S(2)}, u32[]{:S(2)}) %collective-permute-start.1) | collective-permute-done | bytes 524320 | tf_op jit(solution)/shard_map/ppermute | solution.py:611
  17.6 1.8 %collective-permute-done.2.refs_2_ = bf16[128,2048]{1,0:T(8,128)(2,1)S(1)} collective-permute-done((bf16[128,2048]{1,0:T(8,128)(2,1)}, bf16[128,2048]{1,0:T(8,128)(2,1)S(1)}, u32[]{:S(2)}, u32[]{:S(2)}) %collective-permute-start.2) | collective-permute-done | bytes 524320 | tf_op jit(solution)/shard_map/ppermute | solution.py:614
  20.2 1.6 collective-permute-start.5
  21.7 1.5 collective-permute-start.6
  23.3 2.2 %collective-permute-start.7 = (bf16[128,2048]{1,0:T(8,128)(2,1)S(1)}, bf16[128,2048]{1,0:T(8,128)(2,1)}, u32[]{:S(2)}, u32[]{:S(2)}) collective-permute-start(bf16[128,2048]{1,0:T(8,128)(2,1)S(1)} %get-tuple-element.53.refs_0_), channel_id=1, source_target_pairs={{1,2},{2,1},{5,6},{6,5},{9,10},{10,9},{13,14},{14,13},{17,18},{18,... | collective-permute-start | bytes 1572872 | tf_op jit(solution)/shard_map/ppermute | solution.py:611
  27.4 1.4 convert_add_fusion.1
  29.7 4.8 %collective-permute-done.5.refs_1_ = bf16[128,2048]{1,0:T(8,128)(2,1)} collective-permute-done((bf16[128,2048]{1,0:T(8,128)(2,1)S(1)}, bf16[128,2048]{1,0:T(8,128)(2,1)}, u32[]{:S(2)}, u32[]{:S(2)}) %collective-permute-start.5) | collective-permute-done | bytes 524320 | tf_op jit(solution)/shard_map/ppermute | solution.py:614
  34.5 3.4 %collective-permute-start.21 = (bf16[1024,128]{1,0:T(8,128)(2,1)}, bf16[1024,128]{1,0:T(8,128)(2,1)S(1)}, u32[]{:S(2)}, u32[]{:S(2)}) collective-permute-start(bf16[1024,128]{1,0:T(8,128)(2,1)} %fusion.8), channel_id=1, source_target_pairs={{0,8},{4,20},{8,0},{12,28},{16,24},{24,16},{1,9},{5,21},{9,1},{13,... | collective-permute-start | bytes 786440 | tf_op jit(solution)/shard_map/ppermute | solution.py:555
  39.0 3.9 %collective-permute-done.4.refs_0_ = bf16[128,2048]{1,0:T(8,128)(2,1)S(1)} collective-permute-done((bf16[128,2048]{1,0:T(8,128)(2,1)S(1)}, bf16[128,2048]{1,0:T(8,128)(2,1)S(1)}, u32[]{:S(2)}, u32[]{:S(2)}) %collective-permute-start.4) | collective-permute-done | bytes 524320 | tf_op jit(solution)/shard_map/ppermute | solution.py:617
  46.6 1.5 collective-permute-start.10
  48.9 3.3 %collective-permute-start.11 = (bf16[128,2048]{1,0:T(8,128)(2,1)}, bf16[128,2048]{1,0:T(8,128)(2,1)}, u32[]{:S(2)}, u32[]{:S(2)}) collective-permute-start(bf16[128,2048]{1,0:T(8,128)(2,1)} %broadcast_select_fusion.1.refs_0_), channel_id=1, source_target_pairs={{0,16},{4,12},{8,24},{12,4},{16,0},{20,28},{24,8},{28,20},{1,17},{... | collective-permute-start | bytes 1572872 | tf_op jit(solution)/shard_map/ppermute | solution.py:614
  53.1 2.1 %collective-permute-start.12 = (bf16[128,2048]{1,0:T(8,128)(2,1)}, bf16[128,2048]{1,0:T(8,128)(2,1)}, u32[]{:S(2)}, u32[]{:S(2)}) collective-permute-start(bf16[128,2048]{1,0:T(8,128)(2,1)} %get-tuple-element.56), channel_id=1, source_target_pairs={{1,0},{2,3},{5,4},{6,7},{9,8},{10,11},{13,12},{14,15},{17,16},{18,... | collective-permute-start | bytes 1572872 | tf_op jit(solution)/shard_map/ppermute | solution.py:611
  65.6 3.7 %project.1 = (f32[384,2048]{1,0:T(8,128)S(1)}, f32[8,128]{1,0:T(8,128)S(1)}) custom-call(s32[8]{0:T(128)S(1)} %stack.134.places_ref, bf16[128,2048]{1,0:T(8,128)(2,1)S(1)} %copy-done.40, bf16[128,2048]{1,0:T(8,128)(2,1)S(1)} %copy-done.17, bf16[128,2048]{1,0:T(8,128)(2,1)S(1)} %copy-done.20, bf16[128,2048]{1,0:T(8,128)(2,1)S(1)} %copy-done.14, ...), custom_call_target="tpu_custom_call" | custom-call | flops 1610612736 | tf_op jit(solution)/shard_map/project/pallas_call | solution.py:74
  71.7 1.9 %collective-permute-start.18 = (bf16[128,2048]{1,0:T(8,128)(2,1)S(1)}, bf16[128,2048]{1,0:T(8,128)(2,1)}, u32[]{:S(2)}, u32[]{:S(2)}) collective-permute-start(bf16[128,2048]{1,0:T(8,128)(2,1)S(1)} %broadcast_select_fusion.refs_0_), channel_id=1, source_target_pairs={{0,8},{4,20},{8,0},{12,28},{16,24},{20,4},{24,16},{28,12},{1,9},{5... | collective-permute-start | bytes 1572872 | tf_op jit(solution)/shard_map/ppermute | solution.py:614
  77.3 5.8 %masked_grad.1 = (bf16[384,2048]{1,0:T(8,128)(2,1)S(1)}, bf16[384,2048]{1,0:T(8,128)(2,1)S(1)}, bf16[384,2048]{1,0:T(8,128)(2,1)S(1)}, f32[8,128]{1,0:T(8,128)}) custom-call(bf16[384,2048]{1,0:T(8,128)(2,1)} %bitcast.51, s32[384,2048]{1,0:T(8,128)} %bitcast.50, bf16[384,2048]{1,0:T(8,128)(2,1)S(1)} %copy-done.28, bf16[384,2048]{1,0:T(8,128)(2,1)S(1)} %copy-done.23, ...), custom_call_target="tpu_custom_call" | custom-call | flops 2415919104 | bytes 9437184 | tf_op jit(solution)/shard_map/masked_grad/pallas_call | solution.py:74
  84.4 3.3 %grad_tokens.2 = (bf16[384,4096]{1,0:T(8,128)(2,1)}, f32[8,128]{1,0:T(8,128)S(1)}) custom-call(s32[8]{0:T(128)S(1)} %stack.134.places_ref, bf16[128,2048]{1,0:T(8,128)(2,1)S(1)} %copy-done.41, bf16[128,2048]{1,0:T(8,128)(2,1)S(1)} %copy-done.18, bf16[128,2048]{1,0:T(8,128)(2,1)S(1)} %copy-done.21, bf16[128,2048]{1,0:T(8,128)(2,1)S(1)} %copy-done.15, ...), custom_call_target="tpu_custom_call" | custom-call | flops 1610612736 | tf_op jit(solution)/shard_map/grad_tokens/pallas_call | solution.py:74
  88.3 5.7 %products.2 = (f32[384,2048]{1,0:T(8,128)S(1)}, bf16[384,4096]{1,0:T(8,128)(2,1)}, f32[8,128]{1,0:T(8,128)S(1)}) custom-call(s32[8]{0:T(128)S(1)} %stack.143.places_ref, bf16[128,2048]{1,0:T(8,128)(2,1)S(1)} %copy-done.12, bf16[128,2048]{1,0:T(8,128)(2,1)} %get-tuple-element.55.refs_1_, ...), custom_call_target="tpu_custom_call", output_to_operand_aliasing={{0}: (10, {}), {1}: (12, {})} | custom-call | flops 3221225472 | tf_op jit(solution)/shard_map/products/pallas_call | solution.py:74
  97.3 1.4 copy-done.1
  98.7 6.7 %products.3 = (f32[384,2048]{1,0:T(8,128)S(1)}, bf16[384,4096]{1,0:T(8,128)(2,1)}, f32[8,128]{1,0:T(8,128)S(1)}) custom-call(s32[8]{0:T(128)S(1)} %stack.125.places_ref, bf16[128,2048]{1,0:T(8,128)(2,1)} %broadcast_select_fusion.1.refs_0_, bf16[128,2048]{1,0:T(8,128)(2,1)} %get-tuple-element.60.refs_1_, ...), custom_call_target="tpu_custom_call", output_to_operand_aliasing={{0}: (10, {}), {1}: (12, {})} | custom-call | flops 3221225472 | tf_op jit(solution)/shard_map/products/pallas_call | solution.py:74
  106.0 1.8 %collective-permute-done.36.refs_7_ = bf16[128,2048]{1,0:T(8,128)(2,1)} collective-permute-done((bf16[128,2048]{1,0:T(8,128)(2,1)}, bf16[128,2048]{1,0:T(8,128)(2,1)}, u32[]{:S(2)}, u32[]{:S(2)}) %collective-permute-start.36) | collective-permute-done | bytes 524320 | tf_op jit(solution)/shard_map/ppermute | solution.py:608
  109.8 1.4 copy-done.31
  112.6 6.1 %queries.1 = (bf16[384,2048]{1,0:T(8,128)(2,1)S(1)}, f32[2048,128]{1,0:T(8,128)S(1)}, bf16[2048,128]{1,0:T(8,128)(2,1)S(1)}) custom-call(s32[8]{0:T(128)S(1)} %stack.116.places_ref, bf16[384,4096]{1,0:T(8,128)(2,1)} %bitcast.45, f32[384,2048]{1,0:T(8,128)S(1)} %get-tuple-element.77.sum_ref, bf16[384,2048]{1,0:T(8,128)(2,1)S(1)} %copy-done.34, ...), custom_call_target="tpu_custom_call" | custom-call | flops 1610612736 | tf_op jit(solution)/shard_map/queries/pallas_call | solution.py:74
  119.2 1.5 collective-permute-done.37
  122.6 3.0 %collective-permute-start.38 = (bf16[1024,128]{1,0:T(8,128)(2,1)}, bf16[1024,128]{1,0:T(8,128)(2,1)S(1)}, u32[]{:S(2)}, u32[]{:S(2)}) collective-permute-start(bf16[1024,128]{1,0:T(8,128)(2,1)} %fusion.9), channel_id=1, source_target_pairs={{0,8},{8,0},{16,24},{20,4},{24,16},{28,12},{1,9},{9,1},{17,25},{21... | collective-permute-start | bytes 786440 | tf_op jit(solution)/shard_map/ppermute | solution.py:555
  129.2 5.1 %attended.1 = (bf16[384,2048]{1,0:T(8,128)(2,1)}, f32[8,128]{1,0:T(8,128)S(1)}) custom-call(bf16[384,2048]{1,0:T(8,128)(2,1)S(1)} %copy-done.55, bf16[384,2048]{1,0:T(8,128)(2,1)S(1)} %copy-done.24, bf16[384,2048]{1,0:T(8,128)(2,1)S(1)} %copy-done.29, bf16[2048,128]{1,0:T(8,128)(2,1)S(1)} %copy-done.39, bf16[2048,128]{1,0:T(8,128)(2,1)S(1)} %copy-done.37), custom_call_target="tpu_custom_call" | custom-call | flops 2415919104 | bytes 6291456 | tf_op jit(solution)/shard_map/attended/pallas_call | solution.py:74
  134.4 3.1 %collective-permute-start.39 = (bf16[1024,128]{1,0:T(8,128)(2,1)S(1)}, bf16[1024,128]{1,0:T(8,128)(2,1)S(1)}, u32[]{:S(2)}, u32[]{:S(2)}) collective-permute-start(bf16[1024,128]{1,0:T(8,128)(2,1)S(1)} %join.12), channel_id=1, source_target_pairs={{4,12},{12,4},{16,0},{20,28},{24,8},{28,20},{5,13},{13,5},{17,1},{... | collective-permute-start | bytes 786440 | tf_op jit(solution)/shard_map/ppermute | solution.py:573
  137.6 6.9 %inner.1 = (f32[384,2048]{1,0:T(8,128)S(1)}, f32[384,2048]{1,0:T(8,128)S(1)}, f32[8,128]{1,0:T(8,128)S(1)}) custom-call(bf16[384,2048]{1,0:T(8,128)(2,1)S(1)} %copy-done.56, bf16[384,2048]{1,0:T(8,128)(2,1)S(1)} %copy-done.24, bf16[384,2048]{1,0:T(8,128)(2,1)S(1)} %copy-done.29, bf16[384,2048]{1,0:T(8,128)(2,1)S(1)} %copy-done.32), custom_call_target="tpu_custom_call" | custom-call | flops 3623878656 | bytes 12582912 | tf_op jit(solution)/shard_map/inner/pallas_call | solution.py:74
  146.0 5.2 %grad_tokens.3 = (bf16[384,4096]{1,0:T(8,128)(2,1)}, f32[8,128]{1,0:T(8,128)}) custom-call(s32[8]{0:T(128)S(1)} %stack.116.places_ref, bf16[128,2048]{1,0:T(8,128)(2,1)S(1)} %copy-done.8, bf16[128,2048]{1,0:T(8,128)(2,1)} %get-tuple-element.80.refs_1_, bf16[128,2048]{1,0:T(8,128)(2,1)S(1)} %copy-done.5, ...), custom_call_target="tpu_custom_call", output_to_operand_aliasing={{0}: (10, {})} | custom-call | flops 1610612736 | tf_op jit(solution)/shard_map/grad_tokens/pallas_call | solution.py:74
  152.8 3.5 %outer.1 = (bf16[384,2048]{1,0:T(8,128)(2,1)}, bf16[384,2048]{1,0:T(8,128)(2,1)}) custom-call(f32[384,2048]{1,0:T(8,128)S(1)} %get-tuple-element.87.key_ref, f32[384,2048]{1,0:T(8,128)S(1)} %get-tuple-element.88.val_ref, bf16[384,2048]{1,0:T(8,128)(2,1)S(1)} %copy-done.24, bf16[384,2048]{1,0:T(8,128)(2,1)S(1)} %copy-done.29, ...), custom_call_target="tpu_custom_call" | custom-call | flops 805306368 | bytes 15728640 | tf_op jit(solution)/shard_map/outer/pallas_call | solution.py:74
  (212 shorter events, 48.4 us)
Async XLA Ops:
  0.6 13.9 %collective-permute-start = (bf16[128,2048]{1,0:T(8,128)(2,1)}, bf16[128,2048]{1,0:T(8,128)(2,1)S(1)}, u32[]{:S(2)}, u32[]{:S(2)}) collective-permute-start(bf16[128,2048]{1,0:T(8,128)(2,1)} %refs_0_.3), channel_id=1, source_target_pairs={{0,1},{1,0},{2,3},{3,2},{4,5},{5,4},{6,7},{7,6},{8,9},{9,8},{10,11... | collective-permute-start | bytes 1572872 | tf_op jit(solution)/shard_map/ppermute | solution.py:611
  1.1 16.4 %collective-permute-start.1 = (bf16[128,2048]{1,0:T(8,128)(2,1)}, bf16[128,2048]{1,0:T(8,128)(2,1)S(1)}, u32[]{:S(2)}, u32[]{:S(2)}) collective-permute-start(bf16[128,2048]{1,0:T(8,128)(2,1)} %refs_0_.3), channel_id=1, source_target_pairs={{1,2},{2,1},{5,6},{6,5},{9,10},{10,9},{13,14},{14,13},{17,18},{18,... | collective-permute-start | bytes 1572872 | tf_op jit(solution)/shard_map/ppermute | solution.py:611
  5.8 13.6 %collective-permute-start.2 = (bf16[128,2048]{1,0:T(8,128)(2,1)}, bf16[128,2048]{1,0:T(8,128)(2,1)S(1)}, u32[]{:S(2)}, u32[]{:S(2)}) collective-permute-start(bf16[128,2048]{1,0:T(8,128)(2,1)} %refs_0_.3), channel_id=1, source_target_pairs={{0,8},{4,20},{8,0},{12,28},{16,24},{20,4},{24,16},{28,12},{1,9},{5... | collective-permute-start | bytes 1572872 | tf_op jit(solution)/shard_map/ppermute | solution.py:614
  7.3 12.1 %collective-permute-start.3 = (bf16[128,2048]{1,0:T(8,128)(2,1)}, bf16[128,2048]{1,0:T(8,128)(2,1)S(1)}, u32[]{:S(2)}, u32[]{:S(2)}) collective-permute-start(bf16[128,2048]{1,0:T(8,128)(2,1)} %refs_0_.3), channel_id=1, source_target_pairs={{0,16},{4,12},{8,24},{12,4},{16,0},{20,28},{24,8},{28,20},{1,17},{... | collective-permute-start | bytes 1572872 | tf_op jit(solution)/shard_map/ppermute | solution.py:614
  20.2 14.3 %collective-permute-start.5 = (bf16[128,2048]{1,0:T(8,128)(2,1)S(1)}, bf16[128,2048]{1,0:T(8,128)(2,1)}, u32[]{:S(2)}, u32[]{:S(2)}) collective-permute-start(bf16[128,2048]{1,0:T(8,128)(2,1)S(1)} %get-tuple-element.53.refs_0_), channel_id=1, source_target_pairs={{0,8},{4,20},{8,0},{12,28},{16,24},{20,4},{24,16},{28,12},{1,9},{5... | collective-permute-start | bytes 1572872 | tf_op jit(solution)/shard_map/ppermute | solution.py:614
  21.7 16.2 %collective-permute-start.6 = (bf16[128,2048]{1,0:T(8,128)(2,1)S(1)}, bf16[128,2048]{1,0:T(8,128)(2,1)S(1)}, u32[]{:S(2)}, u32[]{:S(2)}) collective-permute-start(bf16[128,2048]{1,0:T(8,128)(2,1)S(1)} %get-tuple-element.53.refs_0_), channel_id=1, source_target_pairs={{0,16},{4,12},{8,24},{12,4},{16,0},{20,28},{24,8},{28,20},{1,17},{... | collective-permute-start | bytes 1572872 | tf_op jit(solution)/shard_map/ppermute | solution.py:614
  23.3 15.7 %collective-permute-start.7 = (bf16[128,2048]{1,0:T(8,128)(2,1)S(1)}, bf16[128,2048]{1,0:T(8,128)(2,1)}, u32[]{:S(2)}, u32[]{:S(2)}) collective-permute-start(bf16[128,2048]{1,0:T(8,128)(2,1)S(1)} %get-tuple-element.53.refs_0_), channel_id=1, source_target_pairs={{1,2},{2,1},{5,6},{6,5},{9,10},{10,9},{13,14},{14,13},{17,18},{18,... | collective-permute-start | bytes 1572872 | tf_op jit(solution)/shard_map/ppermute | solution.py:611
  25.5 17.4 %collective-permute-start.4 = (bf16[128,2048]{1,0:T(8,128)(2,1)S(1)}, bf16[128,2048]{1,0:T(8,128)(2,1)S(1)}, u32[]{:S(2)}, u32[]{:S(2)}) collective-permute-start(bf16[128,2048]{1,0:T(8,128)(2,1)S(1)} %get-tuple-element.52.refs_1_), channel_id=1, source_target_pairs={{0,16},{4,12},{8,24},{12,4},{16,0},{20,28},{24,8},{28,20},{1,17},{... | collective-permute-start | bytes 1572872 | tf_op jit(solution)/shard_map/ppermute | solution.py:617
  26.0 16.8 %collective-permute-start.8 = (bf16[128,2048]{1,0:T(8,128)(2,1)S(1)}, bf16[128,2048]{1,0:T(8,128)(2,1)S(1)}, u32[]{:S(2)}, u32[]{:S(2)}) collective-permute-start(bf16[128,2048]{1,0:T(8,128)(2,1)S(1)} %get-tuple-element.51), channel_id=1, source_target_pairs={{1,0},{2,3},{5,4},{6,7},{9,8},{10,11},{13,12},{14,15},{17,16},{18,... | collective-permute-start | bytes 1572872 | tf_op jit(solution)/shard_map/ppermute | solution.py:611
  34.5 9.0 %collective-permute-start.21 = (bf16[1024,128]{1,0:T(8,128)(2,1)}, bf16[1024,128]{1,0:T(8,128)(2,1)S(1)}, u32[]{:S(2)}, u32[]{:S(2)}) collective-permute-start(bf16[1024,128]{1,0:T(8,128)(2,1)} %fusion.8), channel_id=1, source_target_pairs={{0,8},{4,20},{8,0},{12,28},{16,24},{24,16},{1,9},{5,21},{9,1},{13,... | collective-permute-start | bytes 786440 | tf_op jit(solution)/shard_map/ppermute | solution.py:555
  39.0 9.2 %collective-permute-start.14 = (bf16[128,2048]{1,0:T(8,128)(2,1)S(1)}, bf16[128,2048]{1,0:T(8,128)(2,1)S(1)}, u32[]{:S(2)}, u32[]{:S(2)}) collective-permute-start(bf16[128,2048]{1,0:T(8,128)(2,1)S(1)} %get-tuple-element.52.refs_1_), channel_id=1, source_target_pairs={{0,4},{4,0},{1,5},{5,1},{2,6},{6,2},{3,7},{7,3},{8,12},{12,8},{9,1... | collective-permute-start | bytes 1572872 | tf_op jit(solution)/shard_map/ppermute | solution.py:608
  42.9 9.4 %collective-permute-start.15 = (bf16[128,2048]{1,0:T(8,128)(2,1)}, bf16[128,2048]{1,0:T(8,128)(2,1)S(1)}, u32[]{:S(2)}, u32[]{:S(2)}) collective-permute-start(bf16[128,2048]{1,0:T(8,128)(2,1)} %copy-done.19), channel_id=1, source_target_pairs={{0,4},{4,0},{1,5},{5,1},{2,6},{6,2},{3,7},{7,3},{8,12},{12,8},{9,1... | collective-permute-start | bytes 1572872 | tf_op jit(solution)/shard_map/ppermute | solution.py:608
  42.9 13.5 %collective-permute-start.16 = (bf16[128,2048]{1,0:T(8,128)(2,1)S(1)}, bf16[128,2048]{1,0:T(8,128)(2,1)S(1)}, u32[]{:S(2)}, u32[]{:S(2)}) collective-permute-start(bf16[128,2048]{1,0:T(8,128)(2,1)S(1)} %get-tuple-element.58.refs_3_), channel_id=1, source_target_pairs={{0,4},{4,0},{1,5},{5,1},{2,6},{6,2},{3,7},{7,3},{8,12},{12,8},{9,1... | collective-permute-start | bytes 1572872 | tf_op jit(solution)/shard_map/ppermute | solution.py:608
  43.6 9.5 %collective-permute-start.22 = (bf16[1024,128]{1,0:T(8,128)(2,1)S(1)}, bf16[1024,128]{1,0:T(8,128)(2,1)}, u32[]{:S(2)}, u32[]{:S(2)}) collective-permute-start(bf16[1024,128]{1,0:T(8,128)(2,1)S(1)} %fusion.3), channel_id=1, source_target_pairs={{0,16},{4,12},{8,24},{12,4},{20,28},{28,20},{1,17},{5,13},{9,25},{... | collective-permute-start | bytes 786440 | tf_op jit(solution)/shard_map/ppermute | solution.py:573
  46.6 22.7 %collective-permute-start.10 = (bf16[128,2048]{1,0:T(8,128)(2,1)}, bf16[128,2048]{1,0:T(8,128)(2,1)}, u32[]{:S(2)}, u32[]{:S(2)}) collective-permute-start(bf16[128,2048]{1,0:T(8,128)(2,1)} %broadcast_select_fusion.1.refs_0_), channel_id=1, source_target_pairs={{0,8},{4,20},{8,0},{12,28},{16,24},{20,4},{24,16},{28,12},{1,9},{5... | collective-permute-start | bytes 1572872 | tf_op jit(solution)/shard_map/ppermute | solution.py:614
  48.9 21.0 %collective-permute-start.11 = (bf16[128,2048]{1,0:T(8,128)(2,1)}, bf16[128,2048]{1,0:T(8,128)(2,1)}, u32[]{:S(2)}, u32[]{:S(2)}) collective-permute-start(bf16[128,2048]{1,0:T(8,128)(2,1)} %broadcast_select_fusion.1.refs_0_), channel_id=1, source_target_pairs={{0,16},{4,12},{8,24},{12,4},{16,0},{20,28},{24,8},{28,20},{1,17},{... | collective-permute-start | bytes 1572872 | tf_op jit(solution)/shard_map/ppermute | solution.py:614
  53.1 16.9 %collective-permute-start.9 = (bf16[128,2048]{1,0:T(8,128)(2,1)}, bf16[128,2048]{1,0:T(8,128)(2,1)}, u32[]{:S(2)}, u32[]{:S(2)}) collective-permute-start(bf16[128,2048]{1,0:T(8,128)(2,1)} %get-tuple-element.55.refs_1_), channel_id=1, source_target_pairs={{0,16},{4,12},{8,24},{12,4},{16,0},{20,28},{24,8},{28,20},{1,17},{... | collective-permute-start | bytes 1572872 | tf_op jit(solution)/shard_map/ppermute | solution.py:617
  53.1 17.4 %collective-permute-start.12 = (bf16[128,2048]{1,0:T(8,128)(2,1)}, bf16[128,2048]{1,0:T(8,128)(2,1)}, u32[]{:S(2)}, u32[]{:S(2)}) collective-permute-start(bf16[128,2048]{1,0:T(8,128)(2,1)} %get-tuple-element.56), channel_id=1, source_target_pairs={{1,0},{2,3},{5,4},{6,7},{9,8},{10,11},{13,12},{14,15},{17,16},{18,... | collective-permute-start | bytes 1572872 | tf_op jit(solution)/shard_map/ppermute | solution.py:611
  57.3 14.4 %collective-permute-start.23 = (f32[1024,128]{1,0:T(8,128)S(1)}, f32[1024,128]{1,0:T(8,128)S(1)}, u32[]{:S(2)}, u32[]{:S(2)}) collective-permute-start(f32[1024,128]{1,0:T(8,128)S(1)} %fusion.2), channel_id=1, source_target_pairs={{0,4},{4,0},{1,5},{5,1},{2,6},{6,2},{3,7},{7,3},{8,12},{12,8},{9,1... | collective-permute-start | bytes 1572872 | tf_op jit(solution)/shard_map/ppermute | solution.py:577
  70.0 17.7 %collective-permute-start.26 = (bf16[128,2048]{1,0:T(8,128)(2,1)S(1)}, bf16[128,2048]{1,0:T(8,128)(2,1)S(1)}, u32[]{:S(2)}, u32[]{:S(2)}) collective-permute-start(bf16[128,2048]{1,0:T(8,128)(2,1)S(1)} %copy-done.10), channel_id=1, source_target_pairs={{0,4},{4,0},{1,5},{5,1},{2,6},{6,2},{3,7},{7,3},{8,12},{12,8},{9,1... | collective-permute-start | bytes 1572872 | tf_op jit(solution)/shard_map/ppermute | solution.py:608
  70.5 17.3 %collective-permute-start.27 = (bf16[128,2048]{1,0:T(8,128)(2,1)}, bf16[128,2048]{1,0:T(8,128)(2,1)S(1)}, u32[]{:S(2)}, u32[]{:S(2)}) collective-permute-start(bf16[128,2048]{1,0:T(8,128)(2,1)} %get-tuple-element.70.refs_3_), channel_id=1, source_target_pairs={{0,4},{4,0},{1,5},{5,1},{2,6},{6,2},{3,7},{7,3},{8,12},{12,8},{9,1... | collective-permute-start | bytes 1572872 | tf_op jit(solution)/shard_map/ppermute | solution.py:608
  71.7 22.3 %collective-permute-start.18 = (bf16[128,2048]{1,0:T(8,128)(2,1)S(1)}, bf16[128,2048]{1,0:T(8,128)(2,1)}, u32[]{:S(2)}, u32[]{:S(2)}) collective-permute-start(bf16[128,2048]{1,0:T(8,128)(2,1)S(1)} %broadcast_select_fusion.refs_0_), channel_id=1, source_target_pairs={{0,8},{4,20},{8,0},{12,28},{16,24},{20,4},{24,16},{28,12},{1,9},{5... | collective-permute-start | bytes 1572872 | tf_op jit(solution)/shard_map/ppermute | solution.py:614
  75.1 19.0 %collective-permute-start.19 = (bf16[128,2048]{1,0:T(8,128)(2,1)S(1)}, bf16[128,2048]{1,0:T(8,128)(2,1)S(1)}, u32[]{:S(2)}, u32[]{:S(2)}) collective-permute-start(bf16[128,2048]{1,0:T(8,128)(2,1)S(1)} %broadcast_select_fusion.refs_0_), channel_id=1, source_target_pairs={{0,16},{4,12},{8,24},{12,4},{16,0},{20,28},{24,8},{28,20},{1,17},{... | collective-permute-start | bytes 1572872 | tf_op jit(solution)/shard_map/ppermute | solution.py:614
  75.9 18.3 %collective-permute-start.17 = (bf16[128,2048]{1,0:T(8,128)(2,1)}, bf16[128,2048]{1,0:T(8,128)(2,1)}, u32[]{:S(2)}, u32[]{:S(2)}) collective-permute-start(bf16[128,2048]{1,0:T(8,128)(2,1)} %get-tuple-element.60.refs_1_), channel_id=1, source_target_pairs={{0,16},{4,12},{8,24},{12,4},{16,0},{20,28},{24,8},{28,20},{1,17},{... | collective-permute-start | bytes 1572872 | tf_op jit(solution)/shard_map/ppermute | solution.py:617
  87.7 8.5 %collective-permute-start.28 = (bf16[128,2048]{1,0:T(8,128)(2,1)}, bf16[128,2048]{1,0:T(8,128)(2,1)}, u32[]{:S(2)}, u32[]{:S(2)}) collective-permute-start(bf16[128,2048]{1,0:T(8,128)(2,1)} %broadcast_select_fusion.1.refs_0_), channel_id=1, source_target_pairs={{0,4},{4,0},{1,5},{5,1},{2,6},{6,2},{3,7},{7,3},{8,12},{12,8},{9,1... | collective-permute-start | bytes 1572872 | tf_op jit(solution)/shard_map/ppermute | solution.py:608
  87.8 8.5 %collective-permute-start.29 = (bf16[128,2048]{1,0:T(8,128)(2,1)}, bf16[128,2048]{1,0:T(8,128)(2,1)}, u32[]{:S(2)}, u32[]{:S(2)}) collective-permute-start(bf16[128,2048]{1,0:T(8,128)(2,1)} %get-tuple-element.60.refs_1_), channel_id=1, source_target_pairs={{0,4},{4,0},{1,5},{5,1},{2,6},{6,2},{3,7},{7,3},{8,12},{12,8},{9,1... | collective-permute-start | bytes 1572872 | tf_op jit(solution)/shard_map/ppermute | solution.py:608
  95.4 10.0 %collective-permute-start.32 = (bf16[128,2048]{1,0:T(8,128)(2,1)}, bf16[128,2048]{1,0:T(8,128)(2,1)}, u32[]{:S(2)}, u32[]{:S(2)}) collective-permute-start(bf16[128,2048]{1,0:T(8,128)(2,1)} %get-tuple-element.80.refs_1_), channel_id=1, source_target_pairs={{0,16},{4,12},{8,24},{12,4},{16,0},{20,28},{24,8},{28,20},{1,17},{... | collective-permute-start | bytes 1572872 | tf_op jit(solution)/shard_map/ppermute | solution.py:617
  96.2 9.7 %collective-permute-start.33 = (bf16[128,2048]{1,0:T(8,128)(2,1)}, bf16[128,2048]{1,0:T(8,128)(2,1)}, u32[]{:S(2)}, u32[]{:S(2)}) collective-permute-start(bf16[128,2048]{1,0:T(8,128)(2,1)} %copy-done.6), channel_id=1, source_target_pairs={{0,4},{4,0},{1,5},{5,1},{2,6},{6,2},{3,7},{7,3},{8,12},{12,8},{9,1... | collective-permute-start | bytes 1572872 | tf_op jit(solution)/shard_map/ppermute | solution.py:608
  96.3 9.6 %collective-permute-start.34 = (bf16[128,2048]{1,0:T(8,128)(2,1)}, bf16[128,2048]{1,0:T(8,128)(2,1)}, u32[]{:S(2)}, u32[]{:S(2)}) collective-permute-start(bf16[128,2048]{1,0:T(8,128)(2,1)} %get-tuple-element.80.refs_1_), channel_id=1, source_target_pairs={{0,4},{4,0},{1,5},{5,1},{2,6},{6,2},{3,7},{7,3},{8,12},{12,8},{9,1... | collective-permute-start | bytes 1572872 | tf_op jit(solution)/shard_map/ppermute | solution.py:608
  96.8 9.2 %collective-permute-start.35 = (bf16[128,2048]{1,0:T(8,128)(2,1)}, bf16[128,2048]{1,0:T(8,128)(2,1)}, u32[]{:S(2)}, u32[]{:S(2)}) collective-permute-start(bf16[128,2048]{1,0:T(8,128)(2,1)} %copy-done.3), channel_id=1, source_target_pairs={{0,4},{4,0},{1,5},{5,1},{2,6},{6,2},{3,7},{7,3},{8,12},{12,8},{9,1... | collective-permute-start | bytes 1572872 | tf_op jit(solution)/shard_map/ppermute | solution.py:608
  122.6 11.7 %collective-permute-start.38 = (bf16[1024,128]{1,0:T(8,128)(2,1)}, bf16[1024,128]{1,0:T(8,128)(2,1)S(1)}, u32[]{:S(2)}, u32[]{:S(2)}) collective-permute-start(bf16[1024,128]{1,0:T(8,128)(2,1)} %fusion.9), channel_id=1, source_target_pairs={{0,8},{8,0},{16,24},{20,4},{24,16},{28,12},{1,9},{9,1},{17,25},{21... | collective-permute-start | bytes 786440 | tf_op jit(solution)/shard_map/ppermute | solution.py:555
  134.4 10.0 %collective-permute-start.39 = (bf16[1024,128]{1,0:T(8,128)(2,1)S(1)}, bf16[1024,128]{1,0:T(8,128)(2,1)S(1)}, u32[]{:S(2)}, u32[]{:S(2)}) collective-permute-start(bf16[1024,128]{1,0:T(8,128)(2,1)S(1)} %join.12), channel_id=1, source_target_pairs={{4,12},{12,4},{16,0},{20,28},{24,8},{28,20},{5,13},{13,5},{17,1},{... | collective-permute-start | bytes 786440 | tf_op jit(solution)/shard_map/ppermute | solution.py:573
  (72 other events, 270.5 us)

commit v5 on v4

--- a/solution.py
+++ b/solution.py
@@ -14,7 +14,7 @@
 CTX = ("chip", "core")
 SWAP = [(0, 1), (1, 0)]
 f32, bf16 = jnp.float32, jnp.bfloat16
-VMEM_LIMIT = 26 * 1024 * 1024
+VMEM_LIMIT = 18 * 1024 * 1024
 
 
 def nn(a, b):
@@ -88,6 +88,28 @@
         return copy
 
 
+def crossed(side):
+    return (0, 1 + side, 2 - side, 3)
+
+
+def all_places(special, number):
+    if not special:
+        return list(range(number))
+    chip, core, layer = (lax.axis_index(name) for name in ("chip", "core", "dp"))
+    upper = layer < 2
+    layers = [layer, layer ^ 1, jnp.where(upper, 2, 1), jnp.where(upper, 3, 0)]
+    return [
+        ((chip ^ flip) * 2 + side) * 4 + one
+        for one in layers
+        for side in (core, 1 - core)
+        for flip in crossed(side)
+    ]
+
+
+def piece_columns(place):
+    return (slice(None), pl.ds(pl.multiple_of(place * PIECE, PIECE), PIECE))
+
+
 def columns(at, wide=None):
     return (slice(None), pl.ds(at, wide or WIDE))
 
@@ -103,16 +125,21 @@
 
 
 def memory_kernel(
-    key_ref, spike_ref, value_ref, keys_ref, mask_ref, values_ref, own_ref, sent_ref, mark_ref,
+    special, key_ref, spike_ref, value_ref, tokens_ref,
+    keys_ref, mask_ref, values_ref, own_ref, sent_ref, some_ref,
     key_in, spike_in, sems,
 ):
-    set_mark(mark_ref)
     copies = Copies(sems)
     wide = range(0, keys_ref.shape[1], WIDE)
     pairs = ((key_ref, key_in), (spike_ref, spike_in), (value_ref, values_ref))
     parts = [
         [copies.start(here.at[columns(at)], there.at[columns(at)]) for here, there in pairs]
         for at in wide
+    ]
+    places = all_places(special, some_ref.shape[1] // PIECE)
+    ordered = [
+        copies.start(tokens_ref.at[piece_columns(place)], some_ref.at[piece_columns(piece)])
+        for piece, place in enumerate(places)
     ]
     for at, part in zip(wide, parts):
         for copy in part:
@@ -127,23 +154,25 @@
             own = tn(keys[:, head : head + HEAD], values_ref[:, here])
             own_ref[here, :] = own
             sent_ref[here, :] = own.astype(bf16)
-
-
-def memory_call(key_input, k_spikes, values):
+    for copy in ordered:
+        copy.wait()
+
+
+def memory_call(special, key_input, k_spikes, values, tokens):
     length, total = values.shape
     block, state = (length, total), (total, HEAD)
     return kernel_call(
-        memory_kernel,
-        "HHH",
-        (key_input, k_spikes, values),
+        functools.partial(memory_kernel, special),
+        "HHHH",
+        (key_input, k_spikes, values, tokens),
         "VVVVVV",
-        [(block, bf16)] * 3 + [(state, f32), (state, bf16), (MARK.shape, f32)],
+        [(block, bf16)] * 3 + [(state, f32), (state, bf16), (tokens.shape, bf16)],
         "own_memory",
         (2 * length * total * HEAD, 12 * length * total),
         [
             pltpu.VMEM(block, bf16),
             pltpu.VMEM(block, jnp.int32),
-            pltpu.SemaphoreType.DMA((3 * total // WIDE,)),
+            pltpu.SemaphoreType.DMA((3 * total // WIDE + tokens.shape[1] // PIECE,)),
         ],
     )
 
@@ -257,19 +286,7 @@
             at += 1
 
 
-def load_tokens(copies, places_ref, tokens_ref, some_ref):
-    bring = []
-    for piece in range(some_ref.shape[1] // PIECE):
-        place = pl.multiple_of(places_ref[piece] * PIECE, PIECE)
-        bring.append(
-            copies.start(
-                tokens_ref.at[:, pl.ds(place, PIECE)], some_ref.at[:, pl.ds(piece * PIECE, PIECE)]
-            )
-        )
-    return bring
-
-
-def back_part(copies, places_ref, masked, blocks, out_ref, round_ref):
+def back_part(copies, places, masked, blocks, out_ref, round_ref):
     going = []
     pieces = list(back_blocks(blocks))
     for (first, upper), (second, lower) in zip(pieces[::2], pieces[1::2]):
@@ -277,18 +294,17 @@
         made = nt(masked[...], jnp.concatenate([upper, lower], axis=0))
         round_ref[:, both] = made.astype(bf16)
         for piece in (first, second):
-            place = pl.multiple_of(places_ref[piece] * PIECE, PIECE)
             going.append(
                 copies.start(
-                    round_ref.at[:, pl.ds(piece * PIECE, PIECE)],
-                    out_ref.at[:, pl.ds(place, PIECE)],
+                    round_ref.at[piece_columns(piece)], out_ref.at[piece_columns(places[piece])]
                 )
             )
     return going
 
 
-def products_kernel(size, project, back, has_sum, has_back, places_ref, *refs):
+def products_kernel(special, start, size, project, back, has_sum, has_back, *refs):
     blocks, refs = refs[:size], list(refs[size:])
+    depth = rows_of(blocks)
     tokens_ref = refs.pop(0) if project else None
     before_ref = refs.pop(0) if has_sum else None
     masked = refs.pop(0) if back else None
@@ -297,21 +313,20 @@
     sum_ref = refs.pop(0) if project else None
     back_out = refs.pop(0) if back else None
     mark_ref = refs.pop(0)
-    sems = refs.pop()
     set_mark(mark_ref)
-    copies = Copies(sems)
     going = []
+    if back:
+        round_ref, sems = refs
+        places = all_places(special, back_out.shape[1] // PIECE)[start:]
+        going = back_part(Copies(sems), places, masked, blocks, back_out, round_ref)
     if project:
-        some_ref = refs.pop(0)
-        bring = load_tokens(copies, places_ref, tokens_ref, some_ref)
-    if back:
-        going = back_part(copies, places_ref, masked, blocks, back_out, refs.pop(0))
-    if project:
-        for copy in bring:
-            copy.wait()
+        cols = slice(start * PIECE, start * PIECE + depth)
         for at in range(0, sum_ref.shape[1], WIDE):
             part = slice(at, at + WIDE)
-            made = nn(some_ref[...], jnp.concatenate([block[:, part] for block in blocks], axis=0))
+            made = nn(
+                tokens_ref[:, cols],
+                jnp.concatenate([block[:, part] for block in blocks], axis=0),
+            )
             if has_sum:
                 made = made + before_ref[:, part]
             sum_ref[:, part] = made
@@ -319,32 +334,35 @@
         copy.wait()
 
 
-def products_call(places, blocks, tokens, partial=None, masked=None, grad=None, project=True):
+def products_call(
+    special, start, blocks, tokens, partial=None, masked=None, grad=None, project=True
+):
     length, width = tokens.shape
     total = blocks[0].shape[1]
     depth = rows_of(blocks)
-    number = depth // PIECE
     back = masked is not None
-    places_in, args = "S" + "V" * len(blocks), [places, *blocks]
+    places_in, args = "V" * len(blocks), list(blocks)
     places_out, outs = "", []
     scratch, aliases = [], {}
     if project:
-        places_in, args = places_in + "H", args + [tokens]
+        places_in, args = places_in + "V", args + [tokens]
         if partial is not None:
             aliases[len(args)] = 0
             places_in, args = places_in + "V", args + [partial]
         places_out, outs = "V", [((length, total), f32)]
-        scratch.append(pltpu.VMEM((length, depth), bf16))
     if back:
         places_in, args = places_in + "V", args + [masked]
         if grad is not None:
             aliases[len(args)] = len(outs)
             places_in, args = places_in + "H", args + [grad]
         places_out, outs = places_out + "H", outs + [((length, width), bf16)]
-        scratch.append(pltpu.VMEM((length, depth), bf16))
+        scratch = [
+            pltpu.VMEM((length, depth), bf16), pltpu.SemaphoreType.DMA((depth // PIECE,))
+        ]
     made = kernel_call(
         functools.partial(
-            products_kernel, len(blocks), project, back, partial is not None, grad is not None
+            products_kernel, special, start, len(blocks), project, back,
+            partial is not None, grad is not None,
         ),
         places_in,
         args,
@@ -352,7 +370,7 @@
         outs + [(MARK.shape, f32)],
         "products" if project and back else "project" if project else "grad_tokens",
         (2 * (project + back) * length * depth * total, 0),
-        scratch + [pltpu.SemaphoreType.DMA((2 * number,))],
+        scratch,
         aliases,
     )
     made = list(made)
@@ -361,16 +379,15 @@
     return partial, grad, made[0]
 
 
-def query_kernel(size, places_ref, tokens_ref, sum_ref, mask_ref, grad_ref, *refs):
+def query_kernel(start, size, tokens_ref, sum_ref, mask_ref, grad_ref, *refs):
     blocks = refs[:size]
-    queries, own_ref, sent_ref, some_ref, sems = refs[size:]
-    copies = Copies(sems)
-    bring = load_tokens(copies, places_ref, tokens_ref, some_ref)
-    for copy in bring:
-        copy.wait()
+    queries, own_ref, sent_ref = refs[size:]
+    cols = slice(start * PIECE, start * PIECE + rows_of(blocks))
     for at in range(0, queries.shape[1], WIDE):
         part = slice(at, at + WIDE)
-        made = nn(some_ref[...], jnp.concatenate([block[:, part] for block in blocks], axis=0))
+        made = nn(
+            tokens_ref[:, cols], jnp.concatenate([block[:, part] for block in blocks], axis=0)
+        )
         made = made + sum_ref[:, part]
         made = (made * mask_ref[:, part].astype(f32)).astype(bf16)
         queries[:, part] = made
@@ -381,20 +398,18 @@
             sent_ref[here, :] = own.astype(bf16)
 
 
-def query_call(places, tokens, blocks, before, q_mask, cotangent):
+def query_call(start, tokens, blocks, before, q_mask, cotangent):
     length = tokens.shape[0]
     total = blocks[0].shape[1]
     depth = rows_of(blocks)
-    number = depth // PIECE
     return kernel_call(
-        functools.partial(query_kernel, len(blocks)),
-        "SHVVV" + "V" * len(blocks),
-        (places, tokens, before, q_mask, cotangent, *blocks),
+        functools.partial(query_kernel, start, len(blocks)),
+        "VVVV" + "V" * len(blocks),
+        (tokens, before, q_mask, cotangent, *blocks),
         "VVV",
         [((length, total), bf16), ((total, HEAD), f32), ((total, HEAD), bf16)],
         "queries",
         (2 * length * depth * total, 0),
-        [pltpu.VMEM((length, depth), bf16), pltpu.SemaphoreType.DMA((number,))],
     )
 
 
@@ -545,19 +560,6 @@
     return pairs
 
 
-def scan_first(own, sent, reverse):
-    chip, core = lax.axis_index("chip"), lax.axis_index("core")
-    low_bit = 1 - chip % 2 if reverse else chip % 2
-    half = own.shape[0] // 2
-    sibling = lax.ppermute(sent, "core", SWAP)
-    both = own + sibling.astype(f32)
-    both = jnp.where(core == 0, both[:half], both[half:])
-    got = lax.ppermute(both.astype(bf16), CTX, links(1, upward(reverse))).astype(f32)
-    first = jnp.where((core == 1) | (low_bit == 1), got, 0.0)
-    message = (got + jnp.where((core == 0) | (low_bit == 0), both, 0.0)).astype(bf16)
-    return message, first, sibling
-
-
 def upward(reverse):
     flip = 3 if reverse else 0
 
@@ -568,28 +570,120 @@
     return keep
 
 
-def scan_second(message, first, sibling, reverse, others=()):
+def half_rows(array_ref, core):
+    half = array_ref.shape[0] // 2
+    return array_ref[pl.ds(pl.multiple_of(core * half, half), half), :]
+
+
+def both_kernel(own_ref, sibling_ref, both_ref, sent_ref):
     core = lax.axis_index("core")
-    more = lax.ppermute(message, CTX, links(2, upward(reverse))).astype(f32)
-    state = first + more
-    if others:
-        state, = join([state], others)
+    both = half_rows(own_ref, core) + half_rows(sibling_ref, core).astype(f32)
+    both_ref[...] = both
+    sent_ref[...] = both.astype(bf16)
+
+
+def low_bit(reverse):
+    chip = lax.axis_index("chip")
+    return 1 - chip % 2 if reverse else chip % 2
+
+
+def message_kernel(reverse, got_ref, both_ref, *refs):
+    core = lax.axis_index("core")
+    adds = jnp.where((core == 0) | (low_bit(reverse) == 0), 1.0, 0.0)
+    refs[-1][...] = (got_ref[...].astype(f32) + adds * both_ref[...]).astype(bf16)
+
+
+def state_kernel(reverse, got_ref, more_ref, *refs):
+    core = lax.axis_index("core")
+    adds = jnp.where((core == 1) | (low_bit(reverse) == 1), 1.0, 0.0)
+    refs[-1][...] = adds * got_ref[...].astype(f32) + more_ref[...].astype(f32)
+
+
+def whole_kernel(reverse, state_ref, other_ref, sibling_ref, high_ref, low_ref):
+    core = lax.axis_index("core")
+    adds = jnp.where(core == (0 if reverse else 1), 1.0, 0.0)
+    half = state_ref.shape[0]
+    for ref, side in ((state_ref, core), (other_ref, 1 - core)):
+        rows = pl.ds(pl.multiple_of(side * half, half), half)
+        whole = ref[...] + adds * sibling_ref[rows, :].astype(f32)
+        high = whole.astype(bf16)
+        high_ref[rows, :] = high
+        low_ref[rows, :] = (whole - high.astype(f32)).astype(bf16)
+
+
+def scan_first(own, sent, reverse, others=()):
+    rows = own.shape[0]
+    half = (rows // 2, HEAD)
+    sibling = lax.ppermute(sent, "core", SWAP)
+    both, sent = kernel_call(
+        both_kernel, "VV", (own, sibling), "VV", [(half, f32), (half, bf16)], "both", (0, 0)
+    )
+    got = lax.ppermute(sent, CTX, links(1, upward(reverse)))
+    (message,) = kernel_call(
+        functools.partial(message_kernel, reverse),
+        "VV" + "A" * len(others),
+        (got, both, *others),
+        "V",
+        [(half, bf16)],
+        "message",
+        (0, 0),
+    )
+    return message, got, sibling
+
+
+def scan_second(message, got, sibling, reverse, others=()):
+    half, full = message.shape, sibling.shape
+    more = lax.ppermute(message, CTX, links(2, upward(reverse)))
+    (state,) = kernel_call(
+        functools.partial(state_kernel, reverse),
+        "VV" + "A" * len(others),
+        (got, more, *others),
+        "V",
+        [(half, f32)],
+        "state",
+        (0, 0),
+    )
     other = lax.ppermute(state, "core", SWAP)
-    whole = jnp.concatenate(
-        [jnp.where(core == 0, state, other), jnp.where(core == 0, other, state)], axis=0
-    )
-    return halves(whole + jnp.where(core == (0 if reverse else 1), sibling.astype(f32), 0.0))
+    return kernel_call(
+        functools.partial(whole_kernel, reverse),
+        "VVV",
+        (state, other, sibling),
+        "VV",
+        [(full, bf16)] * 2,
+        "whole",
+        (0, 0),
+    )
 
 
 def gather_any(q_weight):
     whole = lax.all_gather(q_weight, ("chip", "core", "dp"), axis=0, tiled=True)
     cut = whole.shape[0] // (2 * PIECE) * PIECE
-    number = whole.shape[0] // PIECE
-    return [whole[:cut], whole[cut:]], jnp.arange(number, dtype=jnp.int32)
-
-
-def crossed(side):
-    return (0, 1 + side, 2 - side, 3)
+    return [whole[:cut], whole[cut:]]
+
+
+def choose_kernel(inner_ref, end_ref, out_ref, sem):
+    del end_ref
+    layer = lax.axis_index("dp")
+
+    @pl.when((layer == 1) | (layer == 2))
+    def _():
+        copy = pltpu.make_async_copy(inner_ref, out_ref, sem)
+        copy.start()
+        copy.wait()
+
+
+def choose(inner, end):
+    return kernel_call(
+        choose_kernel,
+        "AA",
+        (fast(inner), fast(end)),
+        "A",
+        [(inner.shape, inner.dtype)],
+        "choose",
+        (0, 0),
+        [pltpu.SemaphoreType.DMA],
+        {1: 0},
+    )[0]
 
 
 def per_device(tokens, key_input, values, q_weight, q_spikes, k_spikes, cotangent):
@@ -616,10 +710,10 @@
     def onward(array):
         return lax.ppermute(array, CTX, links(2))
 
-    keys, k_mask, values, own, sent, own_mark = memory_call(key_input, k_spikes, values)
+    keys, k_mask, values, own, sent, tokens = memory_call(
+        special, key_input, k_spikes, values, tokens
+    )
     if special:
-        chip, core, layer = (lax.axis_index(name) for name in ("chip", "core", "dp"))
-        within = (layer == 1) | (layer == 2)
         ends = [(0, 1), (1, 0), (2, 3), (3, 2)]
         middle = [(1, 2), (2, 1)]
         outward = [(1, 0), (2, 3)]
@@ -630,23 +724,10 @@
         near, mid, first_0, second_0, sent = join([near, mid, first_0, second_0, sent])
         message, *rest = scan_first(own, sent, False)
     else:
-        arrived, places = gather_any(q_weight)
+        arrived = gather_any(q_weight)
         high, low = halves(scan_any(own, sent, chips * 2, False))
 
     if special:
-
-        def numbers(sides, layers):
-            return jnp.stack(
-                [
-                    ((chip ^ flip) * 2 + side) * spread + one
-                    for one in layers
-                    for side in sides
-                    for flip in crossed(side)
-                ]
-            ).astype(jnp.int32)
-
-        sides = (core, 1 - core)
-        levels = [layer, layer ^ 1, jnp.where(layer < 2, 2, 1), jnp.where(layer < 2, 3, 0)]
         third_0 = onward(first_0)
         first_1, second_1 = cross(near)
         far = along(near, middle)
@@ -655,18 +736,17 @@
             [third_0, first_1, second_1, far, mid_out]
         )
         third_1 = onward(first_1)
-        next_layer = jnp.where(within, mid, mid_out)
+        next_layer = choose(mid, mid_out)
         first_2, second_2 = cross(next_layer)
         far_out = along(far, outward)
         own_blocks = [q_weight, first_0, second_0, third_0, other_0]
         own_blocks += [sibling(one) for one in own_blocks[1:4]]
-        own_places = numbers(sides, levels[:1])
-        partial, _, own_mark = products_call(own_places, own_blocks, tokens)
+        partial, _, own_mark = products_call(special, 0, own_blocks, tokens)
         third_1, first_2, second_2, far_out = join(
             [third_1, first_2, second_2, far_out], [own_mark]
         )
         third_2 = onward(first_2)
-        last_layer = jnp.where(within, far, far_out)
+        last_layer = choose(far, far_out)
         first_3, second_3 = cross(last_layer)
 
         def whole(*mine):
@@ -677,39 +757,38 @@
             factor, cotangent, q_spikes, values, keys, high, low
         )
         _, grad, mark_0 = products_call(
-            own_places, own_blocks, tokens, masked=masked, project=False
+            special, 0, own_blocks, tokens, masked=masked, project=False
         )
         blocks = whole(near, first_1, second_1, third_1)
         partial, grad, mark_1 = products_call(
-            numbers(sides, levels[1:2]), blocks, tokens, partial, masked, grad
+            special, 8, blocks, tokens, partial, masked, grad
         )
         third_2, first_3, second_3 = join([third_2, first_3, second_3], [mark_0, mark_1])
         third_3 = onward(first_3)
         blocks = whole(next_layer, first_2, second_2, third_2)
         partial, grad, mark = products_call(
-            numbers(sides, levels[2:3]), blocks, tokens, partial, masked, grad
+            special, 16, blocks, tokens, partial, masked, grad
         )
         third_3, = join([third_3], [mark])
         late = whole(last_layer, first_3, second_3, third_3)
-        late_places = numbers(sides, levels[3:])
+        start = 24
     else:
         masked, q_mask, cotangent, _ = masked_call(
             factor, cotangent, q_spikes, values, keys, high, low
         )
-        half = places.shape[0] // 2
-        partial, grad, _ = products_call(places[:half], arrived[:1], tokens, masked=masked)
-        late, late_places = arrived[1:], places[half:]
-    queries, own, sent = query_call(late_places, tokens, late, partial, q_mask, cotangent)
+        start = arrived[0].shape[0] // PIECE
+        partial, grad, _ = products_call(special, 0, arrived[:1], tokens, masked=masked)
+        late = arrived[1:]
+    queries, own, sent = query_call(start, tokens, late, partial, q_mask, cotangent)
     attended, attended_mark = attend_call(factor, queries, keys, values, high, low)
     key_part, value_part, inner_mark = inner_call(queries, keys, values, cotangent)
     if special:
-        message, *rest = scan_first(own, sent, True)
-        message, = join([message], [attended_mark])
+        message, *rest = scan_first(own, sent, True, [attended_mark])
         adjoint = scan_second(message, *rest, True, [inner_mark])
     else:
         adjoint = halves(scan_any(own, sent, chips * 2, True))
     _, grad_tokens, _ = products_call(
-        late_places, late, tokens, masked=masked, grad=grad, project=False
+        special, start, late, tokens, masked=masked, grad=grad, project=False
     )
     grad_keys, grad_values = outer_call(
         factor, key_part, value_part, keys, values, k_mask, *adjoint

time: 158 us -> 136 us (0.86)
  the two profiles are of different devices: /device:TPU:12 before, /device:TPU:1 now
where the time goes in v5:
time: 136 us; the launch traced here: 135 us
  waiting for transfers between devices  50.9 us (37%)
  Pallas kernels  45.4 us (33%)
  starting transfers between devices  37.5 us (28%)
    pallas_call x26, Pallas kernels, kernel_call(): made(*[holds[place](one) if place in holds else one for place, one in zip...  45.4 us
    ppermute x5, waiting for transfers between devices, along(): return lax.ppermute(array, 'dp', pairs)  14.3 us
    ppermute x2, waiting for transfers between devices, scan_second(): more = lax.ppermute(message, CTX, links(2, upward(reverse)))  11.2 us
    ppermute x16, starting transfers between devices, sibling(): return lax.ppermute(array, 'core', SWAP)  9.59 us
    ppermute x4, waiting for transfers between devices, onward(): return lax.ppermute(array, CTX, links(2))  9.2 us
    ppermute x4, waiting for transfers between devices, cross(): lax.ppermute(array, CTX, links(1))  8.2 us
    ppermute x5, starting transfers between devices, along(): return lax.ppermute(array, 'dp', pairs)  6.12 us
    ppermute x4, starting transfers between devices, cross(): lax.ppermute(array, CTX, links(1))  5.1 us
  transfers between devices with their start and end apart: 41, of which 13 were waited for; matrix products, arithmetic and copies ran while one was open for 0% of the time, Pallas kernels for 28%

profile of v5, /device:TPU:1, one launch (start us, length us, event | category | flops | bytes accessed | tf_op | source)
XLA Modules:
  0.0 135.0 jit_solution(4785553965668744219)
XLA Ops:
  0.6 2.2 %collective-permute-start = (bf16[128,2048]{1,0:T(8,128)(2,1)}, bf16[128,2048]{1,0:T(8,128)(2,1)S(1)}, u32[]{:S(2)}, u32[]{:S(2)}) collective-permute-start(bf16[128,2048]{1,0:T(8,128)(2,1)} %refs_0_.3), channel_id=1, source_target_pairs={{0,1},{1,0},{2,3},{3,2},{4,5},{5,4},{6,7},{7,6},{8,9},{9,8},{10,11... | collective-permute-start | bytes 1572872 | tf_op jit(solution)/shard_map/ppermute | solution.py:705
  3.5 1.3 collective-permute-start.2
  6.0 4.2 %own_memory.1 = (bf16[384,2048]{1,0:T(8,128)(2,1)S(1)}, bf16[384,2048]{1,0:T(8,128)(2,1)S(1)}, bf16[384,2048]{1,0:T(8,128)(2,1)S(1)}, f32[2048,128]{1,0:T(8,128)...) custom-call(bf16[384,2048]{1,0:T(8,128)(2,1)} %bitcast.13, s32[384,2048]{1,0:T(8,128)} %bitcast.11, ...), custom_call_target="tpu_custom_call" | custom-call | flops 201326592 | bytes 9437184 | tf_op jit(solution)/shard_map/own_memory/pallas_call | solution.py:74
  10.3 4.4 %collective-permute-done.refs_0_ = bf16[128,2048]{1,0:T(8,128)(2,1)S(1)} collective-permute-done((bf16[128,2048]{1,0:T(8,128)(2,1)}, bf16[128,2048]{1,0:T(8,128)(2,1)S(1)}, u32[]{:S(2)}, u32[]{:S(2)}) %collective-permute-start) | collective-permute-done | bytes 524320 | tf_op jit(solution)/shard_map/ppermute | solution.py:705
  14.8 4.0 %collective-permute-done.3.refs_3_ = bf16[128,2048]{1,0:T(8,128)(2,1)S(1)} collective-permute-done((bf16[128,2048]{1,0:T(8,128)(2,1)}, bf16[128,2048]{1,0:T(8,128)(2,1)S(1)}, u32[]{:S(2)}, u32[]{:S(2)}) %collective-permute-start.3) | collective-permute-done | bytes 524320 | tf_op jit(solution)/shard_map/ppermute | solution.py:708
  23.1 8.1 %collective-permute-done.5.refs_1_ = bf16[128,2048]{1,0:T(8,128)(2,1)S(1)} collective-permute-done((bf16[128,2048]{1,0:T(8,128)(2,1)S(1)}, bf16[128,2048]{1,0:T(8,128)(2,1)S(1)}, u32[]{:S(2)}, u32[]{:S(2)}) %collective-permute-start.5) | collective-permute-done | bytes 524320 | tf_op jit(solution)/shard_map/ppermute | solution.py:708
  31.2 3.0 %collective-permute-start.13 = (bf16[128,2048]{1,0:T(8,128)(2,1)S(1)}, bf16[128,2048]{1,0:T(8,128)(2,1)S(1)}, u32[]{:S(2)}, u32[]{:S(2)}) collective-permute-start(bf16[128,2048]{1,0:T(8,128)(2,1)S(1)} %copy-done), channel_id=1, source_target_pairs={{0,4},{4,0},{1,5},{5,1},{2,6},{6,2},{3,7},{7,3},{8,12},{12,8},{9,1... | collective-permute-start | bytes 1572872 | tf_op jit(solution)/shard_map/ppermute | solution.py:702
  34.4 1.7 %collective-permute-start.21 = (bf16[1024,128]{1,0:T(8,128)(2,1)S(1)}, bf16[1024,128]{1,0:T(8,128)(2,1)S(1)}, u32[]{:S(2)}, u32[]{:S(2)}) collective-permute-start(bf16[1024,128]{1,0:T(8,128)(2,1)S(1)} %get-tuple-element.77), channel_id=1, source_target_pairs={{0,8},{4,20},{8,0},{12,28},{16,24},{24,16},{1,9},{5,21},{9,1},{13,... | collective-permute-start | bytes 786440 | tf_op jit(solution)/shard_map/ppermute | solution.py:621
  36.1 3.1 %collective-permute-done.4.refs_0_ = bf16[128,2048]{1,0:T(8,128)(2,1)S(1)} collective-permute-done((bf16[128,2048]{1,0:T(8,128)(2,1)S(1)}, bf16[128,2048]{1,0:T(8,128)(2,1)S(1)}, u32[]{:S(2)}, u32[]{:S(2)}) %collective-permute-start.4) | collective-permute-done | bytes 524320 | tf_op jit(solution)/shard_map/ppermute | solution.py:711
  39.3 1.7 %collective-permute-start.16 = (bf16[128,2048]{1,0:T(8,128)(2,1)S(1)}, bf16[128,2048]{1,0:T(8,128)(2,1)S(1)}, u32[]{:S(2)}, u32[]{:S(2)}) collective-permute-start(bf16[128,2048]{1,0:T(8,128)(2,1)S(1)} %get-tuple-element.68.refs_3_), channel_id=1, source_target_pairs={{0,4},{4,0},{1,5},{5,1},{2,6},{6,2},{3,7},{7,3},{8,12},{12,8},{9,1... | collective-permute-start | bytes 1572872 | tf_op jit(solution)/shard_map/ppermute | solution.py:702
  41.0 1.3 collective-permute-start.10
  43.6 2.2 %collective-permute-start.22 = (bf16[1024,128]{1,0:T(8,128)(2,1)S(1)}, bf16[1024,128]{1,0:T(8,128)(2,1)S(1)}, u32[]{:S(2)}, u32[]{:S(2)}) collective-permute-start(bf16[1024,128]{1,0:T(8,128)(2,1)S(1)} %message.2), channel_id=1, source_target_pairs={{0,16},{4,12},{8,24},{12,4},{20,28},{28,20},{1,17},{5,13},{9,25},{... | collective-permute-start | bytes 786440 | tf_op jit(solution)/shard_map/ppermute | solution.py:636
  47.1 11.2 %collective-permute-done.22.more_ref = bf16[1024,128]{1,0:T(8,128)(2,1)S(1)} collective-permute-done((bf16[1024,128]{1,0:T(8,128)(2,1)S(1)}, bf16[1024,128]{1,0:T(8,128)(2,1)S(1)}, u32[]{:S(2)}, u32[]{:S(2)}) %collective-permute-start.22) | collective-permute-done | bytes 262176 | tf_op jit(solution)/shard_map/ppermute | solution.py:636
  60.4 1.8 %project.1 = (f32[384,2048]{1,0:T(8,128)S(1)}, f32[8,128]{1,0:T(8,128)S(1)}) custom-call(bf16[128,2048]{1,0:T(8,128)(2,1)S(1)} %copy-done, bf16[128,2048]{1,0:T(8,128)(2,1)S(1)} %get-tuple-element.62.refs_1_, bf16[128,2048]{1,0:T(8,128)(2,1)S(1)} %get-tuple-element.67.refs_2_, bf16[128,2048]{1,0:T(8,128)(2,1)S(1)} %get-tuple-element.68.refs_3_, ...), custom_call_target="tpu_custom_call" | custom-call | flops 1610612736 | tf_op jit(solution)/shard_map/project/pallas_call | solution.py:74
  62.2 1.7 %collective-permute-done.9.refs_0_ = bf16[128,2048]{1,0:T(8,128)(2,1)S(1)} collective-permute-done((bf16[128,2048]{1,0:T(8,128)(2,1)S(1)}, bf16[128,2048]{1,0:T(8,128)(2,1)S(1)}, u32[]{:S(2)}, u32[]{:S(2)}) %collective-permute-start.9) | collective-permute-done | bytes 524320 | tf_op jit(solution)/shard_map/ppermute | solution.py:711
  63.9 9.9 %collective-permute-done.12.refs_3_ = bf16[128,2048]{1,0:T(8,128)(2,1)S(1)} collective-permute-done((bf16[128,2048]{1,0:T(8,128)(2,1)S(1)}, bf16[128,2048]{1,0:T(8,128)(2,1)S(1)}, u32[]{:S(2)}, u32[]{:S(2)}) %collective-permute-start.12) | collective-permute-done | bytes 524320 | tf_op jit(solution)/shard_map/ppermute | solution.py:705
  73.9 2.3 %collective-permute-start.18 = (bf16[128,2048]{1,0:T(8,128)(2,1)S(1)}, bf16[128,2048]{1,0:T(8,128)(2,1)S(1)}, u32[]{:S(2)}, u32[]{:S(2)}) collective-permute-start(bf16[128,2048]{1,0:T(8,128)(2,1)S(1)} %choose.3.refs_0_), channel_id=1, source_target_pairs={{0,8},{4,20},{8,0},{12,28},{16,24},{20,4},{24,16},{28,12},{1,9},{5... | collective-permute-start | bytes 1572872 | tf_op jit(solution)/shard_map/ppermute | solution.py:708
  77.9 5.7 %masked_grad.1 = (bf16[384,2048]{1,0:T(8,128)(2,1)S(1)}, bf16[384,2048]{1,0:T(8,128)(2,1)S(1)}, bf16[384,2048]{1,0:T(8,128)(2,1)S(1)}, f32[8,128]{1,0:T(8,128)}) custom-call(bf16[384,2048]{1,0:T(8,128)(2,1)} %bitcast.16, s32[384,2048]{1,0:T(8,128)} %bitcast.15, bf16[384,2048]{1,0:T(8,128)(2,1)S(1)} %get-tuple-element.73.value_ref, ...), custom_call_target="tpu_custom_call" | custom-call | flops 2415919104 | bytes 9437184 | tf_op jit(solution)/shard_map/masked_grad/pallas_call | solution.py:74
  83.6 2.7 %grad_tokens.2 = (bf16[384,4096]{1,0:T(8,128)(2,1)}, f32[8,128]{1,0:T(8,128)S(1)}) custom-call(bf16[128,2048]{1,0:T(8,128)(2,1)S(1)} %copy-done, bf16[128,2048]{1,0:T(8,128)(2,1)S(1)} %get-tuple-element.62.refs_1_, bf16[128,2048]{1,0:T(8,128)(2,1)S(1)} %get-tuple-element.67.refs_2_, bf16[128,2048]{1,0:T(8,128)(2,1)S(1)} %get-tuple-element.68.refs_3_, ...), custom_call_target="tpu_custom_call" | custom-call | flops 1610612736 | tf_op jit(solution)/shard_map/grad_tokens/pallas_call | solution.py:74
  86.9 4.2 %products.2 = (f32[384,2048]{1,0:T(8,128)S(1)}, bf16[384,4096]{1,0:T(8,128)(2,1)}, f32[8,128]{1,0:T(8,128)S(1)}) custom-call(bf16[128,2048]{1,0:T(8,128)(2,1)S(1)} %get-tuple-element.63.refs_0_, bf16[128,2048]{1,0:T(8,128)(2,1)S(1)} %get-tuple-element.65.refs_1_, ...), custom_call_target="tpu_custom_call", output_to_operand_aliasing={{0}: (9, {}), {1}: (11, {})} | custom-call | flops 3221225472 | tf_op jit(solution)/shard_map/products/pallas_call | solution.py:74
  91.6 2.7 %collective-permute-done.17.refs_0_ = bf16[128,2048]{1,0:T(8,128)(2,1)S(1)} collective-permute-done((bf16[128,2048]{1,0:T(8,128)(2,1)S(1)}, bf16[128,2048]{1,0:T(8,128)(2,1)S(1)}, u32[]{:S(2)}, u32[]{:S(2)}) %collective-permute-start.17) | collective-permute-done | bytes 524320 | tf_op jit(solution)/shard_map/ppermute | solution.py:711
  97.1 4.1 %products.3 = (f32[384,2048]{1,0:T(8,128)S(1)}, bf16[384,4096]{1,0:T(8,128)(2,1)}, f32[8,128]{1,0:T(8,128)S(1)}) custom-call(bf16[128,2048]{1,0:T(8,128)(2,1)S(1)} %choose.2.refs_0_, bf16[128,2048]{1,0:T(8,128)(2,1)S(1)} %get-tuple-element.70.refs_1_, ...), custom_call_target="tpu_custom_call", output_to_operand_aliasing={{0}: (9, {}), {1}: (11, {})} | custom-call | flops 3221225472 | tf_op jit(solution)/shard_map/products/pallas_call | solution.py:74
  101.2 1.7 %collective-permute-done.32.refs_0_ = bf16[128,2048]{1,0:T(8,128)(2,1)S(1)} collective-permute-done((bf16[128,2048]{1,0:T(8,128)(2,1)S(1)}, bf16[128,2048]{1,0:T(8,128)(2,1)S(1)}, u32[]{:S(2)}, u32[]{:S(2)}) %collective-permute-start.32) | collective-permute-done | bytes 524320 | tf_op jit(solution)/shard_map/ppermute | solution.py:711
  104.0 1.5 %collective-permute-done.36.refs_7_ = bf16[128,2048]{1,0:T(8,128)(2,1)S(1)} collective-permute-done((bf16[128,2048]{1,0:T(8,128)(2,1)S(1)}, bf16[128,2048]{1,0:T(8,128)(2,1)S(1)}, u32[]{:S(2)}, u32[]{:S(2)}) %collective-permute-start.36) | collective-permute-done | bytes 524320 | tf_op jit(solution)/shard_map/ppermute | solution.py:702
  105.5 3.0 %queries.1 = (bf16[384,2048]{1,0:T(8,128)(2,1)S(1)}, f32[2048,128]{1,0:T(8,128)S(1)}, bf16[2048,128]{1,0:T(8,128)(2,1)S(1)}) custom-call(bf16[384,4096]{1,0:T(8,128)(2,1)S(1)} %get-tuple-element.59.refs_8_.tokens_ref, f32[384,2048]{1,0:T(8,128)S(1)} %get-tuple-element.91.sum_ref, bf16[384,2048]{1,0:T(8,128)(2,1)S(1)} %get-tuple-element.92.mask_ref, ...), custom_call_target="tpu_custom_call" | custom-call | flops 1610612736 | tf_op jit(solution)/shard_map/queries/pallas_call | solution.py:74
  108.9 1.5 %collective-permute-done.37.sibling_ref = bf16[2048,128]{1,0:T(8,128)(2,1)S(1)} collective-permute-done((bf16[2048,128]{1,0:T(8,128)(2,1)S(1)}, bf16[2048,128]{1,0:T(8,128)(2,1)S(1)}, u32[]{:S(2)}, u32[]{:S(2)}) %collective-permute-start.37) | collective-permute-done | bytes 524320 | tf_op jit(solution)/shard_map/ppermute | solution.py:617
  110.5 1.5 %collective-permute-start.38 = (bf16[1024,128]{1,0:T(8,128)(2,1)S(1)}, bf16[1024,128]{1,0:T(8,128)(2,1)S(1)}, u32[]{:S(2)}, u32[]{:S(2)}) collective-permute-start(bf16[1024,128]{1,0:T(8,128)(2,1)S(1)} %get-tuple-element.106), channel_id=1, source_target_pairs={{0,8},{8,0},{16,24},{20,4},{24,16},{28,12},{1,9},{9,1},{17,25},{21... | collective-permute-start | bytes 786440 | tf_op jit(solution)/shard_map/ppermute | solution.py:621
  112.0 5.1 %attended.1 = (bf16[384,2048]{1,0:T(8,128)(2,1)}, f32[8,128]{1,0:T(8,128)S(1)}) custom-call(bf16[384,2048]{1,0:T(8,128)(2,1)S(1)} %get-tuple-element.97.query_ref, bf16[384,2048]{1,0:T(8,128)(2,1)S(1)} %get-tuple-element.74.keys_ref, bf16[384,2048]{1,0:T(8,128)(2,1)S(1)} %get-tuple-element.73.value_ref, bf16[2048,128]{1,0:T(8,128)(2,1)S(1)} %get-tuple-element.79.high_ref, ...), custom_call_target="tpu_custom_call" | custom-call | flops 2415919104 | bytes 6291456 | tf_op jit(solution)/shard_map/attended/pallas_call | solution.py:74
  118.0 2.7 %collective-permute-start.39 = (bf16[1024,128]{1,0:T(8,128)(2,1)S(1)}, bf16[1024,128]{1,0:T(8,128)(2,1)S(1)}, u32[]{:S(2)}, u32[]{:S(2)}) collective-permute-start(bf16[1024,128]{1,0:T(8,128)(2,1)S(1)} %message.3), channel_id=1, source_target_pairs={{4,12},{12,4},{16,0},{20,28},{24,8},{28,20},{5,13},{13,5},{17,1},{... | collective-permute-start | bytes 786440 | tf_op jit(solution)/shard_map/ppermute | solution.py:636
  120.7 6.9 %inner.1 = (f32[384,2048]{1,0:T(8,128)S(1)}, f32[384,2048]{1,0:T(8,128)S(1)}, f32[8,128]{1,0:T(8,128)S(1)}) custom-call(bf16[384,2048]{1,0:T(8,128)(2,1)S(1)} %get-tuple-element.97.query_ref, bf16[384,2048]{1,0:T(8,128)(2,1)S(1)} %get-tuple-element.74.keys_ref, bf16[384,2048]{1,0:T(8,128)(2,1)S(1)} %get-tuple-element.73.value_ref, ...), custom_call_target="tpu_custom_call" | custom-call | flops 3623878656 | bytes 12582912 | tf_op jit(solution)/shard_map/inner/pallas_call | solution.py:74
  127.7 3.3 %grad_tokens.3 = (bf16[384,4096]{1,0:T(8,128)(2,1)}, f32[8,128]{1,0:T(8,128)}) custom-call(bf16[128,2048]{1,0:T(8,128)(2,1)S(1)} %choose.3.refs_0_, bf16[128,2048]{1,0:T(8,128)(2,1)S(1)} %get-tuple-element.94.refs_1_, bf16[128,2048]{1,0:T(8,128)(2,1)S(1)} %get-tuple-element.95.refs_2_, ...), custom_call_target="tpu_custom_call", output_to_operand_aliasing={{0}: (9, {})} | custom-call | flops 1610612736 | tf_op jit(solution)/shard_map/grad_tokens/pallas_call | solution.py:74
  131.3 3.5 %outer.1 = (bf16[384,2048]{1,0:T(8,128)(2,1)}, bf16[384,2048]{1,0:T(8,128)(2,1)}) custom-call(f32[384,2048]{1,0:T(8,128)S(1)} %get-tuple-element.101.key_ref, f32[384,2048]{1,0:T(8,128)S(1)} %get-tuple-element.102.val_ref, bf16[384,2048]{1,0:T(8,128)(2,1)S(1)} %get-tuple-element.74.keys_ref, bf16[384,2048]{1,0:T(8,128)(2,1)S(1)} %get-tuple-element.73.value_ref, ...), custom_call_target="tpu_custom_call" | custom-call | flops 805306368 | bytes 15728640 | tf_op jit(solution)/shard_map/outer/pallas_call | solution.py:74
  (78 shorter events, 19.6 us)
Async XLA Ops:
  0.6 14.1 %collective-permute-start = (bf16[128,2048]{1,0:T(8,128)(2,1)}, bf16[128,2048]{1,0:T(8,128)(2,1)S(1)}, u32[]{:S(2)}, u32[]{:S(2)}) collective-permute-start(bf16[128,2048]{1,0:T(8,128)(2,1)} %refs_0_.3), channel_id=1, source_target_pairs={{0,1},{1,0},{2,3},{3,2},{4,5},{5,4},{6,7},{7,6},{8,9},{9,8},{10,11... | collective-permute-start | bytes 1572872 | tf_op jit(solution)/shard_map/ppermute | solution.py:705
  2.8 11.9 %collective-permute-start.1 = (bf16[128,2048]{1,0:T(8,128)(2,1)}, bf16[128,2048]{1,0:T(8,128)(2,1)S(1)}, u32[]{:S(2)}, u32[]{:S(2)}) collective-permute-start(bf16[128,2048]{1,0:T(8,128)(2,1)} %refs_0_.3), channel_id=1, source_target_pairs={{1,2},{2,1},{5,6},{6,5},{9,10},{10,9},{13,14},{14,13},{17,18},{18,... | collective-permute-start | bytes 1572872 | tf_op jit(solution)/shard_map/ppermute | solution.py:705
  3.5 11.2 %collective-permute-start.2 = (bf16[128,2048]{1,0:T(8,128)(2,1)}, bf16[128,2048]{1,0:T(8,128)(2,1)S(1)}, u32[]{:S(2)}, u32[]{:S(2)}) collective-permute-start(bf16[128,2048]{1,0:T(8,128)(2,1)} %refs_0_.3), channel_id=1, source_target_pairs={{0,8},{4,20},{8,0},{12,28},{16,24},{20,4},{24,16},{28,12},{1,9},{5... | collective-permute-start | bytes 1572872 | tf_op jit(solution)/shard_map/ppermute | solution.py:708
  4.8 14.0 %collective-permute-start.3 = (bf16[128,2048]{1,0:T(8,128)(2,1)}, bf16[128,2048]{1,0:T(8,128)(2,1)S(1)}, u32[]{:S(2)}, u32[]{:S(2)}) collective-permute-start(bf16[128,2048]{1,0:T(8,128)(2,1)} %refs_0_.3), channel_id=1, source_target_pairs={{0,16},{4,12},{8,24},{12,4},{16,0},{20,28},{24,8},{28,20},{1,17},{... | collective-permute-start | bytes 1572872 | tf_op jit(solution)/shard_map/ppermute | solution.py:708
  19.4 11.9 %collective-permute-start.5 = (bf16[128,2048]{1,0:T(8,128)(2,1)S(1)}, bf16[128,2048]{1,0:T(8,128)(2,1)S(1)}, u32[]{:S(2)}, u32[]{:S(2)}) collective-permute-start(bf16[128,2048]{1,0:T(8,128)(2,1)S(1)} %get-tuple-element.63.refs_0_), channel_id=1, source_target_pairs={{0,8},{4,20},{8,0},{12,28},{16,24},{20,4},{24,16},{28,12},{1,9},{5... | collective-permute-start | bytes 1572872 | tf_op jit(solution)/shard_map/ppermute | solution.py:708
  19.6 14.6 %collective-permute-start.6 = (bf16[128,2048]{1,0:T(8,128)(2,1)S(1)}, bf16[128,2048]{1,0:T(8,128)(2,1)S(1)}, u32[]{:S(2)}, u32[]{:S(2)}) collective-permute-start(bf16[128,2048]{1,0:T(8,128)(2,1)S(1)} %get-tuple-element.63.refs_0_), channel_id=1, source_target_pairs={{0,16},{4,12},{8,24},{12,4},{16,0},{20,28},{24,8},{28,20},{1,17},{... | collective-permute-start | bytes 1572872 | tf_op jit(solution)/shard_map/ppermute | solution.py:708
  20.8 13.6 %collective-permute-start.7 = (bf16[128,2048]{1,0:T(8,128)(2,1)S(1)}, bf16[128,2048]{1,0:T(8,128)(2,1)S(1)}, u32[]{:S(2)}, u32[]{:S(2)}) collective-permute-start(bf16[128,2048]{1,0:T(8,128)(2,1)S(1)} %get-tuple-element.63.refs_0_), channel_id=1, source_target_pairs={{1,2},{2,1},{5,6},{6,5},{9,10},{10,9},{13,14},{14,13},{17,18},{18,... | collective-permute-start | bytes 1572872 | tf_op jit(solution)/shard_map/ppermute | solution.py:705
  21.5 17.7 %collective-permute-start.4 = (bf16[128,2048]{1,0:T(8,128)(2,1)S(1)}, bf16[128,2048]{1,0:T(8,128)(2,1)S(1)}, u32[]{:S(2)}, u32[]{:S(2)}) collective-permute-start(bf16[128,2048]{1,0:T(8,128)(2,1)S(1)} %get-tuple-element.62.refs_1_), channel_id=1, source_target_pairs={{0,16},{4,12},{8,24},{12,4},{16,0},{20,28},{24,8},{28,20},{1,17},{... | collective-permute-start | bytes 1572872 | tf_op jit(solution)/shard_map/ppermute | solution.py:711
  21.8 17.5 %collective-permute-start.8 = (bf16[128,2048]{1,0:T(8,128)(2,1)S(1)}, bf16[128,2048]{1,0:T(8,128)(2,1)S(1)}, u32[]{:S(2)}, u32[]{:S(2)}) collective-permute-start(bf16[128,2048]{1,0:T(8,128)(2,1)S(1)} %get-tuple-element.61.inner_ref), channel_id=1, source_target_pairs={{1,0},{2,3},{5,4},{6,7},{9,8},{10,11},{13,12},{14,15},{17,16},{18,... | collective-permute-start | bytes 1572872 | tf_op jit(solution)/shard_map/ppermute | solution.py:705
  31.2 9.8 %collective-permute-start.13 = (bf16[128,2048]{1,0:T(8,128)(2,1)S(1)}, bf16[128,2048]{1,0:T(8,128)(2,1)S(1)}, u32[]{:S(2)}, u32[]{:S(2)}) collective-permute-start(bf16[128,2048]{1,0:T(8,128)(2,1)S(1)} %copy-done), channel_id=1, source_target_pairs={{0,4},{4,0},{1,5},{5,1},{2,6},{6,2},{3,7},{7,3},{8,12},{12,8},{9,1... | collective-permute-start | bytes 1572872 | tf_op jit(solution)/shard_map/ppermute | solution.py:702
  34.2 9.4 %collective-permute-start.14 = (bf16[128,2048]{1,0:T(8,128)(2,1)S(1)}, bf16[128,2048]{1,0:T(8,128)(2,1)S(1)}, u32[]{:S(2)}, u32[]{:S(2)}) collective-permute-start(bf16[128,2048]{1,0:T(8,128)(2,1)S(1)} %get-tuple-element.62.refs_1_), channel_id=1, source_target_pairs={{0,4},{4,0},{1,5},{5,1},{2,6},{6,2},{3,7},{7,3},{8,12},{12,8},{9,1... | collective-permute-start | bytes 1572872 | tf_op jit(solution)/shard_map/ppermute | solution.py:702
  34.4 7.9 %collective-permute-start.21 = (bf16[1024,128]{1,0:T(8,128)(2,1)S(1)}, bf16[1024,128]{1,0:T(8,128)(2,1)S(1)}, u32[]{:S(2)}, u32[]{:S(2)}) collective-permute-start(bf16[1024,128]{1,0:T(8,128)(2,1)S(1)} %get-tuple-element.77), channel_id=1, source_target_pairs={{0,8},{4,20},{8,0},{12,28},{16,24},{24,16},{1,9},{5,21},{9,1},{13,... | collective-permute-start | bytes 786440 | tf_op jit(solution)/shard_map/ppermute | solution.py:621
  39.3 20.4 %collective-permute-start.16 = (bf16[128,2048]{1,0:T(8,128)(2,1)S(1)}, bf16[128,2048]{1,0:T(8,128)(2,1)S(1)}, u32[]{:S(2)}, u32[]{:S(2)}) collective-permute-start(bf16[128,2048]{1,0:T(8,128)(2,1)S(1)} %get-tuple-element.68.refs_3_), channel_id=1, source_target_pairs={{0,4},{4,0},{1,5},{5,1},{2,6},{6,2},{3,7},{7,3},{8,12},{12,8},{9,1... | collective-permute-start | bytes 1572872 | tf_op jit(solution)/shard_map/ppermute | solution.py:702
  41.0 18.8 %collective-permute-start.10 = (bf16[128,2048]{1,0:T(8,128)(2,1)S(1)}, bf16[128,2048]{1,0:T(8,128)(2,1)S(1)}, u32[]{:S(2)}, u32[]{:S(2)}) collective-permute-start(bf16[128,2048]{1,0:T(8,128)(2,1)S(1)} %choose.2.refs_0_), channel_id=1, source_target_pairs={{0,8},{4,20},{8,0},{12,28},{16,24},{20,4},{24,16},{28,12},{1,9},{5... | collective-permute-start | bytes 1572872 | tf_op jit(solution)/shard_map/ppermute | solution.py:708
  42.3 18.0 %collective-permute-start.11 = (bf16[128,2048]{1,0:T(8,128)(2,1)S(1)}, bf16[128,2048]{1,0:T(8,128)(2,1)S(1)}, u32[]{:S(2)}, u32[]{:S(2)}) collective-permute-start(bf16[128,2048]{1,0:T(8,128)(2,1)S(1)} %choose.2.refs_0_), channel_id=1, source_target_pairs={{0,16},{4,12},{8,24},{12,4},{16,0},{20,28},{24,8},{28,20},{1,17},{... | collective-permute-start | bytes 1572872 | tf_op jit(solution)/shard_map/ppermute | solution.py:708
  43.6 14.7 %collective-permute-start.22 = (bf16[1024,128]{1,0:T(8,128)(2,1)S(1)}, bf16[1024,128]{1,0:T(8,128)(2,1)S(1)}, u32[]{:S(2)}, u32[]{:S(2)}) collective-permute-start(bf16[1024,128]{1,0:T(8,128)(2,1)S(1)} %message.2), channel_id=1, source_target_pairs={{0,16},{4,12},{8,24},{12,4},{20,28},{28,20},{1,17},{5,13},{9,25},{... | collective-permute-start | bytes 786440 | tf_op jit(solution)/shard_map/ppermute | solution.py:636
  45.8 18.1 %collective-permute-start.9 = (bf16[128,2048]{1,0:T(8,128)(2,1)S(1)}, bf16[128,2048]{1,0:T(8,128)(2,1)S(1)}, u32[]{:S(2)}, u32[]{:S(2)}) collective-permute-start(bf16[128,2048]{1,0:T(8,128)(2,1)S(1)} %get-tuple-element.65.refs_1_), channel_id=1, source_target_pairs={{0,16},{4,12},{8,24},{12,4},{16,0},{20,28},{24,8},{28,20},{1,17},{... | collective-permute-start | bytes 1572872 | tf_op jit(solution)/shard_map/ppermute | solution.py:711
  58.3 15.5 %collective-permute-start.12 = (bf16[128,2048]{1,0:T(8,128)(2,1)S(1)}, bf16[128,2048]{1,0:T(8,128)(2,1)S(1)}, u32[]{:S(2)}, u32[]{:S(2)}) collective-permute-start(bf16[128,2048]{1,0:T(8,128)(2,1)S(1)} %get-tuple-element.66.inner_ref), channel_id=1, source_target_pairs={{1,0},{2,3},{5,4},{6,7},{9,8},{10,11},{13,12},{14,15},{17,16},{18,... | collective-permute-start | bytes 1572872 | tf_op jit(solution)/shard_map/ppermute | solution.py:705
  59.7 14.2 %collective-permute-start.23 = (f32[1024,128]{1,0:T(8,128)S(1)}, f32[1024,128]{1,0:T(8,128)S(1)}, u32[]{:S(2)}, u32[]{:S(2)}) collective-permute-start(f32[1024,128]{1,0:T(8,128)S(1)} %state.2.state_ref), channel_id=1, source_target_pairs={{0,4},{4,0},{1,5},{5,1},{2,6},{6,2},{3,7},{7,3},{8,12},{12,8},{9,1... | collective-permute-start | bytes 1572872 | tf_op jit(solution)/shard_map/ppermute | solution.py:646
  59.8 16.6 %collective-permute-start.24 = (bf16[128,2048]{1,0:T(8,128)(2,1)S(1)}, bf16[128,2048]{1,0:T(8,128)(2,1)S(1)}, u32[]{:S(2)}, u32[]{:S(2)}) collective-permute-start(bf16[128,2048]{1,0:T(8,128)(2,1)S(1)} %get-tuple-element.63.refs_0_), channel_id=1, source_target_pairs={{0,4},{4,0},{1,5},{5,1},{2,6},{6,2},{3,7},{7,3},{8,12},{12,8},{9,1... | collective-permute-start | bytes 1572872 | tf_op jit(solution)/shard_map/ppermute | solution.py:702
  60.3 16.9 %collective-permute-start.25 = (bf16[128,2048]{1,0:T(8,128)(2,1)S(1)}, bf16[128,2048]{1,0:T(8,128)(2,1)S(1)}, u32[]{:S(2)}, u32[]{:S(2)}) collective-permute-start(bf16[128,2048]{1,0:T(8,128)(2,1)S(1)} %get-tuple-element.65.refs_1_), channel_id=1, source_target_pairs={{0,4},{4,0},{1,5},{5,1},{2,6},{6,2},{3,7},{7,3},{8,12},{12,8},{9,1... | collective-permute-start | bytes 1572872 | tf_op jit(solution)/shard_map/ppermute | solution.py:702
  63.9 22.4 %collective-permute-start.26 = (bf16[128,2048]{1,0:T(8,128)(2,1)S(1)}, bf16[128,2048]{1,0:T(8,128)(2,1)S(1)}, u32[]{:S(2)}, u32[]{:S(2)}) collective-permute-start(bf16[128,2048]{1,0:T(8,128)(2,1)S(1)} %get-tuple-element.83.refs_2_), channel_id=1, source_target_pairs={{0,4},{4,0},{1,5},{5,1},{2,6},{6,2},{3,7},{7,3},{8,12},{12,8},{9,1... | collective-permute-start | bytes 1572872 | tf_op jit(solution)/shard_map/ppermute | solution.py:702
  73.9 13.0 %collective-permute-start.27 = (bf16[128,2048]{1,0:T(8,128)(2,1)S(1)}, bf16[128,2048]{1,0:T(8,128)(2,1)S(1)}, u32[]{:S(2)}, u32[]{:S(2)}) collective-permute-start(bf16[128,2048]{1,0:T(8,128)(2,1)S(1)} %get-tuple-element.84.refs_3_), channel_id=1, source_target_pairs={{0,4},{4,0},{1,5},{5,1},{2,6},{6,2},{3,7},{7,3},{8,12},{12,8},{9,1... | collective-permute-start | bytes 1572872 | tf_op jit(solution)/shard_map/ppermute | solution.py:702
  73.9 17.2 %collective-permute-start.18 = (bf16[128,2048]{1,0:T(8,128)(2,1)S(1)}, bf16[128,2048]{1,0:T(8,128)(2,1)S(1)}, u32[]{:S(2)}, u32[]{:S(2)}) collective-permute-start(bf16[128,2048]{1,0:T(8,128)(2,1)S(1)} %choose.3.refs_0_), channel_id=1, source_target_pairs={{0,8},{4,20},{8,0},{12,28},{16,24},{20,4},{24,16},{28,12},{1,9},{5... | collective-permute-start | bytes 1572872 | tf_op jit(solution)/shard_map/ppermute | solution.py:708
  76.4 15.2 %collective-permute-start.19 = (bf16[128,2048]{1,0:T(8,128)(2,1)S(1)}, bf16[128,2048]{1,0:T(8,128)(2,1)S(1)}, u32[]{:S(2)}, u32[]{:S(2)}) collective-permute-start(bf16[128,2048]{1,0:T(8,128)(2,1)S(1)} %choose.3.refs_0_), channel_id=1, source_target_pairs={{0,16},{4,12},{8,24},{12,4},{16,0},{20,28},{24,8},{28,20},{1,17},{... | collective-permute-start | bytes 1572872 | tf_op jit(solution)/shard_map/ppermute | solution.py:708
  77.2 17.0 %collective-permute-start.17 = (bf16[128,2048]{1,0:T(8,128)(2,1)S(1)}, bf16[128,2048]{1,0:T(8,128)(2,1)S(1)}, u32[]{:S(2)}, u32[]{:S(2)}) collective-permute-start(bf16[128,2048]{1,0:T(8,128)(2,1)S(1)} %get-tuple-element.70.refs_1_), channel_id=1, source_target_pairs={{0,16},{4,12},{8,24},{12,4},{16,0},{20,28},{24,8},{28,20},{1,17},{... | collective-permute-start | bytes 1572872 | tf_op jit(solution)/shard_map/ppermute | solution.py:711
  86.3 9.1 %collective-permute-start.28 = (bf16[128,2048]{1,0:T(8,128)(2,1)S(1)}, bf16[128,2048]{1,0:T(8,128)(2,1)S(1)}, u32[]{:S(2)}, u32[]{:S(2)}) collective-permute-start(bf16[128,2048]{1,0:T(8,128)(2,1)S(1)} %choose.2.refs_0_), channel_id=1, source_target_pairs={{0,4},{4,0},{1,5},{5,1},{2,6},{6,2},{3,7},{7,3},{8,12},{12,8},{9,1... | collective-permute-start | bytes 1572872 | tf_op jit(solution)/shard_map/ppermute | solution.py:702
  86.8 9.7 %collective-permute-start.29 = (bf16[128,2048]{1,0:T(8,128)(2,1)S(1)}, bf16[128,2048]{1,0:T(8,128)(2,1)S(1)}, u32[]{:S(2)}, u32[]{:S(2)}) collective-permute-start(bf16[128,2048]{1,0:T(8,128)(2,1)S(1)} %get-tuple-element.70.refs_1_), channel_id=1, source_target_pairs={{0,4},{4,0},{1,5},{5,1},{2,6},{6,2},{3,7},{7,3},{8,12},{12,8},{9,1... | collective-permute-start | bytes 1572872 | tf_op jit(solution)/shard_map/ppermute | solution.py:702
  94.7 8.3 %collective-permute-start.32 = (bf16[128,2048]{1,0:T(8,128)(2,1)S(1)}, bf16[128,2048]{1,0:T(8,128)(2,1)S(1)}, u32[]{:S(2)}, u32[]{:S(2)}) collective-permute-start(bf16[128,2048]{1,0:T(8,128)(2,1)S(1)} %get-tuple-element.94.refs_1_), channel_id=1, source_target_pairs={{0,16},{4,12},{8,24},{12,4},{16,0},{20,28},{24,8},{28,20},{1,17},{... | collective-permute-start | bytes 1572872 | tf_op jit(solution)/shard_map/ppermute | solution.py:711
  95.4 8.5 %collective-permute-start.33 = (bf16[128,2048]{1,0:T(8,128)(2,1)S(1)}, bf16[128,2048]{1,0:T(8,128)(2,1)S(1)}, u32[]{:S(2)}, u32[]{:S(2)}) collective-permute-start(bf16[128,2048]{1,0:T(8,128)(2,1)S(1)} %choose.3.refs_0_), channel_id=1, source_target_pairs={{0,4},{4,0},{1,5},{5,1},{2,6},{6,2},{3,7},{7,3},{8,12},{12,8},{9,1... | collective-permute-start | bytes 1572872 | tf_op jit(solution)/shard_map/ppermute | solution.py:702
  110.5 7.4 %collective-permute-start.38 = (bf16[1024,128]{1,0:T(8,128)(2,1)S(1)}, bf16[1024,128]{1,0:T(8,128)(2,1)S(1)}, u32[]{:S(2)}, u32[]{:S(2)}) collective-permute-start(bf16[1024,128]{1,0:T(8,128)(2,1)S(1)} %get-tuple-element.106), channel_id=1, source_target_pairs={{0,8},{8,0},{16,24},{20,4},{24,16},{28,12},{1,9},{9,1},{17,25},{21... | collective-permute-start | bytes 786440 | tf_op jit(solution)/shard_map/ppermute | solution.py:621
  118.0 9.6 %collective-permute-start.39 = (bf16[1024,128]{1,0:T(8,128)(2,1)S(1)}, bf16[1024,128]{1,0:T(8,128)(2,1)S(1)}, u32[]{:S(2)}, u32[]{:S(2)}) collective-permute-start(bf16[1024,128]{1,0:T(8,128)(2,1)S(1)} %message.3), channel_id=1, source_target_pairs={{4,12},{12,4},{16,0},{20,28},{24,8},{28,20},{5,13},{13,5},{17,1},{... | collective-permute-start | bytes 786440 | tf_op jit(solution)/shard_map/ppermute | solution.py:636
  (10 other events, 65.8 us)

commit v6 on v5

--- a/solution.py
+++ b/solution.py
@@ -98,12 +98,16 @@
     chip, core, layer = (lax.axis_index(name) for name in ("chip", "core", "dp"))
     upper = layer < 2
     layers = [layer, layer ^ 1, jnp.where(upper, 2, 1), jnp.where(upper, 3, 0)]
-    return [
-        ((chip ^ flip) * 2 + side) * 4 + one
-        for one in layers
-        for side in (core, 1 - core)
-        for flip in crossed(side)
-    ]
+
+    def some(one, flips):
+        return [
+            ((chip ^ crossed(side)[flip]) * 2 + side) * 4 + one
+            for side in (core, 1 - core)
+            for flip in flips
+        ]
+
+    first = [place for one in layers[:3] for place in some(one, range(4))]
+    return first + some(layers[3], range(3)) + some(layers[3], [3])
 
 
 def piece_columns(place):
@@ -570,88 +574,63 @@
     return keep
 
 
-def half_rows(array_ref, core):
-    half = array_ref.shape[0] // 2
-    return array_ref[pl.ds(pl.multiple_of(core * half, half), half), :]
-
-
-def both_kernel(own_ref, sibling_ref, both_ref, sent_ref):
-    core = lax.axis_index("core")
-    both = half_rows(own_ref, core) + half_rows(sibling_ref, core).astype(f32)
-    both_ref[...] = both
-    sent_ref[...] = both.astype(bf16)
-
-
 def low_bit(reverse):
     chip = lax.axis_index("chip")
     return 1 - chip % 2 if reverse else chip % 2
 
 
-def message_kernel(reverse, got_ref, both_ref, *refs):
+def between_kernel(reverse, got_ref, own_ref, *refs):
     core = lax.axis_index("core")
     adds = jnp.where((core == 0) | (low_bit(reverse) == 0), 1.0, 0.0)
-    refs[-1][...] = (got_ref[...].astype(f32) + adds * both_ref[...]).astype(bf16)
-
-
-def state_kernel(reverse, got_ref, more_ref, *refs):
+    refs[-1][...] = (got_ref[...].astype(f32) + adds * own_ref[...]).astype(bf16)
+
+
+def chips_kernel(reverse, got_ref, more_ref, own_ref, *refs):
     core = lax.axis_index("core")
     adds = jnp.where((core == 1) | (low_bit(reverse) == 1), 1.0, 0.0)
-    refs[-1][...] = adds * got_ref[...].astype(f32) + more_ref[...].astype(f32)
-
-
-def whole_kernel(reverse, state_ref, other_ref, sibling_ref, high_ref, low_ref):
-    core = lax.axis_index("core")
-    adds = jnp.where(core == (0 if reverse else 1), 1.0, 0.0)
-    half = state_ref.shape[0]
-    for ref, side in ((state_ref, core), (other_ref, 1 - core)):
-        rows = pl.ds(pl.multiple_of(side * half, half), half)
-        whole = ref[...] + adds * sibling_ref[rows, :].astype(f32)
-        high = whole.astype(bf16)
-        high_ref[rows, :] = high
-        low_ref[rows, :] = (whole - high.astype(f32)).astype(bf16)
-
-
-def scan_first(own, sent, reverse, others=()):
-    rows = own.shape[0]
-    half = (rows // 2, HEAD)
-    sibling = lax.ppermute(sent, "core", SWAP)
-    both, sent = kernel_call(
-        both_kernel, "VV", (own, sibling), "VV", [(half, f32), (half, bf16)], "both", (0, 0)
-    )
-    got = lax.ppermute(sent, CTX, links(1, upward(reverse)))
+    mine = adds * got_ref[...].astype(f32) + more_ref[...].astype(f32)
+    gives = jnp.where(core == (1 if reverse else 0), 1.0, 0.0)
+    refs[-2][...] = mine
+    refs[-1][...] = mine + gives * own_ref[...]
+
+
+def add_kernel(mine_ref, other_ref, high_ref, low_ref):
+    whole = mine_ref[...] + other_ref[...]
+    high = whole.astype(bf16)
+    high_ref[...] = high
+    low_ref[...] = (whole - high.astype(f32)).astype(bf16)
+
+
+def send_first(sent, reverse):
+    return lax.ppermute(sent, CTX, links(1, upward(reverse)))
+
+
+def send_second(got, own, reverse, others=()):
     (message,) = kernel_call(
-        functools.partial(message_kernel, reverse),
+        functools.partial(between_kernel, reverse),
         "VV" + "A" * len(others),
-        (got, both, *others),
+        (got, own, *others),
         "V",
-        [(half, bf16)],
+        [(own.shape, bf16)],
         "message",
         (0, 0),
     )
-    return message, got, sibling
-
-
-def scan_second(message, got, sibling, reverse, others=()):
-    half, full = message.shape, sibling.shape
-    more = lax.ppermute(message, CTX, links(2, upward(reverse)))
-    (state,) = kernel_call(
-        functools.partial(state_kernel, reverse),
-        "VV" + "A" * len(others),
-        (got, more, *others),
-        "V",
-        [(half, f32)],
-        "state",
+    return lax.ppermute(message, CTX, links(2, upward(reverse)))
+
+
+def add_cores(got, more, own, reverse, others=()):
+    mine, gives = kernel_call(
+        functools.partial(chips_kernel, reverse),
+        "VVV" + "A" * len(others),
+        (got, more, own, *others),
+        "VV",
+        [(own.shape, f32)] * 2,
+        "chips",
         (0, 0),
     )
-    other = lax.ppermute(state, "core", SWAP)
+    other = lax.ppermute(gives, "core", SWAP)
     return kernel_call(
-        functools.partial(whole_kernel, reverse),
-        "VVV",
-        (state, other, sibling),
-        "VV",
-        [(full, bf16)] * 2,
-        "whole",
-        (0, 0),
+        add_kernel, "VV", (mine, other), "VV", [(own.shape, bf16)] * 2, "whole", (0, 0)
     )
 
 
@@ -659,6 +638,34 @@
     whole = lax.all_gather(q_weight, ("chip", "core", "dp"), axis=0, tiled=True)
     cut = whole.shape[0] // (2 * PIECE) * PIECE
     return [whole[:cut], whole[cut:]]
+
+
+def pack_kernel(*refs):
+    *arrays, out_ref, sems = refs
+    copies = Copies(sems)
+    rows = out_ref.shape[0] // len(arrays)
+    going = [
+        copies.start(array, out_ref.at[pl.ds(at * rows, rows), :])
+        for at, array in enumerate(arrays)
+    ]
+    for copy in going:
+        copy.wait()
+
+
+def pack(*arrays):
+    rows, total = arrays[0].shape
+    number = len(arrays)
+    (made,) = kernel_call(
+        pack_kernel,
+        "A" * number,
+        arrays,
+        "V",
+        [((number * rows, total), arrays[0].dtype)],
+        "pack",
+        (0, 0),
+        [pltpu.SemaphoreType.DMA((number,))],
+    )
+    return [made, lax.ppermute(made, "core", SWAP)]
 
 
 def choose_kernel(inner_ref, end_ref, out_ref, sem):
@@ -720,9 +727,7 @@
         near = along(q_weight, ends)
         mid = along(q_weight, middle)
         first_0, second_0 = cross(q_weight)
-        other_0 = sibling(q_weight)
         near, mid, first_0, second_0, sent = join([near, mid, first_0, second_0, sent])
-        message, *rest = scan_first(own, sent, False)
     else:
         arrived = gather_any(q_weight)
         high, low = halves(scan_any(own, sent, chips * 2, False))
@@ -732,46 +737,46 @@
         first_1, second_1 = cross(near)
         far = along(near, middle)
         mid_out = along(mid, outward)
-        third_0, first_1, second_1, far, mid_out = join(
-            [third_0, first_1, second_1, far, mid_out]
+        got = send_first(sent, False)
+        third_0, first_1, second_1, far, mid_out, got = join(
+            [third_0, first_1, second_1, far, mid_out, got]
         )
         third_1 = onward(first_1)
         next_layer = choose(mid, mid_out)
         first_2, second_2 = cross(next_layer)
         far_out = along(far, outward)
-        own_blocks = [q_weight, first_0, second_0, third_0, other_0]
-        own_blocks += [sibling(one) for one in own_blocks[1:4]]
+        more = send_second(got, own, False)
+        own_blocks = pack(q_weight, first_0, second_0, third_0)
         partial, _, own_mark = products_call(special, 0, own_blocks, tokens)
-        third_1, first_2, second_2, far_out = join(
-            [third_1, first_2, second_2, far_out], [own_mark]
+        third_1, first_2, second_2, far_out, more = join(
+            [third_1, first_2, second_2, far_out, more], [own_mark]
         )
         third_2 = onward(first_2)
         last_layer = choose(far, far_out)
         first_3, second_3 = cross(last_layer)
 
-        def whole(*mine):
-            return list(mine) + [sibling(one) for one in mine]
-
-        high, low = scan_second(message, *rest, False)
+        high, low = add_cores(got, more, own, False)
         masked, q_mask, cotangent, _ = masked_call(
             factor, cotangent, q_spikes, values, keys, high, low
         )
         _, grad, mark_0 = products_call(
             special, 0, own_blocks, tokens, masked=masked, project=False
         )
-        blocks = whole(near, first_1, second_1, third_1)
+        blocks = pack(near, first_1, second_1, third_1)
         partial, grad, mark_1 = products_call(
             special, 8, blocks, tokens, partial, masked, grad
         )
         third_2, first_3, second_3 = join([third_2, first_3, second_3], [mark_0, mark_1])
         third_3 = onward(first_3)
-        blocks = whole(next_layer, first_2, second_2, third_2)
+        blocks = pack(next_layer, first_2, second_2, third_2)
         partial, grad, mark = products_call(
             special, 16, blocks, tokens, partial, masked, grad
         )
         third_3, = join([third_3], [mark])
-        late = whole(last_layer, first_3, second_3, third_3)
-        start = 24
+        blocks = pack(last_layer, first_3, second_3)
+        partial, grad, _ = products_call(special, 24, blocks, tokens, partial, masked, grad)
+        late = [third_3, sibling(third_3)]
+        start = 30
     else:
         masked, q_mask, cotangent, _ = masked_call(
             factor, cotangent, q_spikes, values, keys, high, low
@@ -783,8 +788,9 @@
     attended, attended_mark = attend_call(factor, queries, keys, values, high, low)
     key_part, value_part, inner_mark = inner_call(queries, keys, values, cotangent)
     if special:
-        message, *rest = scan_first(own, sent, True, [attended_mark])
-        adjoint = scan_second(message, *rest, True, [inner_mark])
+        got = send_first(sent, True)
+        more = send_second(got, own, True, [attended_mark])
+        adjoint = add_cores(got, more, own, True, [inner_mark])
     else:
         adjoint = halves(scan_any(own, sent, chips * 2, True))
     _, grad_tokens, _ = products_call(

time: 136 us -> 139 us (1.022)
  waiting for transfers between devices: 50.9 us -> 56.2 us
  starting transfers between devices: 37.5 us -> 32.3 us
  Pallas kernels: 45.4 us -> 47.2 us
    ppermute x5, waiting for transfers between devices: 14.3 us -> 4.48 us  [along(): return lax.ppermute(array, 'dp', pairs)]
    ppermute x16 -> x1, starting transfers between devices: 9.59 us -> 1.06 us  [sibling(): return lax.ppermute(array, 'core', SWAP)]
    ppermute x4, waiting for transfers between devices: 9.2 us -> 15.4 us  [onward(): return lax.ppermute(array, CTX, links(2))]
    ppermute x8 -> x10, starting transfers between devices: 9.18 us -> 14.8 us  [the longest x2 5.28 us: send_second(): return lax.ppermute(message, CTX, links(2, upward(reverse)))]
    ppermute x8 -> x10, waiting for transfers between devices: 13.5 us -> 18.4 us  [the longest x2 7.22 us: send_first(): return lax.ppermute(sent, CTX, links(1, upward(reverse)))]
    ppermute x4, waiting for transfers between devices: 8.2 us -> 11.5 us  [cross(): lax.ppermute(array, CTX, links(1))]
    ppermute x4, starting transfers between devices: 5.1 us -> 2.33 us  [cross(): lax.ppermute(array, CTX, links(1))]
    ppermute x4, waiting for transfers between devices: 4.05 us -> 6.4 us  [cross(): lax.ppermute(array, CTX, links(2))]
  transfers between devices with their start and end apart: 41 -> 28, of which waited for: 13 -> 17; matrix products, arithmetic and copies ran while one was open for 0% -> 0% of each run, Pallas kernels for 28% -> 30%
where the time goes in v6:
time: 139 us; the launch traced here: 137 us
  waiting for transfers between devices  56.2 us (40%)
  Pallas kernels  47.2 us (34%)
  starting transfers between devices  32.3 us (23%)
    pallas_call x29, Pallas kernels, kernel_call(): made(*[holds[place](one) if place in holds else one for place, one in zip...  47.2 us
    ppermute x4, waiting for transfers between devices, onward(): return lax.ppermute(array, CTX, links(2))  15.4 us
    ppermute x4, waiting for transfers between devices, cross(): lax.ppermute(array, CTX, links(1))  11.5 us
    ppermute x2, waiting for transfers between devices, send_first(): return lax.ppermute(sent, CTX, links(1, upward(reverse)))  7.22 us
    ppermute x4, waiting for transfers between devices, cross(): lax.ppermute(array, CTX, links(2))  6.4 us
    ppermute x5, starting transfers between devices, along(): return lax.ppermute(array, 'dp', pairs)  6.12 us
    ppermute x2, waiting for transfers between devices, send_second(): return lax.ppermute(message, CTX, links(2, upward(reverse)))  5.93 us
    ppermute x2, starting transfers between devices, send_second(): return lax.ppermute(message, CTX, links(2, upward(reverse)))  5.28 us
  transfers between devices with their start and end apart: 28, of which 17 were waited for; matrix products, arithmetic and copies ran while one was open for 0% of the time, Pallas kernels for 30%

profile of v6, /device:TPU:1, one launch (start us, length us, event | category | flops | bytes accessed | tf_op | source)
XLA Modules:
  0.0 136.8 jit_solution(2581173912585533193)
XLA Ops:
  0.6 2.2 %collective-permute-start = (bf16[128,2048]{1,0:T(8,128)(2,1)}, bf16[128,2048]{1,0:T(8,128)(2,1)S(1)}, u32[]{:S(2)}, u32[]{:S(2)}) collective-permute-start(bf16[128,2048]{1,0:T(8,128)(2,1)} %refs_0_.1), channel_id=1, source_target_pairs={{0,1},{1,0},{2,3},{3,2},{4,5},{5,4},{6,7},{7,6},{8,9},{9,8},{10,11... | collective-permute-start | bytes 1572872 | tf_op jit(solution)/shard_map/ppermute | solution.py:712
  3.5 1.3 collective-permute-start.2
  6.0 4.2 %own_memory.1 = (bf16[384,2048]{1,0:T(8,128)(2,1)S(1)}, bf16[384,2048]{1,0:T(8,128)(2,1)S(1)}, bf16[384,2048]{1,0:T(8,128)(2,1)S(1)}, f32[2048,128]{1,0:T(8,128)...) custom-call(bf16[384,2048]{1,0:T(8,128)(2,1)} %bitcast.13, s32[384,2048]{1,0:T(8,128)} %bitcast.11, ...), custom_call_target="tpu_custom_call" | custom-call | flops 201326592 | bytes 9437184 | tf_op jit(solution)/shard_map/own_memory/pallas_call | solution.py:74
  10.2 4.5 %collective-permute-done.refs_0_ = bf16[128,2048]{1,0:T(8,128)(2,1)S(1)} collective-permute-done((bf16[128,2048]{1,0:T(8,128)(2,1)}, bf16[128,2048]{1,0:T(8,128)(2,1)S(1)}, u32[]{:S(2)}, u32[]{:S(2)}) %collective-permute-start) | collective-permute-done | bytes 524320 | tf_op jit(solution)/shard_map/ppermute | solution.py:712
  14.8 4.0 %collective-permute-done.3.refs_3_ = bf16[128,2048]{1,0:T(8,128)(2,1)S(1)} collective-permute-done((bf16[128,2048]{1,0:T(8,128)(2,1)}, bf16[128,2048]{1,0:T(8,128)(2,1)S(1)}, u32[]{:S(2)}, u32[]{:S(2)}) %collective-permute-start.3) | collective-permute-done | bytes 524320 | tf_op jit(solution)/shard_map/ppermute | solution.py:715
  22.3 7.8 %collective-permute-done.5.refs_1_ = bf16[128,2048]{1,0:T(8,128)(2,1)S(1)} collective-permute-done((bf16[128,2048]{1,0:T(8,128)(2,1)S(1)}, bf16[128,2048]{1,0:T(8,128)(2,1)S(1)}, u32[]{:S(2)}, u32[]{:S(2)}) %collective-permute-start.5) | collective-permute-done | bytes 524320 | tf_op jit(solution)/shard_map/ppermute | solution.py:715
  30.2 1.7 %collective-permute-start.9 = (bf16[2048,128]{1,0:T(8,128)(2,1)S(1)}, bf16[2048,128]{1,0:T(8,128)(2,1)S(1)}, u32[]{:S(2)}, u32[]{:S(2)}) collective-permute-start(bf16[2048,128]{1,0:T(8,128)(2,1)S(1)} %get-tuple-element.68), channel_id=1, source_target_pairs={{0,8},{4,20},{8,0},{12,28},{16,24},{24,16},{1,9},{5,21},{9,1},{13,... | collective-permute-start | bytes 1572872 | tf_op jit(solution)/shard_map/ppermute | solution.py:605
  31.9 6.5 %collective-permute-done.4.refs_0_ = bf16[128,2048]{1,0:T(8,128)(2,1)S(1)} collective-permute-done((bf16[128,2048]{1,0:T(8,128)(2,1)S(1)}, bf16[128,2048]{1,0:T(8,128)(2,1)S(1)}, u32[]{:S(2)}, u32[]{:S(2)}) %collective-permute-start.4) | collective-permute-done | bytes 524320 | tf_op jit(solution)/shard_map/ppermute | solution.py:718
  38.4 3.4 %collective-permute-done.9.refs_5_ = bf16[2048,128]{1,0:T(8,128)(2,1)S(1)} collective-permute-done((bf16[2048,128]{1,0:T(8,128)(2,1)S(1)}, bf16[2048,128]{1,0:T(8,128)(2,1)S(1)}, u32[]{:S(2)}, u32[]{:S(2)}) %collective-permute-start.9) | collective-permute-done | bytes 524320 | tf_op jit(solution)/shard_map/ppermute | solution.py:605
  42.0 3.5 %collective-permute-start.15 = (bf16[512,2048]{1,0:T(8,128)(2,1)S(1)}, bf16[512,2048]{1,0:T(8,128)(2,1)S(1)}, u32[]{:S(2)}, u32[]{:S(2)}) collective-permute-start(bf16[512,2048]{1,0:T(8,128)(2,1)S(1)} %pack.4.refs_0_), channel_id=1, source_target_pairs={{0,4},{4,0},{1,5},{5,1},{2,6},{6,2},{3,7},{7,3},{8,12},{12,8},{9,1... | collective-permute-start | bytes 6291464 | tf_op jit(solution)/shard_map/ppermute | solution.py:668
  47.3 2.2 %collective-permute-start.14 = (bf16[2048,128]{1,0:T(8,128)(2,1)S(1)}, bf16[2048,128]{1,0:T(8,128)(2,1)S(1)}, u32[]{:S(2)}, u32[]{:S(2)}) collective-permute-start(bf16[2048,128]{1,0:T(8,128)(2,1)S(1)} %message.2), channel_id=1, source_target_pairs={{0,16},{4,12},{8,24},{12,4},{20,28},{28,20},{1,17},{5,13},{9,25},{... | collective-permute-start | bytes 1572872 | tf_op jit(solution)/shard_map/ppermute | solution.py:618
  52.1 1.8 %project.1 = (f32[384,2048]{1,0:T(8,128)S(1)}, f32[8,128]{1,0:T(8,128)S(1)}) custom-call(bf16[512,2048]{1,0:T(8,128)(2,1)S(1)} %pack.4.refs_0_, bf16[512,2048]{1,0:T(8,128)(2,1)S(1)} %collective-permute-done.15.refs_1_, bf16[384,4096]{1,0:T(8,128)(2,1)S(1)} %get-tuple-element.63.refs_2_.tokens_ref), custom_call_target="tpu_custom_call" | custom-call | flops 1610612736 | tf_op jit(solution)/shard_map/project/pallas_call | solution.py:74
  53.9 3.6 %collective-permute-done.11.refs_1_ = bf16[128,2048]{1,0:T(8,128)(2,1)S(1)} collective-permute-done((bf16[128,2048]{1,0:T(8,128)(2,1)S(1)}, bf16[128,2048]{1,0:T(8,128)(2,1)S(1)}, u32[]{:S(2)}, u32[]{:S(2)}) %collective-permute-start.11) | collective-permute-done | bytes 524320 | tf_op jit(solution)/shard_map/ppermute | solution.py:715
  57.5 2.4 %collective-permute-done.12.refs_2_ = bf16[128,2048]{1,0:T(8,128)(2,1)S(1)} collective-permute-done((bf16[128,2048]{1,0:T(8,128)(2,1)S(1)}, bf16[128,2048]{1,0:T(8,128)(2,1)S(1)}, u32[]{:S(2)}, u32[]{:S(2)}) %collective-permute-start.12) | collective-permute-done | bytes 524320 | tf_op jit(solution)/shard_map/ppermute | solution.py:715
  59.8 5.7 %collective-permute-done.14.refs_4_ = bf16[2048,128]{1,0:T(8,128)(2,1)S(1)} collective-permute-done((bf16[2048,128]{1,0:T(8,128)(2,1)S(1)}, bf16[2048,128]{1,0:T(8,128)(2,1)S(1)}, u32[]{:S(2)}, u32[]{:S(2)}) %collective-permute-start.14) | collective-permute-done | bytes 524320 | tf_op jit(solution)/shard_map/ppermute | solution.py:618
  65.5 5.3 %collective-permute-done.10.refs_0_ = bf16[128,2048]{1,0:T(8,128)(2,1)S(1)} collective-permute-done((bf16[128,2048]{1,0:T(8,128)(2,1)S(1)}, bf16[128,2048]{1,0:T(8,128)(2,1)S(1)}, u32[]{:S(2)}, u32[]{:S(2)}) %collective-permute-start.10) | collective-permute-done | bytes 524320 | tf_op jit(solution)/shard_map/ppermute | solution.py:718
  74.0 2.8 %collective-permute-done.19.other_ref = f32[2048,128]{1,0:T(8,128)S(1)} collective-permute-done((f32[2048,128]{1,0:T(8,128)S(1)}, f32[2048,128]{1,0:T(8,128)S(1)}, u32[]{:S(2)}, u32[]{:S(2)}) %collective-permute-start.19) | collective-permute-done | bytes 1048608 | tf_op jit(solution)/shard_map/ppermute | solution.py:631
  77.1 5.7 %masked_grad.1 = (bf16[384,2048]{1,0:T(8,128)(2,1)S(1)}, bf16[384,2048]{1,0:T(8,128)(2,1)S(1)}, bf16[384,2048]{1,0:T(8,128)(2,1)S(1)}, f32[8,128]{1,0:T(8,128)}) custom-call(bf16[384,2048]{1,0:T(8,128)(2,1)} %bitcast.16, s32[384,2048]{1,0:T(8,128)} %bitcast.15, bf16[384,2048]{1,0:T(8,128)(2,1)S(1)} %get-tuple-element.79.value_ref, ...), custom_call_target="tpu_custom_call" | custom-call | flops 2415919104 | bytes 9437184 | tf_op jit(solution)/shard_map/masked_grad/pallas_call | solution.py:74
  82.8 2.7 %grad_tokens.2 = (bf16[384,4096]{1,0:T(8,128)(2,1)}, f32[8,128]{1,0:T(8,128)S(1)}) custom-call(bf16[512,2048]{1,0:T(8,128)(2,1)S(1)} %pack.4.refs_0_, bf16[512,2048]{1,0:T(8,128)(2,1)S(1)} %collective-permute-done.15.refs_1_, bf16[384,2048]{1,0:T(8,128)(2,1)S(1)} %get-tuple-element.86.refs_2_.refs_4_), custom_call_target="tpu_custom_call" | custom-call | flops 1610612736 | tf_op jit(solution)/shard_map/grad_tokens/pallas_call | solution.py:74
  85.4 3.9 %products.3 = (f32[384,2048]{1,0:T(8,128)S(1)}, bf16[384,4096]{1,0:T(8,128)(2,1)}, f32[8,128]{1,0:T(8,128)S(1)}) custom-call(bf16[512,2048]{1,0:T(8,128)(2,1)S(1)} %pack.5.refs_0_, bf16[512,2048]{1,0:T(8,128)(2,1)S(1)} %collective-permute-done.20.refs_1_, ...), custom_call_target="tpu_custom_call", output_to_operand_aliasing={{0}: (3, {}), {1}: (5, {})} | custom-call | flops 3221225472 | tf_op jit(solution)/shard_map/products/pallas_call | solution.py:74
  89.4 2.4 %collective-permute-done.16.refs_0_ = bf16[128,2048]{1,0:T(8,128)(2,1)S(1)} collective-permute-done((bf16[128,2048]{1,0:T(8,128)(2,1)S(1)}, bf16[128,2048]{1,0:T(8,128)(2,1)S(1)}, u32[]{:S(2)}, u32[]{:S(2)}) %collective-permute-start.16) | collective-permute-done | bytes 524320 | tf_op jit(solution)/shard_map/ppermute | solution.py:718
  94.2 2.0 %collective-permute-done.22.refs_1_ = bf16[512,2048]{1,0:T(8,128)(2,1)S(1)} collective-permute-done((bf16[512,2048]{1,0:T(8,128)(2,1)S(1)}, bf16[512,2048]{1,0:T(8,128)(2,1)S(1)}, u32[]{:S(2)}, u32[]{:S(2)}) %collective-permute-start.22) | collective-permute-done | bytes 2097184 | tf_op jit(solution)/shard_map/ppermute | solution.py:668
  96.2 3.9 %products.4 = (f32[384,2048]{1,0:T(8,128)S(1)}, bf16[384,4096]{1,0:T(8,128)(2,1)}, f32[8,128]{1,0:T(8,128)S(1)}) custom-call(bf16[512,2048]{1,0:T(8,128)(2,1)S(1)} %pack.7.refs_0_, bf16[512,2048]{1,0:T(8,128)(2,1)S(1)} %collective-permute-done.22.refs_1_, ...), custom_call_target="tpu_custom_call", output_to_operand_aliasing={{0}: (3, {}), {1}: (5, {})} | custom-call | flops 3221225472 | tf_op jit(solution)/shard_map/products/pallas_call | solution.py:74
  102.3 3.9 %products.5 = (f32[384,2048]{1,0:T(8,128)S(1)}, bf16[384,4096]{1,0:T(8,128)(2,1)}, f32[8,128]{1,0:T(8,128)}) custom-call(bf16[384,2048]{1,0:T(8,128)(2,1)S(1)} %pack.6.refs_0_, bf16[384,2048]{1,0:T(8,128)(2,1)S(1)} %collective-permute-done.21.refs_1_, ...), custom_call_target="tpu_custom_call", output_to_operand_aliasing={{0}: (3, {}), {1}: (5, {})} | custom-call | flops 2415919104 | tf_op jit(solution)/shard_map/products/pallas_call | solution.py:74
  106.3 1.7 %queries.1 = (bf16[384,2048]{1,0:T(8,128)(2,1)S(1)}, f32[2048,128]{1,0:T(8,128)S(1)}, bf16[2048,128]{1,0:T(8,128)(2,1)S(1)}) custom-call(bf16[384,4096]{1,0:T(8,128)(2,1)S(1)} %get-tuple-element.63.refs_2_.tokens_ref, f32[384,2048]{1,0:T(8,128)S(1)} %get-tuple-element.101.sum_ref, bf16[384,2048]{1,0:T(8,128)(2,1)S(1)} %get-tuple-element.102.mask_ref, ...), custom_call_target="tpu_custom_call" | custom-call | flops 402653184 | tf_op jit(solution)/shard_map/queries/pallas_call | solution.py:74
  109.3 5.1 %attended.1 = (bf16[384,2048]{1,0:T(8,128)(2,1)}, f32[8,128]{1,0:T(8,128)S(1)}) custom-call(bf16[384,2048]{1,0:T(8,128)(2,1)S(1)} %get-tuple-element.105.query_ref, bf16[384,2048]{1,0:T(8,128)(2,1)S(1)} %get-tuple-element.80.keys_ref, bf16[384,2048]{1,0:T(8,128)(2,1)S(1)} %get-tuple-element.79.value_ref, bf16[2048,128]{1,0:T(8,128)(2,1)S(1)} %get-tuple-element.84.high_ref, ...), custom_call_target="tpu_custom_call" | custom-call | flops 2415919104 | bytes 6291456 | tf_op jit(solution)/shard_map/attended/pallas_call | solution.py:74
  114.4 3.8 %collective-permute-done.25.got_ref = bf16[2048,128]{1,0:T(8,128)(2,1)S(1)} collective-permute-done((bf16[2048,128]{1,0:T(8,128)(2,1)S(1)}, bf16[2048,128]{1,0:T(8,128)(2,1)S(1)}, u32[]{:S(2)}, u32[]{:S(2)}) %collective-permute-start.25) | collective-permute-done | bytes 524320 | tf_op jit(solution)/shard_map/ppermute | solution.py:605
  118.3 3.1 %collective-permute-start.26 = (bf16[2048,128]{1,0:T(8,128)(2,1)S(1)}, bf16[2048,128]{1,0:T(8,128)(2,1)S(1)}, u32[]{:S(2)}, u32[]{:S(2)}) collective-permute-start(bf16[2048,128]{1,0:T(8,128)(2,1)S(1)} %message.3), channel_id=1, source_target_pairs={{4,12},{12,4},{16,0},{20,28},{24,8},{28,20},{5,13},{13,5},{17,1},{... | collective-permute-start | bytes 1572872 | tf_op jit(solution)/shard_map/ppermute | solution.py:618
  121.5 6.9 %inner.1 = (f32[384,2048]{1,0:T(8,128)S(1)}, f32[384,2048]{1,0:T(8,128)S(1)}, f32[8,128]{1,0:T(8,128)S(1)}) custom-call(bf16[384,2048]{1,0:T(8,128)(2,1)S(1)} %get-tuple-element.105.query_ref, bf16[384,2048]{1,0:T(8,128)(2,1)S(1)} %get-tuple-element.80.keys_ref, bf16[384,2048]{1,0:T(8,128)(2,1)S(1)} %get-tuple-element.79.value_ref, ...), custom_call_target="tpu_custom_call" | custom-call | flops 3623878656 | bytes 12582912 | tf_op jit(solution)/shard_map/inner/pallas_call | solution.py:74
  128.8 1.8 %collective-permute-start.27 = (f32[2048,128]{1,0:T(8,128)S(1)}, f32[2048,128]{1,0:T(8,128)S(1)}, u32[]{:S(2)}, u32[]{:S(2)}) collective-permute-start(f32[2048,128]{1,0:T(8,128)S(1)} %get-tuple-element.117), channel_id=1, source_target_pairs={{0,4},{4,0},{1,5},{5,1},{2,6},{6,2},{3,7},{7,3},{8,12},{12,8},{9,1... | collective-permute-start | bytes 3145736 | tf_op jit(solution)/shard_map/ppermute | solution.py:631
  130.6 1.9 %grad_tokens.3 = (bf16[384,4096]{1,0:T(8,128)(2,1)}, f32[8,128]{1,0:T(8,128)}) custom-call(bf16[128,2048]{1,0:T(8,128)(2,1)S(1)} %join.9.refs_0_, bf16[128,2048]{1,0:T(8,128)(2,1)S(1)} %collective-permute-done.24.refs_1_, bf16[384,2048]{1,0:T(8,128)(2,1)S(1)} %get-tuple-element.86.refs_2_.refs_4_, ...), custom_call_target="tpu_custom_call", output_to_operand_aliasing={{0}: (3, {})} | custom-call | flops 402653184 | tf_op jit(solution)/shard_map/grad_tokens/pallas_call | solution.py:74
  133.1 3.5 %outer.1 = (bf16[384,2048]{1,0:T(8,128)(2,1)}, bf16[384,2048]{1,0:T(8,128)(2,1)}) custom-call(f32[384,2048]{1,0:T(8,128)S(1)} %get-tuple-element.109.key_ref, f32[384,2048]{1,0:T(8,128)S(1)} %get-tuple-element.110.val_ref, bf16[384,2048]{1,0:T(8,128)(2,1)S(1)} %get-tuple-element.80.keys_ref, bf16[384,2048]{1,0:T(8,128)(2,1)S(1)} %get-tuple-element.79.value_ref, ...), custom_call_target="tpu_custom_call" | custom-call | flops 805306368 | bytes 15728640 | tf_op jit(solution)/shard_map/outer/pallas_call | solution.py:74
  (55 shorter events, 20.5 us)
Async XLA Ops:
  0.6 14.1 %collective-permute-start = (bf16[128,2048]{1,0:T(8,128)(2,1)}, bf16[128,2048]{1,0:T(8,128)(2,1)S(1)}, u32[]{:S(2)}, u32[]{:S(2)}) collective-permute-start(bf16[128,2048]{1,0:T(8,128)(2,1)} %refs_0_.1), channel_id=1, source_target_pairs={{0,1},{1,0},{2,3},{3,2},{4,5},{5,4},{6,7},{7,6},{8,9},{9,8},{10,11... | collective-permute-start | bytes 1572872 | tf_op jit(solution)/shard_map/ppermute | solution.py:712
  2.8 11.9 %collective-permute-start.1 = (bf16[128,2048]{1,0:T(8,128)(2,1)}, bf16[128,2048]{1,0:T(8,128)(2,1)S(1)}, u32[]{:S(2)}, u32[]{:S(2)}) collective-permute-start(bf16[128,2048]{1,0:T(8,128)(2,1)} %refs_0_.1), channel_id=1, source_target_pairs={{1,2},{2,1},{5,6},{6,5},{9,10},{10,9},{13,14},{14,13},{17,18},{18,... | collective-permute-start | bytes 1572872 | tf_op jit(solution)/shard_map/ppermute | solution.py:712
  3.5 11.2 %collective-permute-start.2 = (bf16[128,2048]{1,0:T(8,128)(2,1)}, bf16[128,2048]{1,0:T(8,128)(2,1)S(1)}, u32[]{:S(2)}, u32[]{:S(2)}) collective-permute-start(bf16[128,2048]{1,0:T(8,128)(2,1)} %refs_0_.1), channel_id=1, source_target_pairs={{0,8},{4,20},{8,0},{12,28},{16,24},{20,4},{24,16},{28,12},{1,9},{5... | collective-permute-start | bytes 1572872 | tf_op jit(solution)/shard_map/ppermute | solution.py:715
  4.8 14.0 %collective-permute-start.3 = (bf16[128,2048]{1,0:T(8,128)(2,1)}, bf16[128,2048]{1,0:T(8,128)(2,1)S(1)}, u32[]{:S(2)}, u32[]{:S(2)}) collective-permute-start(bf16[128,2048]{1,0:T(8,128)(2,1)} %refs_0_.1), channel_id=1, source_target_pairs={{0,16},{4,12},{8,24},{12,4},{16,0},{20,28},{24,8},{28,20},{1,17},{... | collective-permute-start | bytes 1572872 | tf_op jit(solution)/shard_map/ppermute | solution.py:715
  18.8 23.0 %copy-start = (bf16[128,2048]{1,0:T(8,128)(2,1)S(1)}, bf16[128,2048]{1,0:T(8,128)(2,1)}, u32[]{:S(2)}) copy-start(bf16[128,2048]{1,0:T(8,128)(2,1)} %refs_0_.1) | copy-start | bytes 1572868
  18.8 11.3 %collective-permute-start.5 = (bf16[128,2048]{1,0:T(8,128)(2,1)S(1)}, bf16[128,2048]{1,0:T(8,128)(2,1)S(1)}, u32[]{:S(2)}, u32[]{:S(2)}) collective-permute-start(bf16[128,2048]{1,0:T(8,128)(2,1)S(1)} %get-tuple-element.66.refs_0_), channel_id=1, source_target_pairs={{0,8},{4,20},{8,0},{12,28},{16,24},{20,4},{24,16},{28,12},{1,9},{5... | collective-permute-start | bytes 1572872 | tf_op jit(solution)/shard_map/ppermute | solution.py:715
  18.8 13.1 %collective-permute-start.6 = (bf16[128,2048]{1,0:T(8,128)(2,1)S(1)}, bf16[128,2048]{1,0:T(8,128)(2,1)S(1)}, u32[]{:S(2)}, u32[]{:S(2)}) collective-permute-start(bf16[128,2048]{1,0:T(8,128)(2,1)S(1)} %get-tuple-element.66.refs_0_), channel_id=1, source_target_pairs={{0,16},{4,12},{8,24},{12,4},{16,0},{20,28},{24,8},{28,20},{1,17},{... | collective-permute-start | bytes 1572872 | tf_op jit(solution)/shard_map/ppermute | solution.py:715
  20.0 11.9 %collective-permute-start.7 = (bf16[128,2048]{1,0:T(8,128)(2,1)S(1)}, bf16[128,2048]{1,0:T(8,128)(2,1)S(1)}, u32[]{:S(2)}, u32[]{:S(2)}) collective-permute-start(bf16[128,2048]{1,0:T(8,128)(2,1)S(1)} %get-tuple-element.66.refs_0_), channel_id=1, source_target_pairs={{1,2},{2,1},{5,6},{6,5},{9,10},{10,9},{13,14},{14,13},{17,18},{18,... | collective-permute-start | bytes 1572872 | tf_op jit(solution)/shard_map/ppermute | solution.py:712
  20.7 17.7 %collective-permute-start.4 = (bf16[128,2048]{1,0:T(8,128)(2,1)S(1)}, bf16[128,2048]{1,0:T(8,128)(2,1)S(1)}, u32[]{:S(2)}, u32[]{:S(2)}) collective-permute-start(bf16[128,2048]{1,0:T(8,128)(2,1)S(1)} %get-tuple-element.65.refs_1_), channel_id=1, source_target_pairs={{0,16},{4,12},{8,24},{12,4},{16,0},{20,28},{24,8},{28,20},{1,17},{... | collective-permute-start | bytes 1572872 | tf_op jit(solution)/shard_map/ppermute | solution.py:718
  21.0 17.3 %collective-permute-start.8 = (bf16[128,2048]{1,0:T(8,128)(2,1)S(1)}, bf16[128,2048]{1,0:T(8,128)(2,1)S(1)}, u32[]{:S(2)}, u32[]{:S(2)}) collective-permute-start(bf16[128,2048]{1,0:T(8,128)(2,1)S(1)} %get-tuple-element.67.inner_ref), channel_id=1, source_target_pairs={{1,0},{2,3},{5,4},{6,7},{9,8},{10,11},{13,12},{14,15},{17,16},{18,... | collective-permute-start | bytes 1572872 | tf_op jit(solution)/shard_map/ppermute | solution.py:712
  30.2 11.6 %collective-permute-start.9 = (bf16[2048,128]{1,0:T(8,128)(2,1)S(1)}, bf16[2048,128]{1,0:T(8,128)(2,1)S(1)}, u32[]{:S(2)}, u32[]{:S(2)}) collective-permute-start(bf16[2048,128]{1,0:T(8,128)(2,1)S(1)} %get-tuple-element.68), channel_id=1, source_target_pairs={{0,8},{4,20},{8,0},{12,28},{16,24},{24,16},{1,9},{5,21},{9,1},{13,... | collective-permute-start | bytes 1572872 | tf_op jit(solution)/shard_map/ppermute | solution.py:605
  42.0 8.8 %collective-permute-start.15 = (bf16[512,2048]{1,0:T(8,128)(2,1)S(1)}, bf16[512,2048]{1,0:T(8,128)(2,1)S(1)}, u32[]{:S(2)}, u32[]{:S(2)}) collective-permute-start(bf16[512,2048]{1,0:T(8,128)(2,1)S(1)} %pack.4.refs_0_), channel_id=1, source_target_pairs={{0,4},{4,0},{1,5},{5,1},{2,6},{6,2},{3,7},{7,3},{8,12},{12,8},{9,1... | collective-permute-start | bytes 6291464 | tf_op jit(solution)/shard_map/ppermute | solution.py:668
  45.5 12.0 %collective-permute-start.11 = (bf16[128,2048]{1,0:T(8,128)(2,1)S(1)}, bf16[128,2048]{1,0:T(8,128)(2,1)S(1)}, u32[]{:S(2)}, u32[]{:S(2)}) collective-permute-start(bf16[128,2048]{1,0:T(8,128)(2,1)S(1)} %choose.2.refs_0_), channel_id=1, source_target_pairs={{0,8},{4,20},{8,0},{12,28},{16,24},{20,4},{24,16},{28,12},{1,9},{5... | collective-permute-start | bytes 1572872 | tf_op jit(solution)/shard_map/ppermute | solution.py:715
  46.0 13.9 %collective-permute-start.12 = (bf16[128,2048]{1,0:T(8,128)(2,1)S(1)}, bf16[128,2048]{1,0:T(8,128)(2,1)S(1)}, u32[]{:S(2)}, u32[]{:S(2)}) collective-permute-start(bf16[128,2048]{1,0:T(8,128)(2,1)S(1)} %choose.2.refs_0_), channel_id=1, source_target_pairs={{0,16},{4,12},{8,24},{12,4},{16,0},{20,28},{24,8},{28,20},{1,17},{... | collective-permute-start | bytes 1572872 | tf_op jit(solution)/shard_map/ppermute | solution.py:715
  47.3 18.2 %collective-permute-start.14 = (bf16[2048,128]{1,0:T(8,128)(2,1)S(1)}, bf16[2048,128]{1,0:T(8,128)(2,1)S(1)}, u32[]{:S(2)}, u32[]{:S(2)}) collective-permute-start(bf16[2048,128]{1,0:T(8,128)(2,1)S(1)} %message.2), channel_id=1, source_target_pairs={{0,16},{4,12},{8,24},{12,4},{20,28},{28,20},{1,17},{5,13},{9,25},{... | collective-permute-start | bytes 1572872 | tf_op jit(solution)/shard_map/ppermute | solution.py:618
  49.5 21.4 %collective-permute-start.10 = (bf16[128,2048]{1,0:T(8,128)(2,1)S(1)}, bf16[128,2048]{1,0:T(8,128)(2,1)S(1)}, u32[]{:S(2)}, u32[]{:S(2)}) collective-permute-start(bf16[128,2048]{1,0:T(8,128)(2,1)S(1)} %get-tuple-element.70.refs_1_), channel_id=1, source_target_pairs={{0,16},{4,12},{8,24},{12,4},{16,0},{20,28},{24,8},{28,20},{1,17},{... | collective-permute-start | bytes 1572872 | tf_op jit(solution)/shard_map/ppermute | solution.py:718
  50.8 20.1 %collective-permute-start.13 = (bf16[128,2048]{1,0:T(8,128)(2,1)S(1)}, bf16[128,2048]{1,0:T(8,128)(2,1)S(1)}, u32[]{:S(2)}, u32[]{:S(2)}) collective-permute-start(bf16[128,2048]{1,0:T(8,128)(2,1)S(1)} %get-tuple-element.69.inner_ref), channel_id=1, source_target_pairs={{1,0},{2,3},{5,4},{6,7},{9,8},{10,11},{13,12},{14,15},{17,16},{18,... | collective-permute-start | bytes 1572872 | tf_op jit(solution)/shard_map/ppermute | solution.py:712
  71.1 14.4 %collective-permute-start.20 = (bf16[512,2048]{1,0:T(8,128)(2,1)S(1)}, bf16[512,2048]{1,0:T(8,128)(2,1)S(1)}, u32[]{:S(2)}, u32[]{:S(2)}) collective-permute-start(bf16[512,2048]{1,0:T(8,128)(2,1)S(1)} %pack.5.refs_0_), channel_id=1, source_target_pairs={{0,4},{4,0},{1,5},{5,1},{2,6},{6,2},{3,7},{7,3},{8,12},{12,8},{9,1... | collective-permute-start | bytes 6291464 | tf_op jit(solution)/shard_map/ppermute | solution.py:668
  71.4 5.4 %collective-permute-start.19 = (f32[2048,128]{1,0:T(8,128)S(1)}, f32[2048,128]{1,0:T(8,128)S(1)}, u32[]{:S(2)}, u32[]{:S(2)}) collective-permute-start(f32[2048,128]{1,0:T(8,128)S(1)} %get-tuple-element.83), channel_id=1, source_target_pairs={{0,4},{4,0},{1,5},{5,1},{2,6},{6,2},{3,7},{7,3},{8,12},{12,8},{9,1... | collective-permute-start | bytes 3145736 | tf_op jit(solution)/shard_map/ppermute | solution.py:631
  72.0 17.4 %collective-permute-start.17 = (bf16[128,2048]{1,0:T(8,128)(2,1)S(1)}, bf16[128,2048]{1,0:T(8,128)(2,1)S(1)}, u32[]{:S(2)}, u32[]{:S(2)}) collective-permute-start(bf16[128,2048]{1,0:T(8,128)(2,1)S(1)} %choose.3.refs_0_), channel_id=1, source_target_pairs={{0,8},{4,20},{8,0},{12,28},{16,24},{20,4},{24,16},{28,12},{1,9},{5... | collective-permute-start | bytes 1572872 | tf_op jit(solution)/shard_map/ppermute | solution.py:715
  72.5 16.8 %collective-permute-start.18 = (bf16[128,2048]{1,0:T(8,128)(2,1)S(1)}, bf16[128,2048]{1,0:T(8,128)(2,1)S(1)}, u32[]{:S(2)}, u32[]{:S(2)}) collective-permute-start(bf16[128,2048]{1,0:T(8,128)(2,1)S(1)} %choose.3.refs_0_), channel_id=1, source_target_pairs={{0,16},{4,12},{8,24},{12,4},{16,0},{20,28},{24,8},{28,20},{1,17},{... | collective-permute-start | bytes 1572872 | tf_op jit(solution)/shard_map/ppermute | solution.py:715
  73.7 18.1 %collective-permute-start.16 = (bf16[128,2048]{1,0:T(8,128)(2,1)S(1)}, bf16[128,2048]{1,0:T(8,128)(2,1)S(1)}, u32[]{:S(2)}, u32[]{:S(2)}) collective-permute-start(bf16[128,2048]{1,0:T(8,128)(2,1)S(1)} %get-tuple-element.78.refs_1_), channel_id=1, source_target_pairs={{0,16},{4,12},{8,24},{12,4},{16,0},{20,28},{24,8},{28,20},{1,17},{... | collective-permute-start | bytes 1572872 | tf_op jit(solution)/shard_map/ppermute | solution.py:718
  92.0 4.2 %collective-permute-start.22 = (bf16[512,2048]{1,0:T(8,128)(2,1)S(1)}, bf16[512,2048]{1,0:T(8,128)(2,1)S(1)}, u32[]{:S(2)}, u32[]{:S(2)}) collective-permute-start(bf16[512,2048]{1,0:T(8,128)(2,1)S(1)} %pack.7.refs_0_), channel_id=1, source_target_pairs={{0,4},{4,0},{1,5},{5,1},{2,6},{6,2},{3,7},{7,3},{8,12},{12,8},{9,1... | collective-permute-start | bytes 6291464 | tf_op jit(solution)/shard_map/ppermute | solution.py:668
  92.6 9.8 %collective-permute-start.21 = (bf16[384,2048]{1,0:T(8,128)(2,1)S(1)}, bf16[384,2048]{1,0:T(8,128)(2,1)S(1)}, u32[]{:S(2)}, u32[]{:S(2)}) collective-permute-start(bf16[384,2048]{1,0:T(8,128)(2,1)S(1)} %pack.6.refs_0_), channel_id=1, source_target_pairs={{0,4},{4,0},{1,5},{5,1},{2,6},{6,2},{3,7},{7,3},{8,12},{12,8},{9,1... | collective-permute-start | bytes 4718600 | tf_op jit(solution)/shard_map/ppermute | solution.py:668
  93.0 8.3 %collective-permute-start.23 = (bf16[128,2048]{1,0:T(8,128)(2,1)S(1)}, bf16[128,2048]{1,0:T(8,128)(2,1)S(1)}, u32[]{:S(2)}, u32[]{:S(2)}) collective-permute-start(bf16[128,2048]{1,0:T(8,128)(2,1)S(1)} %get-tuple-element.93.refs_1_), channel_id=1, source_target_pairs={{0,16},{4,12},{8,24},{12,4},{16,0},{20,28},{24,8},{28,20},{1,17},{... | collective-permute-start | bytes 1572872 | tf_op jit(solution)/shard_map/ppermute | solution.py:718
  101.3 5.0 %collective-permute-start.24 = (bf16[128,2048]{1,0:T(8,128)(2,1)S(1)}, bf16[128,2048]{1,0:T(8,128)(2,1)S(1)}, u32[]{:S(2)}, u32[]{:S(2)}) collective-permute-start(bf16[128,2048]{1,0:T(8,128)(2,1)S(1)} %join.9.refs_0_), channel_id=1, source_target_pairs={{0,4},{4,0},{1,5},{5,1},{2,6},{6,2},{3,7},{7,3},{8,12},{12,8},{9,1... | collective-permute-start | bytes 1572872 | tf_op jit(solution)/shard_map/ppermute | solution.py:709
  108.0 10.2 %collective-permute-start.25 = (bf16[2048,128]{1,0:T(8,128)(2,1)S(1)}, bf16[2048,128]{1,0:T(8,128)(2,1)S(1)}, u32[]{:S(2)}, u32[]{:S(2)}) collective-permute-start(bf16[2048,128]{1,0:T(8,128)(2,1)S(1)} %get-tuple-element.112), channel_id=1, source_target_pairs={{0,8},{8,0},{16,24},{20,4},{24,16},{28,12},{1,9},{9,1},{17,25},{21... | collective-permute-start | bytes 1572872 | tf_op jit(solution)/shard_map/ppermute | solution.py:605
  118.3 10.2 %collective-permute-start.26 = (bf16[2048,128]{1,0:T(8,128)(2,1)S(1)}, bf16[2048,128]{1,0:T(8,128)(2,1)S(1)}, u32[]{:S(2)}, u32[]{:S(2)}) collective-permute-start(bf16[2048,128]{1,0:T(8,128)(2,1)S(1)} %message.3), channel_id=1, source_target_pairs={{4,12},{12,4},{16,0},{20,28},{24,8},{28,20},{5,13},{13,5},{17,1},{... | collective-permute-start | bytes 1572872 | tf_op jit(solution)/shard_map/ppermute | solution.py:618
  128.8 4.1 %collective-permute-start.27 = (f32[2048,128]{1,0:T(8,128)S(1)}, f32[2048,128]{1,0:T(8,128)S(1)}, u32[]{:S(2)}, u32[]{:S(2)}) collective-permute-start(f32[2048,128]{1,0:T(8,128)S(1)} %get-tuple-element.117), channel_id=1, source_target_pairs={{0,4},{4,0},{1,5},{5,1},{2,6},{6,2},{3,7},{7,3},{8,12},{12,8},{9,1... | collective-permute-start | bytes 3145736 | tf_op jit(solution)/shard_map/ppermute | solution.py:631

commit v7 on v5

--- a/solution.py
+++ b/solution.py
@@ -98,12 +98,22 @@
     chip, core, layer = (lax.axis_index(name) for name in ("chip", "core", "dp"))
     upper = layer < 2
     layers = [layer, layer ^ 1, jnp.where(upper, 2, 1), jnp.where(upper, 3, 0)]
-    return [
-        ((chip ^ flip) * 2 + side) * 4 + one
-        for one in layers
-        for side in (core, 1 - core)
-        for flip in crossed(side)
-    ]
+
+    def some(*arrivals):
+        return [
+            ((chip ^ crossed(side)[flip]) * 2 + side) * 4 + layers[one]
+            for side in (core, 1 - core)
+            for one, flips in arrivals
+            for flip in flips
+        ]
+
+    three = (0, 1, 2)
+    return (
+        some((0, (0, 1, 2, 3)), (1, three))
+        + some((2, three))
+        + some((1, (3,)), (2, (3,)), (3, three))
+        + some((3, (3,)))
+    )
 
 
 def piece_columns(place):
@@ -570,6 +580,11 @@
     return keep
 
 
+def low_bit(reverse):
+    chip = lax.axis_index("chip")
+    return 1 - chip % 2 if reverse else chip % 2
+
+
 def half_rows(array_ref, core):
     half = array_ref.shape[0] // 2
     return array_ref[pl.ds(pl.multiple_of(core * half, half), half), :]
@@ -580,11 +595,6 @@
     both = half_rows(own_ref, core) + half_rows(sibling_ref, core).astype(f32)
     both_ref[...] = both
     sent_ref[...] = both.astype(bf16)
-
-
-def low_bit(reverse):
-    chip = lax.axis_index("chip")
-    return 1 - chip % 2 if reverse else chip % 2
 
 
 def message_kernel(reverse, got_ref, both_ref, *refs):
@@ -611,35 +621,35 @@
         low_ref[rows, :] = (whole - high.astype(f32)).astype(bf16)
 
 
-def scan_first(own, sent, reverse, others=()):
-    rows = own.shape[0]
-    half = (rows // 2, HEAD)
+def send_first(own, sent, reverse):
+    half = (own.shape[0] // 2, HEAD)
     sibling = lax.ppermute(sent, "core", SWAP)
     both, sent = kernel_call(
         both_kernel, "VV", (own, sibling), "VV", [(half, f32), (half, bf16)], "both", (0, 0)
     )
-    got = lax.ppermute(sent, CTX, links(1, upward(reverse)))
+    return sibling, both, lax.ppermute(sent, CTX, links(1, upward(reverse)))
+
+
+def send_second(got, both, reverse, others=()):
     (message,) = kernel_call(
         functools.partial(message_kernel, reverse),
         "VV" + "A" * len(others),
         (got, both, *others),
         "V",
-        [(half, bf16)],
+        [(both.shape, bf16)],
         "message",
         (0, 0),
     )
-    return message, got, sibling
-
-
-def scan_second(message, got, sibling, reverse, others=()):
-    half, full = message.shape, sibling.shape
-    more = lax.ppermute(message, CTX, links(2, upward(reverse)))
+    return lax.ppermute(message, CTX, links(2, upward(reverse)))
+
+
+def add_up(got, more, sibling, reverse, others=()):
     (state,) = kernel_call(
         functools.partial(state_kernel, reverse),
         "VV" + "A" * len(others),
         (got, more, *others),
         "V",
-        [(half, f32)],
+        [(got.shape, f32)],
         "state",
         (0, 0),
     )
@@ -649,7 +659,7 @@
         "VVV",
         (state, other, sibling),
         "VV",
-        [(full, bf16)] * 2,
+        [(sibling.shape, bf16)] * 2,
         "whole",
         (0, 0),
     )
@@ -659,6 +669,34 @@
     whole = lax.all_gather(q_weight, ("chip", "core", "dp"), axis=0, tiled=True)
     cut = whole.shape[0] // (2 * PIECE) * PIECE
     return [whole[:cut], whole[cut:]]
+
+
+def pack_kernel(*refs):
+    *arrays, out_ref, sems = refs
+    copies = Copies(sems)
+    rows = out_ref.shape[0] // len(arrays)
+    going = [
+        copies.start(array, out_ref.at[pl.ds(at * rows, rows), :])
+        for at, array in enumerate(arrays)
+    ]
+    for copy in going:
+        copy.wait()
+
+
+def pack(*arrays):
+    rows, total = arrays[0].shape
+    number = len(arrays)
+    (made,) = kernel_call(
+        pack_kernel,
+        "A" * number,
+        arrays,
+        "V",
+        [((number * rows, total), arrays[0].dtype)],
+        "pack",
+        (0, 0),
+        [pltpu.SemaphoreType.DMA((number,))],
+    )
+    return [made, lax.ppermute(made, "core", SWAP)]
 
 
 def choose_kernel(inner_ref, end_ref, out_ref, sem):
@@ -720,9 +758,7 @@
         near = along(q_weight, ends)
         mid = along(q_weight, middle)
         first_0, second_0 = cross(q_weight)
-        other_0 = sibling(q_weight)
         near, mid, first_0, second_0, sent = join([near, mid, first_0, second_0, sent])
-        message, *rest = scan_first(own, sent, False)
     else:
         arrived = gather_any(q_weight)
         high, low = halves(scan_any(own, sent, chips * 2, False))
@@ -732,46 +768,41 @@
         first_1, second_1 = cross(near)
         far = along(near, middle)
         mid_out = along(mid, outward)
-        third_0, first_1, second_1, far, mid_out = join(
-            [third_0, first_1, second_1, far, mid_out]
+        twin, both, got = send_first(own, sent, False)
+        third_0, first_1, second_1, far, mid_out, got = join(
+            [third_0, first_1, second_1, far, mid_out, got]
         )
-        third_1 = onward(first_1)
+        more = send_second(got, both, False)
         next_layer = choose(mid, mid_out)
         first_2, second_2 = cross(next_layer)
         far_out = along(far, outward)
-        own_blocks = [q_weight, first_0, second_0, third_0, other_0]
-        own_blocks += [sibling(one) for one in own_blocks[1:4]]
-        partial, _, own_mark = products_call(special, 0, own_blocks, tokens)
-        third_1, first_2, second_2, far_out = join(
-            [third_1, first_2, second_2, far_out], [own_mark]
+        early = pack(q_weight, first_0, second_0, third_0, near, first_1, second_1)
+        partial, _, mark = products_call(special, 0, early, tokens)
+        third_0, first_2, second_2, far_out, more = join(
+            [third_0, first_2, second_2, far_out, more], [mark]
         )
+        third_1 = along(third_0, ends)
         third_2 = onward(first_2)
         last_layer = choose(far, far_out)
         first_3, second_3 = cross(last_layer)
-
-        def whole(*mine):
-            return list(mine) + [sibling(one) for one in mine]
-
-        high, low = scan_second(message, *rest, False)
+        high, low = add_up(got, more, twin, False)
         masked, q_mask, cotangent, _ = masked_call(
             factor, cotangent, q_spikes, values, keys, high, low
         )
         _, grad, mark_0 = products_call(
-            special, 0, own_blocks, tokens, masked=masked, project=False
+            special, 0, early, tokens, masked=masked, project=False
         )
-        blocks = whole(near, first_1, second_1, third_1)
-        partial, grad, mark_1 = products_call(
-            special, 8, blocks, tokens, partial, masked, grad
+        blocks = pack(next_layer, first_2, second_2)
+        partial, grad, mark_1 = products_call(special, 14, blocks, tokens, partial, masked, grad)
+        third_1, third_2, first_3, second_3 = join(
+            [third_1, third_2, first_3, second_3], [mark_0, mark_1]
         )
-        third_2, first_3, second_3 = join([third_2, first_3, second_3], [mark_0, mark_1])
         third_3 = onward(first_3)
-        blocks = whole(next_layer, first_2, second_2, third_2)
-        partial, grad, mark = products_call(
-            special, 16, blocks, tokens, partial, masked, grad
-        )
+        blocks = pack(third_1, third_2, last_layer, first_3, second_3)
+        partial, grad, mark = products_call(special, 20, blocks, tokens, partial, masked, grad)
         third_3, = join([third_3], [mark])
-        late = whole(last_layer, first_3, second_3, third_3)
-        start = 24
+        late = [third_3, sibling(third_3)]
+        start = 30
     else:
         masked, q_mask, cotangent, _ = masked_call(
             factor, cotangent, q_spikes, values, keys, high, low
@@ -783,8 +814,9 @@
     attended, attended_mark = attend_call(factor, queries, keys, values, high, low)
     key_part, value_part, inner_mark = inner_call(queries, keys, values, cotangent)
     if special:
-        message, *rest = scan_first(own, sent, True, [attended_mark])
-        adjoint = scan_second(message, *rest, True, [inner_mark])
+        twin, both, got = send_first(own, sent, True)
+        more = send_second(got, both, True, [attended_mark])
+        adjoint = add_up(got, more, twin, True, [inner_mark])
     else:
         adjoint = halves(scan_any(own, sent, chips * 2, True))
     _, grad_tokens, _ = products_call(

time: 136 us -> 123 us (0.904)
  waiting for transfers between devices: 50.9 us -> 43.7 us
  starting transfers between devices: 37.5 us -> 31.3 us
    ppermute x16 -> x1, starting transfers between devices: 9.59 us -> 0.43 us  [sibling(): return lax.ppermute(array, 'core', SWAP)]
    ppermute x5 -> x6, waiting for transfers between devices: 14.3 us -> 5.82 us  [along(): return lax.ppermute(array, 'dp', pairs)]
    ppermute x4, waiting for transfers between devices: 8.2 us -> 0.98 us  [cross(): lax.ppermute(array, CTX, links(1))]
    ppermute x4, waiting for transfers between devices: 4.05 us -> 9.94 us  [cross(): lax.ppermute(array, CTX, links(2))]
    ppermute x8 -> x11, starting transfers between devices: 9.18 us -> 13.9 us  [the longest x2 5.16 us: send_second(): return lax.ppermute(message, CTX, links(2, upward(reverse)))]
    ppermute x8 -> x11, waiting for transfers between devices: 13.5 us -> 16.3 us  [the longest x2 8.28 us: send_second(): return lax.ppermute(message, CTX, links(2, upward(reverse)))]
    ppermute x4, starting transfers between devices: 5.1 us -> 3.16 us  [cross(): lax.ppermute(array, CTX, links(1))]
    ppermute x5 -> x6, starting transfers between devices: 6.12 us -> 7.6 us  [along(): return lax.ppermute(array, 'dp', pairs)]
  transfers between devices with their start and end apart: 41 -> 29, of which waited for: 13 -> 16; matrix products, arithmetic and copies ran while one was open for 0% -> 0% of each run, Pallas kernels for 28% -> 32%
where the time goes in v7:
time: 123 us; the launch traced here: 122 us
  Pallas kernels  46.1 us (37%)
  waiting for transfers between devices  43.7 us (36%)
  starting transfers between devices  31.3 us (25%)
    pallas_call x29, Pallas kernels, kernel_call(): made(*[holds[place](one) if place in holds else one for place, one in zip...  46.1 us
    ppermute x4, waiting for transfers between devices, cross(): lax.ppermute(array, CTX, links(2))  9.94 us
    ppermute x3, waiting for transfers between devices, onward(): return lax.ppermute(array, CTX, links(2))  9.09 us
    ppermute x2, waiting for transfers between devices, send_second(): return lax.ppermute(message, CTX, links(2, upward(reverse)))  8.28 us
    ppermute x6, starting transfers between devices, along(): return lax.ppermute(array, 'dp', pairs)  7.6 us
    ppermute x6, waiting for transfers between devices, along(): return lax.ppermute(array, 'dp', pairs)  5.82 us
    ppermute x2, starting transfers between devices, send_second(): return lax.ppermute(message, CTX, links(2, upward(reverse)))  5.16 us
    ppermute x3, starting transfers between devices, pack(): return [made, lax.ppermute(made, 'core', SWAP)]  4.75 us
  transfers between devices with their start and end apart: 29, of which 16 were waited for; matrix products, arithmetic and copies ran while one was open for 0% of the time, Pallas kernels for 32%

profile of v7, /device:TPU:1, one launch (start us, length us, event | category | flops | bytes accessed | tf_op | source)
XLA Modules:
  0.0 122.2 jit_solution(9808393569701665738)
XLA Ops:
  0.6 2.2 %collective-permute-start = (bf16[128,2048]{1,0:T(8,128)(2,1)}, bf16[128,2048]{1,0:T(8,128)(2,1)S(1)}, u32[]{:S(2)}, u32[]{:S(2)}) collective-permute-start(bf16[128,2048]{1,0:T(8,128)(2,1)} %refs_0_.1), channel_id=1, source_target_pairs={{0,1},{1,0},{2,3},{3,2},{4,5},{5,4},{6,7},{7,6},{8,9},{9,8},{10,11... | collective-permute-start | bytes 1572872 | tf_op jit(solution)/shard_map/ppermute | solution.py:743
  3.5 1.3 %collective-permute-start.2 = (bf16[128,2048]{1,0:T(8,128)(2,1)}, bf16[128,2048]{1,0:T(8,128)(2,1)S(1)}, u32[]{:S(2)}, u32[]{:S(2)}) collective-permute-start(bf16[128,2048]{1,0:T(8,128)(2,1)} %refs_0_.1), channel_id=1, source_target_pairs={{0,8},{4,20},{8,0},{12,28},{16,24},{20,4},{24,16},{28,12},{1,9},{5... | collective-permute-start | bytes 1572872 | tf_op jit(solution)/shard_map/ppermute | solution.py:746
  6.0 4.2 %own_memory.1 = (bf16[384,2048]{1,0:T(8,128)(2,1)S(1)}, bf16[384,2048]{1,0:T(8,128)(2,1)S(1)}, bf16[384,2048]{1,0:T(8,128)(2,1)S(1)}, f32[2048,128]{1,0:T(8,128)...) custom-call(bf16[384,2048]{1,0:T(8,128)(2,1)} %bitcast.13, s32[384,2048]{1,0:T(8,128)} %bitcast.11, ...), custom_call_target="tpu_custom_call" | custom-call | flops 201326592 | bytes 9437184 | tf_op jit(solution)/shard_map/own_memory/pallas_call | solution.py:74
  10.2 4.5 %collective-permute-done.refs_0_ = bf16[128,2048]{1,0:T(8,128)(2,1)S(1)} collective-permute-done((bf16[128,2048]{1,0:T(8,128)(2,1)}, bf16[128,2048]{1,0:T(8,128)(2,1)S(1)}, u32[]{:S(2)}, u32[]{:S(2)}) %collective-permute-start) | collective-permute-done | bytes 524320 | tf_op jit(solution)/shard_map/ppermute | solution.py:743
  14.8 4.0 %collective-permute-done.3.refs_3_ = bf16[128,2048]{1,0:T(8,128)(2,1)S(1)} collective-permute-done((bf16[128,2048]{1,0:T(8,128)(2,1)}, bf16[128,2048]{1,0:T(8,128)(2,1)S(1)}, u32[]{:S(2)}, u32[]{:S(2)}) %collective-permute-start.3) | collective-permute-done | bytes 524320 | tf_op jit(solution)/shard_map/ppermute | solution.py:746
  21.8 1.3 %collective-permute-start.8 = (bf16[128,2048]{1,0:T(8,128)(2,1)S(1)}, bf16[128,2048]{1,0:T(8,128)(2,1)S(1)}, u32[]{:S(2)}, u32[]{:S(2)}) collective-permute-start(bf16[128,2048]{1,0:T(8,128)(2,1)S(1)} %get-tuple-element.66.inner_ref), channel_id=1, source_target_pairs={{1,0},{2,3},{5,4},{6,7},{9,8},{10,11},{13,12},{14,15},{17,16},{18,... | collective-permute-start | bytes 1572872 | tf_op jit(solution)/shard_map/ppermute | solution.py:743
  23.2 9.1 %collective-permute-done.4.refs_0_ = bf16[128,2048]{1,0:T(8,128)(2,1)S(1)} collective-permute-done((bf16[128,2048]{1,0:T(8,128)(2,1)S(1)}, bf16[128,2048]{1,0:T(8,128)(2,1)S(1)}, u32[]{:S(2)}, u32[]{:S(2)}) %collective-permute-start.4) | collective-permute-done | bytes 524320 | tf_op jit(solution)/shard_map/ppermute | solution.py:749
  32.3 1.3 %collective-permute-start.10 = (bf16[1024,128]{1,0:T(8,128)(2,1)S(1)}, bf16[1024,128]{1,0:T(8,128)(2,1)S(1)}, u32[]{:S(2)}, u32[]{:S(2)}) collective-permute-start(bf16[1024,128]{1,0:T(8,128)(2,1)S(1)} %get-tuple-element.69), channel_id=1, source_target_pairs={{0,8},{4,20},{8,0},{12,28},{16,24},{24,16},{1,9},{5,21},{9,1},{13,... | collective-permute-start | bytes 786440 | tf_op jit(solution)/shard_map/ppermute | solution.py:630
  34.5 4.7 %collective-permute-done.6.refs_2_ = bf16[128,2048]{1,0:T(8,128)(2,1)S(1)} collective-permute-done((bf16[128,2048]{1,0:T(8,128)(2,1)S(1)}, bf16[128,2048]{1,0:T(8,128)(2,1)S(1)}, u32[]{:S(2)}, u32[]{:S(2)}) %collective-permute-start.6) | collective-permute-done | bytes 524320 | tf_op jit(solution)/shard_map/ppermute | solution.py:746
  40.1 2.5 %collective-permute-start.15 = (bf16[896,2048]{1,0:T(8,128)(2,1)S(1)}, bf16[896,2048]{1,0:T(8,128)(2,1)S(1)}, u32[]{:S(2)}, u32[]{:S(2)}) collective-permute-start(bf16[896,2048]{1,0:T(8,128)(2,1)S(1)} %pack.3.refs_0_), channel_id=1, source_target_pairs={{0,4},{4,0},{1,5},{5,1},{2,6},{6,2},{3,7},{7,3},{8,12},{12,8},{9,1... | collective-permute-start | bytes 11010056 | tf_op jit(solution)/shard_map/ppermute | solution.py:699
  44.4 1.3 %collective-permute-start.13 = (bf16[128,2048]{1,0:T(8,128)(2,1)S(1)}, bf16[128,2048]{1,0:T(8,128)(2,1)S(1)}, u32[]{:S(2)}, u32[]{:S(2)}) collective-permute-start(bf16[128,2048]{1,0:T(8,128)(2,1)S(1)} %get-tuple-element.72.inner_ref), channel_id=1, source_target_pairs={{1,0},{2,3},{5,4},{6,7},{9,8},{10,11},{13,12},{14,15},{17,16},{18,... | collective-permute-start | bytes 1572872 | tf_op jit(solution)/shard_map/ppermute | solution.py:743
  45.7 2.4 %collective-permute-start.14 = (bf16[1024,128]{1,0:T(8,128)(2,1)S(1)}, bf16[1024,128]{1,0:T(8,128)(2,1)S(1)}, u32[]{:S(2)}, u32[]{:S(2)}) collective-permute-start(bf16[1024,128]{1,0:T(8,128)(2,1)S(1)} %message.2), channel_id=1, source_target_pairs={{0,16},{4,12},{8,24},{12,4},{20,28},{28,20},{1,17},{5,13},{9,25},{... | collective-permute-start | bytes 786440 | tf_op jit(solution)/shard_map/ppermute | solution.py:643
  48.6 3.0 %project.1 = (f32[384,2048]{1,0:T(8,128)S(1)}, f32[8,128]{1,0:T(8,128)S(1)}) custom-call(bf16[896,2048]{1,0:T(8,128)(2,1)S(1)} %pack.3.refs_0_, bf16[896,2048]{1,0:T(8,128)(2,1)S(1)} %collective-permute-done.15.refs_1_, bf16[384,4096]{1,0:T(8,128)(2,1)S(1)} %get-tuple-element.62.refs_2_.tokens_ref), custom_call_target="tpu_custom_call" | custom-call | flops 2818572288 | tf_op jit(solution)/shard_map/project/pallas_call | solution.py:74
  51.6 8.3 %collective-permute-done.14.refs_4_ = bf16[1024,128]{1,0:T(8,128)(2,1)S(1)} collective-permute-done((bf16[1024,128]{1,0:T(8,128)(2,1)S(1)}, bf16[1024,128]{1,0:T(8,128)(2,1)S(1)}, u32[]{:S(2)}, u32[]{:S(2)}) %collective-permute-start.14) | collective-permute-done | bytes 262176 | tf_op jit(solution)/shard_map/ppermute | solution.py:643
  59.9 1.3 %collective-permute-done.13.refs_3_ = bf16[128,2048]{1,0:T(8,128)(2,1)S(1)} collective-permute-done((bf16[128,2048]{1,0:T(8,128)(2,1)S(1)}, bf16[128,2048]{1,0:T(8,128)(2,1)S(1)}, u32[]{:S(2)}, u32[]{:S(2)}) %collective-permute-start.13) | collective-permute-done | bytes 524320 | tf_op jit(solution)/shard_map/ppermute | solution.py:743
  64.1 1.3 %collective-permute-start.19 = (bf16[128,2048]{1,0:T(8,128)(2,1)S(1)}, bf16[128,2048]{1,0:T(8,128)(2,1)S(1)}, u32[]{:S(2)}, u32[]{:S(2)}) collective-permute-start(bf16[128,2048]{1,0:T(8,128)(2,1)S(1)} %choose.3.refs_2_), channel_id=1, source_target_pairs={{0,16},{4,12},{8,24},{12,4},{16,0},{20,28},{24,8},{28,20},{1,17},{... | collective-permute-start | bytes 1572872 | tf_op jit(solution)/shard_map/ppermute | solution.py:746
  66.3 1.5 %collective-permute-start.16 = (bf16[128,2048]{1,0:T(8,128)(2,1)S(1)}, bf16[128,2048]{1,0:T(8,128)(2,1)S(1)}, u32[]{:S(2)}, u32[]{:S(2)}) collective-permute-start(bf16[128,2048]{1,0:T(8,128)(2,1)S(1)} %get-tuple-element.79), channel_id=1, source_target_pairs={{0,1},{1,0},{2,3},{3,2},{4,5},{5,4},{6,7},{7,6},{8,9},{9,8},{10,11... | collective-permute-start | bytes 1572872 | tf_op jit(solution)/shard_map/ppermute | solution.py:743
  68.0 5.7 %masked_grad.1 = (bf16[384,2048]{1,0:T(8,128)(2,1)S(1)}, bf16[384,2048]{1,0:T(8,128)(2,1)S(1)}, bf16[384,2048]{1,0:T(8,128)(2,1)S(1)}, f32[8,128]{1,0:T(8,128)}) custom-call(bf16[384,2048]{1,0:T(8,128)(2,1)} %bitcast.16, s32[384,2048]{1,0:T(8,128)} %bitcast.15, bf16[384,2048]{1,0:T(8,128)(2,1)S(1)} %get-tuple-element.82.value_ref, ...), custom_call_target="tpu_custom_call" | custom-call | flops 2415919104 | bytes 9437184 | tf_op jit(solution)/shard_map/masked_grad/pallas_call | solution.py:74
  73.8 3.9 %grad_tokens.2 = (bf16[384,4096]{1,0:T(8,128)(2,1)}, f32[8,128]{1,0:T(8,128)S(1)}) custom-call(bf16[896,2048]{1,0:T(8,128)(2,1)S(1)} %pack.3.refs_0_, bf16[896,2048]{1,0:T(8,128)(2,1)S(1)} %collective-permute-done.15.refs_1_, bf16[384,2048]{1,0:T(8,128)(2,1)S(1)} %get-tuple-element.87.refs_2_.refs_4_), custom_call_target="tpu_custom_call" | custom-call | flops 2818572288 | tf_op jit(solution)/shard_map/grad_tokens/pallas_call | solution.py:74
  77.7 3.4 %products.2 = (f32[384,2048]{1,0:T(8,128)S(1)}, bf16[384,4096]{1,0:T(8,128)(2,1)}, f32[8,128]{1,0:T(8,128)S(1)}) custom-call(bf16[384,2048]{1,0:T(8,128)(2,1)S(1)} %pack.4.refs_0_, bf16[384,2048]{1,0:T(8,128)(2,1)S(1)} %collective-permute-done.21.refs_1_, ...), custom_call_target="tpu_custom_call", output_to_operand_aliasing={{0}: (3, {}), {1}: (5, {})} | custom-call | flops 2415919104 | tf_op jit(solution)/shard_map/products/pallas_call | solution.py:74
  81.1 1.2 %collective-permute-done.19.refs_3_ = bf16[128,2048]{1,0:T(8,128)(2,1)S(1)} collective-permute-done((bf16[128,2048]{1,0:T(8,128)(2,1)S(1)}, bf16[128,2048]{1,0:T(8,128)(2,1)S(1)}, u32[]{:S(2)}, u32[]{:S(2)}) %collective-permute-start.19) | collective-permute-done | bytes 524320 | tf_op jit(solution)/shard_map/ppermute | solution.py:746
  84.5 3.7 %collective-permute-done.22.refs_1_ = bf16[640,2048]{1,0:T(8,128)(2,1)S(1)} collective-permute-done((bf16[640,2048]{1,0:T(8,128)(2,1)S(1)}, bf16[640,2048]{1,0:T(8,128)(2,1)S(1)}, u32[]{:S(2)}, u32[]{:S(2)}) %collective-permute-start.22) | collective-permute-done | bytes 2621472 | tf_op jit(solution)/shard_map/ppermute | solution.py:699
  88.2 5.1 %products.3 = (f32[384,2048]{1,0:T(8,128)S(1)}, bf16[384,4096]{1,0:T(8,128)(2,1)}, f32[8,128]{1,0:T(8,128)S(1)}) custom-call(bf16[640,2048]{1,0:T(8,128)(2,1)S(1)} %pack.5.refs_0_, bf16[640,2048]{1,0:T(8,128)(2,1)S(1)} %collective-permute-done.22.refs_1_, ...), custom_call_target="tpu_custom_call", output_to_operand_aliasing={{0}: (3, {}), {1}: (5, {})} | custom-call | flops 4026531840 | tf_op jit(solution)/shard_map/products/pallas_call | solution.py:74
  93.7 1.5 %collective-permute-done.24.refs_1_ = bf16[128,2048]{1,0:T(8,128)(2,1)S(1)} collective-permute-done((bf16[128,2048]{1,0:T(8,128)(2,1)S(1)}, bf16[128,2048]{1,0:T(8,128)(2,1)S(1)}, u32[]{:S(2)}, u32[]{:S(2)}) %collective-permute-start.24) | collective-permute-done | bytes 524320 | tf_op jit(solution)/shard_map/ppermute | solution.py:740
  95.3 1.7 %queries.1 = (bf16[384,2048]{1,0:T(8,128)(2,1)S(1)}, f32[2048,128]{1,0:T(8,128)S(1)}, bf16[2048,128]{1,0:T(8,128)(2,1)S(1)}) custom-call(bf16[384,4096]{1,0:T(8,128)(2,1)S(1)} %get-tuple-element.62.refs_2_.tokens_ref, f32[384,2048]{1,0:T(8,128)S(1)} %get-tuple-element.99.sum_ref, bf16[384,2048]{1,0:T(8,128)(2,1)S(1)} %get-tuple-element.100.mask_ref, ...), custom_call_target="tpu_custom_call" | custom-call | flops 402653184 | tf_op jit(solution)/shard_map/queries/pallas_call | solution.py:74
  97.4 1.5 %collective-permute-done.25.sibling_ref = bf16[2048,128]{1,0:T(8,128)(2,1)S(1)} collective-permute-done((bf16[2048,128]{1,0:T(8,128)(2,1)S(1)}, bf16[2048,128]{1,0:T(8,128)(2,1)S(1)}, u32[]{:S(2)}, u32[]{:S(2)}) %collective-permute-start.25) | collective-permute-done | bytes 524320 | tf_op jit(solution)/shard_map/ppermute | solution.py:626
  99.1 1.5 %collective-permute-start.26 = (bf16[1024,128]{1,0:T(8,128)(2,1)S(1)}, bf16[1024,128]{1,0:T(8,128)(2,1)S(1)}, u32[]{:S(2)}, u32[]{:S(2)}) collective-permute-start(bf16[1024,128]{1,0:T(8,128)(2,1)S(1)} %get-tuple-element.112), channel_id=1, source_target_pairs={{0,8},{8,0},{16,24},{20,4},{24,16},{28,12},{1,9},{9,1},{17,25},{21... | collective-permute-start | bytes 786440 | tf_op jit(solution)/shard_map/ppermute | solution.py:630
  100.6 5.1 %attended.1 = (bf16[384,2048]{1,0:T(8,128)(2,1)}, f32[8,128]{1,0:T(8,128)S(1)}) custom-call(bf16[384,2048]{1,0:T(8,128)(2,1)S(1)} %get-tuple-element.103.query_ref, bf16[384,2048]{1,0:T(8,128)(2,1)S(1)} %get-tuple-element.83.keys_ref, bf16[384,2048]{1,0:T(8,128)(2,1)S(1)} %get-tuple-element.82.value_ref, bf16[2048,128]{1,0:T(8,128)(2,1)S(1)} %get-tuple-element.85.high_ref, ...), custom_call_target="tpu_custom_call" | custom-call | flops 2415919104 | bytes 6291456 | tf_op jit(solution)/shard_map/attended/pallas_call | solution.py:74
  106.6 2.7 %collective-permute-start.27 = (bf16[1024,128]{1,0:T(8,128)(2,1)S(1)}, bf16[1024,128]{1,0:T(8,128)(2,1)S(1)}, u32[]{:S(2)}, u32[]{:S(2)}) collective-permute-start(bf16[1024,128]{1,0:T(8,128)(2,1)S(1)} %message.3), channel_id=1, source_target_pairs={{4,12},{12,4},{16,0},{20,28},{24,8},{28,20},{5,13},{13,5},{17,1},{... | collective-permute-start | bytes 786440 | tf_op jit(solution)/shard_map/ppermute | solution.py:643
  109.3 6.9 %inner.1 = (f32[384,2048]{1,0:T(8,128)S(1)}, f32[384,2048]{1,0:T(8,128)S(1)}, f32[8,128]{1,0:T(8,128)S(1)}) custom-call(bf16[384,2048]{1,0:T(8,128)(2,1)S(1)} %get-tuple-element.103.query_ref, bf16[384,2048]{1,0:T(8,128)(2,1)S(1)} %get-tuple-element.83.keys_ref, bf16[384,2048]{1,0:T(8,128)(2,1)S(1)} %get-tuple-element.82.value_ref, ...), custom_call_target="tpu_custom_call" | custom-call | flops 3623878656 | bytes 12582912 | tf_op jit(solution)/shard_map/inner/pallas_call | solution.py:74
  116.3 1.9 %grad_tokens.3 = (bf16[384,4096]{1,0:T(8,128)(2,1)}, f32[8,128]{1,0:T(8,128)}) custom-call(bf16[128,2048]{1,0:T(8,128)(2,1)S(1)} %join.9.refs_0_, bf16[128,2048]{1,0:T(8,128)(2,1)S(1)} %collective-permute-done.24.refs_1_, bf16[384,2048]{1,0:T(8,128)(2,1)S(1)} %get-tuple-element.87.refs_2_.refs_4_, ...), custom_call_target="tpu_custom_call", output_to_operand_aliasing={{0}: (3, {})} | custom-call | flops 402653184 | tf_op jit(solution)/shard_map/grad_tokens/pallas_call | solution.py:74
  118.5 3.5 %outer.1 = (bf16[384,2048]{1,0:T(8,128)(2,1)}, bf16[384,2048]{1,0:T(8,128)(2,1)}) custom-call(f32[384,2048]{1,0:T(8,128)S(1)} %get-tuple-element.107.key_ref, f32[384,2048]{1,0:T(8,128)S(1)} %get-tuple-element.108.val_ref, bf16[384,2048]{1,0:T(8,128)(2,1)S(1)} %get-tuple-element.83.keys_ref, bf16[384,2048]{1,0:T(8,128)(2,1)S(1)} %get-tuple-element.82.value_ref, ...), custom_call_target="tpu_custom_call" | custom-call | flops 805306368 | bytes 15728640 | tf_op jit(solution)/shard_map/outer/pallas_call | solution.py:74
  (57 shorter events, 17.5 us)
Async XLA Ops:
  0.6 14.1 %collective-permute-start = (bf16[128,2048]{1,0:T(8,128)(2,1)}, bf16[128,2048]{1,0:T(8,128)(2,1)S(1)}, u32[]{:S(2)}, u32[]{:S(2)}) collective-permute-start(bf16[128,2048]{1,0:T(8,128)(2,1)} %refs_0_.1), channel_id=1, source_target_pairs={{0,1},{1,0},{2,3},{3,2},{4,5},{5,4},{6,7},{7,6},{8,9},{9,8},{10,11... | collective-permute-start | bytes 1572872 | tf_op jit(solution)/shard_map/ppermute | solution.py:743
  2.8 11.9 %collective-permute-start.1 = (bf16[128,2048]{1,0:T(8,128)(2,1)}, bf16[128,2048]{1,0:T(8,128)(2,1)S(1)}, u32[]{:S(2)}, u32[]{:S(2)}) collective-permute-start(bf16[128,2048]{1,0:T(8,128)(2,1)} %refs_0_.1), channel_id=1, source_target_pairs={{1,2},{2,1},{5,6},{6,5},{9,10},{10,9},{13,14},{14,13},{17,18},{18,... | collective-permute-start | bytes 1572872 | tf_op jit(solution)/shard_map/ppermute | solution.py:743
  3.5 11.2 %collective-permute-start.2 = (bf16[128,2048]{1,0:T(8,128)(2,1)}, bf16[128,2048]{1,0:T(8,128)(2,1)S(1)}, u32[]{:S(2)}, u32[]{:S(2)}) collective-permute-start(bf16[128,2048]{1,0:T(8,128)(2,1)} %refs_0_.1), channel_id=1, source_target_pairs={{0,8},{4,20},{8,0},{12,28},{16,24},{20,4},{24,16},{28,12},{1,9},{5... | collective-permute-start | bytes 1572872 | tf_op jit(solution)/shard_map/ppermute | solution.py:746
  4.8 14.0 %collective-permute-start.3 = (bf16[128,2048]{1,0:T(8,128)(2,1)}, bf16[128,2048]{1,0:T(8,128)(2,1)S(1)}, u32[]{:S(2)}, u32[]{:S(2)}) collective-permute-start(bf16[128,2048]{1,0:T(8,128)(2,1)} %refs_0_.1), channel_id=1, source_target_pairs={{0,16},{4,12},{8,24},{12,4},{16,0},{20,28},{24,8},{28,20},{1,17},{... | collective-permute-start | bytes 1572872 | tf_op jit(solution)/shard_map/ppermute | solution.py:746
  18.8 20.9 %copy-start = (bf16[128,2048]{1,0:T(8,128)(2,1)S(1)}, bf16[128,2048]{1,0:T(8,128)(2,1)}, u32[]{:S(2)}) copy-start(bf16[128,2048]{1,0:T(8,128)(2,1)} %refs_0_.1) | copy-start | bytes 1572868
  18.8 3.0 %collective-permute-start.9 = (bf16[2048,128]{1,0:T(8,128)(2,1)S(1)}, bf16[2048,128]{1,0:T(8,128)(2,1)S(1)}, u32[]{:S(2)}, u32[]{:S(2)}) collective-permute-start(bf16[2048,128]{1,0:T(8,128)(2,1)S(1)} %get-tuple-element.68), channel_id=1, source_target_pairs={{0,4},{4,0},{1,5},{5,1},{2,6},{6,2},{3,7},{7,3},{8,12},{12,8},{9,1... | collective-permute-start | bytes 1572872 | tf_op jit(solution)/shard_map/ppermute | solution.py:626
  19.4 12.9 %collective-permute-start.4 = (bf16[128,2048]{1,0:T(8,128)(2,1)S(1)}, bf16[128,2048]{1,0:T(8,128)(2,1)S(1)}, u32[]{:S(2)}, u32[]{:S(2)}) collective-permute-start(bf16[128,2048]{1,0:T(8,128)(2,1)S(1)} %get-tuple-element.64.refs_1_), channel_id=1, source_target_pairs={{0,16},{4,12},{8,24},{12,4},{16,0},{20,28},{24,8},{28,20},{1,17},{... | collective-permute-start | bytes 1572872 | tf_op jit(solution)/shard_map/ppermute | solution.py:749
  20.6 13.9 %collective-permute-start.5 = (bf16[128,2048]{1,0:T(8,128)(2,1)S(1)}, bf16[128,2048]{1,0:T(8,128)(2,1)S(1)}, u32[]{:S(2)}, u32[]{:S(2)}) collective-permute-start(bf16[128,2048]{1,0:T(8,128)(2,1)S(1)} %get-tuple-element.65.refs_4_), channel_id=1, source_target_pairs={{0,8},{4,20},{8,0},{12,28},{16,24},{20,4},{24,16},{28,12},{1,9},{5... | collective-permute-start | bytes 1572872 | tf_op jit(solution)/shard_map/ppermute | solution.py:746
  20.8 18.3 %collective-permute-start.6 = (bf16[128,2048]{1,0:T(8,128)(2,1)S(1)}, bf16[128,2048]{1,0:T(8,128)(2,1)S(1)}, u32[]{:S(2)}, u32[]{:S(2)}) collective-permute-start(bf16[128,2048]{1,0:T(8,128)(2,1)S(1)} %get-tuple-element.65.refs_4_), channel_id=1, source_target_pairs={{0,16},{4,12},{8,24},{12,4},{16,0},{20,28},{24,8},{28,20},{1,17},{... | collective-permute-start | bytes 1572872 | tf_op jit(solution)/shard_map/ppermute | solution.py:746
  21.1 18.1 %collective-permute-start.7 = (bf16[128,2048]{1,0:T(8,128)(2,1)S(1)}, bf16[128,2048]{1,0:T(8,128)(2,1)S(1)}, u32[]{:S(2)}, u32[]{:S(2)}) collective-permute-start(bf16[128,2048]{1,0:T(8,128)(2,1)S(1)} %get-tuple-element.65.refs_4_), channel_id=1, source_target_pairs={{1,2},{2,1},{5,6},{6,5},{9,10},{10,9},{13,14},{14,13},{17,18},{18,... | collective-permute-start | bytes 1572872 | tf_op jit(solution)/shard_map/ppermute | solution.py:743
  21.8 17.4 %collective-permute-start.8 = (bf16[128,2048]{1,0:T(8,128)(2,1)S(1)}, bf16[128,2048]{1,0:T(8,128)(2,1)S(1)}, u32[]{:S(2)}, u32[]{:S(2)}) collective-permute-start(bf16[128,2048]{1,0:T(8,128)(2,1)S(1)} %get-tuple-element.66.inner_ref), channel_id=1, source_target_pairs={{1,0},{2,3},{5,4},{6,7},{9,8},{10,11},{13,12},{14,15},{17,16},{18,... | collective-permute-start | bytes 1572872 | tf_op jit(solution)/shard_map/ppermute | solution.py:743
  32.3 7.5 %collective-permute-start.10 = (bf16[1024,128]{1,0:T(8,128)(2,1)S(1)}, bf16[1024,128]{1,0:T(8,128)(2,1)S(1)}, u32[]{:S(2)}, u32[]{:S(2)}) collective-permute-start(bf16[1024,128]{1,0:T(8,128)(2,1)S(1)} %get-tuple-element.69), channel_id=1, source_target_pairs={{0,8},{4,20},{8,0},{12,28},{16,24},{24,16},{1,9},{5,21},{9,1},{13,... | collective-permute-start | bytes 786440 | tf_op jit(solution)/shard_map/ppermute | solution.py:630
  40.1 8.5 %collective-permute-start.15 = (bf16[896,2048]{1,0:T(8,128)(2,1)S(1)}, bf16[896,2048]{1,0:T(8,128)(2,1)S(1)}, u32[]{:S(2)}, u32[]{:S(2)}) collective-permute-start(bf16[896,2048]{1,0:T(8,128)(2,1)S(1)} %pack.3.refs_0_), channel_id=1, source_target_pairs={{0,4},{4,0},{1,5},{5,1},{2,6},{6,2},{3,7},{7,3},{8,12},{12,8},{9,1... | collective-permute-start | bytes 11010056 | tf_op jit(solution)/shard_map/ppermute | solution.py:699
  42.6 17.3 %collective-permute-start.11 = (bf16[128,2048]{1,0:T(8,128)(2,1)S(1)}, bf16[128,2048]{1,0:T(8,128)(2,1)S(1)}, u32[]{:S(2)}, u32[]{:S(2)}) collective-permute-start(bf16[128,2048]{1,0:T(8,128)(2,1)S(1)} %choose.2.refs_0_), channel_id=1, source_target_pairs={{0,8},{4,20},{8,0},{12,28},{16,24},{20,4},{24,16},{28,12},{1,9},{5... | collective-permute-start | bytes 1572872 | tf_op jit(solution)/shard_map/ppermute | solution.py:746
  43.4 16.4 %collective-permute-start.12 = (bf16[128,2048]{1,0:T(8,128)(2,1)S(1)}, bf16[128,2048]{1,0:T(8,128)(2,1)S(1)}, u32[]{:S(2)}, u32[]{:S(2)}) collective-permute-start(bf16[128,2048]{1,0:T(8,128)(2,1)S(1)} %choose.2.refs_0_), channel_id=1, source_target_pairs={{0,16},{4,12},{8,24},{12,4},{16,0},{20,28},{24,8},{28,20},{1,17},{... | collective-permute-start | bytes 1572872 | tf_op jit(solution)/shard_map/ppermute | solution.py:746
  44.4 16.9 %collective-permute-start.13 = (bf16[128,2048]{1,0:T(8,128)(2,1)S(1)}, bf16[128,2048]{1,0:T(8,128)(2,1)S(1)}, u32[]{:S(2)}, u32[]{:S(2)}) collective-permute-start(bf16[128,2048]{1,0:T(8,128)(2,1)S(1)} %get-tuple-element.72.inner_ref), channel_id=1, source_target_pairs={{1,0},{2,3},{5,4},{6,7},{9,8},{10,11},{13,12},{14,15},{17,16},{18,... | collective-permute-start | bytes 1572872 | tf_op jit(solution)/shard_map/ppermute | solution.py:743
  45.7 14.1 %collective-permute-start.14 = (bf16[1024,128]{1,0:T(8,128)(2,1)S(1)}, bf16[1024,128]{1,0:T(8,128)(2,1)S(1)}, u32[]{:S(2)}, u32[]{:S(2)}) collective-permute-start(bf16[1024,128]{1,0:T(8,128)(2,1)S(1)} %message.2), channel_id=1, source_target_pairs={{0,16},{4,12},{8,24},{12,4},{20,28},{28,20},{1,17},{5,13},{9,25},{... | collective-permute-start | bytes 786440 | tf_op jit(solution)/shard_map/ppermute | solution.py:643
  61.4 16.4 %collective-permute-start.21 = (bf16[384,2048]{1,0:T(8,128)(2,1)S(1)}, bf16[384,2048]{1,0:T(8,128)(2,1)S(1)}, u32[]{:S(2)}, u32[]{:S(2)}) collective-permute-start(bf16[384,2048]{1,0:T(8,128)(2,1)S(1)} %pack.4.refs_0_), channel_id=1, source_target_pairs={{0,4},{4,0},{1,5},{5,1},{2,6},{6,2},{3,7},{7,3},{8,12},{12,8},{9,1... | collective-permute-start | bytes 4718600 | tf_op jit(solution)/shard_map/ppermute | solution.py:699
  62.6 3.7 %collective-permute-start.20 = (f32[1024,128]{1,0:T(8,128)S(1)}, f32[1024,128]{1,0:T(8,128)S(1)}, u32[]{:S(2)}, u32[]{:S(2)}) collective-permute-start(f32[1024,128]{1,0:T(8,128)S(1)} %state.2.state_ref), channel_id=1, source_target_pairs={{0,4},{4,0},{1,5},{5,1},{2,6},{6,2},{3,7},{7,3},{8,12},{12,8},{9,1... | collective-permute-start | bytes 1572872 | tf_op jit(solution)/shard_map/ppermute | solution.py:656
  62.7 18.4 %collective-permute-start.17 = (bf16[128,2048]{1,0:T(8,128)(2,1)S(1)}, bf16[128,2048]{1,0:T(8,128)(2,1)S(1)}, u32[]{:S(2)}, u32[]{:S(2)}) collective-permute-start(bf16[128,2048]{1,0:T(8,128)(2,1)S(1)} %get-tuple-element.80.refs_1_), channel_id=1, source_target_pairs={{0,16},{4,12},{8,24},{12,4},{16,0},{20,28},{24,8},{28,20},{1,17},{... | collective-permute-start | bytes 1572872 | tf_op jit(solution)/shard_map/ppermute | solution.py:749
  63.3 17.8 %collective-permute-start.18 = (bf16[128,2048]{1,0:T(8,128)(2,1)S(1)}, bf16[128,2048]{1,0:T(8,128)(2,1)S(1)}, u32[]{:S(2)}, u32[]{:S(2)}) collective-permute-start(bf16[128,2048]{1,0:T(8,128)(2,1)S(1)} %choose.3.refs_2_), channel_id=1, source_target_pairs={{0,8},{4,20},{8,0},{12,28},{16,24},{20,4},{24,16},{28,12},{1,9},{5... | collective-permute-start | bytes 1572872 | tf_op jit(solution)/shard_map/ppermute | solution.py:746
  64.1 18.2 %collective-permute-start.19 = (bf16[128,2048]{1,0:T(8,128)(2,1)S(1)}, bf16[128,2048]{1,0:T(8,128)(2,1)S(1)}, u32[]{:S(2)}, u32[]{:S(2)}) collective-permute-start(bf16[128,2048]{1,0:T(8,128)(2,1)S(1)} %choose.3.refs_2_), channel_id=1, source_target_pairs={{0,16},{4,12},{8,24},{12,4},{16,0},{20,28},{24,8},{28,20},{1,17},{... | collective-permute-start | bytes 1572872 | tf_op jit(solution)/shard_map/ppermute | solution.py:746
  66.3 14.7 %collective-permute-start.16 = (bf16[128,2048]{1,0:T(8,128)(2,1)S(1)}, bf16[128,2048]{1,0:T(8,128)(2,1)S(1)}, u32[]{:S(2)}, u32[]{:S(2)}) collective-permute-start(bf16[128,2048]{1,0:T(8,128)(2,1)S(1)} %get-tuple-element.79), channel_id=1, source_target_pairs={{0,1},{1,0},{2,3},{3,2},{4,5},{5,4},{6,7},{7,6},{8,9},{9,8},{10,11... | collective-permute-start | bytes 1572872 | tf_op jit(solution)/shard_map/ppermute | solution.py:743
  82.6 5.6 %collective-permute-start.22 = (bf16[640,2048]{1,0:T(8,128)(2,1)S(1)}, bf16[640,2048]{1,0:T(8,128)(2,1)S(1)}, u32[]{:S(2)}, u32[]{:S(2)}) collective-permute-start(bf16[640,2048]{1,0:T(8,128)(2,1)S(1)} %pack.5.refs_0_), channel_id=1, source_target_pairs={{0,4},{4,0},{1,5},{5,1},{2,6},{6,2},{3,7},{7,3},{8,12},{12,8},{9,1... | collective-permute-start | bytes 7864328 | tf_op jit(solution)/shard_map/ppermute | solution.py:699
  83.7 9.6 %collective-permute-start.23 = (bf16[128,2048]{1,0:T(8,128)(2,1)S(1)}, bf16[128,2048]{1,0:T(8,128)(2,1)S(1)}, u32[]{:S(2)}, u32[]{:S(2)}) collective-permute-start(bf16[128,2048]{1,0:T(8,128)(2,1)S(1)} %get-tuple-element.95.refs_3_), channel_id=1, source_target_pairs={{0,16},{4,12},{8,24},{12,4},{16,0},{20,28},{24,8},{28,20},{1,17},{... | collective-permute-start | bytes 1572872 | tf_op jit(solution)/shard_map/ppermute | solution.py:749
  93.3 2.0 %collective-permute-start.24 = (bf16[128,2048]{1,0:T(8,128)(2,1)S(1)}, bf16[128,2048]{1,0:T(8,128)(2,1)S(1)}, u32[]{:S(2)}, u32[]{:S(2)}) collective-permute-start(bf16[128,2048]{1,0:T(8,128)(2,1)S(1)} %join.9.refs_0_), channel_id=1, source_target_pairs={{0,4},{4,0},{1,5},{5,1},{2,6},{6,2},{3,7},{7,3},{8,12},{12,8},{9,1... | collective-permute-start | bytes 1572872 | tf_op jit(solution)/shard_map/ppermute | solution.py:740
  97.0 2.0 %collective-permute-start.25 = (bf16[2048,128]{1,0:T(8,128)(2,1)S(1)}, bf16[2048,128]{1,0:T(8,128)(2,1)S(1)}, u32[]{:S(2)}, u32[]{:S(2)}) collective-permute-start(bf16[2048,128]{1,0:T(8,128)(2,1)S(1)} %get-tuple-element.111), channel_id=1, source_target_pairs={{0,4},{4,0},{1,5},{5,1},{2,6},{6,2},{3,7},{7,3},{8,12},{12,8},{9,1... | collective-permute-start | bytes 1572872 | tf_op jit(solution)/shard_map/ppermute | solution.py:626
  99.1 7.4 %collective-permute-start.26 = (bf16[1024,128]{1,0:T(8,128)(2,1)S(1)}, bf16[1024,128]{1,0:T(8,128)(2,1)S(1)}, u32[]{:S(2)}, u32[]{:S(2)}) collective-permute-start(bf16[1024,128]{1,0:T(8,128)(2,1)S(1)} %get-tuple-element.112), channel_id=1, source_target_pairs={{0,8},{8,0},{16,24},{20,4},{24,16},{28,12},{1,9},{9,1},{17,25},{21... | collective-permute-start | bytes 786440 | tf_op jit(solution)/shard_map/ppermute | solution.py:630
  106.6 9.6 %collective-permute-start.27 = (bf16[1024,128]{1,0:T(8,128)(2,1)S(1)}, bf16[1024,128]{1,0:T(8,128)(2,1)S(1)}, u32[]{:S(2)}, u32[]{:S(2)}) collective-permute-start(bf16[1024,128]{1,0:T(8,128)(2,1)S(1)} %message.3), channel_id=1, source_target_pairs={{4,12},{12,4},{16,0},{20,28},{24,8},{28,20},{5,13},{13,5},{17,1},{... | collective-permute-start | bytes 786440 | tf_op jit(solution)/shard_map/ppermute | solution.py:643
  116.3 2.0 %collective-permute-start.28 = (f32[1024,128]{1,0:T(8,128)S(1)}, f32[1024,128]{1,0:T(8,128)S(1)}, u32[]{:S(2)}, u32[]{:S(2)}) collective-permute-start(f32[1024,128]{1,0:T(8,128)S(1)} %state.3.state_ref), channel_id=1, source_target_pairs={{0,4},{4,0},{1,5},{5,1},{2,6},{6,2},{3,7},{7,3},{8,12},{12,8},{9,1... | collective-permute-start | bytes 1572872 | tf_op jit(solution)/shard_map/ppermute | solution.py:656

commit v8 on v7

--- a/solution.py
+++ b/solution.py
@@ -110,8 +110,8 @@
     three = (0, 1, 2)
     return (
         some((0, (0, 1, 2, 3)), (1, three))
-        + some((2, three))
-        + some((1, (3,)), (2, (3,)), (3, three))
+        + some((2, three), (3, (0,)))
+        + some((1, (3,)), (2, (3,)), (3, (1, 2)))
         + some((3, (3,)))
     )
 
@@ -135,8 +135,8 @@
 
 
 def memory_kernel(
-    special, key_ref, spike_ref, value_ref, tokens_ref,
-    keys_ref, mask_ref, values_ref, own_ref, sent_ref, some_ref,
+    special, key_ref, spike_ref, value_ref, tokens_ref, grad_ref,
+    keys_ref, mask_ref, values_ref, own_ref, sent_ref, some_ref, grads_ref,
     key_in, spike_in, sems,
 ):
     copies = Copies(sems)
@@ -151,6 +151,7 @@
         copies.start(tokens_ref.at[piece_columns(place)], some_ref.at[piece_columns(piece)])
         for piece, place in enumerate(places)
     ]
+    ordered.append(copies.start(grad_ref, grads_ref))
     for at, part in zip(wide, parts):
         for copy in part:
             copy.wait()
@@ -168,21 +169,22 @@
         copy.wait()
 
 
-def memory_call(special, key_input, k_spikes, values, tokens):
+def memory_call(special, key_input, k_spikes, values, tokens, cotangent):
     length, total = values.shape
     block, state = (length, total), (total, HEAD)
     return kernel_call(
         functools.partial(memory_kernel, special),
-        "HHHH",
-        (key_input, k_spikes, values, tokens),
-        "VVVVVV",
-        [(block, bf16)] * 3 + [(state, f32), (state, bf16), (tokens.shape, bf16)],
+        "HHHHH",
+        (key_input, k_spikes, values, tokens, cotangent),
+        "VVVVVVV",
+        [(block, bf16)] * 3
+        + [(state, f32), (state, bf16), (tokens.shape, bf16), (block, bf16)],
         "own_memory",
         (2 * length * total * HEAD, 12 * length * total),
         [
             pltpu.VMEM(block, bf16),
             pltpu.VMEM(block, jnp.int32),
-            pltpu.SemaphoreType.DMA((3 * total // WIDE + tokens.shape[1] // PIECE,)),
+            pltpu.SemaphoreType.DMA((3 * total // WIDE + tokens.shape[1] // PIECE + 1,)),
         ],
     )
 
@@ -238,29 +240,25 @@
 
 
 def masked_kernel(
-    factor, grad_ref, spike_ref, value_ref, keys_ref, high_ref, low_ref,
-    out_ref, mask_ref, grads_ref, mark_ref, spike_in, sems,
+    factor, spike_ref, grad_ref, value_ref, keys_ref, high_ref, low_ref,
+    out_ref, mask_ref, spike_in, sems,
 ):
-    set_mark(mark_ref)
     total = out_ref.shape[1]
 
-    def copies(group, at):
-        return [
-            pltpu.make_async_copy(grad_ref.at[columns(at)], grads_ref.at[columns(at)], sems.at[0, group]),
-            pltpu.make_async_copy(spike_ref.at[columns(at)], spike_in.at[columns(at)], sems.at[1, group]),
-        ]
+    def bring(group, at):
+        return pltpu.make_async_copy(
+            spike_ref.at[columns(at)], spike_in.at[columns(at)], sems.at[group]
+        )
 
     for group in range(total // WIDE):
-        for copy in copies(group, group * WIDE):
-            copy.start()
+        bring(group, group * WIDE).start()
 
     def work(group, at):
-        for copy in copies(group, at):
-            copy.wait()
+        bring(group, at).wait()
         for part in heads(at):
             mask = spike_in[:, part].astype(f32)
             mask_ref[:, part] = mask.astype(bf16)
-            grad, value, keys = grads_ref[:, part], value_ref[:, part], keys_ref[:, part]
+            grad, value, keys = grad_ref[:, part], value_ref[:, part], keys_ref[:, part]
             state = jnp.concatenate([high_ref[part, :], low_ref[part, :]], axis=1)
             for rows, cols, scores in causal(grad, value):
                 made = nn(scores, keys[cols]) + nt(twice(grad[rows]), state)
@@ -269,18 +267,49 @@
     groups(total, work)
 
 
-def masked_call(factor, cotangent, q_spikes, values, keys, high, low):
+def masked_call(factor, q_spikes, cotangent, values, keys, high, low):
     length, total = values.shape
     block = (length, total)
     return kernel_call(
         functools.partial(masked_kernel, factor),
-        "HHVVVV",
-        (cotangent, q_spikes, values, keys, high, low),
-        "VVVV",
-        [(block, bf16)] * 3 + [(MARK.shape, f32)],
+        "HVVVVV",
+        (q_spikes, cotangent, values, keys, high, low),
+        "VV",
+        [(block, bf16)] * 2,
         "masked_grad",
         (8 * length * total * length, 12 * length * total),
-        [pltpu.VMEM(block, jnp.int32), pltpu.SemaphoreType.DMA((2, total // WIDE))],
+        [pltpu.VMEM(block, jnp.int32), pltpu.SemaphoreType.DMA((total // WIDE,))],
+    )
+
+
+def turned_kernel(value_ref, grad_ref, after_ref, top_ref, bottom_ref, mark_ref):
+    del after_ref
+    set_mark(mark_ref)
+    length, total = value_ref.shape
+    rest = length - HEAD
+    number = WIDE // HEAD
+
+    def work(group, at):
+        for head, part in enumerate(heads(at)):
+            (_, _, top), (_, _, bottom) = causal_turned(value_ref[:, part], grad_ref[:, part])
+            place = group * number + head
+            top_ref[:, pl.ds(pl.multiple_of(place * length, HEAD), length)] = top
+            bottom_ref[:, pl.ds(pl.multiple_of(place * rest, HEAD), rest)] = bottom
+
+    groups(total, work)
+
+
+def turned_call(values, cotangent, after):
+    length, total = values.shape
+    number, rest = total // HEAD, length - HEAD
+    return kernel_call(
+        turned_kernel,
+        "VVA",
+        (values, cotangent, after),
+        "VVV",
+        [((HEAD, number * length), bf16), ((rest, number * rest), bf16), (MARK.shape, f32)],
+        "turned",
+        (4 * length * total * length, 0),
     )
 
 
@@ -391,7 +420,7 @@
 
 def query_kernel(start, size, tokens_ref, sum_ref, mask_ref, grad_ref, *refs):
     blocks = refs[:size]
-    queries, own_ref, sent_ref = refs[size:]
+    queries, own_ref, sent_ref = refs[-3:]
     cols = slice(start * PIECE, start * PIECE + rows_of(blocks))
     for at in range(0, queries.shape[1], WIDE):
         part = slice(at, at + WIDE)
@@ -408,14 +437,14 @@
             sent_ref[here, :] = own.astype(bf16)
 
 
-def query_call(start, tokens, blocks, before, q_mask, cotangent):
+def query_call(start, tokens, blocks, before, q_mask, cotangent, others):
     length = tokens.shape[0]
     total = blocks[0].shape[1]
     depth = rows_of(blocks)
     return kernel_call(
         functools.partial(query_kernel, start, len(blocks)),
-        "VVVV" + "V" * len(blocks),
-        (tokens, before, q_mask, cotangent, *blocks),
+        "VVVV" + "V" * len(blocks) + "A" * len(others),
+        (tokens, before, q_mask, cotangent, *blocks, *others),
         "VVV",
         [((length, total), bf16), ((total, HEAD), f32), ((total, HEAD), bf16)],
         "queries",
@@ -464,33 +493,59 @@
     )
 
 
-def inner_kernel(query_ref, keys_ref, value_ref, grad_ref, key_ref, val_ref, mark_ref):
+def value_kernel(query_ref, keys_ref, grad_ref, val_ref, mark_ref):
     set_mark(mark_ref)
 
     def work(group, at):
         for part in heads(at):
-            query, keys = query_ref[:, part], keys_ref[:, part]
-            value, grad = value_ref[:, part], grad_ref[:, part]
+            query, keys, grad = query_ref[:, part], keys_ref[:, part], grad_ref[:, part]
             for rows, cols, scores in causal_turned(keys, query):
                 val_ref[rows, part] = nn(scores, grad[cols])
-            for rows, cols, scores in causal_turned(value, grad):
-                key_ref[rows, part] = nn(scores, query[cols])
 
     groups(query_ref.shape[1], work)
 
 
-def inner_call(queries, keys, values, cotangent):
-    length, total = values.shape
-    block = (length, total)
-    return kernel_call(
-        inner_kernel,
-        "VVVV",
-        (queries, keys, values, cotangent),
+def value_call(queries, keys, cotangent):
+    length, total = keys.shape
+    return kernel_call(
+        value_kernel,
         "VVV",
-        [(block, f32), (block, f32), (MARK.shape, f32)],
-        "inner",
-        (12 * length * total * length, 16 * length * total),
-    )
+        (queries, keys, cotangent),
+        "VV",
+        [((length, total), f32), (MARK.shape, f32)],
+        "value_part",
+        (6 * length * total * length, 0),
+    )
+
+
+def key_kernel(query_ref, top_ref, bottom_ref, key_ref):
+    length, total = query_ref.shape
+    rest = length - HEAD
+    number = WIDE // HEAD
+
+    def work(group, at):
+        for head, part in enumerate(heads(at)):
+            query = query_ref[:, part]
+            place = group * number + head
+            top = top_ref[:, pl.ds(pl.multiple_of(place * length, HEAD), length)]
+            bottom = bottom_ref[:, pl.ds(pl.multiple_of(place * rest, HEAD), rest)]
+            key_ref[:HEAD, part] = nn(top, query)
+            key_ref[HEAD:, part] = nn(bottom, query[HEAD:])
+
+    groups(total, work)
+
+
+def key_call(queries, top, bottom):
+    length, total = queries.shape
+    return kernel_call(
+        key_kernel,
+        "VVV",
+        (queries, top, bottom),
+        "V",
+        [((length, total), f32)],
+        "key_part",
+        (4 * length * total * length, 0),
+    )[0]
 
 
 def outer_kernel(
@@ -590,7 +645,8 @@
     return array_ref[pl.ds(pl.multiple_of(core * half, half), half), :]
 
 
-def both_kernel(own_ref, sibling_ref, both_ref, sent_ref):
+def both_kernel(own_ref, sibling_ref, *refs):
+    both_ref, sent_ref = refs[-2:]
     core = lax.axis_index("core")
     both = half_rows(own_ref, core) + half_rows(sibling_ref, core).astype(f32)
     both_ref[...] = both
@@ -621,11 +677,17 @@
         low_ref[rows, :] = (whole - high.astype(f32)).astype(bf16)
 
 
-def send_first(own, sent, reverse):
+def send_first(own, sent, reverse, others=()):
     half = (own.shape[0] // 2, HEAD)
     sibling = lax.ppermute(sent, "core", SWAP)
     both, sent = kernel_call(
-        both_kernel, "VV", (own, sibling), "VV", [(half, f32), (half, bf16)], "both", (0, 0)
+        both_kernel,
+        "VV" + "A" * len(others),
+        (own, sibling, *others),
+        "VV",
+        [(half, f32), (half, bf16)],
+        "both",
+        (0, 0),
     )
     return sibling, both, lax.ppermute(sent, CTX, links(1, upward(reverse)))
 
@@ -748,8 +810,8 @@
     def onward(array):
         return lax.ppermute(array, CTX, links(2))
 
-    keys, k_mask, values, own, sent, tokens = memory_call(
-        special, key_input, k_spikes, values, tokens
+    keys, k_mask, values, own, sent, tokens, cotangent = memory_call(
+        special, key_input, k_spikes, values, tokens, cotangent
     )
     if special:
         ends = [(0, 1), (1, 0), (2, 3), (3, 2)]
@@ -778,50 +840,52 @@
         far_out = along(far, outward)
         early = pack(q_weight, first_0, second_0, third_0, near, first_1, second_1)
         partial, _, mark = products_call(special, 0, early, tokens)
+        top, bottom, turned_mark = turned_call(values, cotangent, got)
         third_0, first_2, second_2, far_out, more = join(
-            [third_0, first_2, second_2, far_out, more], [mark]
+            [third_0, first_2, second_2, far_out, more], [mark, turned_mark]
         )
         third_1 = along(third_0, ends)
         third_2 = onward(first_2)
         last_layer = choose(far, far_out)
         first_3, second_3 = cross(last_layer)
         high, low = add_up(got, more, twin, False)
-        masked, q_mask, cotangent, _ = masked_call(
-            factor, cotangent, q_spikes, values, keys, high, low
-        )
+        masked, q_mask = masked_call(factor, q_spikes, cotangent, values, keys, high, low)
         _, grad, mark_0 = products_call(
             special, 0, early, tokens, masked=masked, project=False
         )
-        blocks = pack(next_layer, first_2, second_2)
+        blocks = pack(next_layer, first_2, second_2, last_layer)
         partial, grad, mark_1 = products_call(special, 14, blocks, tokens, partial, masked, grad)
         third_1, third_2, first_3, second_3 = join(
             [third_1, third_2, first_3, second_3], [mark_0, mark_1]
         )
         third_3 = onward(first_3)
-        blocks = pack(third_1, third_2, last_layer, first_3, second_3)
-        partial, grad, mark = products_call(special, 20, blocks, tokens, partial, masked, grad)
+        blocks = pack(third_1, third_2, first_3, second_3)
+        partial, _, mark = products_call(special, 22, blocks, tokens, partial)
         third_3, = join([third_3], [mark])
+        _, grad, mark = products_call(
+            special, 22, blocks, tokens, masked=masked, grad=grad, project=False
+        )
         late = [third_3, sibling(third_3)]
         start = 30
     else:
-        masked, q_mask, cotangent, _ = masked_call(
-            factor, cotangent, q_spikes, values, keys, high, low
-        )
+        masked, q_mask = masked_call(factor, q_spikes, cotangent, values, keys, high, low)
+        top, bottom, _ = turned_call(values, cotangent, own)
         start = arrived[0].shape[0] // PIECE
-        partial, grad, _ = products_call(special, 0, arrived[:1], tokens, masked=masked)
+        partial, grad, mark = products_call(special, 0, arrived[:1], tokens, masked=masked)
         late = arrived[1:]
-    queries, own, sent = query_call(start, tokens, late, partial, q_mask, cotangent)
+    queries, own, sent = query_call(start, tokens, late, partial, q_mask, cotangent, [mark])
     attended, attended_mark = attend_call(factor, queries, keys, values, high, low)
-    key_part, value_part, inner_mark = inner_call(queries, keys, values, cotangent)
+    value_part, value_mark = value_call(queries, keys, cotangent)
+    key_part = key_call(queries, top, bottom)
+    _, grad_tokens, back_mark = products_call(
+        special, start, late, tokens, masked=masked, grad=grad, project=False
+    )
     if special:
-        twin, both, got = send_first(own, sent, True)
+        twin, both, got = send_first(own, sent, True, [back_mark])
         more = send_second(got, both, True, [attended_mark])
-        adjoint = add_up(got, more, twin, True, [inner_mark])
+        adjoint = add_up(got, more, twin, True, [value_mark])
     else:
         adjoint = halves(scan_any(own, sent, chips * 2, True))
-    _, grad_tokens, _ = products_call(
-        special, start, late, tokens, masked=masked, grad=grad, project=False
-    )
     grad_keys, grad_values = outer_call(
         factor, key_part, value_part, keys, values, k_mask, *adjoint
     )

time: 123 us -> 123 us (level)
  waiting for transfers between devices: 43.7 us -> 40.4 us
  starting transfers between devices: 31.3 us -> 33.7 us
    ppermute x3, waiting for transfers between devices: 9.09 us -> 11.6 us  [onward(): return lax.ppermute(array, CTX, links(2))]
    ppermute x2, starting transfers between devices: 0.15 us -> 2.21 us  [add_up(): other = lax.ppermute(state, 'core', SWAP)]
    ppermute x1, waiting for transfers between devices: 1.55 us -> 0.01 us  [sibling(): return lax.ppermute(array, 'core', SWAP)]
    ppermute x3, waiting for transfers between devices: 4.13 us -> 2.64 us  [pack(): return [made, lax.ppermute(made, 'core', SWAP)]]
    pallas_call x29 -> x32, Pallas kernels: 46.1 us -> 47.3 us  [kernel_call(): made(*[holds[place](one) if place in holds else one for place, one in zip...]
  transfers between devices with their start and end apart: 29 -> 29, of which waited for: 16 -> 15; matrix products, arithmetic and copies ran while one was open for 0% -> 0% of each run, Pallas kernels for 32% -> 33%
where the time goes in v8:
time: 123 us
  Pallas kernels  47.3 us (38%)
  waiting for transfers between devices  40.4 us (33%)
  starting transfers between devices  33.7 us (27%)
    pallas_call x32, Pallas kernels, kernel_call(): made(*[holds[place](one) if place in holds else one for place, one in zip...  47.3 us
    ppermute x3, waiting for transfers between devices, onward(): return lax.ppermute(array, CTX, links(2))  11.6 us
    ppermute x4, waiting for transfers between devices, cross(): lax.ppermute(array, CTX, links(2))  8.73 us
    ppermute x6, starting transfers between devices, along(): return lax.ppermute(array, 'dp', pairs)  7.82 us
    ppermute x2, waiting for transfers between devices, send_second(): return lax.ppermute(message, CTX, links(2, upward(reverse)))  7.29 us
    ppermute x2, starting transfers between devices, send_second(): return lax.ppermute(message, CTX, links(2, upward(reverse)))  5.49 us
    ppermute x6, waiting for transfers between devices, along(): return lax.ppermute(array, 'dp', pairs)  5.25 us
    ppermute x3, starting transfers between devices, pack(): return [made, lax.ppermute(made, 'core', SWAP)]  4.24 us
  transfers between devices with their start and end apart: 29, of which 15 were waited for; matrix products, arithmetic and copies ran while one was open for 0% of the time, Pallas kernels for 33%

profile of v8, /device:TPU:1, one launch (start us, length us, event | category | flops | bytes accessed | tf_op | source)
XLA Modules:
  0.0 122.5 jit_solution(10300426524450120149)
XLA Ops:
  0.6 2.2 %collective-permute-start = (bf16[128,2048]{1,0:T(8,128)(2,1)}, bf16[128,2048]{1,0:T(8,128)(2,1)S(1)}, u32[]{:S(2)}, u32[]{:S(2)}) collective-permute-start(bf16[128,2048]{1,0:T(8,128)(2,1)} %refs_0_.1), channel_id=1, source_target_pairs={{0,1},{1,0},{2,3},{3,2},{4,5},{5,4},{6,7},{7,6},{8,9},{9,8},{10,11... | collective-permute-start | bytes 1572872 | tf_op jit(solution)/shard_map/ppermute | solution.py:805
  3.5 1.3 %collective-permute-start.2 = (bf16[128,2048]{1,0:T(8,128)(2,1)}, bf16[128,2048]{1,0:T(8,128)(2,1)S(1)}, u32[]{:S(2)}, u32[]{:S(2)}) collective-permute-start(bf16[128,2048]{1,0:T(8,128)(2,1)} %refs_0_.1), channel_id=1, source_target_pairs={{0,8},{4,20},{8,0},{12,28},{16,24},{20,4},{24,16},{28,12},{1,9},{5... | collective-permute-start | bytes 1572872 | tf_op jit(solution)/shard_map/ppermute | solution.py:808
  6.0 4.7 %own_memory.1 = (bf16[384,2048]{1,0:T(8,128)(2,1)S(1)}, bf16[384,2048]{1,0:T(8,128)(2,1)S(1)}, bf16[384,2048]{1,0:T(8,128)(2,1)S(1)}, f32[2048,128]{1,0:T(8,128)...) custom-call(bf16[384,2048]{1,0:T(8,128)(2,1)} %bitcast.13, ...), custom_call_target="tpu_custom_call" | custom-call | flops 201326592 | bytes 9437184 | tf_op jit(solution)/shard_map/own_memory/pallas_call | solution.py:74
  10.8 3.9 %collective-permute-done.refs_0_ = bf16[128,2048]{1,0:T(8,128)(2,1)S(1)} collective-permute-done((bf16[128,2048]{1,0:T(8,128)(2,1)}, bf16[128,2048]{1,0:T(8,128)(2,1)S(1)}, u32[]{:S(2)}, u32[]{:S(2)}) %collective-permute-start) | collective-permute-done | bytes 524320 | tf_op jit(solution)/shard_map/ppermute | solution.py:805
  14.8 4.0 %collective-permute-done.3.refs_3_ = bf16[128,2048]{1,0:T(8,128)(2,1)S(1)} collective-permute-done((bf16[128,2048]{1,0:T(8,128)(2,1)}, bf16[128,2048]{1,0:T(8,128)(2,1)S(1)}, u32[]{:S(2)}, u32[]{:S(2)}) %collective-permute-start.3) | collective-permute-done | bytes 524320 | tf_op jit(solution)/shard_map/ppermute | solution.py:808
  23.2 9.1 %collective-permute-done.4.refs_0_ = bf16[128,2048]{1,0:T(8,128)(2,1)S(1)} collective-permute-done((bf16[128,2048]{1,0:T(8,128)(2,1)S(1)}, bf16[128,2048]{1,0:T(8,128)(2,1)S(1)}, u32[]{:S(2)}, u32[]{:S(2)}) %collective-permute-start.4) | collective-permute-done | bytes 524320 | tf_op jit(solution)/shard_map/ppermute | solution.py:811
  32.3 1.3 %collective-permute-start.10 = (bf16[1024,128]{1,0:T(8,128)(2,1)S(1)}, bf16[1024,128]{1,0:T(8,128)(2,1)S(1)}, u32[]{:S(2)}, u32[]{:S(2)}) collective-permute-start(bf16[1024,128]{1,0:T(8,128)(2,1)S(1)} %get-tuple-element.73), channel_id=1, source_target_pairs={{0,8},{4,20},{8,0},{12,28},{16,24},{24,16},{1,9},{5,21},{9,1},{13,... | collective-permute-start | bytes 786440 | tf_op jit(solution)/shard_map/ppermute | solution.py:692
  34.5 4.7 %collective-permute-done.6.refs_2_ = bf16[128,2048]{1,0:T(8,128)(2,1)S(1)} collective-permute-done((bf16[128,2048]{1,0:T(8,128)(2,1)S(1)}, bf16[128,2048]{1,0:T(8,128)(2,1)S(1)}, u32[]{:S(2)}, u32[]{:S(2)}) %collective-permute-start.6) | collective-permute-done | bytes 524320 | tf_op jit(solution)/shard_map/ppermute | solution.py:808
  40.1 2.5 %collective-permute-start.15 = (bf16[896,2048]{1,0:T(8,128)(2,1)S(1)}, bf16[896,2048]{1,0:T(8,128)(2,1)S(1)}, u32[]{:S(2)}, u32[]{:S(2)}) collective-permute-start(bf16[896,2048]{1,0:T(8,128)(2,1)S(1)} %pack.3.refs_0_), channel_id=1, source_target_pairs={{0,4},{4,0},{1,5},{5,1},{2,6},{6,2},{3,7},{7,3},{8,12},{12,8},{9,1... | collective-permute-start | bytes 11010056 | tf_op jit(solution)/shard_map/ppermute | solution.py:761
  45.7 2.4 %collective-permute-start.14 = (bf16[1024,128]{1,0:T(8,128)(2,1)S(1)}, bf16[1024,128]{1,0:T(8,128)(2,1)S(1)}, u32[]{:S(2)}, u32[]{:S(2)}) collective-permute-start(bf16[1024,128]{1,0:T(8,128)(2,1)S(1)} %message.2), channel_id=1, source_target_pairs={{0,16},{4,12},{8,24},{12,4},{20,28},{28,20},{1,17},{5,13},{9,25},{... | collective-permute-start | bytes 786440 | tf_op jit(solution)/shard_map/ppermute | solution.py:705
  48.2 1.8 %turned.1 = (bf16[128,6144]{1,0:T(8,128)(2,1)S(1)}, bf16[256,4096]{1,0:T(8,128)(2,1)S(1)}, f32[8,128]{1,0:T(8,128)S(1)}) custom-call(bf16[384,2048]{1,0:T(8,128)(2,1)S(1)} %get-tuple-element.83.value_ref, bf16[384,2048]{1,0:T(8,128)(2,1)S(1)} %get-tuple-element.84.grad_ref, bf16[1024,128]{1,0:T(8,128)(2,1)S(1)} %get-tuple-element.77.got_ref.after_ref), custom_call_target="tpu_custom_call" | custom-call | flops 1207959552 | tf_op jit(solution)/shard_map/turned/pallas_call | solution.py:74
  50.0 3.0 %project.2 = (f32[384,2048]{1,0:T(8,128)S(1)}, f32[8,128]{1,0:T(8,128)S(1)}) custom-call(bf16[896,2048]{1,0:T(8,128)(2,1)S(1)} %pack.3.refs_0_, bf16[896,2048]{1,0:T(8,128)(2,1)S(1)} %collective-permute-done.15.refs_1_, bf16[384,4096]{1,0:T(8,128)(2,1)S(1)} %get-tuple-element.66.refs_2_.tokens_ref), custom_call_target="tpu_custom_call" | custom-call | flops 2818572288 | tf_op jit(solution)/shard_map/project/pallas_call | solution.py:74
  53.0 6.8 %collective-permute-done.14.refs_4_ = bf16[1024,128]{1,0:T(8,128)(2,1)S(1)} collective-permute-done((bf16[1024,128]{1,0:T(8,128)(2,1)S(1)}, bf16[1024,128]{1,0:T(8,128)(2,1)S(1)}, u32[]{:S(2)}, u32[]{:S(2)}) %collective-permute-start.14) | collective-permute-done | bytes 262176 | tf_op jit(solution)/shard_map/ppermute | solution.py:705
  59.9 1.3 %collective-permute-done.13.refs_3_ = bf16[128,2048]{1,0:T(8,128)(2,1)S(1)} collective-permute-done((bf16[128,2048]{1,0:T(8,128)(2,1)S(1)}, bf16[128,2048]{1,0:T(8,128)(2,1)S(1)}, u32[]{:S(2)}, u32[]{:S(2)}) %collective-permute-start.13) | collective-permute-done | bytes 524320 | tf_op jit(solution)/shard_map/ppermute | solution.py:805
  64.1 1.3 %collective-permute-start.19 = (bf16[128,2048]{1,0:T(8,128)(2,1)S(1)}, bf16[128,2048]{1,0:T(8,128)(2,1)S(1)}, u32[]{:S(2)}, u32[]{:S(2)}) collective-permute-start(bf16[128,2048]{1,0:T(8,128)(2,1)S(1)} %choose.3.refs_3_), channel_id=1, source_target_pairs={{0,16},{4,12},{8,24},{12,4},{16,0},{20,28},{24,8},{28,20},{1,17},{... | collective-permute-start | bytes 1572872 | tf_op jit(solution)/shard_map/ppermute | solution.py:808
  65.4 1.8 %collective-permute-done.20.other_ref = f32[1024,128]{1,0:T(8,128)S(1)} collective-permute-done((f32[1024,128]{1,0:T(8,128)S(1)}, f32[1024,128]{1,0:T(8,128)S(1)}, u32[]{:S(2)}, u32[]{:S(2)}) %collective-permute-start.20) | collective-permute-done | bytes 524320 | tf_op jit(solution)/shard_map/ppermute | solution.py:718
  67.2 1.7 %collective-permute-start.16 = (bf16[128,2048]{1,0:T(8,128)(2,1)S(1)}, bf16[128,2048]{1,0:T(8,128)(2,1)S(1)}, u32[]{:S(2)}, u32[]{:S(2)}) collective-permute-start(bf16[128,2048]{1,0:T(8,128)(2,1)S(1)} %get-tuple-element.86), channel_id=1, source_target_pairs={{0,1},{1,0},{2,3},{3,2},{4,5},{5,4},{6,7},{7,6},{8,9},{9,8},{10,11... | collective-permute-start | bytes 1572872 | tf_op jit(solution)/shard_map/ppermute | solution.py:805
  69.1 5.4 %masked_grad.1 = (bf16[384,2048]{1,0:T(8,128)(2,1)S(1)}, bf16[384,2048]{1,0:T(8,128)(2,1)S(1)}) custom-call(s32[384,2048]{1,0:T(8,128)} %bitcast.16, bf16[384,2048]{1,0:T(8,128)(2,1)S(1)} %get-tuple-element.84.grad_ref, bf16[384,2048]{1,0:T(8,128)(2,1)S(1)} %get-tuple-element.83.value_ref, bf16[384,2048]{1,0:T(8,128)(2,1)S(1)} %get-tuple-element.89.keys_ref, ...), custom_call_target="tpu_custom_call" | custom-call | flops 2415919104 | bytes 9437184 | tf_op jit(solution)/shard_map/masked_grad/pallas_call | solution.py:74
  74.5 3.9 %grad_tokens.3 = (bf16[384,4096]{1,0:T(8,128)(2,1)}, f32[8,128]{1,0:T(8,128)S(1)}) custom-call(bf16[896,2048]{1,0:T(8,128)(2,1)S(1)} %pack.3.refs_0_, bf16[896,2048]{1,0:T(8,128)(2,1)S(1)} %collective-permute-done.15.refs_1_, bf16[384,2048]{1,0:T(8,128)(2,1)S(1)} %get-tuple-element.93.refs_2_.refs_4_), custom_call_target="tpu_custom_call" | custom-call | flops 2818572288 | tf_op jit(solution)/shard_map/grad_tokens/pallas_call | solution.py:74
  78.5 4.3 %products.1 = (f32[384,2048]{1,0:T(8,128)S(1)}, bf16[384,4096]{1,0:T(8,128)(2,1)}, f32[8,128]{1,0:T(8,128)S(1)}) custom-call(bf16[512,2048]{1,0:T(8,128)(2,1)S(1)} %pack.4.refs_0_, bf16[512,2048]{1,0:T(8,128)(2,1)S(1)} %collective-permute-done.21.refs_1_, ...), custom_call_target="tpu_custom_call", output_to_operand_aliasing={{0}: (3, {}), {1}: (5, {})} | custom-call | flops 3221225472 | tf_op jit(solution)/shard_map/products/pallas_call | solution.py:74
  85.0 2.6 %collective-permute-done.22.refs_1_ = bf16[512,2048]{1,0:T(8,128)(2,1)S(1)} collective-permute-done((bf16[512,2048]{1,0:T(8,128)(2,1)S(1)}, bf16[512,2048]{1,0:T(8,128)(2,1)S(1)}, u32[]{:S(2)}, u32[]{:S(2)}) %collective-permute-start.22) | collective-permute-done | bytes 2097184 | tf_op jit(solution)/shard_map/ppermute | solution.py:761
  87.6 2.0 %project.3 = (f32[384,2048]{1,0:T(8,128)S(1)}, f32[8,128]{1,0:T(8,128)S(1)}) custom-call(bf16[512,2048]{1,0:T(8,128)(2,1)S(1)} %pack.5.refs_0_, bf16[512,2048]{1,0:T(8,128)(2,1)S(1)} %collective-permute-done.22.refs_1_, bf16[384,4096]{1,0:T(8,128)(2,1)S(1)} %get-tuple-element.66.refs_2_.tokens_ref, ...), custom_call_target="tpu_custom_call", output_to_operand_aliasing={{0}: (3, {})} | custom-call | flops 1610612736 | tf_op jit(solution)/shard_map/project/pallas_call | solution.py:74
  89.7 2.5 %collective-permute-done.23.refs_0_ = bf16[128,2048]{1,0:T(8,128)(2,1)S(1)} collective-permute-done((bf16[128,2048]{1,0:T(8,128)(2,1)S(1)}, bf16[128,2048]{1,0:T(8,128)(2,1)S(1)}, u32[]{:S(2)}, u32[]{:S(2)}) %collective-permute-start.23) | collective-permute-done | bytes 524320 | tf_op jit(solution)/shard_map/ppermute | solution.py:811
  93.1 2.7 %grad_tokens.4 = (bf16[384,4096]{1,0:T(8,128)(2,1)}, f32[8,128]{1,0:T(8,128)S(1)}) custom-call(bf16[512,2048]{1,0:T(8,128)(2,1)S(1)} %pack.5.refs_0_, bf16[512,2048]{1,0:T(8,128)(2,1)S(1)} %collective-permute-done.22.refs_1_, bf16[384,2048]{1,0:T(8,128)(2,1)S(1)} %get-tuple-element.93.refs_2_.refs_4_, ...), custom_call_target="tpu_custom_call", output_to_operand_aliasing={{0}: (3, {})} | custom-call | flops 1610612736 | tf_op jit(solution)/shard_map/grad_tokens/pallas_call | solution.py:74
  95.8 1.7 %queries.1 = (bf16[384,2048]{1,0:T(8,128)(2,1)S(1)}, f32[2048,128]{1,0:T(8,128)S(1)}, bf16[2048,128]{1,0:T(8,128)(2,1)S(1)}) custom-call(bf16[384,4096]{1,0:T(8,128)(2,1)S(1)} %get-tuple-element.66.refs_2_.tokens_ref, f32[384,2048]{1,0:T(8,128)S(1)} %get-tuple-element.104.sum_ref, bf16[384,2048]{1,0:T(8,128)(2,1)S(1)} %get-tuple-element.105.mask_ref, ...), custom_call_target="tpu_custom_call" | custom-call | flops 402653184 | tf_op jit(solution)/shard_map/queries/pallas_call | solution.py:74
  97.6 1.3 %grad_tokens.5 = (bf16[384,4096]{1,0:T(8,128)(2,1)}, f32[8,128]{1,0:T(8,128)S(1)}) custom-call(bf16[128,2048]{1,0:T(8,128)(2,1)S(1)} %join.9.refs_0_, bf16[128,2048]{1,0:T(8,128)(2,1)S(1)} %collective-permute-done.24.refs_1_, bf16[384,2048]{1,0:T(8,128)(2,1)S(1)} %get-tuple-element.93.refs_2_.refs_4_, ...), custom_call_target="tpu_custom_call", output_to_operand_aliasing={{0}: (3, {})} | custom-call | flops 402653184 | tf_op jit(solution)/shard_map/grad_tokens/pallas_call | solution.py:74
  100.9 5.1 %attended.1 = (bf16[384,2048]{1,0:T(8,128)(2,1)}, f32[8,128]{1,0:T(8,128)S(1)}) custom-call(bf16[384,2048]{1,0:T(8,128)(2,1)S(1)} %get-tuple-element.109.query_ref, bf16[384,2048]{1,0:T(8,128)(2,1)S(1)} %get-tuple-element.89.keys_ref, bf16[384,2048]{1,0:T(8,128)(2,1)S(1)} %get-tuple-element.83.value_ref, bf16[2048,128]{1,0:T(8,128)(2,1)S(1)} %get-tuple-element.91.high_ref, ...), custom_call_target="tpu_custom_call" | custom-call | flops 2415919104 | bytes 6291456 | tf_op jit(solution)/shard_map/attended/pallas_call | solution.py:74
  107.1 3.1 %collective-permute-start.27 = (bf16[1024,128]{1,0:T(8,128)(2,1)S(1)}, bf16[1024,128]{1,0:T(8,128)(2,1)S(1)}, u32[]{:S(2)}, u32[]{:S(2)}) collective-permute-start(bf16[1024,128]{1,0:T(8,128)(2,1)S(1)} %message.3), channel_id=1, source_target_pairs={{4,12},{12,4},{16,0},{20,28},{24,8},{28,20},{5,13},{13,5},{17,1},{... | collective-permute-start | bytes 786440 | tf_op jit(solution)/shard_map/ppermute | solution.py:705
  110.1 3.9 %value_part.1 = (f32[384,2048]{1,0:T(8,128)S(1)}, f32[8,128]{1,0:T(8,128)S(1)}) custom-call(bf16[384,2048]{1,0:T(8,128)(2,1)S(1)} %get-tuple-element.109.query_ref, bf16[384,2048]{1,0:T(8,128)(2,1)S(1)} %get-tuple-element.89.keys_ref, bf16[384,2048]{1,0:T(8,128)(2,1)S(1)} %get-tuple-element.84.grad_ref), custom_call_target="tpu_custom_call" | custom-call | flops 1811939328 | tf_op jit(solution)/shard_map/value_part/pallas_call | solution.py:74
  114.6 2.1 %collective-permute-start.28 = (f32[1024,128]{1,0:T(8,128)S(1)}, f32[1024,128]{1,0:T(8,128)S(1)}, u32[]{:S(2)}, u32[]{:S(2)}) collective-permute-start(f32[1024,128]{1,0:T(8,128)S(1)} %state.3.state_ref), channel_id=1, source_target_pairs={{0,4},{4,0},{1,5},{5,1},{2,6},{6,2},{3,7},{7,3},{8,12},{12,8},{9,1... | collective-permute-start | bytes 1572872 | tf_op jit(solution)/shard_map/ppermute | solution.py:718
  116.7 1.9 %key_part.1.key_ref = f32[384,2048]{1,0:T(8,128)S(1)} custom-call(bf16[384,2048]{1,0:T(8,128)(2,1)S(1)} %get-tuple-element.109.query_ref, bf16[128,6144]{1,0:T(8,128)(2,1)S(1)} %get-tuple-element.113.top_ref, bf16[256,4096]{1,0:T(8,128)(2,1)S(1)} %get-tuple-element.114.bottom_ref), custom_call_target="tpu_custom_call" | custom-call | flops 1207959552 | tf_op jit(solution)/shard_map/key_part/pallas_call | solution.py:74
  118.8 3.5 %outer.1 = (bf16[384,2048]{1,0:T(8,128)(2,1)}, bf16[384,2048]{1,0:T(8,128)(2,1)}) custom-call(f32[384,2048]{1,0:T(8,128)S(1)} %key_part.1.key_ref, f32[384,2048]{1,0:T(8,128)S(1)} %get-tuple-element.115.val_ref, bf16[384,2048]{1,0:T(8,128)(2,1)S(1)} %get-tuple-element.89.keys_ref, bf16[384,2048]{1,0:T(8,128)(2,1)S(1)} %get-tuple-element.83.value_ref, ...), custom_call_target="tpu_custom_call" | custom-call | flops 805306368 | bytes 15728640 | tf_op jit(solution)/shard_map/outer/pallas_call | solution.py:74
  (60 shorter events, 21.3 us)
Async XLA Ops:
  0.6 14.1 %collective-permute-start = (bf16[128,2048]{1,0:T(8,128)(2,1)}, bf16[128,2048]{1,0:T(8,128)(2,1)S(1)}, u32[]{:S(2)}, u32[]{:S(2)}) collective-permute-start(bf16[128,2048]{1,0:T(8,128)(2,1)} %refs_0_.1), channel_id=1, source_target_pairs={{0,1},{1,0},{2,3},{3,2},{4,5},{5,4},{6,7},{7,6},{8,9},{9,8},{10,11... | collective-permute-start | bytes 1572872 | tf_op jit(solution)/shard_map/ppermute | solution.py:805
  2.8 11.9 %collective-permute-start.1 = (bf16[128,2048]{1,0:T(8,128)(2,1)}, bf16[128,2048]{1,0:T(8,128)(2,1)S(1)}, u32[]{:S(2)}, u32[]{:S(2)}) collective-permute-start(bf16[128,2048]{1,0:T(8,128)(2,1)} %refs_0_.1), channel_id=1, source_target_pairs={{1,2},{2,1},{5,6},{6,5},{9,10},{10,9},{13,14},{14,13},{17,18},{18,... | collective-permute-start | bytes 1572872 | tf_op jit(solution)/shard_map/ppermute | solution.py:805
  3.5 11.2 %collective-permute-start.2 = (bf16[128,2048]{1,0:T(8,128)(2,1)}, bf16[128,2048]{1,0:T(8,128)(2,1)S(1)}, u32[]{:S(2)}, u32[]{:S(2)}) collective-permute-start(bf16[128,2048]{1,0:T(8,128)(2,1)} %refs_0_.1), channel_id=1, source_target_pairs={{0,8},{4,20},{8,0},{12,28},{16,24},{20,4},{24,16},{28,12},{1,9},{5... | collective-permute-start | bytes 1572872 | tf_op jit(solution)/shard_map/ppermute | solution.py:808
  4.8 14.0 %collective-permute-start.3 = (bf16[128,2048]{1,0:T(8,128)(2,1)}, bf16[128,2048]{1,0:T(8,128)(2,1)S(1)}, u32[]{:S(2)}, u32[]{:S(2)}) collective-permute-start(bf16[128,2048]{1,0:T(8,128)(2,1)} %refs_0_.1), channel_id=1, source_target_pairs={{0,16},{4,12},{8,24},{12,4},{16,0},{20,28},{24,8},{28,20},{1,17},{... | collective-permute-start | bytes 1572872 | tf_op jit(solution)/shard_map/ppermute | solution.py:808
  18.8 3.0 %collective-permute-start.9 = (bf16[2048,128]{1,0:T(8,128)(2,1)S(1)}, bf16[2048,128]{1,0:T(8,128)(2,1)S(1)}, u32[]{:S(2)}, u32[]{:S(2)}) collective-permute-start(bf16[2048,128]{1,0:T(8,128)(2,1)S(1)} %get-tuple-element.72), channel_id=1, source_target_pairs={{0,4},{4,0},{1,5},{5,1},{2,6},{6,2},{3,7},{7,3},{8,12},{12,8},{9,1... | collective-permute-start | bytes 1572872 | tf_op jit(solution)/shard_map/ppermute | solution.py:682
  19.4 12.9 %collective-permute-start.4 = (bf16[128,2048]{1,0:T(8,128)(2,1)S(1)}, bf16[128,2048]{1,0:T(8,128)(2,1)S(1)}, u32[]{:S(2)}, u32[]{:S(2)}) collective-permute-start(bf16[128,2048]{1,0:T(8,128)(2,1)S(1)} %get-tuple-element.68.refs_1_), channel_id=1, source_target_pairs={{0,16},{4,12},{8,24},{12,4},{16,0},{20,28},{24,8},{28,20},{1,17},{... | collective-permute-start | bytes 1572872 | tf_op jit(solution)/shard_map/ppermute | solution.py:811
  20.6 13.9 %collective-permute-start.5 = (bf16[128,2048]{1,0:T(8,128)(2,1)S(1)}, bf16[128,2048]{1,0:T(8,128)(2,1)S(1)}, u32[]{:S(2)}, u32[]{:S(2)}) collective-permute-start(bf16[128,2048]{1,0:T(8,128)(2,1)S(1)} %get-tuple-element.69.refs_4_), channel_id=1, source_target_pairs={{0,8},{4,20},{8,0},{12,28},{16,24},{20,4},{24,16},{28,12},{1,9},{5... | collective-permute-start | bytes 1572872 | tf_op jit(solution)/shard_map/ppermute | solution.py:808
  20.8 18.4 %collective-permute-start.6 = (bf16[128,2048]{1,0:T(8,128)(2,1)S(1)}, bf16[128,2048]{1,0:T(8,128)(2,1)S(1)}, u32[]{:S(2)}, u32[]{:S(2)}) collective-permute-start(bf16[128,2048]{1,0:T(8,128)(2,1)S(1)} %get-tuple-element.69.refs_4_), channel_id=1, source_target_pairs={{0,16},{4,12},{8,24},{12,4},{16,0},{20,28},{24,8},{28,20},{1,17},{... | collective-permute-start | bytes 1572872 | tf_op jit(solution)/shard_map/ppermute | solution.py:808
  21.1 18.1 %collective-permute-start.7 = (bf16[128,2048]{1,0:T(8,128)(2,1)S(1)}, bf16[128,2048]{1,0:T(8,128)(2,1)S(1)}, u32[]{:S(2)}, u32[]{:S(2)}) collective-permute-start(bf16[128,2048]{1,0:T(8,128)(2,1)S(1)} %get-tuple-element.69.refs_4_), channel_id=1, source_target_pairs={{1,2},{2,1},{5,6},{6,5},{9,10},{10,9},{13,14},{14,13},{17,18},{18,... | collective-permute-start | bytes 1572872 | tf_op jit(solution)/shard_map/ppermute | solution.py:805
  21.8 17.4 %collective-permute-start.8 = (bf16[128,2048]{1,0:T(8,128)(2,1)S(1)}, bf16[128,2048]{1,0:T(8,128)(2,1)S(1)}, u32[]{:S(2)}, u32[]{:S(2)}) collective-permute-start(bf16[128,2048]{1,0:T(8,128)(2,1)S(1)} %get-tuple-element.70.inner_ref), channel_id=1, source_target_pairs={{1,0},{2,3},{5,4},{6,7},{9,8},{10,11},{13,12},{14,15},{17,16},{18,... | collective-permute-start | bytes 1572872 | tf_op jit(solution)/shard_map/ppermute | solution.py:805
  23.1 16.7 %copy-start = (bf16[128,2048]{1,0:T(8,128)(2,1)S(1)}, bf16[128,2048]{1,0:T(8,128)(2,1)}, u32[]{:S(2)}) copy-start(bf16[128,2048]{1,0:T(8,128)(2,1)} %refs_0_.1) | copy-start | bytes 1572868
  32.3 7.5 %collective-permute-start.10 = (bf16[1024,128]{1,0:T(8,128)(2,1)S(1)}, bf16[1024,128]{1,0:T(8,128)(2,1)S(1)}, u32[]{:S(2)}, u32[]{:S(2)}) collective-permute-start(bf16[1024,128]{1,0:T(8,128)(2,1)S(1)} %get-tuple-element.73), channel_id=1, source_target_pairs={{0,8},{4,20},{8,0},{12,28},{16,24},{24,16},{1,9},{5,21},{9,1},{13,... | collective-permute-start | bytes 786440 | tf_op jit(solution)/shard_map/ppermute | solution.py:692
  40.1 9.9 %collective-permute-start.15 = (bf16[896,2048]{1,0:T(8,128)(2,1)S(1)}, bf16[896,2048]{1,0:T(8,128)(2,1)S(1)}, u32[]{:S(2)}, u32[]{:S(2)}) collective-permute-start(bf16[896,2048]{1,0:T(8,128)(2,1)S(1)} %pack.3.refs_0_), channel_id=1, source_target_pairs={{0,4},{4,0},{1,5},{5,1},{2,6},{6,2},{3,7},{7,3},{8,12},{12,8},{9,1... | collective-permute-start | bytes 11010056 | tf_op jit(solution)/shard_map/ppermute | solution.py:761
  42.6 17.3 %collective-permute-start.11 = (bf16[128,2048]{1,0:T(8,128)(2,1)S(1)}, bf16[128,2048]{1,0:T(8,128)(2,1)S(1)}, u32[]{:S(2)}, u32[]{:S(2)}) collective-permute-start(bf16[128,2048]{1,0:T(8,128)(2,1)S(1)} %choose.2.refs_0_), channel_id=1, source_target_pairs={{0,8},{4,20},{8,0},{12,28},{16,24},{20,4},{24,16},{28,12},{1,9},{5... | collective-permute-start | bytes 1572872 | tf_op jit(solution)/shard_map/ppermute | solution.py:808
  43.4 16.5 %collective-permute-start.12 = (bf16[128,2048]{1,0:T(8,128)(2,1)S(1)}, bf16[128,2048]{1,0:T(8,128)(2,1)S(1)}, u32[]{:S(2)}, u32[]{:S(2)}) collective-permute-start(bf16[128,2048]{1,0:T(8,128)(2,1)S(1)} %choose.2.refs_0_), channel_id=1, source_target_pairs={{0,16},{4,12},{8,24},{12,4},{16,0},{20,28},{24,8},{28,20},{1,17},{... | collective-permute-start | bytes 1572872 | tf_op jit(solution)/shard_map/ppermute | solution.py:808
  44.4 16.9 %collective-permute-start.13 = (bf16[128,2048]{1,0:T(8,128)(2,1)S(1)}, bf16[128,2048]{1,0:T(8,128)(2,1)S(1)}, u32[]{:S(2)}, u32[]{:S(2)}) collective-permute-start(bf16[128,2048]{1,0:T(8,128)(2,1)S(1)} %get-tuple-element.76.inner_ref), channel_id=1, source_target_pairs={{1,0},{2,3},{5,4},{6,7},{9,8},{10,11},{13,12},{14,15},{17,16},{18,... | collective-permute-start | bytes 1572872 | tf_op jit(solution)/shard_map/ppermute | solution.py:805
  45.7 14.1 %collective-permute-start.14 = (bf16[1024,128]{1,0:T(8,128)(2,1)S(1)}, bf16[1024,128]{1,0:T(8,128)(2,1)S(1)}, u32[]{:S(2)}, u32[]{:S(2)}) collective-permute-start(bf16[1024,128]{1,0:T(8,128)(2,1)S(1)} %message.2), channel_id=1, source_target_pairs={{0,16},{4,12},{8,24},{12,4},{20,28},{28,20},{1,17},{5,13},{9,25},{... | collective-permute-start | bytes 786440 | tf_op jit(solution)/shard_map/ppermute | solution.py:705
  61.4 17.0 %collective-permute-start.21 = (bf16[512,2048]{1,0:T(8,128)(2,1)S(1)}, bf16[512,2048]{1,0:T(8,128)(2,1)S(1)}, u32[]{:S(2)}, u32[]{:S(2)}) collective-permute-start(bf16[512,2048]{1,0:T(8,128)(2,1)S(1)} %pack.4.refs_0_), channel_id=1, source_target_pairs={{0,4},{4,0},{1,5},{5,1},{2,6},{6,2},{3,7},{7,3},{8,12},{12,8},{9,1... | collective-permute-start | bytes 6291464 | tf_op jit(solution)/shard_map/ppermute | solution.py:761
  62.7 4.4 %collective-permute-start.20 = (f32[1024,128]{1,0:T(8,128)S(1)}, f32[1024,128]{1,0:T(8,128)S(1)}, u32[]{:S(2)}, u32[]{:S(2)}) collective-permute-start(f32[1024,128]{1,0:T(8,128)S(1)} %state.2.state_ref), channel_id=1, source_target_pairs={{0,4},{4,0},{1,5},{5,1},{2,6},{6,2},{3,7},{7,3},{8,12},{12,8},{9,1... | collective-permute-start | bytes 1572872 | tf_op jit(solution)/shard_map/ppermute | solution.py:718
  62.8 20.0 %collective-permute-start.17 = (bf16[128,2048]{1,0:T(8,128)(2,1)S(1)}, bf16[128,2048]{1,0:T(8,128)(2,1)S(1)}, u32[]{:S(2)}, u32[]{:S(2)}) collective-permute-start(bf16[128,2048]{1,0:T(8,128)(2,1)S(1)} %get-tuple-element.87.refs_1_), channel_id=1, source_target_pairs={{0,16},{4,12},{8,24},{12,4},{16,0},{20,28},{24,8},{28,20},{1,17},{... | collective-permute-start | bytes 1572872 | tf_op jit(solution)/shard_map/ppermute | solution.py:811
  63.4 19.4 %collective-permute-start.18 = (bf16[128,2048]{1,0:T(8,128)(2,1)S(1)}, bf16[128,2048]{1,0:T(8,128)(2,1)S(1)}, u32[]{:S(2)}, u32[]{:S(2)}) collective-permute-start(bf16[128,2048]{1,0:T(8,128)(2,1)S(1)} %choose.3.refs_3_), channel_id=1, source_target_pairs={{0,8},{4,20},{8,0},{12,28},{16,24},{20,4},{24,16},{28,12},{1,9},{5... | collective-permute-start | bytes 1572872 | tf_op jit(solution)/shard_map/ppermute | solution.py:808
  64.1 18.7 %collective-permute-start.19 = (bf16[128,2048]{1,0:T(8,128)(2,1)S(1)}, bf16[128,2048]{1,0:T(8,128)(2,1)S(1)}, u32[]{:S(2)}, u32[]{:S(2)}) collective-permute-start(bf16[128,2048]{1,0:T(8,128)(2,1)S(1)} %choose.3.refs_3_), channel_id=1, source_target_pairs={{0,16},{4,12},{8,24},{12,4},{16,0},{20,28},{24,8},{28,20},{1,17},{... | collective-permute-start | bytes 1572872 | tf_op jit(solution)/shard_map/ppermute | solution.py:808
  67.2 15.6 %collective-permute-start.16 = (bf16[128,2048]{1,0:T(8,128)(2,1)S(1)}, bf16[128,2048]{1,0:T(8,128)(2,1)S(1)}, u32[]{:S(2)}, u32[]{:S(2)}) collective-permute-start(bf16[128,2048]{1,0:T(8,128)(2,1)S(1)} %get-tuple-element.86), channel_id=1, source_target_pairs={{0,1},{1,0},{2,3},{3,2},{4,5},{5,4},{6,7},{7,6},{8,9},{9,8},{10,11... | collective-permute-start | bytes 1572872 | tf_op jit(solution)/shard_map/ppermute | solution.py:805
  83.2 4.4 %collective-permute-start.22 = (bf16[512,2048]{1,0:T(8,128)(2,1)S(1)}, bf16[512,2048]{1,0:T(8,128)(2,1)S(1)}, u32[]{:S(2)}, u32[]{:S(2)}) collective-permute-start(bf16[512,2048]{1,0:T(8,128)(2,1)S(1)} %pack.5.refs_0_), channel_id=1, source_target_pairs={{0,4},{4,0},{1,5},{5,1},{2,6},{6,2},{3,7},{7,3},{8,12},{12,8},{9,1... | collective-permute-start | bytes 6291464 | tf_op jit(solution)/shard_map/ppermute | solution.py:761
  83.8 8.3 %collective-permute-start.23 = (bf16[128,2048]{1,0:T(8,128)(2,1)S(1)}, bf16[128,2048]{1,0:T(8,128)(2,1)S(1)}, u32[]{:S(2)}, u32[]{:S(2)}) collective-permute-start(bf16[128,2048]{1,0:T(8,128)(2,1)S(1)} %get-tuple-element.101.refs_2_), channel_id=1, source_target_pairs={{0,16},{4,12},{8,24},{12,4},{16,0},{20,28},{24,8},{28,20},{1,17},{... | collective-permute-start | bytes 1572872 | tf_op jit(solution)/shard_map/ppermute | solution.py:811
  92.1 3.6 %collective-permute-start.24 = (bf16[128,2048]{1,0:T(8,128)(2,1)S(1)}, bf16[128,2048]{1,0:T(8,128)(2,1)S(1)}, u32[]{:S(2)}, u32[]{:S(2)}) collective-permute-start(bf16[128,2048]{1,0:T(8,128)(2,1)S(1)} %join.9.refs_0_), channel_id=1, source_target_pairs={{0,4},{4,0},{1,5},{5,1},{2,6},{6,2},{3,7},{7,3},{8,12},{12,8},{9,1... | collective-permute-start | bytes 1572872 | tf_op jit(solution)/shard_map/ppermute | solution.py:802
  97.5 2.0 %collective-permute-start.25 = (bf16[2048,128]{1,0:T(8,128)(2,1)S(1)}, bf16[2048,128]{1,0:T(8,128)(2,1)S(1)}, u32[]{:S(2)}, u32[]{:S(2)}) collective-permute-start(bf16[2048,128]{1,0:T(8,128)(2,1)S(1)} %get-tuple-element.118), channel_id=1, source_target_pairs={{0,4},{4,0},{1,5},{5,1},{2,6},{6,2},{3,7},{7,3},{8,12},{12,8},{9,1... | collective-permute-start | bytes 1572872 | tf_op jit(solution)/shard_map/ppermute | solution.py:682
  99.6 7.4 %collective-permute-start.26 = (bf16[1024,128]{1,0:T(8,128)(2,1)S(1)}, bf16[1024,128]{1,0:T(8,128)(2,1)S(1)}, u32[]{:S(2)}, u32[]{:S(2)}) collective-permute-start(bf16[1024,128]{1,0:T(8,128)(2,1)S(1)} %get-tuple-element.120), channel_id=1, source_target_pairs={{0,8},{8,0},{16,24},{20,4},{24,16},{28,12},{1,9},{9,1},{17,25},{21... | collective-permute-start | bytes 786440 | tf_op jit(solution)/shard_map/ppermute | solution.py:692
  107.1 7.4 %collective-permute-start.27 = (bf16[1024,128]{1,0:T(8,128)(2,1)S(1)}, bf16[1024,128]{1,0:T(8,128)(2,1)S(1)}, u32[]{:S(2)}, u32[]{:S(2)}) collective-permute-start(bf16[1024,128]{1,0:T(8,128)(2,1)S(1)} %message.3), channel_id=1, source_target_pairs={{4,12},{12,4},{16,0},{20,28},{24,8},{28,20},{5,13},{13,5},{17,1},{... | collective-permute-start | bytes 786440 | tf_op jit(solution)/shard_map/ppermute | solution.py:705
  114.6 4.0 %collective-permute-start.28 = (f32[1024,128]{1,0:T(8,128)S(1)}, f32[1024,128]{1,0:T(8,128)S(1)}, u32[]{:S(2)}, u32[]{:S(2)}) collective-permute-start(f32[1024,128]{1,0:T(8,128)S(1)} %state.3.state_ref), channel_id=1, source_target_pairs={{0,4},{4,0},{1,5},{5,1},{2,6},{6,2},{3,7},{7,3},{8,12},{12,8},{9,1... | collective-permute-start | bytes 1572872 | tf_op jit(solution)/shard_map/ppermute | solution.py:718

commit v9 on v8

--- a/solution.py
+++ b/solution.py
@@ -705,6 +705,38 @@
     return lax.ppermute(message, CTX, links(2, upward(reverse)))
 
 
+def sum_kernel(*refs):
+    total = refs[0][...].astype(f32) + refs[1][...].astype(f32)
+    refs[-1][...] = total + refs[2][...].astype(f32)
+
+
+def send_direct(own, sent, reverse, before, beside):
+    half = (own.shape[0] // 2, HEAD)
+    sibling = lax.ppermute(sent, "core", SWAP)
+    _, sent = kernel_call(
+        both_kernel,
+        "VVA",
+        (own, sibling, before),
+        "VV",
+        [(half, f32), (half, bf16)],
+        "both",
+        (0, 0),
+    )
+    got = []
+    for flip in (3, 1, 2):
+        pairs = [
+            (chip * 2 + core, (chip ^ flip) * 2 + core)
+            for chip in range(4)
+            for core in range(2)
+            if (chip ^ flip < chip) == reverse
+        ]
+        got.append(lax.ppermute(sent, CTX, pairs))
+    (state,) = kernel_call(
+        sum_kernel, "VVV" + "A" * len(beside), (*got, *beside), "V", [(half, f32)], "state", (0, 0)
+    )
+    return add_siblings(state, sibling, reverse)
+
+
 def add_up(got, more, sibling, reverse, others=()):
     (state,) = kernel_call(
         functools.partial(state_kernel, reverse),
@@ -715,6 +747,10 @@
         "state",
         (0, 0),
     )
+    return add_siblings(state, sibling, reverse)
+
+
+def add_siblings(state, sibling, reverse):
     other = lax.ppermute(state, "core", SWAP)
     return kernel_call(
         functools.partial(whole_kernel, reverse),
@@ -881,9 +917,7 @@
         special, start, late, tokens, masked=masked, grad=grad, project=False
     )
     if special:
-        twin, both, got = send_first(own, sent, True, [back_mark])
-        more = send_second(got, both, True, [attended_mark])
-        adjoint = add_up(got, more, twin, True, [value_mark])
+        adjoint = send_direct(own, sent, True, back_mark, (attended_mark, value_mark))
     else:
         adjoint = halves(scan_any(own, sent, chips * 2, True))
     grad_keys, grad_values = outer_call(

time: 123 us -> 124 us (level)
  waiting for transfers between devices: 40.4 us -> 42.7 us
  starting transfers between devices: 33.7 us -> 31.6 us
    ppermute x2 -> x6, waiting for transfers between devices: 1.81 us -> 6.15 us  [the longest x3 3.76 us: send_direct(): got.append(lax.ppermute(sent, CTX, pairs))]
    ppermute x2 -> x1, starting transfers between devices: 5.49 us -> 2.43 us  [send_second(): return lax.ppermute(message, CTX, links(2, upward(reverse)))]
    ppermute x2 -> x6, starting transfers between devices: 2.21 us -> 4.54 us  [the longest x3 3.86 us: send_direct(): got.append(lax.ppermute(sent, CTX, pairs))]
    ppermute x2 -> x1, starting transfers between devices: 2.59 us -> 1.29 us  [send_first(): return (sibling, both, lax.ppermute(sent, CTX, links(1, upward(reverse))))]
    pallas_call x32 -> x31, Pallas kernels: 47.3 us -> 48 us  [kernel_call(): made(*[holds[place](one) if place in holds else one for place, one in zip...]
    ppermute x2 -> x1, waiting for transfers between devices: 7.29 us -> 6.84 us  [send_second(): return lax.ppermute(message, CTX, links(2, upward(reverse)))]
  transfers between devices with their start and end apart: 29 -> 30, of which waited for: 15 -> 14; matrix products, arithmetic and copies ran while one was open for 0% -> 0% of each run, Pallas kernels for 33% -> 33%
where the time goes in v9:
time: 124 us; the launch traced here: 123 us
  Pallas kernels  48 us (39%)
  waiting for transfers between devices  42.7 us (34%)
  starting transfers between devices  31.6 us (25%)
    pallas_call x31, Pallas kernels, kernel_call(): made(*[holds[place](one) if place in holds else one for place, one in zip...  48 us
    ppermute x3, waiting for transfers between devices, onward(): return lax.ppermute(array, CTX, links(2))  11.6 us
    ppermute x4, waiting for transfers between devices, cross(): lax.ppermute(array, CTX, links(2))  8.73 us
    ppermute x6, starting transfers between devices, along(): return lax.ppermute(array, 'dp', pairs)  7.82 us
    ppermute x1, waiting for transfers between devices, send_second(): return lax.ppermute(message, CTX, links(2, upward(reverse)))  6.84 us
    ppermute x6, waiting for transfers between devices, along(): return lax.ppermute(array, 'dp', pairs)  5.25 us
    ppermute x3, starting transfers between devices, pack(): return [made, lax.ppermute(made, 'core', SWAP)]  4.24 us
    ppermute x3, starting transfers between devices, send_direct(): got.append(lax.ppermute(sent, CTX, pairs))  3.86 us
  transfers between devices with their start and end apart: 30, of which 14 were waited for; matrix products, arithmetic and copies ran while one was open for 0% of the time, Pallas kernels for 33%

profile of v9, /device:TPU:1, one launch (start us, length us, event | category | flops | bytes accessed | tf_op | source)
XLA Modules:
  0.0 123.5 jit_solution(5931822394816564767)
XLA Ops:
  0.6 2.2 %collective-permute-start = (bf16[128,2048]{1,0:T(8,128)(2,1)}, bf16[128,2048]{1,0:T(8,128)(2,1)S(1)}, u32[]{:S(2)}, u32[]{:S(2)}) collective-permute-start(bf16[128,2048]{1,0:T(8,128)(2,1)} %refs_0_.1), channel_id=1, source_target_pairs={{0,1},{1,0},{2,3},{3,2},{4,5},{5,4},{6,7},{7,6},{8,9},{9,8},{10,11... | collective-permute-start | bytes 1572872 | tf_op jit(solution)/shard_map/ppermute | solution.py:841
  3.5 1.3 %collective-permute-start.2 = (bf16[128,2048]{1,0:T(8,128)(2,1)}, bf16[128,2048]{1,0:T(8,128)(2,1)S(1)}, u32[]{:S(2)}, u32[]{:S(2)}) collective-permute-start(bf16[128,2048]{1,0:T(8,128)(2,1)} %refs_0_.1), channel_id=1, source_target_pairs={{0,8},{4,20},{8,0},{12,28},{16,24},{20,4},{24,16},{28,12},{1,9},{5... | collective-permute-start | bytes 1572872 | tf_op jit(solution)/shard_map/ppermute | solution.py:844
  6.0 4.7 %own_memory.1 = (bf16[384,2048]{1,0:T(8,128)(2,1)S(1)}, bf16[384,2048]{1,0:T(8,128)(2,1)S(1)}, bf16[384,2048]{1,0:T(8,128)(2,1)S(1)}, f32[2048,128]{1,0:T(8,128)...) custom-call(bf16[384,2048]{1,0:T(8,128)(2,1)} %bitcast.13, ...), custom_call_target="tpu_custom_call" | custom-call | flops 201326592 | bytes 9437184 | tf_op jit(solution)/shard_map/own_memory/pallas_call | solution.py:74
  10.8 3.9 %collective-permute-done.refs_0_ = bf16[128,2048]{1,0:T(8,128)(2,1)S(1)} collective-permute-done((bf16[128,2048]{1,0:T(8,128)(2,1)}, bf16[128,2048]{1,0:T(8,128)(2,1)S(1)}, u32[]{:S(2)}, u32[]{:S(2)}) %collective-permute-start) | collective-permute-done | bytes 524320 | tf_op jit(solution)/shard_map/ppermute | solution.py:841
  14.8 4.0 %collective-permute-done.3.refs_3_ = bf16[128,2048]{1,0:T(8,128)(2,1)S(1)} collective-permute-done((bf16[128,2048]{1,0:T(8,128)(2,1)}, bf16[128,2048]{1,0:T(8,128)(2,1)S(1)}, u32[]{:S(2)}, u32[]{:S(2)}) %collective-permute-start.3) | collective-permute-done | bytes 524320 | tf_op jit(solution)/shard_map/ppermute | solution.py:844
  21.8 1.3 %collective-permute-start.8 = (bf16[128,2048]{1,0:T(8,128)(2,1)S(1)}, bf16[128,2048]{1,0:T(8,128)(2,1)S(1)}, u32[]{:S(2)}, u32[]{:S(2)}) collective-permute-start(bf16[128,2048]{1,0:T(8,128)(2,1)S(1)} %get-tuple-element.69.inner_ref), channel_id=1, source_target_pairs={{1,0},{2,3},{5,4},{6,7},{9,8},{10,11},{13,12},{14,15},{17,16},{18,... | collective-permute-start | bytes 1572872 | tf_op jit(solution)/shard_map/ppermute | solution.py:841
  23.2 9.1 %collective-permute-done.4.refs_0_ = bf16[128,2048]{1,0:T(8,128)(2,1)S(1)} collective-permute-done((bf16[128,2048]{1,0:T(8,128)(2,1)S(1)}, bf16[128,2048]{1,0:T(8,128)(2,1)S(1)}, u32[]{:S(2)}, u32[]{:S(2)}) %collective-permute-start.4) | collective-permute-done | bytes 524320 | tf_op jit(solution)/shard_map/ppermute | solution.py:847
  32.3 1.3 %collective-permute-start.10 = (bf16[1024,128]{1,0:T(8,128)(2,1)S(1)}, bf16[1024,128]{1,0:T(8,128)(2,1)S(1)}, u32[]{:S(2)}, u32[]{:S(2)}) collective-permute-start(bf16[1024,128]{1,0:T(8,128)(2,1)S(1)} %get-tuple-element.72), channel_id=1, source_target_pairs={{0,8},{4,20},{8,0},{12,28},{16,24},{24,16},{1,9},{5,21},{9,1},{13,... | collective-permute-start | bytes 786440 | tf_op jit(solution)/shard_map/ppermute | solution.py:692
  34.5 4.7 %collective-permute-done.6.refs_2_ = bf16[128,2048]{1,0:T(8,128)(2,1)S(1)} collective-permute-done((bf16[128,2048]{1,0:T(8,128)(2,1)S(1)}, bf16[128,2048]{1,0:T(8,128)(2,1)S(1)}, u32[]{:S(2)}, u32[]{:S(2)}) %collective-permute-start.6) | collective-permute-done | bytes 524320 | tf_op jit(solution)/shard_map/ppermute | solution.py:844
  40.1 2.5 %collective-permute-start.15 = (bf16[896,2048]{1,0:T(8,128)(2,1)S(1)}, bf16[896,2048]{1,0:T(8,128)(2,1)S(1)}, u32[]{:S(2)}, u32[]{:S(2)}) collective-permute-start(bf16[896,2048]{1,0:T(8,128)(2,1)S(1)} %pack.3.refs_0_), channel_id=1, source_target_pairs={{0,4},{4,0},{1,5},{5,1},{2,6},{6,2},{3,7},{7,3},{8,12},{12,8},{9,1... | collective-permute-start | bytes 11010056 | tf_op jit(solution)/shard_map/ppermute | solution.py:797
  45.7 2.4 %collective-permute-start.14 = (bf16[1024,128]{1,0:T(8,128)(2,1)S(1)}, bf16[1024,128]{1,0:T(8,128)(2,1)S(1)}, u32[]{:S(2)}, u32[]{:S(2)}) collective-permute-start(bf16[1024,128]{1,0:T(8,128)(2,1)S(1)} %message.1), channel_id=1, source_target_pairs={{0,16},{4,12},{8,24},{12,4},{20,28},{28,20},{1,17},{5,13},{9,25},{... | collective-permute-start | bytes 786440 | tf_op jit(solution)/shard_map/ppermute | solution.py:705
  48.2 1.8 %turned.1 = (bf16[128,6144]{1,0:T(8,128)(2,1)S(1)}, bf16[256,4096]{1,0:T(8,128)(2,1)S(1)}, f32[8,128]{1,0:T(8,128)S(1)}) custom-call(bf16[384,2048]{1,0:T(8,128)(2,1)S(1)} %get-tuple-element.82.value_ref, bf16[384,2048]{1,0:T(8,128)(2,1)S(1)} %get-tuple-element.83.grad_ref, bf16[1024,128]{1,0:T(8,128)(2,1)S(1)} %get-tuple-element.76.got_ref.after_ref), custom_call_target="tpu_custom_call" | custom-call | flops 1207959552 | tf_op jit(solution)/shard_map/turned/pallas_call | solution.py:74
  50.0 3.0 %project.2 = (f32[384,2048]{1,0:T(8,128)S(1)}, f32[8,128]{1,0:T(8,128)S(1)}) custom-call(bf16[896,2048]{1,0:T(8,128)(2,1)S(1)} %pack.3.refs_0_, bf16[896,2048]{1,0:T(8,128)(2,1)S(1)} %collective-permute-done.15.refs_1_, bf16[384,4096]{1,0:T(8,128)(2,1)S(1)} %get-tuple-element.65.refs_2_.tokens_ref), custom_call_target="tpu_custom_call" | custom-call | flops 2818572288 | tf_op jit(solution)/shard_map/project/pallas_call | solution.py:74
  53.0 6.8 %collective-permute-done.14.refs_4_ = bf16[1024,128]{1,0:T(8,128)(2,1)S(1)} collective-permute-done((bf16[1024,128]{1,0:T(8,128)(2,1)S(1)}, bf16[1024,128]{1,0:T(8,128)(2,1)S(1)}, u32[]{:S(2)}, u32[]{:S(2)}) %collective-permute-start.14) | collective-permute-done | bytes 262176 | tf_op jit(solution)/shard_map/ppermute | solution.py:705
  59.9 1.3 %collective-permute-done.13.refs_3_ = bf16[128,2048]{1,0:T(8,128)(2,1)S(1)} collective-permute-done((bf16[128,2048]{1,0:T(8,128)(2,1)S(1)}, bf16[128,2048]{1,0:T(8,128)(2,1)S(1)}, u32[]{:S(2)}, u32[]{:S(2)}) %collective-permute-start.13) | collective-permute-done | bytes 524320 | tf_op jit(solution)/shard_map/ppermute | solution.py:841
  64.1 1.3 %collective-permute-start.19 = (bf16[128,2048]{1,0:T(8,128)(2,1)S(1)}, bf16[128,2048]{1,0:T(8,128)(2,1)S(1)}, u32[]{:S(2)}, u32[]{:S(2)}) collective-permute-start(bf16[128,2048]{1,0:T(8,128)(2,1)S(1)} %choose.3.refs_3_), channel_id=1, source_target_pairs={{0,16},{4,12},{8,24},{12,4},{16,0},{20,28},{24,8},{28,20},{1,17},{... | collective-permute-start | bytes 1572872 | tf_op jit(solution)/shard_map/ppermute | solution.py:844
  65.4 1.8 %collective-permute-done.20.other_ref = f32[1024,128]{1,0:T(8,128)S(1)} collective-permute-done((f32[1024,128]{1,0:T(8,128)S(1)}, f32[1024,128]{1,0:T(8,128)S(1)}, u32[]{:S(2)}, u32[]{:S(2)}) %collective-permute-start.20) | collective-permute-done | bytes 524320 | tf_op jit(solution)/shard_map/ppermute | solution.py:754
  67.2 1.7 %collective-permute-start.16 = (bf16[128,2048]{1,0:T(8,128)(2,1)S(1)}, bf16[128,2048]{1,0:T(8,128)(2,1)S(1)}, u32[]{:S(2)}, u32[]{:S(2)}) collective-permute-start(bf16[128,2048]{1,0:T(8,128)(2,1)S(1)} %get-tuple-element.85), channel_id=1, source_target_pairs={{0,1},{1,0},{2,3},{3,2},{4,5},{5,4},{6,7},{7,6},{8,9},{9,8},{10,11... | collective-permute-start | bytes 1572872 | tf_op jit(solution)/shard_map/ppermute | solution.py:841
  69.1 5.4 %masked_grad.1 = (bf16[384,2048]{1,0:T(8,128)(2,1)S(1)}, bf16[384,2048]{1,0:T(8,128)(2,1)S(1)}) custom-call(s32[384,2048]{1,0:T(8,128)} %bitcast.16, bf16[384,2048]{1,0:T(8,128)(2,1)S(1)} %get-tuple-element.83.grad_ref, bf16[384,2048]{1,0:T(8,128)(2,1)S(1)} %get-tuple-element.82.value_ref, bf16[384,2048]{1,0:T(8,128)(2,1)S(1)} %get-tuple-element.88.keys_ref, ...), custom_call_target="tpu_custom_call" | custom-call | flops 2415919104 | bytes 9437184 | tf_op jit(solution)/shard_map/masked_grad/pallas_call | solution.py:74
  74.5 3.9 %grad_tokens.3 = (bf16[384,4096]{1,0:T(8,128)(2,1)}, f32[8,128]{1,0:T(8,128)S(1)}) custom-call(bf16[896,2048]{1,0:T(8,128)(2,1)S(1)} %pack.3.refs_0_, bf16[896,2048]{1,0:T(8,128)(2,1)S(1)} %collective-permute-done.15.refs_1_, bf16[384,2048]{1,0:T(8,128)(2,1)S(1)} %get-tuple-element.92.refs_2_.refs_4_), custom_call_target="tpu_custom_call" | custom-call | flops 2818572288 | tf_op jit(solution)/shard_map/grad_tokens/pallas_call | solution.py:74
  78.5 4.3 %products.1 = (f32[384,2048]{1,0:T(8,128)S(1)}, bf16[384,4096]{1,0:T(8,128)(2,1)}, f32[8,128]{1,0:T(8,128)S(1)}) custom-call(bf16[512,2048]{1,0:T(8,128)(2,1)S(1)} %pack.4.refs_0_, bf16[512,2048]{1,0:T(8,128)(2,1)S(1)} %collective-permute-done.21.refs_1_, ...), custom_call_target="tpu_custom_call", output_to_operand_aliasing={{0}: (3, {}), {1}: (5, {})} | custom-call | flops 3221225472 | tf_op jit(solution)/shard_map/products/pallas_call | solution.py:74
  85.0 2.6 %collective-permute-done.22.refs_1_ = bf16[512,2048]{1,0:T(8,128)(2,1)S(1)} collective-permute-done((bf16[512,2048]{1,0:T(8,128)(2,1)S(1)}, bf16[512,2048]{1,0:T(8,128)(2,1)S(1)}, u32[]{:S(2)}, u32[]{:S(2)}) %collective-permute-start.22) | collective-permute-done | bytes 2097184 | tf_op jit(solution)/shard_map/ppermute | solution.py:797
  87.6 2.0 %project.3 = (f32[384,2048]{1,0:T(8,128)S(1)}, f32[8,128]{1,0:T(8,128)S(1)}) custom-call(bf16[512,2048]{1,0:T(8,128)(2,1)S(1)} %pack.5.refs_0_, bf16[512,2048]{1,0:T(8,128)(2,1)S(1)} %collective-permute-done.22.refs_1_, bf16[384,4096]{1,0:T(8,128)(2,1)S(1)} %get-tuple-element.65.refs_2_.tokens_ref, ...), custom_call_target="tpu_custom_call", output_to_operand_aliasing={{0}: (3, {})} | custom-call | flops 1610612736 | tf_op jit(solution)/shard_map/project/pallas_call | solution.py:74
  89.7 2.5 %collective-permute-done.23.refs_0_ = bf16[128,2048]{1,0:T(8,128)(2,1)S(1)} collective-permute-done((bf16[128,2048]{1,0:T(8,128)(2,1)S(1)}, bf16[128,2048]{1,0:T(8,128)(2,1)S(1)}, u32[]{:S(2)}, u32[]{:S(2)}) %collective-permute-start.23) | collective-permute-done | bytes 524320 | tf_op jit(solution)/shard_map/ppermute | solution.py:847
  93.1 2.7 %grad_tokens.4 = (bf16[384,4096]{1,0:T(8,128)(2,1)}, f32[8,128]{1,0:T(8,128)S(1)}) custom-call(bf16[512,2048]{1,0:T(8,128)(2,1)S(1)} %pack.5.refs_0_, bf16[512,2048]{1,0:T(8,128)(2,1)S(1)} %collective-permute-done.22.refs_1_, bf16[384,2048]{1,0:T(8,128)(2,1)S(1)} %get-tuple-element.92.refs_2_.refs_4_, ...), custom_call_target="tpu_custom_call", output_to_operand_aliasing={{0}: (3, {})} | custom-call | flops 1610612736 | tf_op jit(solution)/shard_map/grad_tokens/pallas_call | solution.py:74
  95.8 1.7 %queries.1 = (bf16[384,2048]{1,0:T(8,128)(2,1)S(1)}, f32[2048,128]{1,0:T(8,128)S(1)}, bf16[2048,128]{1,0:T(8,128)(2,1)S(1)}) custom-call(bf16[384,4096]{1,0:T(8,128)(2,1)S(1)} %get-tuple-element.65.refs_2_.tokens_ref, f32[384,2048]{1,0:T(8,128)S(1)} %get-tuple-element.103.sum_ref, bf16[384,2048]{1,0:T(8,128)(2,1)S(1)} %get-tuple-element.104.mask_ref, ...), custom_call_target="tpu_custom_call" | custom-call | flops 402653184 | tf_op jit(solution)/shard_map/queries/pallas_call | solution.py:74
  97.6 1.3 %grad_tokens.5 = (bf16[384,4096]{1,0:T(8,128)(2,1)}, f32[8,128]{1,0:T(8,128)S(1)}) custom-call(bf16[128,2048]{1,0:T(8,128)(2,1)S(1)} %join.9.refs_0_, bf16[128,2048]{1,0:T(8,128)(2,1)S(1)} %collective-permute-done.24.refs_1_, bf16[384,2048]{1,0:T(8,128)(2,1)S(1)} %get-tuple-element.92.refs_2_.refs_4_, ...), custom_call_target="tpu_custom_call", output_to_operand_aliasing={{0}: (3, {})} | custom-call | flops 402653184 | tf_op jit(solution)/shard_map/grad_tokens/pallas_call | solution.py:74
  104.2 3.9 %value_part.1 = (f32[384,2048]{1,0:T(8,128)S(1)}, f32[8,128]{1,0:T(8,128)S(1)}) custom-call(bf16[384,2048]{1,0:T(8,128)(2,1)S(1)} %get-tuple-element.108.query_ref, bf16[384,2048]{1,0:T(8,128)(2,1)S(1)} %get-tuple-element.88.keys_ref, bf16[384,2048]{1,0:T(8,128)(2,1)S(1)} %get-tuple-element.83.grad_ref), custom_call_target="tpu_custom_call" | custom-call | flops 1811939328 | tf_op jit(solution)/shard_map/value_part/pallas_call | solution.py:74
  108.1 5.1 %attended.1 = (bf16[384,2048]{1,0:T(8,128)(2,1)}, f32[8,128]{1,0:T(8,128)S(1)}) custom-call(bf16[384,2048]{1,0:T(8,128)(2,1)S(1)} %get-tuple-element.108.query_ref, bf16[384,2048]{1,0:T(8,128)(2,1)S(1)} %get-tuple-element.88.keys_ref, bf16[384,2048]{1,0:T(8,128)(2,1)S(1)} %get-tuple-element.82.value_ref, bf16[2048,128]{1,0:T(8,128)(2,1)S(1)} %get-tuple-element.90.high_ref, ...), custom_call_target="tpu_custom_call" | custom-call | flops 2415919104 | bytes 6291456 | tf_op jit(solution)/shard_map/attended/pallas_call | solution.py:74
  113.3 3.8 %collective-permute-done.28.refs_2_ = bf16[1024,128]{1,0:T(8,128)(2,1)S(1)} collective-permute-done((bf16[1024,128]{1,0:T(8,128)(2,1)S(1)}, bf16[1024,128]{1,0:T(8,128)(2,1)S(1)}, u32[]{:S(2)}, u32[]{:S(2)}) %collective-permute-start.28) | collective-permute-done | bytes 262176 | tf_op jit(solution)/shard_map/ppermute | solution.py:733
  117.6 1.9 %key_part.1.key_ref = f32[384,2048]{1,0:T(8,128)S(1)} custom-call(bf16[384,2048]{1,0:T(8,128)(2,1)S(1)} %get-tuple-element.108.query_ref, bf16[128,6144]{1,0:T(8,128)(2,1)S(1)} %get-tuple-element.112.top_ref, bf16[256,4096]{1,0:T(8,128)(2,1)S(1)} %get-tuple-element.113.bottom_ref), custom_call_target="tpu_custom_call" | custom-call | flops 1207959552 | tf_op jit(solution)/shard_map/key_part/pallas_call | solution.py:74
  119.8 3.5 %outer.1 = (bf16[384,2048]{1,0:T(8,128)(2,1)}, bf16[384,2048]{1,0:T(8,128)(2,1)}) custom-call(f32[384,2048]{1,0:T(8,128)S(1)} %key_part.1.key_ref, f32[384,2048]{1,0:T(8,128)S(1)} %get-tuple-element.114.val_ref, bf16[384,2048]{1,0:T(8,128)(2,1)S(1)} %get-tuple-element.88.keys_ref, bf16[384,2048]{1,0:T(8,128)(2,1)S(1)} %get-tuple-element.82.value_ref, ...), custom_call_target="tpu_custom_call" | custom-call | flops 805306368 | bytes 15728640 | tf_op jit(solution)/shard_map/outer/pallas_call | solution.py:74
  (61 shorter events, 22.4 us)
Async XLA Ops:
  0.6 14.1 %collective-permute-start = (bf16[128,2048]{1,0:T(8,128)(2,1)}, bf16[128,2048]{1,0:T(8,128)(2,1)S(1)}, u32[]{:S(2)}, u32[]{:S(2)}) collective-permute-start(bf16[128,2048]{1,0:T(8,128)(2,1)} %refs_0_.1), channel_id=1, source_target_pairs={{0,1},{1,0},{2,3},{3,2},{4,5},{5,4},{6,7},{7,6},{8,9},{9,8},{10,11... | collective-permute-start | bytes 1572872 | tf_op jit(solution)/shard_map/ppermute | solution.py:841
  2.8 11.9 %collective-permute-start.1 = (bf16[128,2048]{1,0:T(8,128)(2,1)}, bf16[128,2048]{1,0:T(8,128)(2,1)S(1)}, u32[]{:S(2)}, u32[]{:S(2)}) collective-permute-start(bf16[128,2048]{1,0:T(8,128)(2,1)} %refs_0_.1), channel_id=1, source_target_pairs={{1,2},{2,1},{5,6},{6,5},{9,10},{10,9},{13,14},{14,13},{17,18},{18,... | collective-permute-start | bytes 1572872 | tf_op jit(solution)/shard_map/ppermute | solution.py:841
  3.5 11.2 %collective-permute-start.2 = (bf16[128,2048]{1,0:T(8,128)(2,1)}, bf16[128,2048]{1,0:T(8,128)(2,1)S(1)}, u32[]{:S(2)}, u32[]{:S(2)}) collective-permute-start(bf16[128,2048]{1,0:T(8,128)(2,1)} %refs_0_.1), channel_id=1, source_target_pairs={{0,8},{4,20},{8,0},{12,28},{16,24},{20,4},{24,16},{28,12},{1,9},{5... | collective-permute-start | bytes 1572872 | tf_op jit(solution)/shard_map/ppermute | solution.py:844
  4.8 14.0 %collective-permute-start.3 = (bf16[128,2048]{1,0:T(8,128)(2,1)}, bf16[128,2048]{1,0:T(8,128)(2,1)S(1)}, u32[]{:S(2)}, u32[]{:S(2)}) collective-permute-start(bf16[128,2048]{1,0:T(8,128)(2,1)} %refs_0_.1), channel_id=1, source_target_pairs={{0,16},{4,12},{8,24},{12,4},{16,0},{20,28},{24,8},{28,20},{1,17},{... | collective-permute-start | bytes 1572872 | tf_op jit(solution)/shard_map/ppermute | solution.py:844
  18.8 3.0 %collective-permute-start.9 = (bf16[2048,128]{1,0:T(8,128)(2,1)S(1)}, bf16[2048,128]{1,0:T(8,128)(2,1)S(1)}, u32[]{:S(2)}, u32[]{:S(2)}) collective-permute-start(bf16[2048,128]{1,0:T(8,128)(2,1)S(1)} %get-tuple-element.71), channel_id=1, source_target_pairs={{0,4},{4,0},{1,5},{5,1},{2,6},{6,2},{3,7},{7,3},{8,12},{12,8},{9,1... | collective-permute-start | bytes 1572872 | tf_op jit(solution)/shard_map/ppermute | solution.py:682
  19.4 12.9 %collective-permute-start.4 = (bf16[128,2048]{1,0:T(8,128)(2,1)S(1)}, bf16[128,2048]{1,0:T(8,128)(2,1)S(1)}, u32[]{:S(2)}, u32[]{:S(2)}) collective-permute-start(bf16[128,2048]{1,0:T(8,128)(2,1)S(1)} %get-tuple-element.67.refs_1_), channel_id=1, source_target_pairs={{0,16},{4,12},{8,24},{12,4},{16,0},{20,28},{24,8},{28,20},{1,17},{... | collective-permute-start | bytes 1572872 | tf_op jit(solution)/shard_map/ppermute | solution.py:847
  20.6 13.9 %collective-permute-start.5 = (bf16[128,2048]{1,0:T(8,128)(2,1)S(1)}, bf16[128,2048]{1,0:T(8,128)(2,1)S(1)}, u32[]{:S(2)}, u32[]{:S(2)}) collective-permute-start(bf16[128,2048]{1,0:T(8,128)(2,1)S(1)} %get-tuple-element.68.refs_4_), channel_id=1, source_target_pairs={{0,8},{4,20},{8,0},{12,28},{16,24},{20,4},{24,16},{28,12},{1,9},{5... | collective-permute-start | bytes 1572872 | tf_op jit(solution)/shard_map/ppermute | solution.py:844
  20.8 18.4 %collective-permute-start.6 = (bf16[128,2048]{1,0:T(8,128)(2,1)S(1)}, bf16[128,2048]{1,0:T(8,128)(2,1)S(1)}, u32[]{:S(2)}, u32[]{:S(2)}) collective-permute-start(bf16[128,2048]{1,0:T(8,128)(2,1)S(1)} %get-tuple-element.68.refs_4_), channel_id=1, source_target_pairs={{0,16},{4,12},{8,24},{12,4},{16,0},{20,28},{24,8},{28,20},{1,17},{... | collective-permute-start | bytes 1572872 | tf_op jit(solution)/shard_map/ppermute | solution.py:844
  21.1 18.1 %collective-permute-start.7 = (bf16[128,2048]{1,0:T(8,128)(2,1)S(1)}, bf16[128,2048]{1,0:T(8,128)(2,1)S(1)}, u32[]{:S(2)}, u32[]{:S(2)}) collective-permute-start(bf16[128,2048]{1,0:T(8,128)(2,1)S(1)} %get-tuple-element.68.refs_4_), channel_id=1, source_target_pairs={{1,2},{2,1},{5,6},{6,5},{9,10},{10,9},{13,14},{14,13},{17,18},{18,... | collective-permute-start | bytes 1572872 | tf_op jit(solution)/shard_map/ppermute | solution.py:841
  21.8 17.4 %collective-permute-start.8 = (bf16[128,2048]{1,0:T(8,128)(2,1)S(1)}, bf16[128,2048]{1,0:T(8,128)(2,1)S(1)}, u32[]{:S(2)}, u32[]{:S(2)}) collective-permute-start(bf16[128,2048]{1,0:T(8,128)(2,1)S(1)} %get-tuple-element.69.inner_ref), channel_id=1, source_target_pairs={{1,0},{2,3},{5,4},{6,7},{9,8},{10,11},{13,12},{14,15},{17,16},{18,... | collective-permute-start | bytes 1572872 | tf_op jit(solution)/shard_map/ppermute | solution.py:841
  23.1 16.7 %copy-start = (bf16[128,2048]{1,0:T(8,128)(2,1)S(1)}, bf16[128,2048]{1,0:T(8,128)(2,1)}, u32[]{:S(2)}) copy-start(bf16[128,2048]{1,0:T(8,128)(2,1)} %refs_0_.1) | copy-start | bytes 1572868
  32.3 7.5 %collective-permute-start.10 = (bf16[1024,128]{1,0:T(8,128)(2,1)S(1)}, bf16[1024,128]{1,0:T(8,128)(2,1)S(1)}, u32[]{:S(2)}, u32[]{:S(2)}) collective-permute-start(bf16[1024,128]{1,0:T(8,128)(2,1)S(1)} %get-tuple-element.72), channel_id=1, source_target_pairs={{0,8},{4,20},{8,0},{12,28},{16,24},{24,16},{1,9},{5,21},{9,1},{13,... | collective-permute-start | bytes 786440 | tf_op jit(solution)/shard_map/ppermute | solution.py:692
  40.1 9.9 %collective-permute-start.15 = (bf16[896,2048]{1,0:T(8,128)(2,1)S(1)}, bf16[896,2048]{1,0:T(8,128)(2,1)S(1)}, u32[]{:S(2)}, u32[]{:S(2)}) collective-permute-start(bf16[896,2048]{1,0:T(8,128)(2,1)S(1)} %pack.3.refs_0_), channel_id=1, source_target_pairs={{0,4},{4,0},{1,5},{5,1},{2,6},{6,2},{3,7},{7,3},{8,12},{12,8},{9,1... | collective-permute-start | bytes 11010056 | tf_op jit(solution)/shard_map/ppermute | solution.py:797
  42.6 17.3 %collective-permute-start.11 = (bf16[128,2048]{1,0:T(8,128)(2,1)S(1)}, bf16[128,2048]{1,0:T(8,128)(2,1)S(1)}, u32[]{:S(2)}, u32[]{:S(2)}) collective-permute-start(bf16[128,2048]{1,0:T(8,128)(2,1)S(1)} %choose.2.refs_0_), channel_id=1, source_target_pairs={{0,8},{4,20},{8,0},{12,28},{16,24},{20,4},{24,16},{28,12},{1,9},{5... | collective-permute-start | bytes 1572872 | tf_op jit(solution)/shard_map/ppermute | solution.py:844
  43.4 16.5 %collective-permute-start.12 = (bf16[128,2048]{1,0:T(8,128)(2,1)S(1)}, bf16[128,2048]{1,0:T(8,128)(2,1)S(1)}, u32[]{:S(2)}, u32[]{:S(2)}) collective-permute-start(bf16[128,2048]{1,0:T(8,128)(2,1)S(1)} %choose.2.refs_0_), channel_id=1, source_target_pairs={{0,16},{4,12},{8,24},{12,4},{16,0},{20,28},{24,8},{28,20},{1,17},{... | collective-permute-start | bytes 1572872 | tf_op jit(solution)/shard_map/ppermute | solution.py:844
  44.4 16.9 %collective-permute-start.13 = (bf16[128,2048]{1,0:T(8,128)(2,1)S(1)}, bf16[128,2048]{1,0:T(8,128)(2,1)S(1)}, u32[]{:S(2)}, u32[]{:S(2)}) collective-permute-start(bf16[128,2048]{1,0:T(8,128)(2,1)S(1)} %get-tuple-element.75.inner_ref), channel_id=1, source_target_pairs={{1,0},{2,3},{5,4},{6,7},{9,8},{10,11},{13,12},{14,15},{17,16},{18,... | collective-permute-start | bytes 1572872 | tf_op jit(solution)/shard_map/ppermute | solution.py:841
  45.7 14.1 %collective-permute-start.14 = (bf16[1024,128]{1,0:T(8,128)(2,1)S(1)}, bf16[1024,128]{1,0:T(8,128)(2,1)S(1)}, u32[]{:S(2)}, u32[]{:S(2)}) collective-permute-start(bf16[1024,128]{1,0:T(8,128)(2,1)S(1)} %message.1), channel_id=1, source_target_pairs={{0,16},{4,12},{8,24},{12,4},{20,28},{28,20},{1,17},{5,13},{9,25},{... | collective-permute-start | bytes 786440 | tf_op jit(solution)/shard_map/ppermute | solution.py:705
  61.4 17.0 %collective-permute-start.21 = (bf16[512,2048]{1,0:T(8,128)(2,1)S(1)}, bf16[512,2048]{1,0:T(8,128)(2,1)S(1)}, u32[]{:S(2)}, u32[]{:S(2)}) collective-permute-start(bf16[512,2048]{1,0:T(8,128)(2,1)S(1)} %pack.4.refs_0_), channel_id=1, source_target_pairs={{0,4},{4,0},{1,5},{5,1},{2,6},{6,2},{3,7},{7,3},{8,12},{12,8},{9,1... | collective-permute-start | bytes 6291464 | tf_op jit(solution)/shard_map/ppermute | solution.py:797
  62.7 4.4 %collective-permute-start.20 = (f32[1024,128]{1,0:T(8,128)S(1)}, f32[1024,128]{1,0:T(8,128)S(1)}, u32[]{:S(2)}, u32[]{:S(2)}) collective-permute-start(f32[1024,128]{1,0:T(8,128)S(1)} %state.2.state_ref), channel_id=1, source_target_pairs={{0,4},{4,0},{1,5},{5,1},{2,6},{6,2},{3,7},{7,3},{8,12},{12,8},{9,1... | collective-permute-start | bytes 1572872 | tf_op jit(solution)/shard_map/ppermute | solution.py:754
  62.8 20.0 %collective-permute-start.17 = (bf16[128,2048]{1,0:T(8,128)(2,1)S(1)}, bf16[128,2048]{1,0:T(8,128)(2,1)S(1)}, u32[]{:S(2)}, u32[]{:S(2)}) collective-permute-start(bf16[128,2048]{1,0:T(8,128)(2,1)S(1)} %get-tuple-element.86.refs_1_), channel_id=1, source_target_pairs={{0,16},{4,12},{8,24},{12,4},{16,0},{20,28},{24,8},{28,20},{1,17},{... | collective-permute-start | bytes 1572872 | tf_op jit(solution)/shard_map/ppermute | solution.py:847
  63.4 19.4 %collective-permute-start.18 = (bf16[128,2048]{1,0:T(8,128)(2,1)S(1)}, bf16[128,2048]{1,0:T(8,128)(2,1)S(1)}, u32[]{:S(2)}, u32[]{:S(2)}) collective-permute-start(bf16[128,2048]{1,0:T(8,128)(2,1)S(1)} %choose.3.refs_3_), channel_id=1, source_target_pairs={{0,8},{4,20},{8,0},{12,28},{16,24},{20,4},{24,16},{28,12},{1,9},{5... | collective-permute-start | bytes 1572872 | tf_op jit(solution)/shard_map/ppermute | solution.py:844
  64.1 18.7 %collective-permute-start.19 = (bf16[128,2048]{1,0:T(8,128)(2,1)S(1)}, bf16[128,2048]{1,0:T(8,128)(2,1)S(1)}, u32[]{:S(2)}, u32[]{:S(2)}) collective-permute-start(bf16[128,2048]{1,0:T(8,128)(2,1)S(1)} %choose.3.refs_3_), channel_id=1, source_target_pairs={{0,16},{4,12},{8,24},{12,4},{16,0},{20,28},{24,8},{28,20},{1,17},{... | collective-permute-start | bytes 1572872 | tf_op jit(solution)/shard_map/ppermute | solution.py:844
  67.2 15.6 %collective-permute-start.16 = (bf16[128,2048]{1,0:T(8,128)(2,1)S(1)}, bf16[128,2048]{1,0:T(8,128)(2,1)S(1)}, u32[]{:S(2)}, u32[]{:S(2)}) collective-permute-start(bf16[128,2048]{1,0:T(8,128)(2,1)S(1)} %get-tuple-element.85), channel_id=1, source_target_pairs={{0,1},{1,0},{2,3},{3,2},{4,5},{5,4},{6,7},{7,6},{8,9},{9,8},{10,11... | collective-permute-start | bytes 1572872 | tf_op jit(solution)/shard_map/ppermute | solution.py:841
  83.2 4.4 %collective-permute-start.22 = (bf16[512,2048]{1,0:T(8,128)(2,1)S(1)}, bf16[512,2048]{1,0:T(8,128)(2,1)S(1)}, u32[]{:S(2)}, u32[]{:S(2)}) collective-permute-start(bf16[512,2048]{1,0:T(8,128)(2,1)S(1)} %pack.5.refs_0_), channel_id=1, source_target_pairs={{0,4},{4,0},{1,5},{5,1},{2,6},{6,2},{3,7},{7,3},{8,12},{12,8},{9,1... | collective-permute-start | bytes 6291464 | tf_op jit(solution)/shard_map/ppermute | solution.py:797
  83.8 8.3 %collective-permute-start.23 = (bf16[128,2048]{1,0:T(8,128)(2,1)S(1)}, bf16[128,2048]{1,0:T(8,128)(2,1)S(1)}, u32[]{:S(2)}, u32[]{:S(2)}) collective-permute-start(bf16[128,2048]{1,0:T(8,128)(2,1)S(1)} %get-tuple-element.100.refs_2_), channel_id=1, source_target_pairs={{0,16},{4,12},{8,24},{12,4},{16,0},{20,28},{24,8},{28,20},{1,17},{... | collective-permute-start | bytes 1572872 | tf_op jit(solution)/shard_map/ppermute | solution.py:847
  92.1 3.6 %collective-permute-start.24 = (bf16[128,2048]{1,0:T(8,128)(2,1)S(1)}, bf16[128,2048]{1,0:T(8,128)(2,1)S(1)}, u32[]{:S(2)}, u32[]{:S(2)}) collective-permute-start(bf16[128,2048]{1,0:T(8,128)(2,1)S(1)} %join.9.refs_0_), channel_id=1, source_target_pairs={{0,4},{4,0},{1,5},{5,1},{2,6},{6,2},{3,7},{7,3},{8,12},{12,8},{9,1... | collective-permute-start | bytes 1572872 | tf_op jit(solution)/shard_map/ppermute | solution.py:838
  97.5 2.0 %collective-permute-start.25 = (bf16[2048,128]{1,0:T(8,128)(2,1)S(1)}, bf16[2048,128]{1,0:T(8,128)(2,1)S(1)}, u32[]{:S(2)}, u32[]{:S(2)}) collective-permute-start(bf16[2048,128]{1,0:T(8,128)(2,1)S(1)} %get-tuple-element.117), channel_id=1, source_target_pairs={{0,4},{4,0},{1,5},{5,1},{2,6},{6,2},{3,7},{7,3},{8,12},{12,8},{9,1... | collective-permute-start | bytes 1572872 | tf_op jit(solution)/shard_map/ppermute | solution.py:715
  100.4 12.9 %collective-permute-start.26 = (bf16[1024,128]{1,0:T(8,128)(2,1)S(1)}, bf16[1024,128]{1,0:T(8,128)(2,1)S(1)}, u32[]{:S(2)}, u32[]{:S(2)}) collective-permute-start(bf16[1024,128]{1,0:T(8,128)(2,1)S(1)} %get-tuple-element.119), channel_id=1, source_target_pairs={{16,8},{20,12},{24,0},{28,4},{17,9},{21,13},{25,1},{29,5},{18,10},... | collective-permute-start | bytes 786440 | tf_op jit(solution)/shard_map/ppermute | solution.py:733
  101.6 11.6 %collective-permute-start.27 = (bf16[1024,128]{1,0:T(8,128)(2,1)S(1)}, bf16[1024,128]{1,0:T(8,128)(2,1)S(1)}, u32[]{:S(2)}, u32[]{:S(2)}) collective-permute-start(bf16[1024,128]{1,0:T(8,128)(2,1)S(1)} %get-tuple-element.119), channel_id=1, source_target_pairs={{8,0},{12,4},{24,16},{28,20},{9,1},{13,5},{25,17},{29,21},{10,2},{... | collective-permute-start | bytes 786440 | tf_op jit(solution)/shard_map/ppermute | solution.py:733
  102.9 14.1 %collective-permute-start.28 = (bf16[1024,128]{1,0:T(8,128)(2,1)S(1)}, bf16[1024,128]{1,0:T(8,128)(2,1)S(1)}, u32[]{:S(2)}, u32[]{:S(2)}) collective-permute-start(bf16[1024,128]{1,0:T(8,128)(2,1)S(1)} %get-tuple-element.119), channel_id=1, source_target_pairs={{16,0},{20,4},{24,8},{28,12},{17,1},{21,5},{25,9},{29,13},{18,2},{... | collective-permute-start | bytes 786440 | tf_op jit(solution)/shard_map/ppermute | solution.py:733
  117.1 2.4 %collective-permute-start.29 = (f32[1024,128]{1,0:T(8,128)S(1)}, f32[1024,128]{1,0:T(8,128)S(1)}, u32[]{:S(2)}, u32[]{:S(2)}) collective-permute-start(f32[1024,128]{1,0:T(8,128)S(1)} %state.3.state_ref), channel_id=1, source_target_pairs={{0,4},{4,0},{1,5},{5,1},{2,6},{6,2},{3,7},{7,3},{8,12},{12,8},{9,1... | collective-permute-start | bytes 1572872 | tf_op jit(solution)/shard_map/ppermute | solution.py:754

commit v10 on v8

--- a/solution.py
+++ b/solution.py
@@ -820,7 +820,7 @@
         near = along(q_weight, ends)
         mid = along(q_weight, middle)
         first_0, second_0 = cross(q_weight)
-        near, mid, first_0, second_0, sent = join([near, mid, first_0, second_0, sent])
+        first_0, second_0, near, mid, sent = join([first_0, second_0, near, mid, sent])
     else:
         arrived = gather_any(q_weight)
         high, low = halves(scan_any(own, sent, chips * 2, False))
@@ -841,8 +841,8 @@
         early = pack(q_weight, first_0, second_0, third_0, near, first_1, second_1)
         partial, _, mark = products_call(special, 0, early, tokens)
         top, bottom, turned_mark = turned_call(values, cotangent, got)
-        third_0, first_2, second_2, far_out, more = join(
-            [third_0, first_2, second_2, far_out, more], [mark, turned_mark]
+        far_out, first_2, second_2, more, third_0 = join(
+            [far_out, first_2, second_2, more, third_0], [mark, turned_mark]
         )
         third_1 = along(third_0, ends)
         third_2 = onward(first_2)

time: 123 us -> 124 us (level)
    ppermute x6, waiting for transfers between devices: 5.25 us -> 2.28 us  [along(): return lax.ppermute(array, 'dp', pairs)]
    ppermute x3, starting transfers between devices: 2.94 us -> 0.73 us  [onward(): return lax.ppermute(array, CTX, links(2))]
    ppermute x3, starting transfers between devices: 4.24 us -> 2.41 us  [pack(): return [made, lax.ppermute(made, 'core', SWAP)]]
    ppermute x2, starting transfers between devices: 0.65 us -> 2.23 us  [send_first(): sibling = lax.ppermute(sent, 'core', SWAP)]
    ppermute x4, starting transfers between devices: 3.06 us -> 4.58 us  [cross(): lax.ppermute(array, CTX, links(1))]
    ppermute x2, waiting for transfers between devices: 7.29 us -> 8.76 us  [send_second(): return lax.ppermute(message, CTX, links(2, upward(reverse)))]
  transfers between devices with their start and end apart: 29 -> 29, of which waited for: 15 -> 13; matrix products, arithmetic and copies ran while one was open for 0% -> 0% of each run, Pallas kernels for 33% -> 33%
where the time goes in v10:
time: 124 us; the launch traced here: 123 us
  Pallas kernels  47.5 us (38%)
  waiting for transfers between devices  40.4 us (33%)
  starting transfers between devices  34.1 us (28%)
    pallas_call x32, Pallas kernels, kernel_call(): made(*[holds[place](one) if place in holds else one for place, one in zip...  47.5 us
    ppermute x3, waiting for transfers between devices, onward(): return lax.ppermute(array, CTX, links(2))  11.6 us
    ppermute x4, waiting for transfers between devices, cross(): lax.ppermute(array, CTX, links(2))  9.08 us
    ppermute x6, starting transfers between devices, along(): return lax.ppermute(array, 'dp', pairs)  8.91 us
    ppermute x2, waiting for transfers between devices, send_second(): return lax.ppermute(message, CTX, links(2, upward(reverse)))  8.76 us
    ppermute x2, starting transfers between devices, send_second(): return lax.ppermute(message, CTX, links(2, upward(reverse)))  5.25 us
    ppermute x4, starting transfers between devices, cross(): lax.ppermute(array, CTX, links(1))  4.58 us
    ppermute x4, starting transfers between devices, cross(): lax.ppermute(array, CTX, links(2))  4.02 us
  transfers between devices with their start and end apart: 29, of which 13 were waited for; matrix products, arithmetic and copies ran while one was open for 0% of the time, Pallas kernels for 33%

profile of v10, /device:TPU:1, one launch (start us, length us, event | category | flops | bytes accessed | tf_op | source)
XLA Modules:
  0.0 123.3 jit_solution(17544740529174070867)
XLA Ops:
  0.6 2.1 %collective-permute-start = (bf16[128,2048]{1,0:T(8,128)(2,1)}, bf16[128,2048]{1,0:T(8,128)(2,1)S(1)}, u32[]{:S(2)}, u32[]{:S(2)}) collective-permute-start(bf16[128,2048]{1,0:T(8,128)(2,1)} %refs_0_.1), channel_id=1, source_target_pairs={{0,8},{4,20},{8,0},{12,28},{16,24},{20,4},{24,16},{28,12},{1,9},{5... | collective-permute-start | bytes 1572872 | tf_op jit(solution)/shard_map/ppermute | solution.py:808
  6.0 4.8 %own_memory.1 = (bf16[384,2048]{1,0:T(8,128)(2,1)S(1)}, bf16[384,2048]{1,0:T(8,128)(2,1)S(1)}, bf16[384,2048]{1,0:T(8,128)(2,1)S(1)}, f32[2048,128]{1,0:T(8,128)...) custom-call(bf16[384,2048]{1,0:T(8,128)(2,1)} %bitcast.13, ...), custom_call_target="tpu_custom_call" | custom-call | flops 201326592 | bytes 9437184 | tf_op jit(solution)/shard_map/own_memory/pallas_call | solution.py:74
  10.7 1.8 %collective-permute-done.refs_0_ = bf16[128,2048]{1,0:T(8,128)(2,1)S(1)} collective-permute-done((bf16[128,2048]{1,0:T(8,128)(2,1)}, bf16[128,2048]{1,0:T(8,128)(2,1)S(1)}, u32[]{:S(2)}, u32[]{:S(2)}) %collective-permute-start) | collective-permute-done | bytes 524320 | tf_op jit(solution)/shard_map/ppermute | solution.py:808
  12.6 3.7 %collective-permute-done.1.refs_1_ = bf16[128,2048]{1,0:T(8,128)(2,1)S(1)} collective-permute-done((bf16[128,2048]{1,0:T(8,128)(2,1)}, bf16[128,2048]{1,0:T(8,128)(2,1)S(1)}, u32[]{:S(2)}, u32[]{:S(2)}) %collective-permute-start.1) | collective-permute-done | bytes 524320 | tf_op jit(solution)/shard_map/ppermute | solution.py:808
  16.4 2.2 %collective-permute-start.9 = (bf16[2048,128]{1,0:T(8,128)(2,1)S(1)}, bf16[2048,128]{1,0:T(8,128)(2,1)S(1)}, u32[]{:S(2)}, u32[]{:S(2)}) collective-permute-start(bf16[2048,128]{1,0:T(8,128)(2,1)S(1)} %get-tuple-element.72), channel_id=1, source_target_pairs={{0,4},{4,0},{1,5},{5,1},{2,6},{6,2},{3,7},{7,3},{8,12},{12,8},{9,1... | collective-permute-start | bytes 1572872 | tf_op jit(solution)/shard_map/ppermute | solution.py:682
  18.9 1.3 %collective-permute-start.6 = (bf16[128,2048]{1,0:T(8,128)(2,1)S(1)}, bf16[128,2048]{1,0:T(8,128)(2,1)S(1)}, u32[]{:S(2)}, u32[]{:S(2)}) collective-permute-start(bf16[128,2048]{1,0:T(8,128)(2,1)S(1)} %get-tuple-element.69.refs_4_), channel_id=1, source_target_pairs={{0,16},{4,12},{8,24},{12,4},{16,0},{20,28},{24,8},{28,20},{1,17},{... | collective-permute-start | bytes 1572872 | tf_op jit(solution)/shard_map/ppermute | solution.py:808
  22.3 9.1 %collective-permute-done.4.refs_0_ = bf16[128,2048]{1,0:T(8,128)(2,1)S(1)} collective-permute-done((bf16[128,2048]{1,0:T(8,128)(2,1)S(1)}, bf16[128,2048]{1,0:T(8,128)(2,1)S(1)}, u32[]{:S(2)}, u32[]{:S(2)}) %collective-permute-start.4) | collective-permute-done | bytes 524320 | tf_op jit(solution)/shard_map/ppermute | solution.py:811
  32.8 5.3 %collective-permute-done.6.refs_2_ = bf16[128,2048]{1,0:T(8,128)(2,1)S(1)} collective-permute-done((bf16[128,2048]{1,0:T(8,128)(2,1)S(1)}, bf16[128,2048]{1,0:T(8,128)(2,1)S(1)}, u32[]{:S(2)}, u32[]{:S(2)}) %collective-permute-start.6) | collective-permute-done | bytes 524320 | tf_op jit(solution)/shard_map/ppermute | solution.py:808
  38.1 2.2 %collective-permute-done.8.refs_4_ = bf16[128,2048]{1,0:T(8,128)(2,1)S(1)} collective-permute-done((bf16[128,2048]{1,0:T(8,128)(2,1)S(1)}, bf16[128,2048]{1,0:T(8,128)(2,1)S(1)}, u32[]{:S(2)}, u32[]{:S(2)}) %collective-permute-start.8) | collective-permute-done | bytes 524320 | tf_op jit(solution)/shard_map/ppermute | solution.py:805
  40.6 1.8 %collective-permute-start.15 = (bf16[896,2048]{1,0:T(8,128)(2,1)S(1)}, bf16[896,2048]{1,0:T(8,128)(2,1)S(1)}, u32[]{:S(2)}, u32[]{:S(2)}) collective-permute-start(bf16[896,2048]{1,0:T(8,128)(2,1)S(1)} %pack.3.refs_0_), channel_id=1, source_target_pairs={{0,4},{4,0},{1,5},{5,1},{2,6},{6,2},{3,7},{7,3},{8,12},{12,8},{9,1... | collective-permute-start | bytes 11010056 | tf_op jit(solution)/shard_map/ppermute | solution.py:761
  45.4 3.1 %collective-permute-start.14 = (bf16[1024,128]{1,0:T(8,128)(2,1)S(1)}, bf16[1024,128]{1,0:T(8,128)(2,1)S(1)}, u32[]{:S(2)}, u32[]{:S(2)}) collective-permute-start(bf16[1024,128]{1,0:T(8,128)(2,1)S(1)} %message.2), channel_id=1, source_target_pairs={{0,16},{4,12},{8,24},{12,4},{20,28},{28,20},{1,17},{5,13},{9,25},{... | collective-permute-start | bytes 786440 | tf_op jit(solution)/shard_map/ppermute | solution.py:705
  48.6 1.8 %turned.1 = (bf16[128,6144]{1,0:T(8,128)(2,1)S(1)}, bf16[256,4096]{1,0:T(8,128)(2,1)S(1)}, f32[8,128]{1,0:T(8,128)S(1)}) custom-call(bf16[384,2048]{1,0:T(8,128)(2,1)S(1)} %get-tuple-element.83.value_ref, bf16[384,2048]{1,0:T(8,128)(2,1)S(1)} %get-tuple-element.84.grad_ref, bf16[1024,128]{1,0:T(8,128)(2,1)S(1)} %get-tuple-element.76.got_ref.after_ref), custom_call_target="tpu_custom_call" | custom-call | flops 1207959552 | tf_op jit(solution)/shard_map/turned/pallas_call | solution.py:74
  50.4 3.0 %project.2 = (f32[384,2048]{1,0:T(8,128)S(1)}, f32[8,128]{1,0:T(8,128)S(1)}) custom-call(bf16[896,2048]{1,0:T(8,128)(2,1)S(1)} %pack.3.refs_0_, bf16[896,2048]{1,0:T(8,128)(2,1)S(1)} %collective-permute-done.15.refs_1_, bf16[384,4096]{1,0:T(8,128)(2,1)S(1)} %get-tuple-element.66.refs_2_.tokens_ref), custom_call_target="tpu_custom_call" | custom-call | flops 2818572288 | tf_op jit(solution)/shard_map/project/pallas_call | solution.py:74
  53.4 7.4 %collective-permute-done.14.refs_3_ = bf16[1024,128]{1,0:T(8,128)(2,1)S(1)} collective-permute-done((bf16[1024,128]{1,0:T(8,128)(2,1)S(1)}, bf16[1024,128]{1,0:T(8,128)(2,1)S(1)}, u32[]{:S(2)}, u32[]{:S(2)}) %collective-permute-start.14) | collective-permute-done | bytes 262176 | tf_op jit(solution)/shard_map/ppermute | solution.py:705
  64.5 1.7 %collective-permute-done.20.other_ref = f32[1024,128]{1,0:T(8,128)S(1)} collective-permute-done((f32[1024,128]{1,0:T(8,128)S(1)}, f32[1024,128]{1,0:T(8,128)S(1)}, u32[]{:S(2)}, u32[]{:S(2)}) %collective-permute-start.20) | collective-permute-done | bytes 524320 | tf_op jit(solution)/shard_map/ppermute | solution.py:718
  66.2 3.7 %collective-permute-start.16 = (bf16[128,2048]{1,0:T(8,128)(2,1)S(1)}, bf16[128,2048]{1,0:T(8,128)(2,1)S(1)}, u32[]{:S(2)}, u32[]{:S(2)}) collective-permute-start(bf16[128,2048]{1,0:T(8,128)(2,1)S(1)} %get-tuple-element.86), channel_id=1, source_target_pairs={{0,1},{1,0},{2,3},{3,2},{4,5},{5,4},{6,7},{7,6},{8,9},{9,8},{10,11... | collective-permute-start | bytes 1572872 | tf_op jit(solution)/shard_map/ppermute | solution.py:805
  70.1 5.4 %masked_grad.1 = (bf16[384,2048]{1,0:T(8,128)(2,1)S(1)}, bf16[384,2048]{1,0:T(8,128)(2,1)S(1)}) custom-call(s32[384,2048]{1,0:T(8,128)} %bitcast.16, bf16[384,2048]{1,0:T(8,128)(2,1)S(1)} %get-tuple-element.84.grad_ref, bf16[384,2048]{1,0:T(8,128)(2,1)S(1)} %get-tuple-element.83.value_ref, bf16[384,2048]{1,0:T(8,128)(2,1)S(1)} %get-tuple-element.89.keys_ref, ...), custom_call_target="tpu_custom_call" | custom-call | flops 2415919104 | bytes 9437184 | tf_op jit(solution)/shard_map/masked_grad/pallas_call | solution.py:74
  75.5 3.9 %grad_tokens.3 = (bf16[384,4096]{1,0:T(8,128)(2,1)}, f32[8,128]{1,0:T(8,128)S(1)}) custom-call(bf16[896,2048]{1,0:T(8,128)(2,1)S(1)} %pack.3.refs_0_, bf16[896,2048]{1,0:T(8,128)(2,1)S(1)} %collective-permute-done.15.refs_1_, bf16[384,2048]{1,0:T(8,128)(2,1)S(1)} %get-tuple-element.93.refs_2_.refs_4_), custom_call_target="tpu_custom_call" | custom-call | flops 2818572288 | tf_op jit(solution)/shard_map/grad_tokens/pallas_call | solution.py:74
  79.5 4.3 %products.1 = (f32[384,2048]{1,0:T(8,128)S(1)}, bf16[384,4096]{1,0:T(8,128)(2,1)}, f32[8,128]{1,0:T(8,128)S(1)}) custom-call(bf16[512,2048]{1,0:T(8,128)(2,1)S(1)} %pack.4.refs_0_, bf16[512,2048]{1,0:T(8,128)(2,1)S(1)} %collective-permute-done.21.refs_1_, ...), custom_call_target="tpu_custom_call", output_to_operand_aliasing={{0}: (3, {}), {1}: (5, {})} | custom-call | flops 3221225472 | tf_op jit(solution)/shard_map/products/pallas_call | solution.py:74
  85.0 3.6 %collective-permute-done.22.refs_1_ = bf16[512,2048]{1,0:T(8,128)(2,1)S(1)} collective-permute-done((bf16[512,2048]{1,0:T(8,128)(2,1)S(1)}, bf16[512,2048]{1,0:T(8,128)(2,1)S(1)}, u32[]{:S(2)}, u32[]{:S(2)}) %collective-permute-start.22) | collective-permute-done | bytes 2097184 | tf_op jit(solution)/shard_map/ppermute | solution.py:761
  88.5 2.0 %project.3 = (f32[384,2048]{1,0:T(8,128)S(1)}, f32[8,128]{1,0:T(8,128)S(1)}) custom-call(bf16[512,2048]{1,0:T(8,128)(2,1)S(1)} %pack.5.refs_0_, bf16[512,2048]{1,0:T(8,128)(2,1)S(1)} %collective-permute-done.22.refs_1_, bf16[384,4096]{1,0:T(8,128)(2,1)S(1)} %get-tuple-element.66.refs_2_.tokens_ref, ...), custom_call_target="tpu_custom_call", output_to_operand_aliasing={{0}: (3, {})} | custom-call | flops 1610612736 | tf_op jit(solution)/shard_map/project/pallas_call | solution.py:74
  90.6 2.5 %collective-permute-done.23.refs_0_ = bf16[128,2048]{1,0:T(8,128)(2,1)S(1)} collective-permute-done((bf16[128,2048]{1,0:T(8,128)(2,1)S(1)}, bf16[128,2048]{1,0:T(8,128)(2,1)S(1)}, u32[]{:S(2)}, u32[]{:S(2)}) %collective-permute-start.23) | collective-permute-done | bytes 524320 | tf_op jit(solution)/shard_map/ppermute | solution.py:811
  94.0 2.7 %grad_tokens.4 = (bf16[384,4096]{1,0:T(8,128)(2,1)}, f32[8,128]{1,0:T(8,128)S(1)}) custom-call(bf16[512,2048]{1,0:T(8,128)(2,1)S(1)} %pack.5.refs_0_, bf16[512,2048]{1,0:T(8,128)(2,1)S(1)} %collective-permute-done.22.refs_1_, bf16[384,2048]{1,0:T(8,128)(2,1)S(1)} %get-tuple-element.93.refs_2_.refs_4_, ...), custom_call_target="tpu_custom_call", output_to_operand_aliasing={{0}: (3, {})} | custom-call | flops 1610612736 | tf_op jit(solution)/shard_map/grad_tokens/pallas_call | solution.py:74
  96.7 1.7 %queries.1 = (bf16[384,2048]{1,0:T(8,128)(2,1)S(1)}, f32[2048,128]{1,0:T(8,128)S(1)}, bf16[2048,128]{1,0:T(8,128)(2,1)S(1)}) custom-call(bf16[384,4096]{1,0:T(8,128)(2,1)S(1)} %get-tuple-element.66.refs_2_.tokens_ref, f32[384,2048]{1,0:T(8,128)S(1)} %get-tuple-element.104.sum_ref, bf16[384,2048]{1,0:T(8,128)(2,1)S(1)} %get-tuple-element.105.mask_ref, ...), custom_call_target="tpu_custom_call" | custom-call | flops 402653184 | tf_op jit(solution)/shard_map/queries/pallas_call | solution.py:74
  98.5 1.3 %grad_tokens.5 = (bf16[384,4096]{1,0:T(8,128)(2,1)}, f32[8,128]{1,0:T(8,128)S(1)}) custom-call(bf16[128,2048]{1,0:T(8,128)(2,1)S(1)} %join.9.refs_0_, bf16[128,2048]{1,0:T(8,128)(2,1)S(1)} %collective-permute-done.24.refs_1_, bf16[384,2048]{1,0:T(8,128)(2,1)S(1)} %get-tuple-element.93.refs_2_.refs_4_, ...), custom_call_target="tpu_custom_call", output_to_operand_aliasing={{0}: (3, {})} | custom-call | flops 402653184 | tf_op jit(solution)/shard_map/grad_tokens/pallas_call | solution.py:74
  101.8 5.1 %attended.1 = (bf16[384,2048]{1,0:T(8,128)(2,1)}, f32[8,128]{1,0:T(8,128)S(1)}) custom-call(bf16[384,2048]{1,0:T(8,128)(2,1)S(1)} %get-tuple-element.109.query_ref, bf16[384,2048]{1,0:T(8,128)(2,1)S(1)} %get-tuple-element.89.keys_ref, bf16[384,2048]{1,0:T(8,128)(2,1)S(1)} %get-tuple-element.83.value_ref, bf16[2048,128]{1,0:T(8,128)(2,1)S(1)} %get-tuple-element.91.high_ref, ...), custom_call_target="tpu_custom_call" | custom-call | flops 2415919104 | bytes 6291456 | tf_op jit(solution)/shard_map/attended/pallas_call | solution.py:74
  108.0 2.1 %collective-permute-start.27 = (bf16[1024,128]{1,0:T(8,128)(2,1)S(1)}, bf16[1024,128]{1,0:T(8,128)(2,1)S(1)}, u32[]{:S(2)}, u32[]{:S(2)}) collective-permute-start(bf16[1024,128]{1,0:T(8,128)(2,1)S(1)} %message.3), channel_id=1, source_target_pairs={{4,12},{12,4},{16,0},{20,28},{24,8},{28,20},{5,13},{13,5},{17,1},{... | collective-permute-start | bytes 786440 | tf_op jit(solution)/shard_map/ppermute | solution.py:705
  110.2 3.9 %value_part.1 = (f32[384,2048]{1,0:T(8,128)S(1)}, f32[8,128]{1,0:T(8,128)S(1)}) custom-call(bf16[384,2048]{1,0:T(8,128)(2,1)S(1)} %get-tuple-element.109.query_ref, bf16[384,2048]{1,0:T(8,128)(2,1)S(1)} %get-tuple-element.89.keys_ref, bf16[384,2048]{1,0:T(8,128)(2,1)S(1)} %get-tuple-element.84.grad_ref), custom_call_target="tpu_custom_call" | custom-call | flops 1811939328 | tf_op jit(solution)/shard_map/value_part/pallas_call | solution.py:74
  114.0 1.4 %collective-permute-done.27.more_ref = bf16[1024,128]{1,0:T(8,128)(2,1)S(1)} collective-permute-done((bf16[1024,128]{1,0:T(8,128)(2,1)S(1)}, bf16[1024,128]{1,0:T(8,128)(2,1)S(1)}, u32[]{:S(2)}, u32[]{:S(2)}) %collective-permute-start.27) | collective-permute-done | bytes 262176 | tf_op jit(solution)/shard_map/ppermute | solution.py:705
  115.5 1.9 %collective-permute-start.28 = (f32[1024,128]{1,0:T(8,128)S(1)}, f32[1024,128]{1,0:T(8,128)S(1)}, u32[]{:S(2)}, u32[]{:S(2)}) collective-permute-start(f32[1024,128]{1,0:T(8,128)S(1)} %state.3.state_ref), channel_id=1, source_target_pairs={{0,4},{4,0},{1,5},{5,1},{2,6},{6,2},{3,7},{7,3},{8,12},{12,8},{9,1... | collective-permute-start | bytes 1572872 | tf_op jit(solution)/shard_map/ppermute | solution.py:718
  117.4 1.8 %key_part.1.key_ref = f32[384,2048]{1,0:T(8,128)S(1)} custom-call(bf16[384,2048]{1,0:T(8,128)(2,1)S(1)} %get-tuple-element.109.query_ref, bf16[128,6144]{1,0:T(8,128)(2,1)S(1)} %get-tuple-element.113.top_ref, bf16[256,4096]{1,0:T(8,128)(2,1)S(1)} %get-tuple-element.114.bottom_ref), custom_call_target="tpu_custom_call" | custom-call | flops 1207959552 | tf_op jit(solution)/shard_map/key_part/pallas_call | solution.py:74
  119.5 3.5 %outer.1 = (bf16[384,2048]{1,0:T(8,128)(2,1)}, bf16[384,2048]{1,0:T(8,128)(2,1)}) custom-call(f32[384,2048]{1,0:T(8,128)S(1)} %key_part.1.key_ref, f32[384,2048]{1,0:T(8,128)S(1)} %get-tuple-element.115.val_ref, bf16[384,2048]{1,0:T(8,128)(2,1)S(1)} %get-tuple-element.89.keys_ref, bf16[384,2048]{1,0:T(8,128)(2,1)S(1)} %get-tuple-element.83.value_ref, ...), custom_call_target="tpu_custom_call" | custom-call | flops 805306368 | bytes 15728640 | tf_op jit(solution)/shard_map/outer/pallas_call | solution.py:74
  (60 shorter events, 19.7 us)
Async XLA Ops:
  0.6 11.9 %collective-permute-start = (bf16[128,2048]{1,0:T(8,128)(2,1)}, bf16[128,2048]{1,0:T(8,128)(2,1)S(1)}, u32[]{:S(2)}, u32[]{:S(2)}) collective-permute-start(bf16[128,2048]{1,0:T(8,128)(2,1)} %refs_0_.1), channel_id=1, source_target_pairs={{0,8},{4,20},{8,0},{12,28},{16,24},{20,4},{24,16},{28,12},{1,9},{5... | collective-permute-start | bytes 1572872 | tf_op jit(solution)/shard_map/ppermute | solution.py:808
  2.8 13.5 %collective-permute-start.1 = (bf16[128,2048]{1,0:T(8,128)(2,1)}, bf16[128,2048]{1,0:T(8,128)(2,1)S(1)}, u32[]{:S(2)}, u32[]{:S(2)}) collective-permute-start(bf16[128,2048]{1,0:T(8,128)(2,1)} %refs_0_.1), channel_id=1, source_target_pairs={{0,16},{4,12},{8,24},{12,4},{16,0},{20,28},{24,8},{28,20},{1,17},{... | collective-permute-start | bytes 1572872 | tf_op jit(solution)/shard_map/ppermute | solution.py:808
  4.0 12.4 %collective-permute-start.2 = (bf16[128,2048]{1,0:T(8,128)(2,1)}, bf16[128,2048]{1,0:T(8,128)(2,1)S(1)}, u32[]{:S(2)}, u32[]{:S(2)}) collective-permute-start(bf16[128,2048]{1,0:T(8,128)(2,1)} %refs_0_.1), channel_id=1, source_target_pairs={{0,1},{1,0},{2,3},{3,2},{4,5},{5,4},{6,7},{7,6},{8,9},{9,8},{10,11... | collective-permute-start | bytes 1572872 | tf_op jit(solution)/shard_map/ppermute | solution.py:805
  5.3 11.1 %collective-permute-start.3 = (bf16[128,2048]{1,0:T(8,128)(2,1)}, bf16[128,2048]{1,0:T(8,128)(2,1)S(1)}, u32[]{:S(2)}, u32[]{:S(2)}) collective-permute-start(bf16[128,2048]{1,0:T(8,128)(2,1)} %refs_0_.1), channel_id=1, source_target_pairs={{1,2},{2,1},{5,6},{6,5},{9,10},{10,9},{13,14},{14,13},{17,18},{18,... | collective-permute-start | bytes 1572872 | tf_op jit(solution)/shard_map/ppermute | solution.py:805
  16.4 4.5 %collective-permute-start.9 = (bf16[2048,128]{1,0:T(8,128)(2,1)S(1)}, bf16[2048,128]{1,0:T(8,128)(2,1)S(1)}, u32[]{:S(2)}, u32[]{:S(2)}) collective-permute-start(bf16[2048,128]{1,0:T(8,128)(2,1)S(1)} %get-tuple-element.72), channel_id=1, source_target_pairs={{0,4},{4,0},{1,5},{5,1},{2,6},{6,2},{3,7},{7,3},{8,12},{12,8},{9,1... | collective-permute-start | bytes 1572872 | tf_op jit(solution)/shard_map/ppermute | solution.py:682
  18.5 12.9 %collective-permute-start.4 = (bf16[128,2048]{1,0:T(8,128)(2,1)S(1)}, bf16[128,2048]{1,0:T(8,128)(2,1)S(1)}, u32[]{:S(2)}, u32[]{:S(2)}) collective-permute-start(bf16[128,2048]{1,0:T(8,128)(2,1)S(1)} %get-tuple-element.68.refs_1_), channel_id=1, source_target_pairs={{0,16},{4,12},{8,24},{12,4},{16,0},{20,28},{24,8},{28,20},{1,17},{... | collective-permute-start | bytes 1572872 | tf_op jit(solution)/shard_map/ppermute | solution.py:811
  18.8 14.0 %collective-permute-start.5 = (bf16[128,2048]{1,0:T(8,128)(2,1)S(1)}, bf16[128,2048]{1,0:T(8,128)(2,1)S(1)}, u32[]{:S(2)}, u32[]{:S(2)}) collective-permute-start(bf16[128,2048]{1,0:T(8,128)(2,1)S(1)} %get-tuple-element.69.refs_4_), channel_id=1, source_target_pairs={{0,8},{4,20},{8,0},{12,28},{16,24},{20,4},{24,16},{28,12},{1,9},{5... | collective-permute-start | bytes 1572872 | tf_op jit(solution)/shard_map/ppermute | solution.py:808
  18.9 19.2 %collective-permute-start.6 = (bf16[128,2048]{1,0:T(8,128)(2,1)S(1)}, bf16[128,2048]{1,0:T(8,128)(2,1)S(1)}, u32[]{:S(2)}, u32[]{:S(2)}) collective-permute-start(bf16[128,2048]{1,0:T(8,128)(2,1)S(1)} %get-tuple-element.69.refs_4_), channel_id=1, source_target_pairs={{0,16},{4,12},{8,24},{12,4},{16,0},{20,28},{24,8},{28,20},{1,17},{... | collective-permute-start | bytes 1572872 | tf_op jit(solution)/shard_map/ppermute | solution.py:808
  20.2 17.9 %collective-permute-start.7 = (bf16[128,2048]{1,0:T(8,128)(2,1)S(1)}, bf16[128,2048]{1,0:T(8,128)(2,1)S(1)}, u32[]{:S(2)}, u32[]{:S(2)}) collective-permute-start(bf16[128,2048]{1,0:T(8,128)(2,1)S(1)} %get-tuple-element.69.refs_4_), channel_id=1, source_target_pairs={{1,2},{2,1},{5,6},{6,5},{9,10},{10,9},{13,14},{14,13},{17,18},{18,... | collective-permute-start | bytes 1572872 | tf_op jit(solution)/shard_map/ppermute | solution.py:805
  20.9 19.4 %collective-permute-start.8 = (bf16[128,2048]{1,0:T(8,128)(2,1)S(1)}, bf16[128,2048]{1,0:T(8,128)(2,1)S(1)}, u32[]{:S(2)}, u32[]{:S(2)}) collective-permute-start(bf16[128,2048]{1,0:T(8,128)(2,1)S(1)} %get-tuple-element.70.inner_ref), channel_id=1, source_target_pairs={{1,0},{2,3},{5,4},{6,7},{9,8},{10,11},{13,12},{14,15},{17,16},{18,... | collective-permute-start | bytes 1572872 | tf_op jit(solution)/shard_map/ppermute | solution.py:805
  22.2 18.1 %copy-start = (bf16[128,2048]{1,0:T(8,128)(2,1)S(1)}, bf16[128,2048]{1,0:T(8,128)(2,1)}, u32[]{:S(2)}) copy-start(bf16[128,2048]{1,0:T(8,128)(2,1)} %refs_0_.1) | copy-start | bytes 1572868
  31.4 8.8 %collective-permute-start.10 = (bf16[1024,128]{1,0:T(8,128)(2,1)S(1)}, bf16[1024,128]{1,0:T(8,128)(2,1)S(1)}, u32[]{:S(2)}, u32[]{:S(2)}) collective-permute-start(bf16[1024,128]{1,0:T(8,128)(2,1)S(1)} %get-tuple-element.73), channel_id=1, source_target_pairs={{0,8},{4,20},{8,0},{12,28},{16,24},{24,16},{1,9},{5,21},{9,1},{13,... | collective-permute-start | bytes 786440 | tf_op jit(solution)/shard_map/ppermute | solution.py:692
  40.6 9.8 %collective-permute-start.15 = (bf16[896,2048]{1,0:T(8,128)(2,1)S(1)}, bf16[896,2048]{1,0:T(8,128)(2,1)S(1)}, u32[]{:S(2)}, u32[]{:S(2)}) collective-permute-start(bf16[896,2048]{1,0:T(8,128)(2,1)S(1)} %pack.3.refs_0_), channel_id=1, source_target_pairs={{0,4},{4,0},{1,5},{5,1},{2,6},{6,2},{3,7},{7,3},{8,12},{12,8},{9,1... | collective-permute-start | bytes 11010056 | tf_op jit(solution)/shard_map/ppermute | solution.py:761
  42.5 18.3 %collective-permute-start.11 = (bf16[128,2048]{1,0:T(8,128)(2,1)S(1)}, bf16[128,2048]{1,0:T(8,128)(2,1)S(1)}, u32[]{:S(2)}, u32[]{:S(2)}) collective-permute-start(bf16[128,2048]{1,0:T(8,128)(2,1)S(1)} %get-tuple-element.74.inner_ref), channel_id=1, source_target_pairs={{1,0},{2,3},{5,4},{6,7},{9,8},{10,11},{13,12},{14,15},{17,16},{18,... | collective-permute-start | bytes 1572872 | tf_op jit(solution)/shard_map/ppermute | solution.py:805
  43.8 17.0 %collective-permute-start.12 = (bf16[128,2048]{1,0:T(8,128)(2,1)S(1)}, bf16[128,2048]{1,0:T(8,128)(2,1)S(1)}, u32[]{:S(2)}, u32[]{:S(2)}) collective-permute-start(bf16[128,2048]{1,0:T(8,128)(2,1)S(1)} %choose.2.refs_0_), channel_id=1, source_target_pairs={{0,8},{4,20},{8,0},{12,28},{16,24},{20,4},{24,16},{28,12},{1,9},{5... | collective-permute-start | bytes 1572872 | tf_op jit(solution)/shard_map/ppermute | solution.py:808
  45.1 15.7 %collective-permute-start.13 = (bf16[128,2048]{1,0:T(8,128)(2,1)S(1)}, bf16[128,2048]{1,0:T(8,128)(2,1)S(1)}, u32[]{:S(2)}, u32[]{:S(2)}) collective-permute-start(bf16[128,2048]{1,0:T(8,128)(2,1)S(1)} %choose.2.refs_0_), channel_id=1, source_target_pairs={{0,16},{4,12},{8,24},{12,4},{16,0},{20,28},{24,8},{28,20},{1,17},{... | collective-permute-start | bytes 1572872 | tf_op jit(solution)/shard_map/ppermute | solution.py:808
  45.4 15.4 %collective-permute-start.14 = (bf16[1024,128]{1,0:T(8,128)(2,1)S(1)}, bf16[1024,128]{1,0:T(8,128)(2,1)S(1)}, u32[]{:S(2)}, u32[]{:S(2)}) collective-permute-start(bf16[1024,128]{1,0:T(8,128)(2,1)S(1)} %message.2), channel_id=1, source_target_pairs={{0,16},{4,12},{8,24},{12,4},{20,28},{28,20},{1,17},{5,13},{9,25},{... | collective-permute-start | bytes 786440 | tf_op jit(solution)/shard_map/ppermute | solution.py:705
  61.2 18.3 %collective-permute-start.21 = (bf16[512,2048]{1,0:T(8,128)(2,1)S(1)}, bf16[512,2048]{1,0:T(8,128)(2,1)S(1)}, u32[]{:S(2)}, u32[]{:S(2)}) collective-permute-start(bf16[512,2048]{1,0:T(8,128)(2,1)S(1)} %pack.4.refs_0_), channel_id=1, source_target_pairs={{0,4},{4,0},{1,5},{5,1},{2,6},{6,2},{3,7},{7,3},{8,12},{12,8},{9,1... | collective-permute-start | bytes 6291464 | tf_op jit(solution)/shard_map/ppermute | solution.py:761
  61.4 4.8 %collective-permute-start.20 = (f32[1024,128]{1,0:T(8,128)S(1)}, f32[1024,128]{1,0:T(8,128)S(1)}, u32[]{:S(2)}, u32[]{:S(2)}) collective-permute-start(f32[1024,128]{1,0:T(8,128)S(1)} %state.2.state_ref), channel_id=1, source_target_pairs={{0,4},{4,0},{1,5},{5,1},{2,6},{6,2},{3,7},{7,3},{8,12},{12,8},{9,1... | collective-permute-start | bytes 1572872 | tf_op jit(solution)/shard_map/ppermute | solution.py:718
  62.0 21.8 %collective-permute-start.17 = (bf16[128,2048]{1,0:T(8,128)(2,1)S(1)}, bf16[128,2048]{1,0:T(8,128)(2,1)S(1)}, u32[]{:S(2)}, u32[]{:S(2)}) collective-permute-start(bf16[128,2048]{1,0:T(8,128)(2,1)S(1)} %get-tuple-element.87.refs_1_), channel_id=1, source_target_pairs={{0,16},{4,12},{8,24},{12,4},{16,0},{20,28},{24,8},{28,20},{1,17},{... | collective-permute-start | bytes 1572872 | tf_op jit(solution)/shard_map/ppermute | solution.py:811
  62.2 21.6 %collective-permute-start.18 = (bf16[128,2048]{1,0:T(8,128)(2,1)S(1)}, bf16[128,2048]{1,0:T(8,128)(2,1)S(1)}, u32[]{:S(2)}, u32[]{:S(2)}) collective-permute-start(bf16[128,2048]{1,0:T(8,128)(2,1)S(1)} %choose.3.refs_3_), channel_id=1, source_target_pairs={{0,8},{4,20},{8,0},{12,28},{16,24},{20,4},{24,16},{28,12},{1,9},{5... | collective-permute-start | bytes 1572872 | tf_op jit(solution)/shard_map/ppermute | solution.py:808
  63.3 20.5 %collective-permute-start.19 = (bf16[128,2048]{1,0:T(8,128)(2,1)S(1)}, bf16[128,2048]{1,0:T(8,128)(2,1)S(1)}, u32[]{:S(2)}, u32[]{:S(2)}) collective-permute-start(bf16[128,2048]{1,0:T(8,128)(2,1)S(1)} %choose.3.refs_3_), channel_id=1, source_target_pairs={{0,16},{4,12},{8,24},{12,4},{16,0},{20,28},{24,8},{28,20},{1,17},{... | collective-permute-start | bytes 1572872 | tf_op jit(solution)/shard_map/ppermute | solution.py:808
  66.2 17.6 %collective-permute-start.16 = (bf16[128,2048]{1,0:T(8,128)(2,1)S(1)}, bf16[128,2048]{1,0:T(8,128)(2,1)S(1)}, u32[]{:S(2)}, u32[]{:S(2)}) collective-permute-start(bf16[128,2048]{1,0:T(8,128)(2,1)S(1)} %get-tuple-element.86), channel_id=1, source_target_pairs={{0,1},{1,0},{2,3},{3,2},{4,5},{5,4},{6,7},{7,6},{8,9},{9,8},{10,11... | collective-permute-start | bytes 1572872 | tf_op jit(solution)/shard_map/ppermute | solution.py:805
  84.2 4.3 %collective-permute-start.22 = (bf16[512,2048]{1,0:T(8,128)(2,1)S(1)}, bf16[512,2048]{1,0:T(8,128)(2,1)S(1)}, u32[]{:S(2)}, u32[]{:S(2)}) collective-permute-start(bf16[512,2048]{1,0:T(8,128)(2,1)S(1)} %pack.5.refs_0_), channel_id=1, source_target_pairs={{0,4},{4,0},{1,5},{5,1},{2,6},{6,2},{3,7},{7,3},{8,12},{12,8},{9,1... | collective-permute-start | bytes 6291464 | tf_op jit(solution)/shard_map/ppermute | solution.py:761
  84.7 8.3 %collective-permute-start.23 = (bf16[128,2048]{1,0:T(8,128)(2,1)S(1)}, bf16[128,2048]{1,0:T(8,128)(2,1)S(1)}, u32[]{:S(2)}, u32[]{:S(2)}) collective-permute-start(bf16[128,2048]{1,0:T(8,128)(2,1)S(1)} %get-tuple-element.101.refs_2_), channel_id=1, source_target_pairs={{0,16},{4,12},{8,24},{12,4},{16,0},{20,28},{24,8},{28,20},{1,17},{... | collective-permute-start | bytes 1572872 | tf_op jit(solution)/shard_map/ppermute | solution.py:811
  93.1 3.6 %collective-permute-start.24 = (bf16[128,2048]{1,0:T(8,128)(2,1)S(1)}, bf16[128,2048]{1,0:T(8,128)(2,1)S(1)}, u32[]{:S(2)}, u32[]{:S(2)}) collective-permute-start(bf16[128,2048]{1,0:T(8,128)(2,1)S(1)} %join.9.refs_0_), channel_id=1, source_target_pairs={{0,4},{4,0},{1,5},{5,1},{2,6},{6,2},{3,7},{7,3},{8,12},{12,8},{9,1... | collective-permute-start | bytes 1572872 | tf_op jit(solution)/shard_map/ppermute | solution.py:802
  98.4 2.0 %collective-permute-start.25 = (bf16[2048,128]{1,0:T(8,128)(2,1)S(1)}, bf16[2048,128]{1,0:T(8,128)(2,1)S(1)}, u32[]{:S(2)}, u32[]{:S(2)}) collective-permute-start(bf16[2048,128]{1,0:T(8,128)(2,1)S(1)} %get-tuple-element.118), channel_id=1, source_target_pairs={{0,4},{4,0},{1,5},{5,1},{2,6},{6,2},{3,7},{7,3},{8,12},{12,8},{9,1... | collective-permute-start | bytes 1572872 | tf_op jit(solution)/shard_map/ppermute | solution.py:682
  100.5 7.4 %collective-permute-start.26 = (bf16[1024,128]{1,0:T(8,128)(2,1)S(1)}, bf16[1024,128]{1,0:T(8,128)(2,1)S(1)}, u32[]{:S(2)}, u32[]{:S(2)}) collective-permute-start(bf16[1024,128]{1,0:T(8,128)(2,1)S(1)} %get-tuple-element.120), channel_id=1, source_target_pairs={{0,8},{8,0},{16,24},{20,4},{24,16},{28,12},{1,9},{9,1},{17,25},{21... | collective-permute-start | bytes 786440 | tf_op jit(solution)/shard_map/ppermute | solution.py:692
  108.0 7.4 %collective-permute-start.27 = (bf16[1024,128]{1,0:T(8,128)(2,1)S(1)}, bf16[1024,128]{1,0:T(8,128)(2,1)S(1)}, u32[]{:S(2)}, u32[]{:S(2)}) collective-permute-start(bf16[1024,128]{1,0:T(8,128)(2,1)S(1)} %message.3), channel_id=1, source_target_pairs={{4,12},{12,4},{16,0},{20,28},{24,8},{28,20},{5,13},{13,5},{17,1},{... | collective-permute-start | bytes 786440 | tf_op jit(solution)/shard_map/ppermute | solution.py:705
  115.5 3.8 %collective-permute-start.28 = (f32[1024,128]{1,0:T(8,128)S(1)}, f32[1024,128]{1,0:T(8,128)S(1)}, u32[]{:S(2)}, u32[]{:S(2)}) collective-permute-start(f32[1024,128]{1,0:T(8,128)S(1)} %state.3.state_ref), channel_id=1, source_target_pairs={{0,4},{4,0},{1,5},{5,1},{2,6},{6,2},{3,7},{7,3},{8,12},{12,8},{9,1... | collective-permute-start | bytes 1572872 | tf_op jit(solution)/shard_map/ppermute | solution.py:718

commit v11 on v10

--- a/solution.py
+++ b/solution.py
@@ -733,8 +733,8 @@
     return [whole[:cut], whole[cut:]]
 
 
-def pack_kernel(*refs):
-    *arrays, out_ref, sems = refs
+def pack_kernel(number, *refs):
+    arrays, (out_ref, sems) = refs[:number], refs[-2:]
     copies = Copies(sems)
     rows = out_ref.shape[0] // len(arrays)
     going = [
@@ -745,13 +745,13 @@
         copy.wait()
 
 
-def pack(*arrays):
+def pack(*arrays, others=()):
     rows, total = arrays[0].shape
     number = len(arrays)
     (made,) = kernel_call(
-        pack_kernel,
-        "A" * number,
-        arrays,
+        functools.partial(pack_kernel, number),
+        "A" * (number + len(others)),
+        (*arrays, *others),
         "V",
         [((number * rows, total), arrays[0].dtype)],
         "pack",
@@ -850,20 +850,20 @@
         first_3, second_3 = cross(last_layer)
         high, low = add_up(got, more, twin, False)
         masked, q_mask = masked_call(factor, q_spikes, cotangent, values, keys, high, low)
-        _, grad, mark_0 = products_call(
-            special, 0, early, tokens, masked=masked, project=False
-        )
-        blocks = pack(next_layer, first_2, second_2, last_layer)
-        partial, grad, mark_1 = products_call(special, 14, blocks, tokens, partial, masked, grad)
-        third_1, third_2, first_3, second_3 = join(
-            [third_1, third_2, first_3, second_3], [mark_0, mark_1]
+        middle = pack(next_layer, first_2, second_2, last_layer)
+        _, grad, mark = products_call(special, 0, early, tokens, masked=masked, project=False)
+        third_2, first_3, second_3, third_1, middle[1] = join(
+            [third_2, first_3, second_3, third_1, middle[1]], [mark]
         )
         third_3 = onward(first_3)
-        blocks = pack(third_1, third_2, first_3, second_3)
-        partial, _, mark = products_call(special, 22, blocks, tokens, partial)
-        third_3, = join([third_3], [mark])
+        late = pack(third_1, third_2, first_3, second_3)
+        partial, grad, mark_0 = products_call(
+            special, 14, middle, tokens, partial, masked, grad
+        )
+        partial, _, mark_1 = products_call(special, 22, late, tokens, partial)
+        third_3, = join([third_3], [mark_0, mark_1])
         _, grad, mark = products_call(
-            special, 22, blocks, tokens, masked=masked, grad=grad, project=False
+            special, 22, late, tokens, masked=masked, grad=grad, project=False
         )
         late = [third_3, sibling(third_3)]
         start = 30

time: 124 us -> 122 us (0.984)
  waiting for transfers between devices: 40.4 us -> 36.1 us
  starting transfers between devices: 34.1 us -> 37 us
    ppermute x4, waiting for transfers between devices: 1.82 us -> 10.8 us  [cross(): lax.ppermute(array, CTX, links(1))]
    ppermute x4, waiting for transfers between devices: 9.08 us -> 3.75 us  [cross(): lax.ppermute(array, CTX, links(2))]
    ppermute x3, waiting for transfers between devices: 3.57 us -> 0.01 us  [pack(): return [made, lax.ppermute(made, 'core', SWAP)]]
    ppermute x3, waiting for transfers between devices: 11.6 us -> 9.09 us  [onward(): return lax.ppermute(array, CTX, links(2))]
    ppermute x3, starting transfers between devices: 0.73 us -> 2.94 us  [onward(): return lax.ppermute(array, CTX, links(2))]
    ppermute x2, waiting for transfers between devices: 8.76 us -> 6.77 us  [send_second(): return lax.ppermute(message, CTX, links(2, upward(reverse)))]
  transfers between devices with their start and end apart: 29 -> 29, of which waited for: 13 -> 14; matrix products, arithmetic and copies ran while one was open for 0% -> 0% of each run, Pallas kernels for 33% -> 33%
where the time goes in v11:
time: 122 us
  Pallas kernels  47.3 us (39%)
  starting transfers between devices  37 us (30%)
  waiting for transfers between devices  36.1 us (30%)
    pallas_call x32, Pallas kernels, kernel_call(): made(*[holds[place](one) if place in holds else one for place, one in zip...  47.3 us
    ppermute x4, waiting for transfers between devices, cross(): lax.ppermute(array, CTX, links(1))  10.8 us
    ppermute x3, waiting for transfers between devices, onward(): return lax.ppermute(array, CTX, links(2))  9.09 us
    ppermute x6, starting transfers between devices, along(): return lax.ppermute(array, 'dp', pairs)  7.73 us
    ppermute x2, waiting for transfers between devices, send_second(): return lax.ppermute(message, CTX, links(2, upward(reverse)))  6.77 us
    ppermute x2, starting transfers between devices, send_second(): return lax.ppermute(message, CTX, links(2, upward(reverse)))  6.24 us
    ppermute x4, starting transfers between devices, cross(): lax.ppermute(array, CTX, links(1))  4.79 us
    ppermute x4, waiting for transfers between devices, cross(): lax.ppermute(array, CTX, links(2))  3.75 us
  transfers between devices with their start and end apart: 29, of which 14 were waited for; matrix products, arithmetic and copies ran while one was open for 0% of the time, Pallas kernels for 33%

profile of v11, /device:TPU:1, one launch (start us, length us, event | category | flops | bytes accessed | tf_op | source)
XLA Modules:
  0.0 121.6 jit_solution(17034099203033378986)
XLA Ops:
  0.6 2.1 %collective-permute-start = (bf16[128,2048]{1,0:T(8,128)(2,1)}, bf16[128,2048]{1,0:T(8,128)(2,1)S(1)}, u32[]{:S(2)}, u32[]{:S(2)}) collective-permute-start(bf16[128,2048]{1,0:T(8,128)(2,1)} %refs_0_.1), channel_id=1, source_target_pairs={{0,8},{4,20},{8,0},{12,28},{16,24},{20,4},{24,16},{28,12},{1,9},{5... | collective-permute-start | bytes 1572872 | tf_op jit(solution)/shard_map/ppermute | solution.py:808
  6.0 4.8 %own_memory.1 = (bf16[384,2048]{1,0:T(8,128)(2,1)S(1)}, bf16[384,2048]{1,0:T(8,128)(2,1)S(1)}, bf16[384,2048]{1,0:T(8,128)(2,1)S(1)}, f32[2048,128]{1,0:T(8,128)...) custom-call(bf16[384,2048]{1,0:T(8,128)(2,1)} %bitcast.13, ...), custom_call_target="tpu_custom_call" | custom-call | flops 201326592 | bytes 9437184 | tf_op jit(solution)/shard_map/own_memory/pallas_call | solution.py:74
  10.7 1.8 %collective-permute-done.refs_0_ = bf16[128,2048]{1,0:T(8,128)(2,1)S(1)} collective-permute-done((bf16[128,2048]{1,0:T(8,128)(2,1)}, bf16[128,2048]{1,0:T(8,128)(2,1)S(1)}, u32[]{:S(2)}, u32[]{:S(2)}) %collective-permute-start) | collective-permute-done | bytes 524320 | tf_op jit(solution)/shard_map/ppermute | solution.py:808
  12.6 3.7 %collective-permute-done.1.refs_1_ = bf16[128,2048]{1,0:T(8,128)(2,1)S(1)} collective-permute-done((bf16[128,2048]{1,0:T(8,128)(2,1)}, bf16[128,2048]{1,0:T(8,128)(2,1)S(1)}, u32[]{:S(2)}, u32[]{:S(2)}) %collective-permute-start.1) | collective-permute-done | bytes 524320 | tf_op jit(solution)/shard_map/ppermute | solution.py:808
  16.4 2.2 %collective-permute-start.9 = (bf16[2048,128]{1,0:T(8,128)(2,1)S(1)}, bf16[2048,128]{1,0:T(8,128)(2,1)S(1)}, u32[]{:S(2)}, u32[]{:S(2)}) collective-permute-start(bf16[2048,128]{1,0:T(8,128)(2,1)S(1)} %get-tuple-element.73), channel_id=1, source_target_pairs={{0,4},{4,0},{1,5},{5,1},{2,6},{6,2},{3,7},{7,3},{8,12},{12,8},{9,1... | collective-permute-start | bytes 1572872 | tf_op jit(solution)/shard_map/ppermute | solution.py:682
  19.6 1.4 %collective-permute-start.4 = (bf16[128,2048]{1,0:T(8,128)(2,1)S(1)}, bf16[128,2048]{1,0:T(8,128)(2,1)S(1)}, u32[]{:S(2)}, u32[]{:S(2)}) collective-permute-start(bf16[128,2048]{1,0:T(8,128)(2,1)S(1)} %get-tuple-element.69.refs_1_), channel_id=1, source_target_pairs={{0,16},{4,12},{8,24},{12,4},{16,0},{20,28},{24,8},{28,20},{1,17},{... | collective-permute-start | bytes 1572872 | tf_op jit(solution)/shard_map/ppermute | solution.py:811
  22.4 9.0 %collective-permute-done.5.refs_1_ = bf16[128,2048]{1,0:T(8,128)(2,1)S(1)} collective-permute-done((bf16[128,2048]{1,0:T(8,128)(2,1)S(1)}, bf16[128,2048]{1,0:T(8,128)(2,1)S(1)}, u32[]{:S(2)}, u32[]{:S(2)}) %collective-permute-start.5) | collective-permute-done | bytes 524320 | tf_op jit(solution)/shard_map/ppermute | solution.py:808
  31.4 2.3 %collective-permute-start.10 = (bf16[1024,128]{1,0:T(8,128)(2,1)S(1)}, bf16[1024,128]{1,0:T(8,128)(2,1)S(1)}, u32[]{:S(2)}, u32[]{:S(2)}) collective-permute-start(bf16[1024,128]{1,0:T(8,128)(2,1)S(1)} %get-tuple-element.74), channel_id=1, source_target_pairs={{0,8},{4,20},{8,0},{12,28},{16,24},{24,16},{1,9},{5,21},{9,1},{13,... | collective-permute-start | bytes 786440 | tf_op jit(solution)/shard_map/ppermute | solution.py:692
  33.7 4.6 %collective-permute-done.4.refs_0_ = bf16[128,2048]{1,0:T(8,128)(2,1)S(1)} collective-permute-done((bf16[128,2048]{1,0:T(8,128)(2,1)S(1)}, bf16[128,2048]{1,0:T(8,128)(2,1)S(1)}, u32[]{:S(2)}, u32[]{:S(2)}) %collective-permute-start.4) | collective-permute-done | bytes 524320 | tf_op jit(solution)/shard_map/ppermute | solution.py:811
  38.3 2.0 %collective-permute-done.8.refs_4_ = bf16[128,2048]{1,0:T(8,128)(2,1)S(1)} collective-permute-done((bf16[128,2048]{1,0:T(8,128)(2,1)S(1)}, bf16[128,2048]{1,0:T(8,128)(2,1)S(1)}, u32[]{:S(2)}, u32[]{:S(2)}) %collective-permute-start.8) | collective-permute-done | bytes 524320 | tf_op jit(solution)/shard_map/ppermute | solution.py:805
  40.7 1.8 %collective-permute-start.15 = (bf16[896,2048]{1,0:T(8,128)(2,1)S(1)}, bf16[896,2048]{1,0:T(8,128)(2,1)S(1)}, u32[]{:S(2)}, u32[]{:S(2)}) collective-permute-start(bf16[896,2048]{1,0:T(8,128)(2,1)S(1)} %pack.3.refs_0_), channel_id=1, source_target_pairs={{0,4},{4,0},{1,5},{5,1},{2,6},{6,2},{3,7},{7,3},{8,12},{12,8},{9,1... | collective-permute-start | bytes 11010056 | tf_op jit(solution)/shard_map/ppermute | solution.py:761
  42.5 1.3 %collective-permute-start.12 = (bf16[128,2048]{1,0:T(8,128)(2,1)S(1)}, bf16[128,2048]{1,0:T(8,128)(2,1)S(1)}, u32[]{:S(2)}, u32[]{:S(2)}) collective-permute-start(bf16[128,2048]{1,0:T(8,128)(2,1)S(1)} %choose.2.refs_0_), channel_id=1, source_target_pairs={{0,8},{4,20},{8,0},{12,28},{16,24},{20,4},{24,16},{28,12},{1,9},{5... | collective-permute-start | bytes 1572872 | tf_op jit(solution)/shard_map/ppermute | solution.py:808
  45.5 3.1 %collective-permute-start.14 = (bf16[1024,128]{1,0:T(8,128)(2,1)S(1)}, bf16[1024,128]{1,0:T(8,128)(2,1)S(1)}, u32[]{:S(2)}, u32[]{:S(2)}) collective-permute-start(bf16[1024,128]{1,0:T(8,128)(2,1)S(1)} %message.2), channel_id=1, source_target_pairs={{0,16},{4,12},{8,24},{12,4},{20,28},{28,20},{1,17},{5,13},{9,25},{... | collective-permute-start | bytes 786440 | tf_op jit(solution)/shard_map/ppermute | solution.py:705
  48.6 1.8 %turned.1 = (bf16[128,6144]{1,0:T(8,128)(2,1)S(1)}, bf16[256,4096]{1,0:T(8,128)(2,1)S(1)}, f32[8,128]{1,0:T(8,128)S(1)}) custom-call(bf16[384,2048]{1,0:T(8,128)(2,1)S(1)} %get-tuple-element.84.value_ref, bf16[384,2048]{1,0:T(8,128)(2,1)S(1)} %get-tuple-element.85.grad_ref, bf16[1024,128]{1,0:T(8,128)(2,1)S(1)} %get-tuple-element.77.got_ref.after_ref), custom_call_target="tpu_custom_call" | custom-call | flops 1207959552 | tf_op jit(solution)/shard_map/turned/pallas_call | solution.py:74
  50.5 3.0 %project.2 = (f32[384,2048]{1,0:T(8,128)S(1)}, f32[8,128]{1,0:T(8,128)S(1)}) custom-call(bf16[896,2048]{1,0:T(8,128)(2,1)S(1)} %pack.3.refs_0_, bf16[896,2048]{1,0:T(8,128)(2,1)S(1)} %collective-permute-done.15.refs_1_, bf16[384,4096]{1,0:T(8,128)(2,1)S(1)} %get-tuple-element.67.refs_2_.tokens_ref), custom_call_target="tpu_custom_call" | custom-call | flops 2818572288 | tf_op jit(solution)/shard_map/project/pallas_call | solution.py:74
  53.5 6.4 %collective-permute-done.14.refs_3_ = bf16[1024,128]{1,0:T(8,128)(2,1)S(1)} collective-permute-done((bf16[1024,128]{1,0:T(8,128)(2,1)S(1)}, bf16[1024,128]{1,0:T(8,128)(2,1)S(1)}, u32[]{:S(2)}, u32[]{:S(2)}) %collective-permute-start.14) | collective-permute-done | bytes 262176 | tf_op jit(solution)/shard_map/ppermute | solution.py:705
  64.3 1.8 %collective-permute-done.21.other_ref = f32[1024,128]{1,0:T(8,128)S(1)} collective-permute-done((f32[1024,128]{1,0:T(8,128)S(1)}, f32[1024,128]{1,0:T(8,128)S(1)}, u32[]{:S(2)}, u32[]{:S(2)}) %collective-permute-start.21) | collective-permute-done | bytes 524320 | tf_op jit(solution)/shard_map/ppermute | solution.py:718
  66.0 2.5 %collective-permute-start.19 = (bf16[128,2048]{1,0:T(8,128)(2,1)S(1)}, bf16[128,2048]{1,0:T(8,128)(2,1)S(1)}, u32[]{:S(2)}, u32[]{:S(2)}) collective-permute-start(bf16[128,2048]{1,0:T(8,128)(2,1)S(1)} %get-tuple-element.89), channel_id=1, source_target_pairs={{0,1},{1,0},{2,3},{3,2},{4,5},{5,4},{6,7},{7,6},{8,9},{9,8},{10,11... | collective-permute-start | bytes 1572872 | tf_op jit(solution)/shard_map/ppermute | solution.py:805
  68.8 5.4 %masked_grad.1 = (bf16[384,2048]{1,0:T(8,128)(2,1)S(1)}, bf16[384,2048]{1,0:T(8,128)(2,1)S(1)}) custom-call(s32[384,2048]{1,0:T(8,128)} %bitcast.16, bf16[384,2048]{1,0:T(8,128)(2,1)S(1)} %get-tuple-element.85.grad_ref, bf16[384,2048]{1,0:T(8,128)(2,1)S(1)} %get-tuple-element.84.value_ref, bf16[384,2048]{1,0:T(8,128)(2,1)S(1)} %get-tuple-element.91.keys_ref, ...), custom_call_target="tpu_custom_call" | custom-call | flops 2415919104 | bytes 9437184 | tf_op jit(solution)/shard_map/masked_grad/pallas_call | solution.py:74
  74.2 3.9 %grad_tokens.3 = (bf16[384,4096]{1,0:T(8,128)(2,1)}, f32[8,128]{1,0:T(8,128)S(1)}) custom-call(bf16[896,2048]{1,0:T(8,128)(2,1)S(1)} %pack.3.refs_0_, bf16[896,2048]{1,0:T(8,128)(2,1)S(1)} %collective-permute-done.15.refs_1_, bf16[384,2048]{1,0:T(8,128)(2,1)S(1)} %get-tuple-element.95.refs_2_.refs_4_), custom_call_target="tpu_custom_call" | custom-call | flops 2818572288 | tf_op jit(solution)/shard_map/grad_tokens/pallas_call | solution.py:74
  78.2 3.7 %collective-permute-done.16.refs_0_ = bf16[128,2048]{1,0:T(8,128)(2,1)S(1)} collective-permute-done((bf16[128,2048]{1,0:T(8,128)(2,1)S(1)}, bf16[128,2048]{1,0:T(8,128)(2,1)S(1)}, u32[]{:S(2)}, u32[]{:S(2)}) %collective-permute-start.16) | collective-permute-done | bytes 524320 | tf_op jit(solution)/shard_map/ppermute | solution.py:811
  83.6 4.3 %products.1 = (f32[384,2048]{1,0:T(8,128)S(1)}, bf16[384,4096]{1,0:T(8,128)(2,1)}, f32[8,128]{1,0:T(8,128)S(1)}) custom-call(bf16[512,2048]{1,0:T(8,128)(2,1)S(1)} %pack.4.refs_0_, bf16[512,2048]{1,0:T(8,128)(2,1)S(1)} %get-tuple-element.101.refs_1_, ...), custom_call_target="tpu_custom_call", output_to_operand_aliasing={{0}: (3, {}), {1}: (5, {})} | custom-call | flops 3221225472 | tf_op jit(solution)/shard_map/products/pallas_call | solution.py:74
  87.9 2.1 %project.3 = (f32[384,2048]{1,0:T(8,128)S(1)}, f32[8,128]{1,0:T(8,128)S(1)}) custom-call(bf16[512,2048]{1,0:T(8,128)(2,1)S(1)} %pack.5.refs_0_, bf16[512,2048]{1,0:T(8,128)(2,1)S(1)} %collective-permute-done.22.refs_1_, bf16[384,4096]{1,0:T(8,128)(2,1)S(1)} %get-tuple-element.67.refs_2_.tokens_ref, ...), custom_call_target="tpu_custom_call", output_to_operand_aliasing={{0}: (3, {})} | custom-call | flops 1610612736 | tf_op jit(solution)/shard_map/project/pallas_call | solution.py:74
  92.0 2.7 %grad_tokens.4 = (bf16[384,4096]{1,0:T(8,128)(2,1)}, f32[8,128]{1,0:T(8,128)S(1)}) custom-call(bf16[512,2048]{1,0:T(8,128)(2,1)S(1)} %pack.5.refs_0_, bf16[512,2048]{1,0:T(8,128)(2,1)S(1)} %collective-permute-done.22.refs_1_, bf16[384,2048]{1,0:T(8,128)(2,1)S(1)} %get-tuple-element.95.refs_2_.refs_4_, ...), custom_call_target="tpu_custom_call", output_to_operand_aliasing={{0}: (3, {})} | custom-call | flops 1610612736 | tf_op jit(solution)/shard_map/grad_tokens/pallas_call | solution.py:74
  94.7 1.8 %queries.1 = (bf16[384,2048]{1,0:T(8,128)(2,1)S(1)}, f32[2048,128]{1,0:T(8,128)S(1)}, bf16[2048,128]{1,0:T(8,128)(2,1)S(1)}) custom-call(bf16[384,4096]{1,0:T(8,128)(2,1)S(1)} %get-tuple-element.67.refs_2_.tokens_ref, f32[384,2048]{1,0:T(8,128)S(1)} %get-tuple-element.105.sum_ref, bf16[384,2048]{1,0:T(8,128)(2,1)S(1)} %get-tuple-element.106.mask_ref, ...), custom_call_target="tpu_custom_call" | custom-call | flops 402653184 | tf_op jit(solution)/shard_map/queries/pallas_call | solution.py:74
  96.6 1.3 %grad_tokens.5 = (bf16[384,4096]{1,0:T(8,128)(2,1)}, f32[8,128]{1,0:T(8,128)S(1)}) custom-call(bf16[128,2048]{1,0:T(8,128)(2,1)S(1)} %join.9.refs_0_, bf16[128,2048]{1,0:T(8,128)(2,1)S(1)} %collective-permute-done.24.refs_1_, bf16[384,2048]{1,0:T(8,128)(2,1)S(1)} %get-tuple-element.95.refs_2_.refs_4_, ...), custom_call_target="tpu_custom_call", output_to_operand_aliasing={{0}: (3, {})} | custom-call | flops 402653184 | tf_op jit(solution)/shard_map/grad_tokens/pallas_call | solution.py:74
  99.9 5.1 %attended.1 = (bf16[384,2048]{1,0:T(8,128)(2,1)}, f32[8,128]{1,0:T(8,128)S(1)}) custom-call(bf16[384,2048]{1,0:T(8,128)(2,1)S(1)} %get-tuple-element.111.query_ref, bf16[384,2048]{1,0:T(8,128)(2,1)S(1)} %get-tuple-element.91.keys_ref, bf16[384,2048]{1,0:T(8,128)(2,1)S(1)} %get-tuple-element.84.value_ref, bf16[2048,128]{1,0:T(8,128)(2,1)S(1)} %get-tuple-element.93.high_ref, ...), custom_call_target="tpu_custom_call" | custom-call | flops 2415919104 | bytes 6291456 | tf_op jit(solution)/shard_map/attended/pallas_call | solution.py:74
  106.0 3.1 %collective-permute-start.27 = (bf16[1024,128]{1,0:T(8,128)(2,1)S(1)}, bf16[1024,128]{1,0:T(8,128)(2,1)S(1)}, u32[]{:S(2)}, u32[]{:S(2)}) collective-permute-start(bf16[1024,128]{1,0:T(8,128)(2,1)S(1)} %message.3), channel_id=1, source_target_pairs={{4,12},{12,4},{16,0},{20,28},{24,8},{28,20},{5,13},{13,5},{17,1},{... | collective-permute-start | bytes 786440 | tf_op jit(solution)/shard_map/ppermute | solution.py:705
  109.2 3.9 %value_part.1 = (f32[384,2048]{1,0:T(8,128)S(1)}, f32[8,128]{1,0:T(8,128)S(1)}) custom-call(bf16[384,2048]{1,0:T(8,128)(2,1)S(1)} %get-tuple-element.111.query_ref, bf16[384,2048]{1,0:T(8,128)(2,1)S(1)} %get-tuple-element.91.keys_ref, bf16[384,2048]{1,0:T(8,128)(2,1)S(1)} %get-tuple-element.85.grad_ref), custom_call_target="tpu_custom_call" | custom-call | flops 1811939328 | tf_op jit(solution)/shard_map/value_part/pallas_call | solution.py:74
  113.5 2.2 %collective-permute-start.28 = (f32[1024,128]{1,0:T(8,128)S(1)}, f32[1024,128]{1,0:T(8,128)S(1)}, u32[]{:S(2)}, u32[]{:S(2)}) collective-permute-start(f32[1024,128]{1,0:T(8,128)S(1)} %state.3.state_ref), channel_id=1, source_target_pairs={{0,4},{4,0},{1,5},{5,1},{2,6},{6,2},{3,7},{7,3},{8,12},{12,8},{9,1... | collective-permute-start | bytes 1572872 | tf_op jit(solution)/shard_map/ppermute | solution.py:718
  115.8 1.9 %key_part.1.key_ref = f32[384,2048]{1,0:T(8,128)S(1)} custom-call(bf16[384,2048]{1,0:T(8,128)(2,1)S(1)} %get-tuple-element.111.query_ref, bf16[128,6144]{1,0:T(8,128)(2,1)S(1)} %get-tuple-element.115.top_ref, bf16[256,4096]{1,0:T(8,128)(2,1)S(1)} %get-tuple-element.116.bottom_ref), custom_call_target="tpu_custom_call" | custom-call | flops 1207959552 | tf_op jit(solution)/shard_map/key_part/pallas_call | solution.py:74
  117.9 3.5 %outer.1 = (bf16[384,2048]{1,0:T(8,128)(2,1)}, bf16[384,2048]{1,0:T(8,128)(2,1)}) custom-call(f32[384,2048]{1,0:T(8,128)S(1)} %key_part.1.key_ref, f32[384,2048]{1,0:T(8,128)S(1)} %get-tuple-element.117.val_ref, bf16[384,2048]{1,0:T(8,128)(2,1)S(1)} %get-tuple-element.91.keys_ref, bf16[384,2048]{1,0:T(8,128)(2,1)S(1)} %get-tuple-element.84.value_ref, ...), custom_call_target="tpu_custom_call" | custom-call | flops 805306368 | bytes 15728640 | tf_op jit(solution)/shard_map/outer/pallas_call | solution.py:74
  (60 shorter events, 19.9 us)
Async XLA Ops:
  0.6 11.9 %collective-permute-start = (bf16[128,2048]{1,0:T(8,128)(2,1)}, bf16[128,2048]{1,0:T(8,128)(2,1)S(1)}, u32[]{:S(2)}, u32[]{:S(2)}) collective-permute-start(bf16[128,2048]{1,0:T(8,128)(2,1)} %refs_0_.1), channel_id=1, source_target_pairs={{0,8},{4,20},{8,0},{12,28},{16,24},{20,4},{24,16},{28,12},{1,9},{5... | collective-permute-start | bytes 1572872 | tf_op jit(solution)/shard_map/ppermute | solution.py:808
  2.8 13.5 %collective-permute-start.1 = (bf16[128,2048]{1,0:T(8,128)(2,1)}, bf16[128,2048]{1,0:T(8,128)(2,1)S(1)}, u32[]{:S(2)}, u32[]{:S(2)}) collective-permute-start(bf16[128,2048]{1,0:T(8,128)(2,1)} %refs_0_.1), channel_id=1, source_target_pairs={{0,16},{4,12},{8,24},{12,4},{16,0},{20,28},{24,8},{28,20},{1,17},{... | collective-permute-start | bytes 1572872 | tf_op jit(solution)/shard_map/ppermute | solution.py:808
  4.0 12.4 %collective-permute-start.2 = (bf16[128,2048]{1,0:T(8,128)(2,1)}, bf16[128,2048]{1,0:T(8,128)(2,1)S(1)}, u32[]{:S(2)}, u32[]{:S(2)}) collective-permute-start(bf16[128,2048]{1,0:T(8,128)(2,1)} %refs_0_.1), channel_id=1, source_target_pairs={{0,1},{1,0},{2,3},{3,2},{4,5},{5,4},{6,7},{7,6},{8,9},{9,8},{10,11... | collective-permute-start | bytes 1572872 | tf_op jit(solution)/shard_map/ppermute | solution.py:805
  5.3 11.1 %collective-permute-start.3 = (bf16[128,2048]{1,0:T(8,128)(2,1)}, bf16[128,2048]{1,0:T(8,128)(2,1)S(1)}, u32[]{:S(2)}, u32[]{:S(2)}) collective-permute-start(bf16[128,2048]{1,0:T(8,128)(2,1)} %refs_0_.1), channel_id=1, source_target_pairs={{1,2},{2,1},{5,6},{6,5},{9,10},{10,9},{13,14},{14,13},{17,18},{18,... | collective-permute-start | bytes 1572872 | tf_op jit(solution)/shard_map/ppermute | solution.py:805
  16.4 4.6 %collective-permute-start.9 = (bf16[2048,128]{1,0:T(8,128)(2,1)S(1)}, bf16[2048,128]{1,0:T(8,128)(2,1)S(1)}, u32[]{:S(2)}, u32[]{:S(2)}) collective-permute-start(bf16[2048,128]{1,0:T(8,128)(2,1)S(1)} %get-tuple-element.73), channel_id=1, source_target_pairs={{0,4},{4,0},{1,5},{5,1},{2,6},{6,2},{3,7},{7,3},{8,12},{12,8},{9,1... | collective-permute-start | bytes 1572872 | tf_op jit(solution)/shard_map/ppermute | solution.py:682
  18.5 12.9 %collective-permute-start.5 = (bf16[128,2048]{1,0:T(8,128)(2,1)S(1)}, bf16[128,2048]{1,0:T(8,128)(2,1)S(1)}, u32[]{:S(2)}, u32[]{:S(2)}) collective-permute-start(bf16[128,2048]{1,0:T(8,128)(2,1)S(1)} %get-tuple-element.70.refs_4_), channel_id=1, source_target_pairs={{0,8},{4,20},{8,0},{12,28},{16,24},{20,4},{24,16},{28,12},{1,9},{5... | collective-permute-start | bytes 1572872 | tf_op jit(solution)/shard_map/ppermute | solution.py:808
  18.8 14.9 %collective-permute-start.6 = (bf16[128,2048]{1,0:T(8,128)(2,1)S(1)}, bf16[128,2048]{1,0:T(8,128)(2,1)S(1)}, u32[]{:S(2)}, u32[]{:S(2)}) collective-permute-start(bf16[128,2048]{1,0:T(8,128)(2,1)S(1)} %get-tuple-element.70.refs_4_), channel_id=1, source_target_pairs={{0,16},{4,12},{8,24},{12,4},{16,0},{20,28},{24,8},{28,20},{1,17},{... | collective-permute-start | bytes 1572872 | tf_op jit(solution)/shard_map/ppermute | solution.py:808
  18.9 14.8 %collective-permute-start.7 = (bf16[128,2048]{1,0:T(8,128)(2,1)S(1)}, bf16[128,2048]{1,0:T(8,128)(2,1)S(1)}, u32[]{:S(2)}, u32[]{:S(2)}) collective-permute-start(bf16[128,2048]{1,0:T(8,128)(2,1)S(1)} %get-tuple-element.70.refs_4_), channel_id=1, source_target_pairs={{1,2},{2,1},{5,6},{6,5},{9,10},{10,9},{13,14},{14,13},{17,18},{18,... | collective-permute-start | bytes 1572872 | tf_op jit(solution)/shard_map/ppermute | solution.py:805
  19.6 18.8 %collective-permute-start.4 = (bf16[128,2048]{1,0:T(8,128)(2,1)S(1)}, bf16[128,2048]{1,0:T(8,128)(2,1)S(1)}, u32[]{:S(2)}, u32[]{:S(2)}) collective-permute-start(bf16[128,2048]{1,0:T(8,128)(2,1)S(1)} %get-tuple-element.69.refs_1_), channel_id=1, source_target_pairs={{0,16},{4,12},{8,24},{12,4},{16,0},{20,28},{24,8},{28,20},{1,17},{... | collective-permute-start | bytes 1572872 | tf_op jit(solution)/shard_map/ppermute | solution.py:811
  21.0 19.4 %collective-permute-start.8 = (bf16[128,2048]{1,0:T(8,128)(2,1)S(1)}, bf16[128,2048]{1,0:T(8,128)(2,1)S(1)}, u32[]{:S(2)}, u32[]{:S(2)}) collective-permute-start(bf16[128,2048]{1,0:T(8,128)(2,1)S(1)} %get-tuple-element.71.inner_ref), channel_id=1, source_target_pairs={{1,0},{2,3},{5,4},{6,7},{9,8},{10,11},{13,12},{14,15},{17,16},{18,... | collective-permute-start | bytes 1572872 | tf_op jit(solution)/shard_map/ppermute | solution.py:805
  22.3 18.1 %copy-start = (bf16[128,2048]{1,0:T(8,128)(2,1)S(1)}, bf16[128,2048]{1,0:T(8,128)(2,1)}, u32[]{:S(2)}) copy-start(bf16[128,2048]{1,0:T(8,128)(2,1)} %refs_0_.1) | copy-start | bytes 1572868
  31.4 8.9 %collective-permute-start.10 = (bf16[1024,128]{1,0:T(8,128)(2,1)S(1)}, bf16[1024,128]{1,0:T(8,128)(2,1)S(1)}, u32[]{:S(2)}, u32[]{:S(2)}) collective-permute-start(bf16[1024,128]{1,0:T(8,128)(2,1)S(1)} %get-tuple-element.74), channel_id=1, source_target_pairs={{0,8},{4,20},{8,0},{12,28},{16,24},{24,16},{1,9},{5,21},{9,1},{13,... | collective-permute-start | bytes 786440 | tf_op jit(solution)/shard_map/ppermute | solution.py:692
  40.7 9.8 %collective-permute-start.15 = (bf16[896,2048]{1,0:T(8,128)(2,1)S(1)}, bf16[896,2048]{1,0:T(8,128)(2,1)S(1)}, u32[]{:S(2)}, u32[]{:S(2)}) collective-permute-start(bf16[896,2048]{1,0:T(8,128)(2,1)S(1)} %pack.3.refs_0_), channel_id=1, source_target_pairs={{0,4},{4,0},{1,5},{5,1},{2,6},{6,2},{3,7},{7,3},{8,12},{12,8},{9,1... | collective-permute-start | bytes 11010056 | tf_op jit(solution)/shard_map/ppermute | solution.py:761
  42.5 17.3 %collective-permute-start.12 = (bf16[128,2048]{1,0:T(8,128)(2,1)S(1)}, bf16[128,2048]{1,0:T(8,128)(2,1)S(1)}, u32[]{:S(2)}, u32[]{:S(2)}) collective-permute-start(bf16[128,2048]{1,0:T(8,128)(2,1)S(1)} %choose.2.refs_0_), channel_id=1, source_target_pairs={{0,8},{4,20},{8,0},{12,28},{16,24},{20,4},{24,16},{28,12},{1,9},{5... | collective-permute-start | bytes 1572872 | tf_op jit(solution)/shard_map/ppermute | solution.py:808
  43.8 16.0 %collective-permute-start.13 = (bf16[128,2048]{1,0:T(8,128)(2,1)S(1)}, bf16[128,2048]{1,0:T(8,128)(2,1)S(1)}, u32[]{:S(2)}, u32[]{:S(2)}) collective-permute-start(bf16[128,2048]{1,0:T(8,128)(2,1)S(1)} %choose.2.refs_0_), channel_id=1, source_target_pairs={{0,16},{4,12},{8,24},{12,4},{16,0},{20,28},{24,8},{28,20},{1,17},{... | collective-permute-start | bytes 1572872 | tf_op jit(solution)/shard_map/ppermute | solution.py:808
  44.1 16.0 %collective-permute-start.11 = (bf16[128,2048]{1,0:T(8,128)(2,1)S(1)}, bf16[128,2048]{1,0:T(8,128)(2,1)S(1)}, u32[]{:S(2)}, u32[]{:S(2)}) collective-permute-start(bf16[128,2048]{1,0:T(8,128)(2,1)S(1)} %get-tuple-element.75.inner_ref), channel_id=1, source_target_pairs={{1,0},{2,3},{5,4},{6,7},{9,8},{10,11},{13,12},{14,15},{17,16},{18,... | collective-permute-start | bytes 1572872 | tf_op jit(solution)/shard_map/ppermute | solution.py:805
  45.5 14.4 %collective-permute-start.14 = (bf16[1024,128]{1,0:T(8,128)(2,1)S(1)}, bf16[1024,128]{1,0:T(8,128)(2,1)S(1)}, u32[]{:S(2)}, u32[]{:S(2)}) collective-permute-start(bf16[1024,128]{1,0:T(8,128)(2,1)S(1)} %message.2), channel_id=1, source_target_pairs={{0,16},{4,12},{8,24},{12,4},{20,28},{28,20},{1,17},{5,13},{9,25},{... | collective-permute-start | bytes 786440 | tf_op jit(solution)/shard_map/ppermute | solution.py:705
  60.3 21.6 %collective-permute-start.20 = (bf16[512,2048]{1,0:T(8,128)(2,1)S(1)}, bf16[512,2048]{1,0:T(8,128)(2,1)S(1)}, u32[]{:S(2)}, u32[]{:S(2)}) collective-permute-start(bf16[512,2048]{1,0:T(8,128)(2,1)S(1)} %pack.4.refs_0_), channel_id=1, source_target_pairs={{0,4},{4,0},{1,5},{5,1},{2,6},{6,2},{3,7},{7,3},{8,12},{12,8},{9,1... | collective-permute-start | bytes 6291464 | tf_op jit(solution)/shard_map/ppermute | solution.py:761
  61.6 4.4 %collective-permute-start.21 = (f32[1024,128]{1,0:T(8,128)S(1)}, f32[1024,128]{1,0:T(8,128)S(1)}, u32[]{:S(2)}, u32[]{:S(2)}) collective-permute-start(f32[1024,128]{1,0:T(8,128)S(1)} %state.2.state_ref), channel_id=1, source_target_pairs={{0,4},{4,0},{1,5},{5,1},{2,6},{6,2},{3,7},{7,3},{8,12},{12,8},{9,1... | collective-permute-start | bytes 1572872 | tf_op jit(solution)/shard_map/ppermute | solution.py:718
  61.7 16.5 %collective-permute-start.17 = (bf16[128,2048]{1,0:T(8,128)(2,1)S(1)}, bf16[128,2048]{1,0:T(8,128)(2,1)S(1)}, u32[]{:S(2)}, u32[]{:S(2)}) collective-permute-start(bf16[128,2048]{1,0:T(8,128)(2,1)S(1)} %choose.3.refs_3_), channel_id=1, source_target_pairs={{0,8},{4,20},{8,0},{12,28},{16,24},{20,4},{24,16},{28,12},{1,9},{5... | collective-permute-start | bytes 1572872 | tf_op jit(solution)/shard_map/ppermute | solution.py:808
  62.8 15.4 %collective-permute-start.18 = (bf16[128,2048]{1,0:T(8,128)(2,1)S(1)}, bf16[128,2048]{1,0:T(8,128)(2,1)S(1)}, u32[]{:S(2)}, u32[]{:S(2)}) collective-permute-start(bf16[128,2048]{1,0:T(8,128)(2,1)S(1)} %choose.3.refs_3_), channel_id=1, source_target_pairs={{0,16},{4,12},{8,24},{12,4},{16,0},{20,28},{24,8},{28,20},{1,17},{... | collective-permute-start | bytes 1572872 | tf_op jit(solution)/shard_map/ppermute | solution.py:808
  64.0 17.9 %collective-permute-start.16 = (bf16[128,2048]{1,0:T(8,128)(2,1)S(1)}, bf16[128,2048]{1,0:T(8,128)(2,1)S(1)}, u32[]{:S(2)}, u32[]{:S(2)}) collective-permute-start(bf16[128,2048]{1,0:T(8,128)(2,1)S(1)} %get-tuple-element.87.refs_1_), channel_id=1, source_target_pairs={{0,16},{4,12},{8,24},{12,4},{16,0},{20,28},{24,8},{28,20},{1,17},{... | collective-permute-start | bytes 1572872 | tf_op jit(solution)/shard_map/ppermute | solution.py:811
  66.0 15.9 %collective-permute-start.19 = (bf16[128,2048]{1,0:T(8,128)(2,1)S(1)}, bf16[128,2048]{1,0:T(8,128)(2,1)S(1)}, u32[]{:S(2)}, u32[]{:S(2)}) collective-permute-start(bf16[128,2048]{1,0:T(8,128)(2,1)S(1)} %get-tuple-element.89), channel_id=1, source_target_pairs={{0,1},{1,0},{2,3},{3,2},{4,5},{5,4},{6,7},{7,6},{8,9},{9,8},{10,11... | collective-permute-start | bytes 1572872 | tf_op jit(solution)/shard_map/ppermute | solution.py:805
  82.3 5.6 %collective-permute-start.22 = (bf16[512,2048]{1,0:T(8,128)(2,1)S(1)}, bf16[512,2048]{1,0:T(8,128)(2,1)S(1)}, u32[]{:S(2)}, u32[]{:S(2)}) collective-permute-start(bf16[512,2048]{1,0:T(8,128)(2,1)S(1)} %pack.5.refs_0_), channel_id=1, source_target_pairs={{0,4},{4,0},{1,5},{5,1},{2,6},{6,2},{3,7},{7,3},{8,12},{12,8},{9,1... | collective-permute-start | bytes 6291464 | tf_op jit(solution)/shard_map/ppermute | solution.py:761
  82.4 8.4 %collective-permute-start.23 = (bf16[128,2048]{1,0:T(8,128)(2,1)S(1)}, bf16[128,2048]{1,0:T(8,128)(2,1)S(1)}, u32[]{:S(2)}, u32[]{:S(2)}) collective-permute-start(bf16[128,2048]{1,0:T(8,128)(2,1)S(1)} %get-tuple-element.99.refs_2_), channel_id=1, source_target_pairs={{0,16},{4,12},{8,24},{12,4},{16,0},{20,28},{24,8},{28,20},{1,17},{... | collective-permute-start | bytes 1572872 | tf_op jit(solution)/shard_map/ppermute | solution.py:811
  90.7 4.0 %collective-permute-start.24 = (bf16[128,2048]{1,0:T(8,128)(2,1)S(1)}, bf16[128,2048]{1,0:T(8,128)(2,1)S(1)}, u32[]{:S(2)}, u32[]{:S(2)}) collective-permute-start(bf16[128,2048]{1,0:T(8,128)(2,1)S(1)} %join.9.refs_0_), channel_id=1, source_target_pairs={{0,4},{4,0},{1,5},{5,1},{2,6},{6,2},{3,7},{7,3},{8,12},{12,8},{9,1... | collective-permute-start | bytes 1572872 | tf_op jit(solution)/shard_map/ppermute | solution.py:802
  96.5 2.0 %collective-permute-start.25 = (bf16[2048,128]{1,0:T(8,128)(2,1)S(1)}, bf16[2048,128]{1,0:T(8,128)(2,1)S(1)}, u32[]{:S(2)}, u32[]{:S(2)}) collective-permute-start(bf16[2048,128]{1,0:T(8,128)(2,1)S(1)} %get-tuple-element.120), channel_id=1, source_target_pairs={{0,4},{4,0},{1,5},{5,1},{2,6},{6,2},{3,7},{7,3},{8,12},{12,8},{9,1... | collective-permute-start | bytes 1572872 | tf_op jit(solution)/shard_map/ppermute | solution.py:682
  98.6 7.4 %collective-permute-start.26 = (bf16[1024,128]{1,0:T(8,128)(2,1)S(1)}, bf16[1024,128]{1,0:T(8,128)(2,1)S(1)}, u32[]{:S(2)}, u32[]{:S(2)}) collective-permute-start(bf16[1024,128]{1,0:T(8,128)(2,1)S(1)} %get-tuple-element.122), channel_id=1, source_target_pairs={{0,8},{8,0},{16,24},{20,4},{24,16},{28,12},{1,9},{9,1},{17,25},{21... | collective-permute-start | bytes 786440 | tf_op jit(solution)/shard_map/ppermute | solution.py:692
  106.0 7.4 %collective-permute-start.27 = (bf16[1024,128]{1,0:T(8,128)(2,1)S(1)}, bf16[1024,128]{1,0:T(8,128)(2,1)S(1)}, u32[]{:S(2)}, u32[]{:S(2)}) collective-permute-start(bf16[1024,128]{1,0:T(8,128)(2,1)S(1)} %message.3), channel_id=1, source_target_pairs={{4,12},{12,4},{16,0},{20,28},{24,8},{28,20},{5,13},{13,5},{17,1},{... | collective-permute-start | bytes 786440 | tf_op jit(solution)/shard_map/ppermute | solution.py:705
  113.5 4.1 %collective-permute-start.28 = (f32[1024,128]{1,0:T(8,128)S(1)}, f32[1024,128]{1,0:T(8,128)S(1)}, u32[]{:S(2)}, u32[]{:S(2)}) collective-permute-start(f32[1024,128]{1,0:T(8,128)S(1)} %state.3.state_ref), channel_id=1, source_target_pairs={{0,4},{4,0},{1,5},{5,1},{2,6},{6,2},{3,7},{7,3},{8,12},{12,8},{9,1... | collective-permute-start | bytes 1572872 | tf_op jit(solution)/shard_map/ppermute | solution.py:718

commit v12 on v11

--- a/solution.py
+++ b/solution.py
@@ -518,7 +518,8 @@
     )
 
 
-def key_kernel(query_ref, top_ref, bottom_ref, key_ref):
+def key_kernel(query_ref, top_ref, bottom_ref, key_ref, mark_ref):
+    set_mark(mark_ref)
     length, total = query_ref.shape
     rest = length - HEAD
     number = WIDE // HEAD
@@ -541,11 +542,11 @@
         key_kernel,
         "VVV",
         (queries, top, bottom),
-        "V",
-        [((length, total), f32)],
+        "VV",
+        [((length, total), f32), (MARK.shape, f32)],
         "key_part",
         (4 * length * total * length, 0),
-    )[0]
+    )
 
 
 def outer_kernel(
@@ -583,6 +584,62 @@
         "outer",
         (8 * length * total * HEAD, 20 * length * total),
         [pltpu.VMEM(block, bf16)] * 2 + [pltpu.SemaphoreType.DMA((total // WIDE,))] * 2,
+    )
+
+
+def half_kernel(
+    factor, mine, has_before,
+    state_ref, sibling_ref, key_ref, val_ref, keys_ref, value_ref, mask_ref, *refs,
+):
+    key_out, val_out, key_made, val_made, key_sems, val_sems = refs[2 if has_before else 0 :]
+    core = lax.axis_index("core")
+    half = state_ref.shape[0]
+    base = (core if mine else 1 - core) * half
+    adds = jnp.where(core == 0, 1.0, 0.0)
+
+    def out_copies(group, at):
+        there = columns(pl.multiple_of(base + at, WIDE))
+        return [
+            pltpu.make_async_copy(made.at[columns(at)], out.at[there], sems.at[group])
+            for made, out, sems in (
+                (key_made, key_out, key_sems), (val_made, val_out, val_sems)
+            )
+        ]
+
+    def work(group, at):
+        for here in heads(at):
+            part = pl.ds(pl.multiple_of(base + here.start, HEAD), HEAD)
+            whole = state_ref[here, :] + adds * sibling_ref[part, :].astype(f32)
+            high = whole.astype(bf16)
+            state = [high, (whole - high.astype(f32)).astype(bf16)]
+            keys, value = keys_ref[:, part], value_ref[:, part]
+            key_grad = key_ref[:, part] + nt(twice(value), jnp.concatenate(state, axis=1))
+            key_made[:, here] = (factor * key_grad * mask_ref[:, part].astype(f32)).astype(bf16)
+            value_grad = val_ref[:, part] + nn(twice(keys), jnp.concatenate(state, axis=0))
+            val_made[:, here] = (factor * value_grad).astype(bf16)
+        for copy in out_copies(group, at):
+            copy.start()
+
+    groups(half, work)
+    for group in range(half // WIDE):
+        for copy in out_copies(group, group * WIDE):
+            copy.wait()
+
+
+def half_call(factor, state, sibling, key_part, value_part, keys, values, k_mask, before=()):
+    length, total = values.shape
+    half = state.shape[0]
+    return kernel_call(
+        functools.partial(half_kernel, factor, not before, bool(before)),
+        "VVVVVVV" + "H" * len(before),
+        (state, sibling, key_part, value_part, keys, values, k_mask, *before),
+        "HH",
+        [((length, total), bf16)] * 2,
+        "outer",
+        (4 * length * total * HEAD, 10 * length * total),
+        [pltpu.VMEM((length, half), bf16)] * 2
+        + [pltpu.SemaphoreType.DMA((half // WIDE,))] * 2,
+        {7 + at: at for at in range(len(before))},
     )
 
 
@@ -705,7 +762,7 @@
     return lax.ppermute(message, CTX, links(2, upward(reverse)))
 
 
-def add_up(got, more, sibling, reverse, others=()):
+def add_halves(got, more, reverse, others=()):
     (state,) = kernel_call(
         functools.partial(state_kernel, reverse),
         "VV" + "A" * len(others),
@@ -715,7 +772,11 @@
         "state",
         (0, 0),
     )
-    other = lax.ppermute(state, "core", SWAP)
+    return state, lax.ppermute(state, "core", SWAP)
+
+
+def add_up(got, more, sibling, reverse):
+    state, other = add_halves(got, more, reverse)
     return kernel_call(
         functools.partial(whole_kernel, reverse),
         "VVV",
@@ -876,19 +937,22 @@
     queries, own, sent = query_call(start, tokens, late, partial, q_mask, cotangent, [mark])
     attended, attended_mark = attend_call(factor, queries, keys, values, high, low)
     value_part, value_mark = value_call(queries, keys, cotangent)
-    key_part = key_call(queries, top, bottom)
+    key_part, key_mark = key_call(queries, top, bottom)
     _, grad_tokens, back_mark = products_call(
         special, start, late, tokens, masked=masked, grad=grad, project=False
     )
     if special:
         twin, both, got = send_first(own, sent, True, [back_mark])
         more = send_second(got, both, True, [attended_mark])
-        adjoint = add_up(got, more, twin, True, [value_mark])
+        state, other = add_halves(got, more, True, [value_mark, key_mark])
+        rest = (twin, key_part, value_part, keys, values, k_mask)
+        made = half_call(factor, state, *rest)
+        grad_keys, grad_values = half_call(factor, other, *rest, made)
     else:
         adjoint = halves(scan_any(own, sent, chips * 2, True))
-    grad_keys, grad_values = outer_call(
-        factor, key_part, value_part, keys, values, k_mask, *adjoint
-    )
+        grad_keys, grad_values = outer_call(
+            factor, key_part, value_part, keys, values, k_mask, *adjoint
+        )
     return tuple(
         array.reshape(1, length, array.shape[1])
         for array in (attended, grad_tokens, grad_keys, grad_values)

time: 122 us -> 121 us (level)
  starting transfers between devices: 37 us -> 35.3 us
    ppermute x2, starting transfers between devices: 2.29 us -> 0.55 us  [add_halves(): return (state, lax.ppermute(state, 'core', SWAP))]
  transfers between devices with their start and end apart: 29 -> 29, of which waited for: 14 -> 13; matrix products, arithmetic and copies ran while one was open for 0% -> 0% of each run, Pallas kernels for 33% -> 36%
where the time goes in v12:
time: 121 us; the launch traced here: 120 us
  Pallas kernels  48.2 us (40%)
  waiting for transfers between devices  35.8 us (30%)
  starting transfers between devices  35.3 us (29%)
    pallas_call x32, Pallas kernels, kernel_call(): made(*[holds[place](one) if place in holds else one for place, one in zip...  48.2 us
    ppermute x4, waiting for transfers between devices, cross(): lax.ppermute(array, CTX, links(1))  10.8 us
    ppermute x3, waiting for transfers between devices, onward(): return lax.ppermute(array, CTX, links(2))  9.1 us
    ppermute x6, starting transfers between devices, along(): return lax.ppermute(array, 'dp', pairs)  7.73 us
    ppermute x2, waiting for transfers between devices, send_second(): return lax.ppermute(message, CTX, links(2, upward(reverse)))  6.39 us
    ppermute x2, starting transfers between devices, send_second(): return lax.ppermute(message, CTX, links(2, upward(reverse)))  6.24 us
    ppermute x4, starting transfers between devices, cross(): lax.ppermute(array, CTX, links(1))  4.79 us
    ppermute x4, waiting for transfers between devices, cross(): lax.ppermute(array, CTX, links(2))  3.75 us
  transfers between devices with their start and end apart: 29, of which 13 were waited for; matrix products, arithmetic and copies ran while one was open for 0% of the time, Pallas kernels for 36%

profile of v12, /device:TPU:1, one launch (start us, length us, event | category | flops | bytes accessed | tf_op | source)
XLA Modules:
  0.0 120.4 jit_solution(8570427452894463479)
XLA Ops:
  0.6 2.1 %collective-permute-start = (bf16[128,2048]{1,0:T(8,128)(2,1)}, bf16[128,2048]{1,0:T(8,128)(2,1)S(1)}, u32[]{:S(2)}, u32[]{:S(2)}) collective-permute-start(bf16[128,2048]{1,0:T(8,128)(2,1)} %refs_0_.1), channel_id=1, source_target_pairs={{0,8},{4,20},{8,0},{12,28},{16,24},{20,4},{24,16},{28,12},{1,9},{5... | collective-permute-start | bytes 1572872 | tf_op jit(solution)/shard_map/ppermute | solution.py:869
  6.0 4.8 %own_memory.1 = (bf16[384,2048]{1,0:T(8,128)(2,1)S(1)}, bf16[384,2048]{1,0:T(8,128)(2,1)S(1)}, bf16[384,2048]{1,0:T(8,128)(2,1)S(1)}, f32[2048,128]{1,0:T(8,128)...) custom-call(bf16[384,2048]{1,0:T(8,128)(2,1)} %bitcast.15, ...), custom_call_target="tpu_custom_call" | custom-call | flops 201326592 | bytes 9437184 | tf_op jit(solution)/shard_map/own_memory/pallas_call | solution.py:74
  10.7 1.8 %collective-permute-done.refs_0_ = bf16[128,2048]{1,0:T(8,128)(2,1)S(1)} collective-permute-done((bf16[128,2048]{1,0:T(8,128)(2,1)}, bf16[128,2048]{1,0:T(8,128)(2,1)S(1)}, u32[]{:S(2)}, u32[]{:S(2)}) %collective-permute-start) | collective-permute-done | bytes 524320 | tf_op jit(solution)/shard_map/ppermute | solution.py:869
  12.6 3.7 %collective-permute-done.1.refs_1_ = bf16[128,2048]{1,0:T(8,128)(2,1)S(1)} collective-permute-done((bf16[128,2048]{1,0:T(8,128)(2,1)}, bf16[128,2048]{1,0:T(8,128)(2,1)S(1)}, u32[]{:S(2)}, u32[]{:S(2)}) %collective-permute-start.1) | collective-permute-done | bytes 524320 | tf_op jit(solution)/shard_map/ppermute | solution.py:869
  16.4 2.2 %collective-permute-start.9 = (bf16[2048,128]{1,0:T(8,128)(2,1)S(1)}, bf16[2048,128]{1,0:T(8,128)(2,1)S(1)}, u32[]{:S(2)}, u32[]{:S(2)}) collective-permute-start(bf16[2048,128]{1,0:T(8,128)(2,1)S(1)} %get-tuple-element.75), channel_id=1, source_target_pairs={{0,4},{4,0},{1,5},{5,1},{2,6},{6,2},{3,7},{7,3},{8,12},{12,8},{9,1... | collective-permute-start | bytes 1572872 | tf_op jit(solution)/shard_map/ppermute | solution.py:739
  19.6 1.4 %collective-permute-start.4 = (bf16[128,2048]{1,0:T(8,128)(2,1)S(1)}, bf16[128,2048]{1,0:T(8,128)(2,1)S(1)}, u32[]{:S(2)}, u32[]{:S(2)}) collective-permute-start(bf16[128,2048]{1,0:T(8,128)(2,1)S(1)} %get-tuple-element.71.refs_1_), channel_id=1, source_target_pairs={{0,16},{4,12},{8,24},{12,4},{16,0},{20,28},{24,8},{28,20},{1,17},{... | collective-permute-start | bytes 1572872 | tf_op jit(solution)/shard_map/ppermute | solution.py:872
  22.4 9.0 %collective-permute-done.5.refs_1_ = bf16[128,2048]{1,0:T(8,128)(2,1)S(1)} collective-permute-done((bf16[128,2048]{1,0:T(8,128)(2,1)S(1)}, bf16[128,2048]{1,0:T(8,128)(2,1)S(1)}, u32[]{:S(2)}, u32[]{:S(2)}) %collective-permute-start.5) | collective-permute-done | bytes 524320 | tf_op jit(solution)/shard_map/ppermute | solution.py:869
  31.4 2.3 %collective-permute-start.10 = (bf16[1024,128]{1,0:T(8,128)(2,1)S(1)}, bf16[1024,128]{1,0:T(8,128)(2,1)S(1)}, u32[]{:S(2)}, u32[]{:S(2)}) collective-permute-start(bf16[1024,128]{1,0:T(8,128)(2,1)S(1)} %get-tuple-element.76), channel_id=1, source_target_pairs={{0,8},{4,20},{8,0},{12,28},{16,24},{24,16},{1,9},{5,21},{9,1},{13,... | collective-permute-start | bytes 786440 | tf_op jit(solution)/shard_map/ppermute | solution.py:749
  33.7 4.6 %collective-permute-done.4.refs_0_ = bf16[128,2048]{1,0:T(8,128)(2,1)S(1)} collective-permute-done((bf16[128,2048]{1,0:T(8,128)(2,1)S(1)}, bf16[128,2048]{1,0:T(8,128)(2,1)S(1)}, u32[]{:S(2)}, u32[]{:S(2)}) %collective-permute-start.4) | collective-permute-done | bytes 524320 | tf_op jit(solution)/shard_map/ppermute | solution.py:872
  38.3 2.0 %collective-permute-done.8.refs_4_ = bf16[128,2048]{1,0:T(8,128)(2,1)S(1)} collective-permute-done((bf16[128,2048]{1,0:T(8,128)(2,1)S(1)}, bf16[128,2048]{1,0:T(8,128)(2,1)S(1)}, u32[]{:S(2)}, u32[]{:S(2)}) %collective-permute-start.8) | collective-permute-done | bytes 524320 | tf_op jit(solution)/shard_map/ppermute | solution.py:866
  40.7 1.8 %collective-permute-start.15 = (bf16[896,2048]{1,0:T(8,128)(2,1)S(1)}, bf16[896,2048]{1,0:T(8,128)(2,1)S(1)}, u32[]{:S(2)}, u32[]{:S(2)}) collective-permute-start(bf16[896,2048]{1,0:T(8,128)(2,1)S(1)} %pack.3.refs_0_), channel_id=1, source_target_pairs={{0,4},{4,0},{1,5},{5,1},{2,6},{6,2},{3,7},{7,3},{8,12},{12,8},{9,1... | collective-permute-start | bytes 11010056 | tf_op jit(solution)/shard_map/ppermute | solution.py:822
  42.5 1.3 %collective-permute-start.12 = (bf16[128,2048]{1,0:T(8,128)(2,1)S(1)}, bf16[128,2048]{1,0:T(8,128)(2,1)S(1)}, u32[]{:S(2)}, u32[]{:S(2)}) collective-permute-start(bf16[128,2048]{1,0:T(8,128)(2,1)S(1)} %choose.2.refs_0_), channel_id=1, source_target_pairs={{0,8},{4,20},{8,0},{12,28},{16,24},{20,4},{24,16},{28,12},{1,9},{5... | collective-permute-start | bytes 1572872 | tf_op jit(solution)/shard_map/ppermute | solution.py:869
  45.5 3.1 %collective-permute-start.14 = (bf16[1024,128]{1,0:T(8,128)(2,1)S(1)}, bf16[1024,128]{1,0:T(8,128)(2,1)S(1)}, u32[]{:S(2)}, u32[]{:S(2)}) collective-permute-start(bf16[1024,128]{1,0:T(8,128)(2,1)S(1)} %message.2), channel_id=1, source_target_pairs={{0,16},{4,12},{8,24},{12,4},{20,28},{28,20},{1,17},{5,13},{9,25},{... | collective-permute-start | bytes 786440 | tf_op jit(solution)/shard_map/ppermute | solution.py:762
  48.6 1.8 %turned.1 = (bf16[128,6144]{1,0:T(8,128)(2,1)S(1)}, bf16[256,4096]{1,0:T(8,128)(2,1)S(1)}, f32[8,128]{1,0:T(8,128)S(1)}) custom-call(bf16[384,2048]{1,0:T(8,128)(2,1)S(1)} %get-tuple-element.86.value_ref, bf16[384,2048]{1,0:T(8,128)(2,1)S(1)} %get-tuple-element.87.grad_ref, bf16[1024,128]{1,0:T(8,128)(2,1)S(1)} %get-tuple-element.79.got_ref.after_ref), custom_call_target="tpu_custom_call" | custom-call | flops 1207959552 | tf_op jit(solution)/shard_map/turned/pallas_call | solution.py:74
  50.5 3.0 %project.2 = (f32[384,2048]{1,0:T(8,128)S(1)}, f32[8,128]{1,0:T(8,128)S(1)}) custom-call(bf16[896,2048]{1,0:T(8,128)(2,1)S(1)} %pack.3.refs_0_, bf16[896,2048]{1,0:T(8,128)(2,1)S(1)} %collective-permute-done.15.refs_1_, bf16[384,4096]{1,0:T(8,128)(2,1)S(1)} %get-tuple-element.69.refs_2_.tokens_ref), custom_call_target="tpu_custom_call" | custom-call | flops 2818572288 | tf_op jit(solution)/shard_map/project/pallas_call | solution.py:74
  53.5 6.4 %collective-permute-done.14.refs_3_ = bf16[1024,128]{1,0:T(8,128)(2,1)S(1)} collective-permute-done((bf16[1024,128]{1,0:T(8,128)(2,1)S(1)}, bf16[1024,128]{1,0:T(8,128)(2,1)S(1)}, u32[]{:S(2)}, u32[]{:S(2)}) %collective-permute-start.14) | collective-permute-done | bytes 262176 | tf_op jit(solution)/shard_map/ppermute | solution.py:762
  64.3 1.8 %collective-permute-done.21.other_ref = f32[1024,128]{1,0:T(8,128)S(1)} collective-permute-done((f32[1024,128]{1,0:T(8,128)S(1)}, f32[1024,128]{1,0:T(8,128)S(1)}, u32[]{:S(2)}, u32[]{:S(2)}) %collective-permute-start.21) | collective-permute-done | bytes 524320 | tf_op jit(solution)/shard_map/ppermute | solution.py:775
  66.0 2.5 %collective-permute-start.19 = (bf16[128,2048]{1,0:T(8,128)(2,1)S(1)}, bf16[128,2048]{1,0:T(8,128)(2,1)S(1)}, u32[]{:S(2)}, u32[]{:S(2)}) collective-permute-start(bf16[128,2048]{1,0:T(8,128)(2,1)S(1)} %get-tuple-element.91), channel_id=1, source_target_pairs={{0,1},{1,0},{2,3},{3,2},{4,5},{5,4},{6,7},{7,6},{8,9},{9,8},{10,11... | collective-permute-start | bytes 1572872 | tf_op jit(solution)/shard_map/ppermute | solution.py:866
  68.8 5.4 %masked_grad.1 = (bf16[384,2048]{1,0:T(8,128)(2,1)S(1)}, bf16[384,2048]{1,0:T(8,128)(2,1)S(1)}) custom-call(s32[384,2048]{1,0:T(8,128)} %bitcast.18, bf16[384,2048]{1,0:T(8,128)(2,1)S(1)} %get-tuple-element.87.grad_ref, bf16[384,2048]{1,0:T(8,128)(2,1)S(1)} %get-tuple-element.86.value_ref, bf16[384,2048]{1,0:T(8,128)(2,1)S(1)} %get-tuple-element.93.keys_ref, ...), custom_call_target="tpu_custom_call" | custom-call | flops 2415919104 | bytes 9437184 | tf_op jit(solution)/shard_map/masked_grad/pallas_call | solution.py:74
  74.2 3.9 %grad_tokens.3 = (bf16[384,4096]{1,0:T(8,128)(2,1)}, f32[8,128]{1,0:T(8,128)S(1)}) custom-call(bf16[896,2048]{1,0:T(8,128)(2,1)S(1)} %pack.3.refs_0_, bf16[896,2048]{1,0:T(8,128)(2,1)S(1)} %collective-permute-done.15.refs_1_, bf16[384,2048]{1,0:T(8,128)(2,1)S(1)} %get-tuple-element.97.refs_2_.refs_4_), custom_call_target="tpu_custom_call" | custom-call | flops 2818572288 | tf_op jit(solution)/shard_map/grad_tokens/pallas_call | solution.py:74
  78.2 3.7 %collective-permute-done.16.refs_0_ = bf16[128,2048]{1,0:T(8,128)(2,1)S(1)} collective-permute-done((bf16[128,2048]{1,0:T(8,128)(2,1)S(1)}, bf16[128,2048]{1,0:T(8,128)(2,1)S(1)}, u32[]{:S(2)}, u32[]{:S(2)}) %collective-permute-start.16) | collective-permute-done | bytes 524320 | tf_op jit(solution)/shard_map/ppermute | solution.py:872
  83.6 4.3 %products.1 = (f32[384,2048]{1,0:T(8,128)S(1)}, bf16[384,4096]{1,0:T(8,128)(2,1)}, f32[8,128]{1,0:T(8,128)S(1)}) custom-call(bf16[512,2048]{1,0:T(8,128)(2,1)S(1)} %pack.4.refs_0_, bf16[512,2048]{1,0:T(8,128)(2,1)S(1)} %get-tuple-element.103.refs_1_, ...), custom_call_target="tpu_custom_call", output_to_operand_aliasing={{0}: (3, {}), {1}: (5, {})} | custom-call | flops 3221225472 | tf_op jit(solution)/shard_map/products/pallas_call | solution.py:74
  87.9 2.1 %project.3 = (f32[384,2048]{1,0:T(8,128)S(1)}, f32[8,128]{1,0:T(8,128)S(1)}) custom-call(bf16[512,2048]{1,0:T(8,128)(2,1)S(1)} %pack.5.refs_0_, bf16[512,2048]{1,0:T(8,128)(2,1)S(1)} %collective-permute-done.22.refs_1_, bf16[384,4096]{1,0:T(8,128)(2,1)S(1)} %get-tuple-element.69.refs_2_.tokens_ref, ...), custom_call_target="tpu_custom_call", output_to_operand_aliasing={{0}: (3, {})} | custom-call | flops 1610612736 | tf_op jit(solution)/shard_map/project/pallas_call | solution.py:74
  92.0 2.7 %grad_tokens.4 = (bf16[384,4096]{1,0:T(8,128)(2,1)}, f32[8,128]{1,0:T(8,128)S(1)}) custom-call(bf16[512,2048]{1,0:T(8,128)(2,1)S(1)} %pack.5.refs_0_, bf16[512,2048]{1,0:T(8,128)(2,1)S(1)} %collective-permute-done.22.refs_1_, bf16[384,2048]{1,0:T(8,128)(2,1)S(1)} %get-tuple-element.97.refs_2_.refs_4_, ...), custom_call_target="tpu_custom_call", output_to_operand_aliasing={{0}: (3, {})} | custom-call | flops 1610612736 | tf_op jit(solution)/shard_map/grad_tokens/pallas_call | solution.py:74
  94.7 1.8 %queries.1 = (bf16[384,2048]{1,0:T(8,128)(2,1)S(1)}, f32[2048,128]{1,0:T(8,128)S(1)}, bf16[2048,128]{1,0:T(8,128)(2,1)S(1)}) custom-call(bf16[384,4096]{1,0:T(8,128)(2,1)S(1)} %get-tuple-element.69.refs_2_.tokens_ref, f32[384,2048]{1,0:T(8,128)S(1)} %get-tuple-element.107.sum_ref, bf16[384,2048]{1,0:T(8,128)(2,1)S(1)} %get-tuple-element.108.mask_ref, ...), custom_call_target="tpu_custom_call" | custom-call | flops 402653184 | tf_op jit(solution)/shard_map/queries/pallas_call | solution.py:74
  96.6 1.3 %grad_tokens.5 = (bf16[384,4096]{1,0:T(8,128)(2,1)}, f32[8,128]{1,0:T(8,128)S(1)}) custom-call(bf16[128,2048]{1,0:T(8,128)(2,1)S(1)} %join.9.refs_0_, bf16[128,2048]{1,0:T(8,128)(2,1)S(1)} %collective-permute-done.24.refs_1_, bf16[384,2048]{1,0:T(8,128)(2,1)S(1)} %get-tuple-element.97.refs_2_.refs_4_, ...), custom_call_target="tpu_custom_call", output_to_operand_aliasing={{0}: (3, {})} | custom-call | flops 402653184 | tf_op jit(solution)/shard_map/grad_tokens/pallas_call | solution.py:74
  99.9 5.1 %attended.1 = (bf16[384,2048]{1,0:T(8,128)(2,1)}, f32[8,128]{1,0:T(8,128)S(1)}) custom-call(bf16[384,2048]{1,0:T(8,128)(2,1)S(1)} %get-tuple-element.113.query_ref, bf16[384,2048]{1,0:T(8,128)(2,1)S(1)} %get-tuple-element.93.keys_ref, bf16[384,2048]{1,0:T(8,128)(2,1)S(1)} %get-tuple-element.86.value_ref, bf16[2048,128]{1,0:T(8,128)(2,1)S(1)} %get-tuple-element.95.high_ref, ...), custom_call_target="tpu_custom_call" | custom-call | flops 2415919104 | bytes 6291456 | tf_op jit(solution)/shard_map/attended/pallas_call | solution.py:74
  106.0 3.1 %collective-permute-start.27 = (bf16[1024,128]{1,0:T(8,128)(2,1)S(1)}, bf16[1024,128]{1,0:T(8,128)(2,1)S(1)}, u32[]{:S(2)}, u32[]{:S(2)}) collective-permute-start(bf16[1024,128]{1,0:T(8,128)(2,1)S(1)} %message.3), channel_id=1, source_target_pairs={{4,12},{12,4},{16,0},{20,28},{24,8},{28,20},{5,13},{13,5},{17,1},{... | collective-permute-start | bytes 786440 | tf_op jit(solution)/shard_map/ppermute | solution.py:762
  109.2 2.1 %key_part.1 = (f32[384,2048]{1,0:T(8,128)S(1)}, f32[8,128]{1,0:T(8,128)S(1)}) custom-call(bf16[384,2048]{1,0:T(8,128)(2,1)S(1)} %get-tuple-element.113.query_ref, bf16[128,6144]{1,0:T(8,128)(2,1)S(1)} %get-tuple-element.124.top_ref, bf16[256,4096]{1,0:T(8,128)(2,1)S(1)} %get-tuple-element.125.bottom_ref), custom_call_target="tpu_custom_call" | custom-call | flops 1207959552 | tf_op jit(solution)/shard_map/key_part/pallas_call | solution.py:74
  111.3 3.9 %value_part.1 = (f32[384,2048]{1,0:T(8,128)S(1)}, f32[8,128]{1,0:T(8,128)S(1)}) custom-call(bf16[384,2048]{1,0:T(8,128)(2,1)S(1)} %get-tuple-element.113.query_ref, bf16[384,2048]{1,0:T(8,128)(2,1)S(1)} %get-tuple-element.93.keys_ref, bf16[384,2048]{1,0:T(8,128)(2,1)S(1)} %get-tuple-element.87.grad_ref), custom_call_target="tpu_custom_call" | custom-call | flops 1811939328 | tf_op jit(solution)/shard_map/value_part/pallas_call | solution.py:74
  115.7 2.2 %outer.2 = (bf16[384,2048]{1,0:T(8,128)(2,1)}, bf16[384,2048]{1,0:T(8,128)(2,1)}) custom-call(f32[1024,128]{1,0:T(8,128)S(1)} %state.3.state_ref, bf16[2048,128]{1,0:T(8,128)(2,1)S(1)} %collective-permute-done.25.sibling_ref, f32[384,2048]{1,0:T(8,128)S(1)} %get-tuple-element.127.key_ref, f32[384,2048]{1,0:T(8,128)S(1)} %get-tuple-element.128.val_ref, ...), custom_call_target="tpu_custom_call" | custom-call | flops 402653184 | bytes 7864320 | tf_op jit(solution)/shard_map/outer/pallas_call | solution.py:74
  118.0 2.2 %outer.3 = (bf16[384,2048]{1,0:T(8,128)(2,1)}, bf16[384,2048]{1,0:T(8,128)(2,1)}) custom-call(f32[1024,128]{1,0:T(8,128)S(1)} %collective-permute-done.28.state_ref, bf16[2048,128]{1,0:T(8,128)(2,1)S(1)} %collective-permute-done.25.sibling_ref, f32[384,2048]{1,0:T(8,128)S(1)} %get-tuple-element.127.key_ref, ...), custom_call_target="tpu_custom_call", output_to_operand_aliasing={{0}: (7, {}), {1}: (8, {})} | custom-call | flops 402653184 | bytes 7864320 | tf_op jit(solution)/shard_map/outer/pallas_call | solution.py:74
  (60 shorter events, 19.7 us)
Async XLA Ops:
  0.6 11.9 %collective-permute-start = (bf16[128,2048]{1,0:T(8,128)(2,1)}, bf16[128,2048]{1,0:T(8,128)(2,1)S(1)}, u32[]{:S(2)}, u32[]{:S(2)}) collective-permute-start(bf16[128,2048]{1,0:T(8,128)(2,1)} %refs_0_.1), channel_id=1, source_target_pairs={{0,8},{4,20},{8,0},{12,28},{16,24},{20,4},{24,16},{28,12},{1,9},{5... | collective-permute-start | bytes 1572872 | tf_op jit(solution)/shard_map/ppermute | solution.py:869
  2.8 13.5 %collective-permute-start.1 = (bf16[128,2048]{1,0:T(8,128)(2,1)}, bf16[128,2048]{1,0:T(8,128)(2,1)S(1)}, u32[]{:S(2)}, u32[]{:S(2)}) collective-permute-start(bf16[128,2048]{1,0:T(8,128)(2,1)} %refs_0_.1), channel_id=1, source_target_pairs={{0,16},{4,12},{8,24},{12,4},{16,0},{20,28},{24,8},{28,20},{1,17},{... | collective-permute-start | bytes 1572872 | tf_op jit(solution)/shard_map/ppermute | solution.py:869
  4.0 12.4 %collective-permute-start.2 = (bf16[128,2048]{1,0:T(8,128)(2,1)}, bf16[128,2048]{1,0:T(8,128)(2,1)S(1)}, u32[]{:S(2)}, u32[]{:S(2)}) collective-permute-start(bf16[128,2048]{1,0:T(8,128)(2,1)} %refs_0_.1), channel_id=1, source_target_pairs={{0,1},{1,0},{2,3},{3,2},{4,5},{5,4},{6,7},{7,6},{8,9},{9,8},{10,11... | collective-permute-start | bytes 1572872 | tf_op jit(solution)/shard_map/ppermute | solution.py:866
  5.3 11.1 %collective-permute-start.3 = (bf16[128,2048]{1,0:T(8,128)(2,1)}, bf16[128,2048]{1,0:T(8,128)(2,1)S(1)}, u32[]{:S(2)}, u32[]{:S(2)}) collective-permute-start(bf16[128,2048]{1,0:T(8,128)(2,1)} %refs_0_.1), channel_id=1, source_target_pairs={{1,2},{2,1},{5,6},{6,5},{9,10},{10,9},{13,14},{14,13},{17,18},{18,... | collective-permute-start | bytes 1572872 | tf_op jit(solution)/shard_map/ppermute | solution.py:866
  16.4 4.6 %collective-permute-start.9 = (bf16[2048,128]{1,0:T(8,128)(2,1)S(1)}, bf16[2048,128]{1,0:T(8,128)(2,1)S(1)}, u32[]{:S(2)}, u32[]{:S(2)}) collective-permute-start(bf16[2048,128]{1,0:T(8,128)(2,1)S(1)} %get-tuple-element.75), channel_id=1, source_target_pairs={{0,4},{4,0},{1,5},{5,1},{2,6},{6,2},{3,7},{7,3},{8,12},{12,8},{9,1... | collective-permute-start | bytes 1572872 | tf_op jit(solution)/shard_map/ppermute | solution.py:739
  18.5 12.9 %collective-permute-start.5 = (bf16[128,2048]{1,0:T(8,128)(2,1)S(1)}, bf16[128,2048]{1,0:T(8,128)(2,1)S(1)}, u32[]{:S(2)}, u32[]{:S(2)}) collective-permute-start(bf16[128,2048]{1,0:T(8,128)(2,1)S(1)} %get-tuple-element.72.refs_4_), channel_id=1, source_target_pairs={{0,8},{4,20},{8,0},{12,28},{16,24},{20,4},{24,16},{28,12},{1,9},{5... | collective-permute-start | bytes 1572872 | tf_op jit(solution)/shard_map/ppermute | solution.py:869
  18.8 14.9 %collective-permute-start.6 = (bf16[128,2048]{1,0:T(8,128)(2,1)S(1)}, bf16[128,2048]{1,0:T(8,128)(2,1)S(1)}, u32[]{:S(2)}, u32[]{:S(2)}) collective-permute-start(bf16[128,2048]{1,0:T(8,128)(2,1)S(1)} %get-tuple-element.72.refs_4_), channel_id=1, source_target_pairs={{0,16},{4,12},{8,24},{12,4},{16,0},{20,28},{24,8},{28,20},{1,17},{... | collective-permute-start | bytes 1572872 | tf_op jit(solution)/shard_map/ppermute | solution.py:869
  18.9 14.8 %collective-permute-start.7 = (bf16[128,2048]{1,0:T(8,128)(2,1)S(1)}, bf16[128,2048]{1,0:T(8,128)(2,1)S(1)}, u32[]{:S(2)}, u32[]{:S(2)}) collective-permute-start(bf16[128,2048]{1,0:T(8,128)(2,1)S(1)} %get-tuple-element.72.refs_4_), channel_id=1, source_target_pairs={{1,2},{2,1},{5,6},{6,5},{9,10},{10,9},{13,14},{14,13},{17,18},{18,... | collective-permute-start | bytes 1572872 | tf_op jit(solution)/shard_map/ppermute | solution.py:866
  19.6 18.8 %collective-permute-start.4 = (bf16[128,2048]{1,0:T(8,128)(2,1)S(1)}, bf16[128,2048]{1,0:T(8,128)(2,1)S(1)}, u32[]{:S(2)}, u32[]{:S(2)}) collective-permute-start(bf16[128,2048]{1,0:T(8,128)(2,1)S(1)} %get-tuple-element.71.refs_1_), channel_id=1, source_target_pairs={{0,16},{4,12},{8,24},{12,4},{16,0},{20,28},{24,8},{28,20},{1,17},{... | collective-permute-start | bytes 1572872 | tf_op jit(solution)/shard_map/ppermute | solution.py:872
  21.0 19.4 %collective-permute-start.8 = (bf16[128,2048]{1,0:T(8,128)(2,1)S(1)}, bf16[128,2048]{1,0:T(8,128)(2,1)S(1)}, u32[]{:S(2)}, u32[]{:S(2)}) collective-permute-start(bf16[128,2048]{1,0:T(8,128)(2,1)S(1)} %get-tuple-element.73.inner_ref), channel_id=1, source_target_pairs={{1,0},{2,3},{5,4},{6,7},{9,8},{10,11},{13,12},{14,15},{17,16},{18,... | collective-permute-start | bytes 1572872 | tf_op jit(solution)/shard_map/ppermute | solution.py:866
  22.3 18.1 %copy-start = (bf16[128,2048]{1,0:T(8,128)(2,1)S(1)}, bf16[128,2048]{1,0:T(8,128)(2,1)}, u32[]{:S(2)}) copy-start(bf16[128,2048]{1,0:T(8,128)(2,1)} %refs_0_.1) | copy-start | bytes 1572868
  31.4 8.9 %collective-permute-start.10 = (bf16[1024,128]{1,0:T(8,128)(2,1)S(1)}, bf16[1024,128]{1,0:T(8,128)(2,1)S(1)}, u32[]{:S(2)}, u32[]{:S(2)}) collective-permute-start(bf16[1024,128]{1,0:T(8,128)(2,1)S(1)} %get-tuple-element.76), channel_id=1, source_target_pairs={{0,8},{4,20},{8,0},{12,28},{16,24},{24,16},{1,9},{5,21},{9,1},{13,... | collective-permute-start | bytes 786440 | tf_op jit(solution)/shard_map/ppermute | solution.py:749
  40.7 9.8 %collective-permute-start.15 = (bf16[896,2048]{1,0:T(8,128)(2,1)S(1)}, bf16[896,2048]{1,0:T(8,128)(2,1)S(1)}, u32[]{:S(2)}, u32[]{:S(2)}) collective-permute-start(bf16[896,2048]{1,0:T(8,128)(2,1)S(1)} %pack.3.refs_0_), channel_id=1, source_target_pairs={{0,4},{4,0},{1,5},{5,1},{2,6},{6,2},{3,7},{7,3},{8,12},{12,8},{9,1... | collective-permute-start | bytes 11010056 | tf_op jit(solution)/shard_map/ppermute | solution.py:822
  42.5 17.3 %collective-permute-start.12 = (bf16[128,2048]{1,0:T(8,128)(2,1)S(1)}, bf16[128,2048]{1,0:T(8,128)(2,1)S(1)}, u32[]{:S(2)}, u32[]{:S(2)}) collective-permute-start(bf16[128,2048]{1,0:T(8,128)(2,1)S(1)} %choose.2.refs_0_), channel_id=1, source_target_pairs={{0,8},{4,20},{8,0},{12,28},{16,24},{20,4},{24,16},{28,12},{1,9},{5... | collective-permute-start | bytes 1572872 | tf_op jit(solution)/shard_map/ppermute | solution.py:869
  43.8 16.0 %collective-permute-start.13 = (bf16[128,2048]{1,0:T(8,128)(2,1)S(1)}, bf16[128,2048]{1,0:T(8,128)(2,1)S(1)}, u32[]{:S(2)}, u32[]{:S(2)}) collective-permute-start(bf16[128,2048]{1,0:T(8,128)(2,1)S(1)} %choose.2.refs_0_), channel_id=1, source_target_pairs={{0,16},{4,12},{8,24},{12,4},{16,0},{20,28},{24,8},{28,20},{1,17},{... | collective-permute-start | bytes 1572872 | tf_op jit(solution)/shard_map/ppermute | solution.py:869
  44.1 16.0 %collective-permute-start.11 = (bf16[128,2048]{1,0:T(8,128)(2,1)S(1)}, bf16[128,2048]{1,0:T(8,128)(2,1)S(1)}, u32[]{:S(2)}, u32[]{:S(2)}) collective-permute-start(bf16[128,2048]{1,0:T(8,128)(2,1)S(1)} %get-tuple-element.77.inner_ref), channel_id=1, source_target_pairs={{1,0},{2,3},{5,4},{6,7},{9,8},{10,11},{13,12},{14,15},{17,16},{18,... | collective-permute-start | bytes 1572872 | tf_op jit(solution)/shard_map/ppermute | solution.py:866
  45.5 14.4 %collective-permute-start.14 = (bf16[1024,128]{1,0:T(8,128)(2,1)S(1)}, bf16[1024,128]{1,0:T(8,128)(2,1)S(1)}, u32[]{:S(2)}, u32[]{:S(2)}) collective-permute-start(bf16[1024,128]{1,0:T(8,128)(2,1)S(1)} %message.2), channel_id=1, source_target_pairs={{0,16},{4,12},{8,24},{12,4},{20,28},{28,20},{1,17},{5,13},{9,25},{... | collective-permute-start | bytes 786440 | tf_op jit(solution)/shard_map/ppermute | solution.py:762
  60.3 21.6 %collective-permute-start.20 = (bf16[512,2048]{1,0:T(8,128)(2,1)S(1)}, bf16[512,2048]{1,0:T(8,128)(2,1)S(1)}, u32[]{:S(2)}, u32[]{:S(2)}) collective-permute-start(bf16[512,2048]{1,0:T(8,128)(2,1)S(1)} %pack.4.refs_0_), channel_id=1, source_target_pairs={{0,4},{4,0},{1,5},{5,1},{2,6},{6,2},{3,7},{7,3},{8,12},{12,8},{9,1... | collective-permute-start | bytes 6291464 | tf_op jit(solution)/shard_map/ppermute | solution.py:822
  61.6 4.4 %collective-permute-start.21 = (f32[1024,128]{1,0:T(8,128)S(1)}, f32[1024,128]{1,0:T(8,128)S(1)}, u32[]{:S(2)}, u32[]{:S(2)}) collective-permute-start(f32[1024,128]{1,0:T(8,128)S(1)} %state.2.state_ref), channel_id=1, source_target_pairs={{0,4},{4,0},{1,5},{5,1},{2,6},{6,2},{3,7},{7,3},{8,12},{12,8},{9,1... | collective-permute-start | bytes 1572872 | tf_op jit(solution)/shard_map/ppermute | solution.py:775
  61.7 16.5 %collective-permute-start.17 = (bf16[128,2048]{1,0:T(8,128)(2,1)S(1)}, bf16[128,2048]{1,0:T(8,128)(2,1)S(1)}, u32[]{:S(2)}, u32[]{:S(2)}) collective-permute-start(bf16[128,2048]{1,0:T(8,128)(2,1)S(1)} %choose.3.refs_3_), channel_id=1, source_target_pairs={{0,8},{4,20},{8,0},{12,28},{16,24},{20,4},{24,16},{28,12},{1,9},{5... | collective-permute-start | bytes 1572872 | tf_op jit(solution)/shard_map/ppermute | solution.py:869
  62.8 15.4 %collective-permute-start.18 = (bf16[128,2048]{1,0:T(8,128)(2,1)S(1)}, bf16[128,2048]{1,0:T(8,128)(2,1)S(1)}, u32[]{:S(2)}, u32[]{:S(2)}) collective-permute-start(bf16[128,2048]{1,0:T(8,128)(2,1)S(1)} %choose.3.refs_3_), channel_id=1, source_target_pairs={{0,16},{4,12},{8,24},{12,4},{16,0},{20,28},{24,8},{28,20},{1,17},{... | collective-permute-start | bytes 1572872 | tf_op jit(solution)/shard_map/ppermute | solution.py:869
  64.0 17.9 %collective-permute-start.16 = (bf16[128,2048]{1,0:T(8,128)(2,1)S(1)}, bf16[128,2048]{1,0:T(8,128)(2,1)S(1)}, u32[]{:S(2)}, u32[]{:S(2)}) collective-permute-start(bf16[128,2048]{1,0:T(8,128)(2,1)S(1)} %get-tuple-element.89.refs_1_), channel_id=1, source_target_pairs={{0,16},{4,12},{8,24},{12,4},{16,0},{20,28},{24,8},{28,20},{1,17},{... | collective-permute-start | bytes 1572872 | tf_op jit(solution)/shard_map/ppermute | solution.py:872
  66.0 15.9 %collective-permute-start.19 = (bf16[128,2048]{1,0:T(8,128)(2,1)S(1)}, bf16[128,2048]{1,0:T(8,128)(2,1)S(1)}, u32[]{:S(2)}, u32[]{:S(2)}) collective-permute-start(bf16[128,2048]{1,0:T(8,128)(2,1)S(1)} %get-tuple-element.91), channel_id=1, source_target_pairs={{0,1},{1,0},{2,3},{3,2},{4,5},{5,4},{6,7},{7,6},{8,9},{9,8},{10,11... | collective-permute-start | bytes 1572872 | tf_op jit(solution)/shard_map/ppermute | solution.py:866
  82.3 5.6 %collective-permute-start.22 = (bf16[512,2048]{1,0:T(8,128)(2,1)S(1)}, bf16[512,2048]{1,0:T(8,128)(2,1)S(1)}, u32[]{:S(2)}, u32[]{:S(2)}) collective-permute-start(bf16[512,2048]{1,0:T(8,128)(2,1)S(1)} %pack.5.refs_0_), channel_id=1, source_target_pairs={{0,4},{4,0},{1,5},{5,1},{2,6},{6,2},{3,7},{7,3},{8,12},{12,8},{9,1... | collective-permute-start | bytes 6291464 | tf_op jit(solution)/shard_map/ppermute | solution.py:822
  82.4 8.4 %collective-permute-start.23 = (bf16[128,2048]{1,0:T(8,128)(2,1)S(1)}, bf16[128,2048]{1,0:T(8,128)(2,1)S(1)}, u32[]{:S(2)}, u32[]{:S(2)}) collective-permute-start(bf16[128,2048]{1,0:T(8,128)(2,1)S(1)} %get-tuple-element.101.refs_2_), channel_id=1, source_target_pairs={{0,16},{4,12},{8,24},{12,4},{16,0},{20,28},{24,8},{28,20},{1,17},{... | collective-permute-start | bytes 1572872 | tf_op jit(solution)/shard_map/ppermute | solution.py:872
  90.7 4.0 %collective-permute-start.24 = (bf16[128,2048]{1,0:T(8,128)(2,1)S(1)}, bf16[128,2048]{1,0:T(8,128)(2,1)S(1)}, u32[]{:S(2)}, u32[]{:S(2)}) collective-permute-start(bf16[128,2048]{1,0:T(8,128)(2,1)S(1)} %join.9.refs_0_), channel_id=1, source_target_pairs={{0,4},{4,0},{1,5},{5,1},{2,6},{6,2},{3,7},{7,3},{8,12},{12,8},{9,1... | collective-permute-start | bytes 1572872 | tf_op jit(solution)/shard_map/ppermute | solution.py:863
  96.5 2.0 %collective-permute-start.25 = (bf16[2048,128]{1,0:T(8,128)(2,1)S(1)}, bf16[2048,128]{1,0:T(8,128)(2,1)S(1)}, u32[]{:S(2)}, u32[]{:S(2)}) collective-permute-start(bf16[2048,128]{1,0:T(8,128)(2,1)S(1)} %get-tuple-element.118), channel_id=1, source_target_pairs={{0,4},{4,0},{1,5},{5,1},{2,6},{6,2},{3,7},{7,3},{8,12},{12,8},{9,1... | collective-permute-start | bytes 1572872 | tf_op jit(solution)/shard_map/ppermute | solution.py:739
  98.6 7.4 %collective-permute-start.26 = (bf16[1024,128]{1,0:T(8,128)(2,1)S(1)}, bf16[1024,128]{1,0:T(8,128)(2,1)S(1)}, u32[]{:S(2)}, u32[]{:S(2)}) collective-permute-start(bf16[1024,128]{1,0:T(8,128)(2,1)S(1)} %get-tuple-element.120), channel_id=1, source_target_pairs={{0,8},{8,0},{16,24},{20,4},{24,16},{28,12},{1,9},{9,1},{17,25},{21... | collective-permute-start | bytes 786440 | tf_op jit(solution)/shard_map/ppermute | solution.py:749
  106.0 9.1 %collective-permute-start.27 = (bf16[1024,128]{1,0:T(8,128)(2,1)S(1)}, bf16[1024,128]{1,0:T(8,128)(2,1)S(1)}, u32[]{:S(2)}, u32[]{:S(2)}) collective-permute-start(bf16[1024,128]{1,0:T(8,128)(2,1)S(1)} %message.3), channel_id=1, source_target_pairs={{4,12},{12,4},{16,0},{20,28},{24,8},{28,20},{5,13},{13,5},{17,1},{... | collective-permute-start | bytes 786440 | tf_op jit(solution)/shard_map/ppermute | solution.py:762
  115.3 2.7 %collective-permute-start.28 = (f32[1024,128]{1,0:T(8,128)S(1)}, f32[1024,128]{1,0:T(8,128)S(1)}, u32[]{:S(2)}, u32[]{:S(2)}) collective-permute-start(f32[1024,128]{1,0:T(8,128)S(1)} %state.3.state_ref), channel_id=1, source_target_pairs={{0,4},{4,0},{1,5},{5,1},{2,6},{6,2},{3,7},{7,3},{8,12},{12,8},{9,1... | collective-permute-start | bytes 1572872 | tf_op jit(solution)/shard_map/ppermute | solution.py:775

commit v13 on v12

--- a/solution.py
+++ b/solution.py
@@ -892,8 +892,8 @@
         far = along(near, middle)
         mid_out = along(mid, outward)
         twin, both, got = send_first(own, sent, False)
-        third_0, first_1, second_1, far, mid_out, got = join(
-            [third_0, first_1, second_1, far, mid_out, got]
+        mid_out, third_0, first_1, second_1, far, got = join(
+            [mid_out, third_0, first_1, second_1, far, got]
         )
         more = send_second(got, both, False)
         next_layer = choose(mid, mid_out)

time: 121 us -> 121 us (level)
    ppermute x3, waiting for transfers between devices: 9.1 us -> 4.51 us  [onward(): return lax.ppermute(array, CTX, links(2))]
    ppermute x6, waiting for transfers between devices: 2.34 us -> 6.53 us  [along(): return lax.ppermute(array, 'dp', pairs)]
  transfers between devices with their start and end apart: 29 -> 29, of which waited for: 13 -> 12; matrix products, arithmetic and copies ran while one was open for 0% -> 0% of each run, Pallas kernels for 36% -> 36%
where the time goes in v13:
time: 121 us; the launch traced here: 120 us
  Pallas kernels  48.2 us (40%)
  waiting for transfers between devices  36.1 us (30%)
  starting transfers between devices  34.9 us (29%)
    pallas_call x32, Pallas kernels, kernel_call(): made(*[holds[place](one) if place in holds else one for place, one in zip...  48.2 us
    ppermute x4, waiting for transfers between devices, cross(): lax.ppermute(array, CTX, links(1))  10.8 us
    ppermute x6, starting transfers between devices, along(): return lax.ppermute(array, 'dp', pairs)  7.74 us
    ppermute x2, waiting for transfers between devices, send_second(): return lax.ppermute(message, CTX, links(2, upward(reverse)))  7.15 us
    ppermute x6, waiting for transfers between devices, along(): return lax.ppermute(array, 'dp', pairs)  6.53 us
    ppermute x2, starting transfers between devices, send_second(): return lax.ppermute(message, CTX, links(2, upward(reverse)))  5.29 us
    ppermute x3, waiting for transfers between devices, onward(): return lax.ppermute(array, CTX, links(2))  4.51 us
    ppermute x4, starting transfers between devices, cross(): lax.ppermute(array, CTX, links(1))  4 us
  transfers between devices with their start and end apart: 29, of which 12 were waited for; matrix products, arithmetic and copies ran while one was open for 0% of the time, Pallas kernels for 36%

profile of v13, /device:TPU:1, one launch (start us, length us, event | category | flops | bytes accessed | tf_op | source)
XLA Modules:
  0.0 120.4 jit_solution(12854336037179034480)
XLA Ops:
  0.6 2.1 %collective-permute-start = (bf16[128,2048]{1,0:T(8,128)(2,1)}, bf16[128,2048]{1,0:T(8,128)(2,1)S(1)}, u32[]{:S(2)}, u32[]{:S(2)}) collective-permute-start(bf16[128,2048]{1,0:T(8,128)(2,1)} %refs_0_.1), channel_id=1, source_target_pairs={{0,8},{4,20},{8,0},{12,28},{16,24},{20,4},{24,16},{28,12},{1,9},{5... | collective-permute-start | bytes 1572872 | tf_op jit(solution)/shard_map/ppermute | solution.py:869
  4.0 1.3 %collective-permute-start.2 = (bf16[128,2048]{1,0:T(8,128)(2,1)}, bf16[128,2048]{1,0:T(8,128)(2,1)S(1)}, u32[]{:S(2)}, u32[]{:S(2)}) collective-permute-start(bf16[128,2048]{1,0:T(8,128)(2,1)} %refs_0_.1), channel_id=1, source_target_pairs={{0,1},{1,0},{2,3},{3,2},{4,5},{5,4},{6,7},{7,6},{8,9},{9,8},{10,11... | collective-permute-start | bytes 1572872 | tf_op jit(solution)/shard_map/ppermute | solution.py:866
  6.0 4.8 %own_memory.1 = (bf16[384,2048]{1,0:T(8,128)(2,1)S(1)}, bf16[384,2048]{1,0:T(8,128)(2,1)S(1)}, bf16[384,2048]{1,0:T(8,128)(2,1)S(1)}, f32[2048,128]{1,0:T(8,128)...) custom-call(bf16[384,2048]{1,0:T(8,128)(2,1)} %bitcast.15, ...), custom_call_target="tpu_custom_call" | custom-call | flops 201326592 | bytes 9437184 | tf_op jit(solution)/shard_map/own_memory/pallas_call | solution.py:74
  10.7 1.8 %collective-permute-done.refs_0_ = bf16[128,2048]{1,0:T(8,128)(2,1)S(1)} collective-permute-done((bf16[128,2048]{1,0:T(8,128)(2,1)}, bf16[128,2048]{1,0:T(8,128)(2,1)S(1)}, u32[]{:S(2)}, u32[]{:S(2)}) %collective-permute-start) | collective-permute-done | bytes 524320 | tf_op jit(solution)/shard_map/ppermute | solution.py:869
  12.6 3.7 %collective-permute-done.1.refs_1_ = bf16[128,2048]{1,0:T(8,128)(2,1)S(1)} collective-permute-done((bf16[128,2048]{1,0:T(8,128)(2,1)}, bf16[128,2048]{1,0:T(8,128)(2,1)S(1)}, u32[]{:S(2)}, u32[]{:S(2)}) %collective-permute-start.1) | collective-permute-done | bytes 524320 | tf_op jit(solution)/shard_map/ppermute | solution.py:869
  16.4 2.2 %collective-permute-start.9 = (bf16[2048,128]{1,0:T(8,128)(2,1)S(1)}, bf16[2048,128]{1,0:T(8,128)(2,1)S(1)}, u32[]{:S(2)}, u32[]{:S(2)}) collective-permute-start(bf16[2048,128]{1,0:T(8,128)(2,1)S(1)} %get-tuple-element.75), channel_id=1, source_target_pairs={{0,4},{4,0},{1,5},{5,1},{2,6},{6,2},{3,7},{7,3},{8,12},{12,8},{9,1... | collective-permute-start | bytes 1572872 | tf_op jit(solution)/shard_map/ppermute | solution.py:739
  19.6 1.3 %collective-permute-start.4 = (bf16[128,2048]{1,0:T(8,128)(2,1)S(1)}, bf16[128,2048]{1,0:T(8,128)(2,1)S(1)}, u32[]{:S(2)}, u32[]{:S(2)}) collective-permute-start(bf16[128,2048]{1,0:T(8,128)(2,1)S(1)} %get-tuple-element.71.inner_ref), channel_id=1, source_target_pairs={{1,0},{2,3},{5,4},{6,7},{9,8},{10,11},{13,12},{14,15},{17,16},{18,... | collective-permute-start | bytes 1572872 | tf_op jit(solution)/shard_map/ppermute | solution.py:866
  20.9 1.4 %collective-permute-start.5 = (bf16[128,2048]{1,0:T(8,128)(2,1)S(1)}, bf16[128,2048]{1,0:T(8,128)(2,1)S(1)}, u32[]{:S(2)}, u32[]{:S(2)}) collective-permute-start(bf16[128,2048]{1,0:T(8,128)(2,1)S(1)} %get-tuple-element.72.refs_1_), channel_id=1, source_target_pairs={{0,16},{4,12},{8,24},{12,4},{16,0},{20,28},{24,8},{28,20},{1,17},{... | collective-permute-start | bytes 1572872 | tf_op jit(solution)/shard_map/ppermute | solution.py:872
  22.4 9.0 %collective-permute-done.6.refs_2_ = bf16[128,2048]{1,0:T(8,128)(2,1)S(1)} collective-permute-done((bf16[128,2048]{1,0:T(8,128)(2,1)S(1)}, bf16[128,2048]{1,0:T(8,128)(2,1)S(1)}, u32[]{:S(2)}, u32[]{:S(2)}) %collective-permute-start.6) | collective-permute-done | bytes 524320 | tf_op jit(solution)/shard_map/ppermute | solution.py:869
  31.4 2.3 %collective-permute-start.10 = (bf16[1024,128]{1,0:T(8,128)(2,1)S(1)}, bf16[1024,128]{1,0:T(8,128)(2,1)S(1)}, u32[]{:S(2)}, u32[]{:S(2)}) collective-permute-start(bf16[1024,128]{1,0:T(8,128)(2,1)S(1)} %get-tuple-element.76), channel_id=1, source_target_pairs={{0,8},{4,20},{8,0},{12,28},{16,24},{24,16},{1,9},{5,21},{9,1},{13,... | collective-permute-start | bytes 786440 | tf_op jit(solution)/shard_map/ppermute | solution.py:749
  33.7 5.7 %collective-permute-done.4.refs_0_ = bf16[128,2048]{1,0:T(8,128)(2,1)S(1)} collective-permute-done((bf16[128,2048]{1,0:T(8,128)(2,1)S(1)}, bf16[128,2048]{1,0:T(8,128)(2,1)S(1)}, u32[]{:S(2)}, u32[]{:S(2)}) %collective-permute-start.4) | collective-permute-done | bytes 524320 | tf_op jit(solution)/shard_map/ppermute | solution.py:866
  39.8 2.3 %collective-permute-start.15 = (bf16[896,2048]{1,0:T(8,128)(2,1)S(1)}, bf16[896,2048]{1,0:T(8,128)(2,1)S(1)}, u32[]{:S(2)}, u32[]{:S(2)}) collective-permute-start(bf16[896,2048]{1,0:T(8,128)(2,1)S(1)} %pack.3.refs_0_), channel_id=1, source_target_pairs={{0,4},{4,0},{1,5},{5,1},{2,6},{6,2},{3,7},{7,3},{8,12},{12,8},{9,1... | collective-permute-start | bytes 11010056 | tf_op jit(solution)/shard_map/ppermute | solution.py:822
  45.2 2.2 %collective-permute-start.14 = (bf16[1024,128]{1,0:T(8,128)(2,1)S(1)}, bf16[1024,128]{1,0:T(8,128)(2,1)S(1)}, u32[]{:S(2)}, u32[]{:S(2)}) collective-permute-start(bf16[1024,128]{1,0:T(8,128)(2,1)S(1)} %message.2), channel_id=1, source_target_pairs={{0,16},{4,12},{8,24},{12,4},{20,28},{28,20},{1,17},{5,13},{9,25},{... | collective-permute-start | bytes 786440 | tf_op jit(solution)/shard_map/ppermute | solution.py:762
  47.3 1.8 %turned.1 = (bf16[128,6144]{1,0:T(8,128)(2,1)S(1)}, bf16[256,4096]{1,0:T(8,128)(2,1)S(1)}, f32[8,128]{1,0:T(8,128)S(1)}) custom-call(bf16[384,2048]{1,0:T(8,128)(2,1)S(1)} %get-tuple-element.86.value_ref, bf16[384,2048]{1,0:T(8,128)(2,1)S(1)} %get-tuple-element.87.grad_ref, bf16[1024,128]{1,0:T(8,128)(2,1)S(1)} %get-tuple-element.79.got_ref.after_ref), custom_call_target="tpu_custom_call" | custom-call | flops 1207959552 | tf_op jit(solution)/shard_map/turned/pallas_call | solution.py:74
  49.2 3.0 %project.2 = (f32[384,2048]{1,0:T(8,128)S(1)}, f32[8,128]{1,0:T(8,128)S(1)}) custom-call(bf16[896,2048]{1,0:T(8,128)(2,1)S(1)} %pack.3.refs_0_, bf16[896,2048]{1,0:T(8,128)(2,1)S(1)} %collective-permute-done.15.refs_1_, bf16[384,4096]{1,0:T(8,128)(2,1)S(1)} %get-tuple-element.69.refs_2_.tokens_ref), custom_call_target="tpu_custom_call" | custom-call | flops 2818572288 | tf_op jit(solution)/shard_map/project/pallas_call | solution.py:74
  52.2 7.1 %collective-permute-done.14.refs_3_ = bf16[1024,128]{1,0:T(8,128)(2,1)S(1)} collective-permute-done((bf16[1024,128]{1,0:T(8,128)(2,1)S(1)}, bf16[1024,128]{1,0:T(8,128)(2,1)S(1)}, u32[]{:S(2)}, u32[]{:S(2)}) %collective-permute-start.14) | collective-permute-done | bytes 262176 | tf_op jit(solution)/shard_map/ppermute | solution.py:762
  64.3 1.8 %collective-permute-done.21.other_ref = f32[1024,128]{1,0:T(8,128)S(1)} collective-permute-done((f32[1024,128]{1,0:T(8,128)S(1)}, f32[1024,128]{1,0:T(8,128)S(1)}, u32[]{:S(2)}, u32[]{:S(2)}) %collective-permute-start.21) | collective-permute-done | bytes 524320 | tf_op jit(solution)/shard_map/ppermute | solution.py:775
  66.0 2.5 %collective-permute-start.19 = (bf16[128,2048]{1,0:T(8,128)(2,1)S(1)}, bf16[128,2048]{1,0:T(8,128)(2,1)S(1)}, u32[]{:S(2)}, u32[]{:S(2)}) collective-permute-start(bf16[128,2048]{1,0:T(8,128)(2,1)S(1)} %get-tuple-element.91), channel_id=1, source_target_pairs={{0,1},{1,0},{2,3},{3,2},{4,5},{5,4},{6,7},{7,6},{8,9},{9,8},{10,11... | collective-permute-start | bytes 1572872 | tf_op jit(solution)/shard_map/ppermute | solution.py:866
  68.8 5.4 %masked_grad.1 = (bf16[384,2048]{1,0:T(8,128)(2,1)S(1)}, bf16[384,2048]{1,0:T(8,128)(2,1)S(1)}) custom-call(s32[384,2048]{1,0:T(8,128)} %bitcast.18, bf16[384,2048]{1,0:T(8,128)(2,1)S(1)} %get-tuple-element.87.grad_ref, bf16[384,2048]{1,0:T(8,128)(2,1)S(1)} %get-tuple-element.86.value_ref, bf16[384,2048]{1,0:T(8,128)(2,1)S(1)} %get-tuple-element.93.keys_ref, ...), custom_call_target="tpu_custom_call" | custom-call | flops 2415919104 | bytes 9437184 | tf_op jit(solution)/shard_map/masked_grad/pallas_call | solution.py:74
  74.2 3.9 %grad_tokens.3 = (bf16[384,4096]{1,0:T(8,128)(2,1)}, f32[8,128]{1,0:T(8,128)S(1)}) custom-call(bf16[896,2048]{1,0:T(8,128)(2,1)S(1)} %pack.3.refs_0_, bf16[896,2048]{1,0:T(8,128)(2,1)S(1)} %collective-permute-done.15.refs_1_, bf16[384,2048]{1,0:T(8,128)(2,1)S(1)} %get-tuple-element.97.refs_2_.refs_4_), custom_call_target="tpu_custom_call" | custom-call | flops 2818572288 | tf_op jit(solution)/shard_map/grad_tokens/pallas_call | solution.py:74
  78.2 3.7 %collective-permute-done.16.refs_0_ = bf16[128,2048]{1,0:T(8,128)(2,1)S(1)} collective-permute-done((bf16[128,2048]{1,0:T(8,128)(2,1)S(1)}, bf16[128,2048]{1,0:T(8,128)(2,1)S(1)}, u32[]{:S(2)}, u32[]{:S(2)}) %collective-permute-start.16) | collective-permute-done | bytes 524320 | tf_op jit(solution)/shard_map/ppermute | solution.py:872
  83.6 4.3 %products.1 = (f32[384,2048]{1,0:T(8,128)S(1)}, bf16[384,4096]{1,0:T(8,128)(2,1)}, f32[8,128]{1,0:T(8,128)S(1)}) custom-call(bf16[512,2048]{1,0:T(8,128)(2,1)S(1)} %pack.4.refs_0_, bf16[512,2048]{1,0:T(8,128)(2,1)S(1)} %get-tuple-element.103.refs_1_, ...), custom_call_target="tpu_custom_call", output_to_operand_aliasing={{0}: (3, {}), {1}: (5, {})} | custom-call | flops 3221225472 | tf_op jit(solution)/shard_map/products/pallas_call | solution.py:74
  87.9 2.1 %project.3 = (f32[384,2048]{1,0:T(8,128)S(1)}, f32[8,128]{1,0:T(8,128)S(1)}) custom-call(bf16[512,2048]{1,0:T(8,128)(2,1)S(1)} %pack.5.refs_0_, bf16[512,2048]{1,0:T(8,128)(2,1)S(1)} %collective-permute-done.22.refs_1_, bf16[384,4096]{1,0:T(8,128)(2,1)S(1)} %get-tuple-element.69.refs_2_.tokens_ref, ...), custom_call_target="tpu_custom_call", output_to_operand_aliasing={{0}: (3, {})} | custom-call | flops 1610612736 | tf_op jit(solution)/shard_map/project/pallas_call | solution.py:74
  92.0 2.7 %grad_tokens.4 = (bf16[384,4096]{1,0:T(8,128)(2,1)}, f32[8,128]{1,0:T(8,128)S(1)}) custom-call(bf16[512,2048]{1,0:T(8,128)(2,1)S(1)} %pack.5.refs_0_, bf16[512,2048]{1,0:T(8,128)(2,1)S(1)} %collective-permute-done.22.refs_1_, bf16[384,2048]{1,0:T(8,128)(2,1)S(1)} %get-tuple-element.97.refs_2_.refs_4_, ...), custom_call_target="tpu_custom_call", output_to_operand_aliasing={{0}: (3, {})} | custom-call | flops 1610612736 | tf_op jit(solution)/shard_map/grad_tokens/pallas_call | solution.py:74
  94.7 1.8 %queries.1 = (bf16[384,2048]{1,0:T(8,128)(2,1)S(1)}, f32[2048,128]{1,0:T(8,128)S(1)}, bf16[2048,128]{1,0:T(8,128)(2,1)S(1)}) custom-call(bf16[384,4096]{1,0:T(8,128)(2,1)S(1)} %get-tuple-element.69.refs_2_.tokens_ref, f32[384,2048]{1,0:T(8,128)S(1)} %get-tuple-element.107.sum_ref, bf16[384,2048]{1,0:T(8,128)(2,1)S(1)} %get-tuple-element.108.mask_ref, ...), custom_call_target="tpu_custom_call" | custom-call | flops 402653184 | tf_op jit(solution)/shard_map/queries/pallas_call | solution.py:74
  96.6 1.3 %grad_tokens.5 = (bf16[384,4096]{1,0:T(8,128)(2,1)}, f32[8,128]{1,0:T(8,128)S(1)}) custom-call(bf16[128,2048]{1,0:T(8,128)(2,1)S(1)} %join.9.refs_0_, bf16[128,2048]{1,0:T(8,128)(2,1)S(1)} %collective-permute-done.24.refs_1_, bf16[384,2048]{1,0:T(8,128)(2,1)S(1)} %get-tuple-element.97.refs_2_.refs_4_, ...), custom_call_target="tpu_custom_call", output_to_operand_aliasing={{0}: (3, {})} | custom-call | flops 402653184 | tf_op jit(solution)/shard_map/grad_tokens/pallas_call | solution.py:74
  99.9 5.1 %attended.1 = (bf16[384,2048]{1,0:T(8,128)(2,1)}, f32[8,128]{1,0:T(8,128)S(1)}) custom-call(bf16[384,2048]{1,0:T(8,128)(2,1)S(1)} %get-tuple-element.113.query_ref, bf16[384,2048]{1,0:T(8,128)(2,1)S(1)} %get-tuple-element.93.keys_ref, bf16[384,2048]{1,0:T(8,128)(2,1)S(1)} %get-tuple-element.86.value_ref, bf16[2048,128]{1,0:T(8,128)(2,1)S(1)} %get-tuple-element.95.high_ref, ...), custom_call_target="tpu_custom_call" | custom-call | flops 2415919104 | bytes 6291456 | tf_op jit(solution)/shard_map/attended/pallas_call | solution.py:74
  106.0 3.1 %collective-permute-start.27 = (bf16[1024,128]{1,0:T(8,128)(2,1)S(1)}, bf16[1024,128]{1,0:T(8,128)(2,1)S(1)}, u32[]{:S(2)}, u32[]{:S(2)}) collective-permute-start(bf16[1024,128]{1,0:T(8,128)(2,1)S(1)} %message.3), channel_id=1, source_target_pairs={{4,12},{12,4},{16,0},{20,28},{24,8},{28,20},{5,13},{13,5},{17,1},{... | collective-permute-start | bytes 786440 | tf_op jit(solution)/shard_map/ppermute | solution.py:762
  109.2 2.1 %key_part.1 = (f32[384,2048]{1,0:T(8,128)S(1)}, f32[8,128]{1,0:T(8,128)S(1)}) custom-call(bf16[384,2048]{1,0:T(8,128)(2,1)S(1)} %get-tuple-element.113.query_ref, bf16[128,6144]{1,0:T(8,128)(2,1)S(1)} %get-tuple-element.124.top_ref, bf16[256,4096]{1,0:T(8,128)(2,1)S(1)} %get-tuple-element.125.bottom_ref), custom_call_target="tpu_custom_call" | custom-call | flops 1207959552 | tf_op jit(solution)/shard_map/key_part/pallas_call | solution.py:74
  111.3 3.9 %value_part.1 = (f32[384,2048]{1,0:T(8,128)S(1)}, f32[8,128]{1,0:T(8,128)S(1)}) custom-call(bf16[384,2048]{1,0:T(8,128)(2,1)S(1)} %get-tuple-element.113.query_ref, bf16[384,2048]{1,0:T(8,128)(2,1)S(1)} %get-tuple-element.93.keys_ref, bf16[384,2048]{1,0:T(8,128)(2,1)S(1)} %get-tuple-element.87.grad_ref), custom_call_target="tpu_custom_call" | custom-call | flops 1811939328 | tf_op jit(solution)/shard_map/value_part/pallas_call | solution.py:74
  115.7 2.2 %outer.2 = (bf16[384,2048]{1,0:T(8,128)(2,1)}, bf16[384,2048]{1,0:T(8,128)(2,1)}) custom-call(f32[1024,128]{1,0:T(8,128)S(1)} %state.3.state_ref, bf16[2048,128]{1,0:T(8,128)(2,1)S(1)} %collective-permute-done.25.sibling_ref, f32[384,2048]{1,0:T(8,128)S(1)} %get-tuple-element.127.key_ref, f32[384,2048]{1,0:T(8,128)S(1)} %get-tuple-element.128.val_ref, ...), custom_call_target="tpu_custom_call" | custom-call | flops 402653184 | bytes 7864320 | tf_op jit(solution)/shard_map/outer/pallas_call | solution.py:74
  118.0 2.2 %outer.3 = (bf16[384,2048]{1,0:T(8,128)(2,1)}, bf16[384,2048]{1,0:T(8,128)(2,1)}) custom-call(f32[1024,128]{1,0:T(8,128)S(1)} %collective-permute-done.28.state_ref, bf16[2048,128]{1,0:T(8,128)(2,1)S(1)} %collective-permute-done.25.sibling_ref, f32[384,2048]{1,0:T(8,128)S(1)} %get-tuple-element.127.key_ref, ...), custom_call_target="tpu_custom_call", output_to_operand_aliasing={{0}: (7, {}), {1}: (8, {})} | custom-call | flops 402653184 | bytes 7864320 | tf_op jit(solution)/shard_map/outer/pallas_call | solution.py:74
  (60 shorter events, 19.1 us)
Async XLA Ops:
  0.6 11.9 %collective-permute-start = (bf16[128,2048]{1,0:T(8,128)(2,1)}, bf16[128,2048]{1,0:T(8,128)(2,1)S(1)}, u32[]{:S(2)}, u32[]{:S(2)}) collective-permute-start(bf16[128,2048]{1,0:T(8,128)(2,1)} %refs_0_.1), channel_id=1, source_target_pairs={{0,8},{4,20},{8,0},{12,28},{16,24},{20,4},{24,16},{28,12},{1,9},{5... | collective-permute-start | bytes 1572872 | tf_op jit(solution)/shard_map/ppermute | solution.py:869
  2.8 13.5 %collective-permute-start.1 = (bf16[128,2048]{1,0:T(8,128)(2,1)}, bf16[128,2048]{1,0:T(8,128)(2,1)S(1)}, u32[]{:S(2)}, u32[]{:S(2)}) collective-permute-start(bf16[128,2048]{1,0:T(8,128)(2,1)} %refs_0_.1), channel_id=1, source_target_pairs={{0,16},{4,12},{8,24},{12,4},{16,0},{20,28},{24,8},{28,20},{1,17},{... | collective-permute-start | bytes 1572872 | tf_op jit(solution)/shard_map/ppermute | solution.py:869
  4.0 12.4 %collective-permute-start.2 = (bf16[128,2048]{1,0:T(8,128)(2,1)}, bf16[128,2048]{1,0:T(8,128)(2,1)S(1)}, u32[]{:S(2)}, u32[]{:S(2)}) collective-permute-start(bf16[128,2048]{1,0:T(8,128)(2,1)} %refs_0_.1), channel_id=1, source_target_pairs={{0,1},{1,0},{2,3},{3,2},{4,5},{5,4},{6,7},{7,6},{8,9},{9,8},{10,11... | collective-permute-start | bytes 1572872 | tf_op jit(solution)/shard_map/ppermute | solution.py:866
  5.3 11.1 %collective-permute-start.3 = (bf16[128,2048]{1,0:T(8,128)(2,1)}, bf16[128,2048]{1,0:T(8,128)(2,1)S(1)}, u32[]{:S(2)}, u32[]{:S(2)}) collective-permute-start(bf16[128,2048]{1,0:T(8,128)(2,1)} %refs_0_.1), channel_id=1, source_target_pairs={{1,2},{2,1},{5,6},{6,5},{9,10},{10,9},{13,14},{14,13},{17,18},{18,... | collective-permute-start | bytes 1572872 | tf_op jit(solution)/shard_map/ppermute | solution.py:866
  16.4 4.5 %collective-permute-start.9 = (bf16[2048,128]{1,0:T(8,128)(2,1)S(1)}, bf16[2048,128]{1,0:T(8,128)(2,1)S(1)}, u32[]{:S(2)}, u32[]{:S(2)}) collective-permute-start(bf16[2048,128]{1,0:T(8,128)(2,1)S(1)} %get-tuple-element.75), channel_id=1, source_target_pairs={{0,4},{4,0},{1,5},{5,1},{2,6},{6,2},{3,7},{7,3},{8,12},{12,8},{9,1... | collective-permute-start | bytes 1572872 | tf_op jit(solution)/shard_map/ppermute | solution.py:739
  18.5 12.9 %collective-permute-start.6 = (bf16[128,2048]{1,0:T(8,128)(2,1)S(1)}, bf16[128,2048]{1,0:T(8,128)(2,1)S(1)}, u32[]{:S(2)}, u32[]{:S(2)}) collective-permute-start(bf16[128,2048]{1,0:T(8,128)(2,1)S(1)} %get-tuple-element.73.refs_4_), channel_id=1, source_target_pairs={{0,8},{4,20},{8,0},{12,28},{16,24},{20,4},{24,16},{28,12},{1,9},{5... | collective-permute-start | bytes 1572872 | tf_op jit(solution)/shard_map/ppermute | solution.py:869
  18.8 14.9 %collective-permute-start.7 = (bf16[128,2048]{1,0:T(8,128)(2,1)S(1)}, bf16[128,2048]{1,0:T(8,128)(2,1)S(1)}, u32[]{:S(2)}, u32[]{:S(2)}) collective-permute-start(bf16[128,2048]{1,0:T(8,128)(2,1)S(1)} %get-tuple-element.73.refs_4_), channel_id=1, source_target_pairs={{0,16},{4,12},{8,24},{12,4},{16,0},{20,28},{24,8},{28,20},{1,17},{... | collective-permute-start | bytes 1572872 | tf_op jit(solution)/shard_map/ppermute | solution.py:869
  18.9 14.8 %collective-permute-start.8 = (bf16[128,2048]{1,0:T(8,128)(2,1)S(1)}, bf16[128,2048]{1,0:T(8,128)(2,1)S(1)}, u32[]{:S(2)}, u32[]{:S(2)}) collective-permute-start(bf16[128,2048]{1,0:T(8,128)(2,1)S(1)} %get-tuple-element.73.refs_4_), channel_id=1, source_target_pairs={{1,2},{2,1},{5,6},{6,5},{9,10},{10,9},{13,14},{14,13},{17,18},{18,... | collective-permute-start | bytes 1572872 | tf_op jit(solution)/shard_map/ppermute | solution.py:866
  19.6 19.8 %collective-permute-start.4 = (bf16[128,2048]{1,0:T(8,128)(2,1)S(1)}, bf16[128,2048]{1,0:T(8,128)(2,1)S(1)}, u32[]{:S(2)}, u32[]{:S(2)}) collective-permute-start(bf16[128,2048]{1,0:T(8,128)(2,1)S(1)} %get-tuple-element.71.inner_ref), channel_id=1, source_target_pairs={{1,0},{2,3},{5,4},{6,7},{9,8},{10,11},{13,12},{14,15},{17,16},{18,... | collective-permute-start | bytes 1572872 | tf_op jit(solution)/shard_map/ppermute | solution.py:866
  20.9 18.5 %collective-permute-start.5 = (bf16[128,2048]{1,0:T(8,128)(2,1)S(1)}, bf16[128,2048]{1,0:T(8,128)(2,1)S(1)}, u32[]{:S(2)}, u32[]{:S(2)}) collective-permute-start(bf16[128,2048]{1,0:T(8,128)(2,1)S(1)} %get-tuple-element.72.refs_1_), channel_id=1, source_target_pairs={{0,16},{4,12},{8,24},{12,4},{16,0},{20,28},{24,8},{28,20},{1,17},{... | collective-permute-start | bytes 1572872 | tf_op jit(solution)/shard_map/ppermute | solution.py:872
  22.3 17.1 %copy-start = (bf16[128,2048]{1,0:T(8,128)(2,1)S(1)}, bf16[128,2048]{1,0:T(8,128)(2,1)}, u32[]{:S(2)}) copy-start(bf16[128,2048]{1,0:T(8,128)(2,1)} %refs_0_.1) | copy-start | bytes 1572868
  31.4 8.0 %collective-permute-start.10 = (bf16[1024,128]{1,0:T(8,128)(2,1)S(1)}, bf16[1024,128]{1,0:T(8,128)(2,1)S(1)}, u32[]{:S(2)}, u32[]{:S(2)}) collective-permute-start(bf16[1024,128]{1,0:T(8,128)(2,1)S(1)} %get-tuple-element.76), channel_id=1, source_target_pairs={{0,8},{4,20},{8,0},{12,28},{16,24},{24,16},{1,9},{5,21},{9,1},{13,... | collective-permute-start | bytes 786440 | tf_op jit(solution)/shard_map/ppermute | solution.py:749
  39.8 9.4 %collective-permute-start.15 = (bf16[896,2048]{1,0:T(8,128)(2,1)S(1)}, bf16[896,2048]{1,0:T(8,128)(2,1)S(1)}, u32[]{:S(2)}, u32[]{:S(2)}) collective-permute-start(bf16[896,2048]{1,0:T(8,128)(2,1)S(1)} %pack.3.refs_0_), channel_id=1, source_target_pairs={{0,4},{4,0},{1,5},{5,1},{2,6},{6,2},{3,7},{7,3},{8,12},{12,8},{9,1... | collective-permute-start | bytes 11010056 | tf_op jit(solution)/shard_map/ppermute | solution.py:822
  42.1 17.3 %collective-permute-start.12 = (bf16[128,2048]{1,0:T(8,128)(2,1)S(1)}, bf16[128,2048]{1,0:T(8,128)(2,1)S(1)}, u32[]{:S(2)}, u32[]{:S(2)}) collective-permute-start(bf16[128,2048]{1,0:T(8,128)(2,1)S(1)} %choose.2.refs_0_), channel_id=1, source_target_pairs={{0,8},{4,20},{8,0},{12,28},{16,24},{20,4},{24,16},{28,12},{1,9},{5... | collective-permute-start | bytes 1572872 | tf_op jit(solution)/shard_map/ppermute | solution.py:869
  42.6 16.8 %collective-permute-start.13 = (bf16[128,2048]{1,0:T(8,128)(2,1)S(1)}, bf16[128,2048]{1,0:T(8,128)(2,1)S(1)}, u32[]{:S(2)}, u32[]{:S(2)}) collective-permute-start(bf16[128,2048]{1,0:T(8,128)(2,1)S(1)} %choose.2.refs_0_), channel_id=1, source_target_pairs={{0,16},{4,12},{8,24},{12,4},{16,0},{20,28},{24,8},{28,20},{1,17},{... | collective-permute-start | bytes 1572872 | tf_op jit(solution)/shard_map/ppermute | solution.py:869
  43.8 16.3 %collective-permute-start.11 = (bf16[128,2048]{1,0:T(8,128)(2,1)S(1)}, bf16[128,2048]{1,0:T(8,128)(2,1)S(1)}, u32[]{:S(2)}, u32[]{:S(2)}) collective-permute-start(bf16[128,2048]{1,0:T(8,128)(2,1)S(1)} %get-tuple-element.77.inner_ref), channel_id=1, source_target_pairs={{1,0},{2,3},{5,4},{6,7},{9,8},{10,11},{13,12},{14,15},{17,16},{18,... | collective-permute-start | bytes 1572872 | tf_op jit(solution)/shard_map/ppermute | solution.py:866
  45.2 14.2 %collective-permute-start.14 = (bf16[1024,128]{1,0:T(8,128)(2,1)S(1)}, bf16[1024,128]{1,0:T(8,128)(2,1)S(1)}, u32[]{:S(2)}, u32[]{:S(2)}) collective-permute-start(bf16[1024,128]{1,0:T(8,128)(2,1)S(1)} %message.2), channel_id=1, source_target_pairs={{0,16},{4,12},{8,24},{12,4},{20,28},{28,20},{1,17},{5,13},{9,25},{... | collective-permute-start | bytes 786440 | tf_op jit(solution)/shard_map/ppermute | solution.py:762
  60.3 21.6 %collective-permute-start.20 = (bf16[512,2048]{1,0:T(8,128)(2,1)S(1)}, bf16[512,2048]{1,0:T(8,128)(2,1)S(1)}, u32[]{:S(2)}, u32[]{:S(2)}) collective-permute-start(bf16[512,2048]{1,0:T(8,128)(2,1)S(1)} %pack.4.refs_0_), channel_id=1, source_target_pairs={{0,4},{4,0},{1,5},{5,1},{2,6},{6,2},{3,7},{7,3},{8,12},{12,8},{9,1... | collective-permute-start | bytes 6291464 | tf_op jit(solution)/shard_map/ppermute | solution.py:822
  61.6 4.4 %collective-permute-start.21 = (f32[1024,128]{1,0:T(8,128)S(1)}, f32[1024,128]{1,0:T(8,128)S(1)}, u32[]{:S(2)}, u32[]{:S(2)}) collective-permute-start(f32[1024,128]{1,0:T(8,128)S(1)} %state.2.state_ref), channel_id=1, source_target_pairs={{0,4},{4,0},{1,5},{5,1},{2,6},{6,2},{3,7},{7,3},{8,12},{12,8},{9,1... | collective-permute-start | bytes 1572872 | tf_op jit(solution)/shard_map/ppermute | solution.py:775
  61.7 16.5 %collective-permute-start.17 = (bf16[128,2048]{1,0:T(8,128)(2,1)S(1)}, bf16[128,2048]{1,0:T(8,128)(2,1)S(1)}, u32[]{:S(2)}, u32[]{:S(2)}) collective-permute-start(bf16[128,2048]{1,0:T(8,128)(2,1)S(1)} %choose.3.refs_3_), channel_id=1, source_target_pairs={{0,8},{4,20},{8,0},{12,28},{16,24},{20,4},{24,16},{28,12},{1,9},{5... | collective-permute-start | bytes 1572872 | tf_op jit(solution)/shard_map/ppermute | solution.py:869
  62.8 15.4 %collective-permute-start.18 = (bf16[128,2048]{1,0:T(8,128)(2,1)S(1)}, bf16[128,2048]{1,0:T(8,128)(2,1)S(1)}, u32[]{:S(2)}, u32[]{:S(2)}) collective-permute-start(bf16[128,2048]{1,0:T(8,128)(2,1)S(1)} %choose.3.refs_3_), channel_id=1, source_target_pairs={{0,16},{4,12},{8,24},{12,4},{16,0},{20,28},{24,8},{28,20},{1,17},{... | collective-permute-start | bytes 1572872 | tf_op jit(solution)/shard_map/ppermute | solution.py:869
  64.0 17.9 %collective-permute-start.16 = (bf16[128,2048]{1,0:T(8,128)(2,1)S(1)}, bf16[128,2048]{1,0:T(8,128)(2,1)S(1)}, u32[]{:S(2)}, u32[]{:S(2)}) collective-permute-start(bf16[128,2048]{1,0:T(8,128)(2,1)S(1)} %get-tuple-element.89.refs_1_), channel_id=1, source_target_pairs={{0,16},{4,12},{8,24},{12,4},{16,0},{20,28},{24,8},{28,20},{1,17},{... | collective-permute-start | bytes 1572872 | tf_op jit(solution)/shard_map/ppermute | solution.py:872
  66.0 15.9 %collective-permute-start.19 = (bf16[128,2048]{1,0:T(8,128)(2,1)S(1)}, bf16[128,2048]{1,0:T(8,128)(2,1)S(1)}, u32[]{:S(2)}, u32[]{:S(2)}) collective-permute-start(bf16[128,2048]{1,0:T(8,128)(2,1)S(1)} %get-tuple-element.91), channel_id=1, source_target_pairs={{0,1},{1,0},{2,3},{3,2},{4,5},{5,4},{6,7},{7,6},{8,9},{9,8},{10,11... | collective-permute-start | bytes 1572872 | tf_op jit(solution)/shard_map/ppermute | solution.py:866
  82.3 5.6 %collective-permute-start.22 = (bf16[512,2048]{1,0:T(8,128)(2,1)S(1)}, bf16[512,2048]{1,0:T(8,128)(2,1)S(1)}, u32[]{:S(2)}, u32[]{:S(2)}) collective-permute-start(bf16[512,2048]{1,0:T(8,128)(2,1)S(1)} %pack.5.refs_0_), channel_id=1, source_target_pairs={{0,4},{4,0},{1,5},{5,1},{2,6},{6,2},{3,7},{7,3},{8,12},{12,8},{9,1... | collective-permute-start | bytes 6291464 | tf_op jit(solution)/shard_map/ppermute | solution.py:822
  82.4 8.4 %collective-permute-start.23 = (bf16[128,2048]{1,0:T(8,128)(2,1)S(1)}, bf16[128,2048]{1,0:T(8,128)(2,1)S(1)}, u32[]{:S(2)}, u32[]{:S(2)}) collective-permute-start(bf16[128,2048]{1,0:T(8,128)(2,1)S(1)} %get-tuple-element.101.refs_2_), channel_id=1, source_target_pairs={{0,16},{4,12},{8,24},{12,4},{16,0},{20,28},{24,8},{28,20},{1,17},{... | collective-permute-start | bytes 1572872 | tf_op jit(solution)/shard_map/ppermute | solution.py:872
  90.7 4.0 %collective-permute-start.24 = (bf16[128,2048]{1,0:T(8,128)(2,1)S(1)}, bf16[128,2048]{1,0:T(8,128)(2,1)S(1)}, u32[]{:S(2)}, u32[]{:S(2)}) collective-permute-start(bf16[128,2048]{1,0:T(8,128)(2,1)S(1)} %join.9.refs_0_), channel_id=1, source_target_pairs={{0,4},{4,0},{1,5},{5,1},{2,6},{6,2},{3,7},{7,3},{8,12},{12,8},{9,1... | collective-permute-start | bytes 1572872 | tf_op jit(solution)/shard_map/ppermute | solution.py:863
  96.5 2.0 %collective-permute-start.25 = (bf16[2048,128]{1,0:T(8,128)(2,1)S(1)}, bf16[2048,128]{1,0:T(8,128)(2,1)S(1)}, u32[]{:S(2)}, u32[]{:S(2)}) collective-permute-start(bf16[2048,128]{1,0:T(8,128)(2,1)S(1)} %get-tuple-element.118), channel_id=1, source_target_pairs={{0,4},{4,0},{1,5},{5,1},{2,6},{6,2},{3,7},{7,3},{8,12},{12,8},{9,1... | collective-permute-start | bytes 1572872 | tf_op jit(solution)/shard_map/ppermute | solution.py:739
  98.6 7.4 %collective-permute-start.26 = (bf16[1024,128]{1,0:T(8,128)(2,1)S(1)}, bf16[1024,128]{1,0:T(8,128)(2,1)S(1)}, u32[]{:S(2)}, u32[]{:S(2)}) collective-permute-start(bf16[1024,128]{1,0:T(8,128)(2,1)S(1)} %get-tuple-element.120), channel_id=1, source_target_pairs={{0,8},{8,0},{16,24},{20,4},{24,16},{28,12},{1,9},{9,1},{17,25},{21... | collective-permute-start | bytes 786440 | tf_op jit(solution)/shard_map/ppermute | solution.py:749
  106.0 9.1 %collective-permute-start.27 = (bf16[1024,128]{1,0:T(8,128)(2,1)S(1)}, bf16[1024,128]{1,0:T(8,128)(2,1)S(1)}, u32[]{:S(2)}, u32[]{:S(2)}) collective-permute-start(bf16[1024,128]{1,0:T(8,128)(2,1)S(1)} %message.3), channel_id=1, source_target_pairs={{4,12},{12,4},{16,0},{20,28},{24,8},{28,20},{5,13},{13,5},{17,1},{... | collective-permute-start | bytes 786440 | tf_op jit(solution)/shard_map/ppermute | solution.py:762
  115.3 2.7 %collective-permute-start.28 = (f32[1024,128]{1,0:T(8,128)S(1)}, f32[1024,128]{1,0:T(8,128)S(1)}, u32[]{:S(2)}, u32[]{:S(2)}) collective-permute-start(f32[1024,128]{1,0:T(8,128)S(1)} %state.3.state_ref), channel_id=1, source_target_pairs={{0,4},{4,0},{1,5},{5,1},{2,6},{6,2},{3,7},{7,3},{8,12},{12,8},{9,1... | collective-permute-start | bytes 1572872 | tf_op jit(solution)/shard_map/ppermute | solution.py:775

commit v14 on v13

--- a/solution.py
+++ b/solution.py
@@ -109,8 +109,8 @@
 
     three = (0, 1, 2)
     return (
-        some((0, (0, 1, 2, 3)), (1, three))
-        + some((2, three), (3, (0,)))
+        some((0, three), (1, three))
+        + some((0, (3,)), (2, three), (3, (0,)))
         + some((1, (3,)), (2, (3,)), (3, (1, 2)))
         + some((3, (3,)))
     )
@@ -887,19 +887,19 @@
         high, low = halves(scan_any(own, sent, chips * 2, False))
 
     if special:
-        third_0 = onward(first_0)
         first_1, second_1 = cross(near)
         far = along(near, middle)
         mid_out = along(mid, outward)
         twin, both, got = send_first(own, sent, False)
-        mid_out, third_0, first_1, second_1, far, got = join(
-            [mid_out, third_0, first_1, second_1, far, got]
+        mid_out, first_1, second_1, far, got, first_0 = join(
+            [mid_out, first_1, second_1, far, got, first_0]
         )
+        third_0 = onward(first_0)
         more = send_second(got, both, False)
         next_layer = choose(mid, mid_out)
         first_2, second_2 = cross(next_layer)
         far_out = along(far, outward)
-        early = pack(q_weight, first_0, second_0, third_0, near, first_1, second_1)
+        early = pack(q_weight, first_0, second_0, near, first_1, second_1)
         partial, _, mark = products_call(special, 0, early, tokens)
         top, bottom, turned_mark = turned_call(values, cotangent, got)
         far_out, first_2, second_2, more, third_0 = join(
@@ -911,7 +911,7 @@
         first_3, second_3 = cross(last_layer)
         high, low = add_up(got, more, twin, False)
         masked, q_mask = masked_call(factor, q_spikes, cotangent, values, keys, high, low)
-        middle = pack(next_layer, first_2, second_2, last_layer)
+        middle = pack(third_0, next_layer, first_2, second_2, last_layer)
         _, grad, mark = products_call(special, 0, early, tokens, masked=masked, project=False)
         third_2, first_3, second_3, third_1, middle[1] = join(
             [third_2, first_3, second_3, third_1, middle[1]], [mark]
@@ -919,7 +919,7 @@
         third_3 = onward(first_3)
         late = pack(third_1, third_2, first_3, second_3)
         partial, grad, mark_0 = products_call(
-            special, 14, middle, tokens, partial, masked, grad
+            special, 12, middle, tokens, partial, masked, grad
         )
         partial, _, mark_1 = products_call(special, 22, late, tokens, partial)
         third_3, = join([third_3], [mark_0, mark_1])

time: 121 us -> 125 us (1.033)
  waiting for transfers between devices: 36.1 us -> 38 us
  starting transfers between devices: 34.9 us -> 36.7 us
    ppermute x6, waiting for transfers between devices: 6.53 us -> 18.7 us  [along(): return lax.ppermute(array, 'dp', pairs)]
    ppermute x4, waiting for transfers between devices: 10.8 us -> 3.3 us  [cross(): lax.ppermute(array, CTX, links(1))]
    ppermute x6, starting transfers between devices: 7.74 us -> 13.1 us  [along(): return lax.ppermute(array, 'dp', pairs)]
    ppermute x4, waiting for transfers between devices: 3.75 us -> 0.01 us  [cross(): lax.ppermute(array, CTX, links(2))]
    ppermute x3, waiting for transfers between devices: 4.51 us -> 1.02 us  [onward(): return lax.ppermute(array, CTX, links(2))]
    ppermute x2, waiting for transfers between devices: 7.15 us -> 10.2 us  [send_second(): return lax.ppermute(message, CTX, links(2, upward(reverse)))]
    ppermute x4, starting transfers between devices: 4 us -> 5.92 us  [cross(): lax.ppermute(array, CTX, links(1))]
    ppermute x4, starting transfers between devices: 3.75 us -> 2.17 us  [cross(): lax.ppermute(array, CTX, links(2))]
  transfers between devices with their start and end apart: 29 -> 29, of which waited for: 12 -> 11; matrix products, arithmetic and copies ran while one was open for 0% -> 0% of each run, Pallas kernels for 36% -> 35%
where the time goes in v14:
time: 125 us; the launch traced here: 124 us
  Pallas kernels  48.1 us (38%)
  waiting for transfers between devices  38 us (30%)
  starting transfers between devices  36.7 us (29%)
    pallas_call x32, Pallas kernels, kernel_call(): made(*[holds[place](one) if place in holds else one for place, one in zip...  48.1 us
    ppermute x6, waiting for transfers between devices, along(): return lax.ppermute(array, 'dp', pairs)  18.7 us
    ppermute x6, starting transfers between devices, along(): return lax.ppermute(array, 'dp', pairs)  13.1 us
    ppermute x2, waiting for transfers between devices, send_second(): return lax.ppermute(message, CTX, links(2, upward(reverse)))  10.2 us
    ppermute x4, starting transfers between devices, cross(): lax.ppermute(array, CTX, links(1))  5.92 us
    ppermute x2, starting transfers between devices, send_second(): return lax.ppermute(message, CTX, links(2, upward(reverse)))  4.32 us
    ppermute x2, starting transfers between devices, send_first(): return (sibling, both, lax.ppermute(sent, CTX, links(1, upward(reverse))))  3.57 us
    ppermute x4, waiting for transfers between devices, cross(): lax.ppermute(array, CTX, links(1))  3.3 us
  transfers between devices with their start and end apart: 29, of which 11 were waited for; matrix products, arithmetic and copies ran while one was open for 0% of the time, Pallas kernels for 35%

profile of v14, /device:TPU:1, one launch (start us, length us, event | category | flops | bytes accessed | tf_op | source)
XLA Modules:
  0.0 124.0 jit_solution(3477070385315650446)
XLA Ops:
  0.6 2.2 %collective-permute-start.2 = (bf16[128,2048]{1,0:T(8,128)(2,1)}, bf16[128,2048]{1,0:T(8,128)(2,1)S(1)}, u32[]{:S(2)}, u32[]{:S(2)}) collective-permute-start(bf16[128,2048]{1,0:T(8,128)(2,1)} %refs_0_.1), channel_id=1, source_target_pairs={{0,1},{1,0},{2,3},{3,2},{4,5},{5,4},{6,7},{7,6},{8,9},{9,8},{10,11... | collective-permute-start | bytes 1572872 | tf_op jit(solution)/shard_map/ppermute | solution.py:866
  4.0 1.2 collective-permute-start
  6.0 4.8 %own_memory.1 = (bf16[384,2048]{1,0:T(8,128)(2,1)S(1)}, bf16[384,2048]{1,0:T(8,128)(2,1)S(1)}, bf16[384,2048]{1,0:T(8,128)(2,1)S(1)}, f32[2048,128]{1,0:T(8,128)...) custom-call(bf16[384,2048]{1,0:T(8,128)(2,1)} %bitcast.15, ...), custom_call_target="tpu_custom_call" | custom-call | flops 201326592 | bytes 9437184 | tf_op jit(solution)/shard_map/own_memory/pallas_call | solution.py:74
  10.7 3.9 %collective-permute-done.2.refs_2_ = bf16[128,2048]{1,0:T(8,128)(2,1)S(1)} collective-permute-done((bf16[128,2048]{1,0:T(8,128)(2,1)}, bf16[128,2048]{1,0:T(8,128)(2,1)S(1)}, u32[]{:S(2)}, u32[]{:S(2)}) %collective-permute-start.2) | collective-permute-done | bytes 524320 | tf_op jit(solution)/shard_map/ppermute | solution.py:866
  14.7 3.3 %collective-permute-done.refs_0_ = bf16[128,2048]{1,0:T(8,128)(2,1)S(1)} collective-permute-done((bf16[128,2048]{1,0:T(8,128)(2,1)}, bf16[128,2048]{1,0:T(8,128)(2,1)S(1)}, u32[]{:S(2)}, u32[]{:S(2)}) %collective-permute-start) | collective-permute-done | bytes 524320 | tf_op jit(solution)/shard_map/ppermute | solution.py:869
  18.7 1.3 %collective-permute-start.4 = (bf16[128,2048]{1,0:T(8,128)(2,1)S(1)}, bf16[128,2048]{1,0:T(8,128)(2,1)S(1)}, u32[]{:S(2)}, u32[]{:S(2)}) collective-permute-start(bf16[128,2048]{1,0:T(8,128)(2,1)S(1)} %get-tuple-element.71.inner_ref), channel_id=1, source_target_pairs={{1,0},{2,3},{5,4},{6,7},{9,8},{10,11},{13,12},{14,15},{17,16},{18,... | collective-permute-start | bytes 1572872 | tf_op jit(solution)/shard_map/ppermute | solution.py:866
  22.3 2.3 %collective-permute-start.9 = (bf16[1024,128]{1,0:T(8,128)(2,1)S(1)}, bf16[1024,128]{1,0:T(8,128)(2,1)S(1)}, u32[]{:S(2)}, u32[]{:S(2)}) collective-permute-start(bf16[1024,128]{1,0:T(8,128)(2,1)S(1)} %get-tuple-element.75), channel_id=1, source_target_pairs={{0,8},{4,20},{8,0},{12,28},{16,24},{24,16},{1,9},{5,21},{9,1},{13,... | collective-permute-start | bytes 786440 | tf_op jit(solution)/shard_map/ppermute | solution.py:749
  24.6 11.8 %collective-permute-done.4.refs_0_ = bf16[128,2048]{1,0:T(8,128)(2,1)S(1)} collective-permute-done((bf16[128,2048]{1,0:T(8,128)(2,1)S(1)}, bf16[128,2048]{1,0:T(8,128)(2,1)S(1)}, u32[]{:S(2)}, u32[]{:S(2)}) %collective-permute-start.4) | collective-permute-done | bytes 524320 | tf_op jit(solution)/shard_map/ppermute | solution.py:866
  39.8 1.3 %collective-permute-start.10 = (bf16[128,2048]{1,0:T(8,128)(2,1)S(1)}, bf16[128,2048]{1,0:T(8,128)(2,1)S(1)}, u32[]{:S(2)}, u32[]{:S(2)}) collective-permute-start(bf16[128,2048]{1,0:T(8,128)(2,1)S(1)} %get-tuple-element.77.inner_ref), channel_id=1, source_target_pairs={{1,0},{2,3},{5,4},{6,7},{9,8},{10,11},{13,12},{14,15},{17,16},{18,... | collective-permute-start | bytes 1572872 | tf_op jit(solution)/shard_map/ppermute | solution.py:866
  41.1 1.3 %collective-permute-start.14 = (bf16[128,2048]{1,0:T(8,128)(2,1)S(1)}, bf16[128,2048]{1,0:T(8,128)(2,1)S(1)}, u32[]{:S(2)}, u32[]{:S(2)}) collective-permute-start(bf16[128,2048]{1,0:T(8,128)(2,1)S(1)} %get-tuple-element.81.refs_1_), channel_id=1, source_target_pairs={{0,16},{4,12},{8,24},{12,4},{16,0},{20,28},{24,8},{28,20},{1,17},{... | collective-permute-start | bytes 1572872 | tf_op jit(solution)/shard_map/ppermute | solution.py:872
  43.5 2.2 %collective-permute-start.13 = (bf16[1024,128]{1,0:T(8,128)(2,1)S(1)}, bf16[1024,128]{1,0:T(8,128)(2,1)S(1)}, u32[]{:S(2)}, u32[]{:S(2)}) collective-permute-start(bf16[1024,128]{1,0:T(8,128)(2,1)S(1)} %message.2), channel_id=1, source_target_pairs={{0,16},{4,12},{8,24},{12,4},{20,28},{28,20},{1,17},{5,13},{9,25},{... | collective-permute-start | bytes 786440 | tf_op jit(solution)/shard_map/ppermute | solution.py:762
  45.7 1.8 %turned.1 = (bf16[128,6144]{1,0:T(8,128)(2,1)S(1)}, bf16[256,4096]{1,0:T(8,128)(2,1)S(1)}, f32[8,128]{1,0:T(8,128)S(1)}) custom-call(bf16[384,2048]{1,0:T(8,128)(2,1)S(1)} %get-tuple-element.86.value_ref, bf16[384,2048]{1,0:T(8,128)(2,1)S(1)} %get-tuple-element.87.grad_ref, bf16[1024,128]{1,0:T(8,128)(2,1)S(1)} %get-tuple-element.79.got_ref.after_ref), custom_call_target="tpu_custom_call" | custom-call | flops 1207959552 | tf_op jit(solution)/shard_map/turned/pallas_call | solution.py:74
  47.5 2.6 %project.2 = (f32[384,2048]{1,0:T(8,128)S(1)}, f32[8,128]{1,0:T(8,128)S(1)}) custom-call(bf16[768,2048]{1,0:T(8,128)(2,1)S(1)} %pack.3.refs_0_, bf16[768,2048]{1,0:T(8,128)(2,1)S(1)} %collective-permute-done.15.refs_1_, bf16[384,4096]{1,0:T(8,128)(2,1)S(1)} %get-tuple-element.69.refs_2_.tokens_ref), custom_call_target="tpu_custom_call" | custom-call | flops 2415919104 | tf_op jit(solution)/shard_map/project/pallas_call | solution.py:74
  50.1 10.2 %collective-permute-done.13.refs_3_ = bf16[1024,128]{1,0:T(8,128)(2,1)S(1)} collective-permute-done((bf16[1024,128]{1,0:T(8,128)(2,1)S(1)}, bf16[1024,128]{1,0:T(8,128)(2,1)S(1)}, u32[]{:S(2)}, u32[]{:S(2)}) %collective-permute-start.13) | collective-permute-done | bytes 262176 | tf_op jit(solution)/shard_map/ppermute | solution.py:762
  61.7 2.2 %collective-permute-start.17 = (bf16[128,2048]{1,0:T(8,128)(2,1)S(1)}, bf16[128,2048]{1,0:T(8,128)(2,1)S(1)}, u32[]{:S(2)}, u32[]{:S(2)}) collective-permute-start(bf16[128,2048]{1,0:T(8,128)(2,1)S(1)} %choose.3.refs_4_), channel_id=1, source_target_pairs={{0,8},{4,20},{8,0},{12,28},{16,24},{20,4},{24,16},{28,12},{1,9},{5... | collective-permute-start | bytes 1572872 | tf_op jit(solution)/shard_map/ppermute | solution.py:869
  64.6 1.8 %collective-permute-done.21.other_ref = f32[1024,128]{1,0:T(8,128)S(1)} collective-permute-done((f32[1024,128]{1,0:T(8,128)S(1)}, f32[1024,128]{1,0:T(8,128)S(1)}, u32[]{:S(2)}, u32[]{:S(2)}) %collective-permute-start.21) | collective-permute-done | bytes 524320 | tf_op jit(solution)/shard_map/ppermute | solution.py:775
  66.4 7.0 %collective-permute-start.19 = (bf16[128,2048]{1,0:T(8,128)(2,1)S(1)}, bf16[128,2048]{1,0:T(8,128)(2,1)S(1)}, u32[]{:S(2)}, u32[]{:S(2)}) collective-permute-start(bf16[128,2048]{1,0:T(8,128)(2,1)S(1)} %get-tuple-element.91.refs_0_), channel_id=1, source_target_pairs={{0,1},{1,0},{2,3},{3,2},{4,5},{5,4},{6,7},{7,6},{8,9},{9,8},{10,11... | collective-permute-start | bytes 1572872 | tf_op jit(solution)/shard_map/ppermute | solution.py:866
  73.6 5.4 %masked_grad.1 = (bf16[384,2048]{1,0:T(8,128)(2,1)S(1)}, bf16[384,2048]{1,0:T(8,128)(2,1)S(1)}) custom-call(s32[384,2048]{1,0:T(8,128)} %bitcast.18, bf16[384,2048]{1,0:T(8,128)(2,1)S(1)} %get-tuple-element.87.grad_ref, bf16[384,2048]{1,0:T(8,128)(2,1)S(1)} %get-tuple-element.86.value_ref, bf16[384,2048]{1,0:T(8,128)(2,1)S(1)} %get-tuple-element.93.keys_ref, ...), custom_call_target="tpu_custom_call" | custom-call | flops 2415919104 | bytes 9437184 | tf_op jit(solution)/shard_map/masked_grad/pallas_call | solution.py:74
  79.0 3.5 %grad_tokens.3 = (bf16[384,4096]{1,0:T(8,128)(2,1)}, f32[8,128]{1,0:T(8,128)S(1)}) custom-call(bf16[768,2048]{1,0:T(8,128)(2,1)S(1)} %pack.3.refs_0_, bf16[768,2048]{1,0:T(8,128)(2,1)S(1)} %collective-permute-done.15.refs_1_, bf16[384,2048]{1,0:T(8,128)(2,1)S(1)} %get-tuple-element.97.refs_2_.refs_4_), custom_call_target="tpu_custom_call" | custom-call | flops 2415919104 | tf_op jit(solution)/shard_map/grad_tokens/pallas_call | solution.py:74
  82.6 2.9 %collective-permute-done.19.refs_3_ = bf16[128,2048]{1,0:T(8,128)(2,1)S(1)} collective-permute-done((bf16[128,2048]{1,0:T(8,128)(2,1)S(1)}, bf16[128,2048]{1,0:T(8,128)(2,1)S(1)}, u32[]{:S(2)}, u32[]{:S(2)}) %collective-permute-start.19) | collective-permute-done | bytes 524320 | tf_op jit(solution)/shard_map/ppermute | solution.py:866
  86.9 5.0 %products.1 = (f32[384,2048]{1,0:T(8,128)S(1)}, bf16[384,4096]{1,0:T(8,128)(2,1)}, f32[8,128]{1,0:T(8,128)S(1)}) custom-call(bf16[640,2048]{1,0:T(8,128)(2,1)S(1)} %pack.4.refs_0_, bf16[640,2048]{1,0:T(8,128)(2,1)S(1)} %get-tuple-element.103.refs_1_, ...), custom_call_target="tpu_custom_call", output_to_operand_aliasing={{0}: (3, {}), {1}: (5, {})} | custom-call | flops 4026531840 | tf_op jit(solution)/shard_map/products/pallas_call | solution.py:74
  91.9 2.1 %project.3 = (f32[384,2048]{1,0:T(8,128)S(1)}, f32[8,128]{1,0:T(8,128)S(1)}) custom-call(bf16[512,2048]{1,0:T(8,128)(2,1)S(1)} %pack.5.refs_0_, bf16[512,2048]{1,0:T(8,128)(2,1)S(1)} %collective-permute-done.22.refs_1_, bf16[384,4096]{1,0:T(8,128)(2,1)S(1)} %get-tuple-element.69.refs_2_.tokens_ref, ...), custom_call_target="tpu_custom_call", output_to_operand_aliasing={{0}: (3, {})} | custom-call | flops 1610612736 | tf_op jit(solution)/shard_map/project/pallas_call | solution.py:74
  95.9 2.7 %grad_tokens.4 = (bf16[384,4096]{1,0:T(8,128)(2,1)}, f32[8,128]{1,0:T(8,128)S(1)}) custom-call(bf16[512,2048]{1,0:T(8,128)(2,1)S(1)} %pack.5.refs_0_, bf16[512,2048]{1,0:T(8,128)(2,1)S(1)} %collective-permute-done.22.refs_1_, bf16[384,2048]{1,0:T(8,128)(2,1)S(1)} %get-tuple-element.97.refs_2_.refs_4_, ...), custom_call_target="tpu_custom_call", output_to_operand_aliasing={{0}: (3, {})} | custom-call | flops 1610612736 | tf_op jit(solution)/shard_map/grad_tokens/pallas_call | solution.py:74
  98.6 1.7 %queries.1 = (bf16[384,2048]{1,0:T(8,128)(2,1)S(1)}, f32[2048,128]{1,0:T(8,128)S(1)}, bf16[2048,128]{1,0:T(8,128)(2,1)S(1)}) custom-call(bf16[384,4096]{1,0:T(8,128)(2,1)S(1)} %get-tuple-element.69.refs_2_.tokens_ref, f32[384,2048]{1,0:T(8,128)S(1)} %get-tuple-element.107.sum_ref, bf16[384,2048]{1,0:T(8,128)(2,1)S(1)} %get-tuple-element.108.mask_ref, ...), custom_call_target="tpu_custom_call" | custom-call | flops 402653184 | tf_op jit(solution)/shard_map/queries/pallas_call | solution.py:74
  100.5 1.3 %grad_tokens.5 = (bf16[384,4096]{1,0:T(8,128)(2,1)}, f32[8,128]{1,0:T(8,128)S(1)}) custom-call(bf16[128,2048]{1,0:T(8,128)(2,1)S(1)} %join.9.refs_0_, bf16[128,2048]{1,0:T(8,128)(2,1)S(1)} %collective-permute-done.24.refs_1_, bf16[384,2048]{1,0:T(8,128)(2,1)S(1)} %get-tuple-element.97.refs_2_.refs_4_, ...), custom_call_target="tpu_custom_call", output_to_operand_aliasing={{0}: (3, {})} | custom-call | flops 402653184 | tf_op jit(solution)/shard_map/grad_tokens/pallas_call | solution.py:74
  102.5 1.3 %collective-permute-start.26 = (bf16[1024,128]{1,0:T(8,128)(2,1)S(1)}, bf16[1024,128]{1,0:T(8,128)(2,1)S(1)}, u32[]{:S(2)}, u32[]{:S(2)}) collective-permute-start(bf16[1024,128]{1,0:T(8,128)(2,1)S(1)} %get-tuple-element.120), channel_id=1, source_target_pairs={{0,8},{8,0},{16,24},{20,4},{24,16},{28,12},{1,9},{9,1},{17,25},{21... | collective-permute-start | bytes 786440 | tf_op jit(solution)/shard_map/ppermute | solution.py:749
  103.8 5.1 %attended.1 = (bf16[384,2048]{1,0:T(8,128)(2,1)}, f32[8,128]{1,0:T(8,128)S(1)}) custom-call(bf16[384,2048]{1,0:T(8,128)(2,1)S(1)} %get-tuple-element.113.query_ref, bf16[384,2048]{1,0:T(8,128)(2,1)S(1)} %get-tuple-element.93.keys_ref, bf16[384,2048]{1,0:T(8,128)(2,1)S(1)} %get-tuple-element.86.value_ref, bf16[2048,128]{1,0:T(8,128)(2,1)S(1)} %get-tuple-element.95.high_ref, ...), custom_call_target="tpu_custom_call" | custom-call | flops 2415919104 | bytes 6291456 | tf_op jit(solution)/shard_map/attended/pallas_call | solution.py:74
  109.9 2.2 %collective-permute-start.27 = (bf16[1024,128]{1,0:T(8,128)(2,1)S(1)}, bf16[1024,128]{1,0:T(8,128)(2,1)S(1)}, u32[]{:S(2)}, u32[]{:S(2)}) collective-permute-start(bf16[1024,128]{1,0:T(8,128)(2,1)S(1)} %message.3), channel_id=1, source_target_pairs={{4,12},{12,4},{16,0},{20,28},{24,8},{28,20},{5,13},{13,5},{17,1},{... | collective-permute-start | bytes 786440 | tf_op jit(solution)/shard_map/ppermute | solution.py:762
  112.1 2.1 %key_part.1 = (f32[384,2048]{1,0:T(8,128)S(1)}, f32[8,128]{1,0:T(8,128)S(1)}) custom-call(bf16[384,2048]{1,0:T(8,128)(2,1)S(1)} %get-tuple-element.113.query_ref, bf16[128,6144]{1,0:T(8,128)(2,1)S(1)} %get-tuple-element.124.top_ref, bf16[256,4096]{1,0:T(8,128)(2,1)S(1)} %get-tuple-element.125.bottom_ref), custom_call_target="tpu_custom_call" | custom-call | flops 1207959552 | tf_op jit(solution)/shard_map/key_part/pallas_call | solution.py:74
  114.2 3.9 %value_part.1 = (f32[384,2048]{1,0:T(8,128)S(1)}, f32[8,128]{1,0:T(8,128)S(1)}) custom-call(bf16[384,2048]{1,0:T(8,128)(2,1)S(1)} %get-tuple-element.113.query_ref, bf16[384,2048]{1,0:T(8,128)(2,1)S(1)} %get-tuple-element.93.keys_ref, bf16[384,2048]{1,0:T(8,128)(2,1)S(1)} %get-tuple-element.87.grad_ref), custom_call_target="tpu_custom_call" | custom-call | flops 1811939328 | tf_op jit(solution)/shard_map/value_part/pallas_call | solution.py:74
  119.4 2.2 %outer.2 = (bf16[384,2048]{1,0:T(8,128)(2,1)}, bf16[384,2048]{1,0:T(8,128)(2,1)}) custom-call(f32[1024,128]{1,0:T(8,128)S(1)} %state.3.state_ref, bf16[2048,128]{1,0:T(8,128)(2,1)S(1)} %collective-permute-done.25.sibling_ref, f32[384,2048]{1,0:T(8,128)S(1)} %get-tuple-element.127.key_ref, f32[384,2048]{1,0:T(8,128)S(1)} %get-tuple-element.128.val_ref, ...), custom_call_target="tpu_custom_call" | custom-call | flops 402653184 | bytes 7864320 | tf_op jit(solution)/shard_map/outer/pallas_call | solution.py:74
  121.6 2.2 %outer.3 = (bf16[384,2048]{1,0:T(8,128)(2,1)}, bf16[384,2048]{1,0:T(8,128)(2,1)}) custom-call(f32[1024,128]{1,0:T(8,128)S(1)} %collective-permute-done.28.state_ref, bf16[2048,128]{1,0:T(8,128)(2,1)S(1)} %collective-permute-done.25.sibling_ref, f32[384,2048]{1,0:T(8,128)S(1)} %get-tuple-element.127.key_ref, ...), custom_call_target="tpu_custom_call", output_to_operand_aliasing={{0}: (7, {}), {1}: (8, {})} | custom-call | flops 402653184 | bytes 7864320 | tf_op jit(solution)/shard_map/outer/pallas_call | solution.py:74
  (60 shorter events, 18.1 us)
Async XLA Ops:
  0.6 14.1 %collective-permute-start.2 = (bf16[128,2048]{1,0:T(8,128)(2,1)}, bf16[128,2048]{1,0:T(8,128)(2,1)S(1)}, u32[]{:S(2)}, u32[]{:S(2)}) collective-permute-start(bf16[128,2048]{1,0:T(8,128)(2,1)} %refs_0_.1), channel_id=1, source_target_pairs={{0,1},{1,0},{2,3},{3,2},{4,5},{5,4},{6,7},{7,6},{8,9},{9,8},{10,11... | collective-permute-start | bytes 1572872 | tf_op jit(solution)/shard_map/ppermute | solution.py:866
  2.8 11.9 %collective-permute-start.1 = (bf16[128,2048]{1,0:T(8,128)(2,1)}, bf16[128,2048]{1,0:T(8,128)(2,1)S(1)}, u32[]{:S(2)}, u32[]{:S(2)}) collective-permute-start(bf16[128,2048]{1,0:T(8,128)(2,1)} %refs_0_.1), channel_id=1, source_target_pairs={{0,16},{4,12},{8,24},{12,4},{16,0},{20,28},{24,8},{28,20},{1,17},{... | collective-permute-start | bytes 1572872 | tf_op jit(solution)/shard_map/ppermute | solution.py:869
  4.0 13.9 %collective-permute-start = (bf16[128,2048]{1,0:T(8,128)(2,1)}, bf16[128,2048]{1,0:T(8,128)(2,1)S(1)}, u32[]{:S(2)}, u32[]{:S(2)}) collective-permute-start(bf16[128,2048]{1,0:T(8,128)(2,1)} %refs_0_.1), channel_id=1, source_target_pairs={{0,8},{4,20},{8,0},{12,28},{16,24},{20,4},{24,16},{28,12},{1,9},{5... | collective-permute-start | bytes 1572872 | tf_op jit(solution)/shard_map/ppermute | solution.py:869
  5.3 12.7 %collective-permute-start.3 = (bf16[128,2048]{1,0:T(8,128)(2,1)}, bf16[128,2048]{1,0:T(8,128)(2,1)S(1)}, u32[]{:S(2)}, u32[]{:S(2)}) collective-permute-start(bf16[128,2048]{1,0:T(8,128)(2,1)} %refs_0_.1), channel_id=1, source_target_pairs={{1,2},{2,1},{5,6},{6,5},{9,10},{10,9},{13,14},{14,13},{17,18},{18,... | collective-permute-start | bytes 1572872 | tf_op jit(solution)/shard_map/ppermute | solution.py:866
  18.0 4.2 %collective-permute-start.8 = (bf16[2048,128]{1,0:T(8,128)(2,1)S(1)}, bf16[2048,128]{1,0:T(8,128)(2,1)S(1)}, u32[]{:S(2)}, u32[]{:S(2)}) collective-permute-start(bf16[2048,128]{1,0:T(8,128)(2,1)S(1)} %get-tuple-element.74), channel_id=1, source_target_pairs={{0,4},{4,0},{1,5},{5,1},{2,6},{6,2},{3,7},{7,3},{8,12},{12,8},{9,1... | collective-permute-start | bytes 1572872 | tf_op jit(solution)/shard_map/ppermute | solution.py:739
  18.7 17.8 %collective-permute-start.4 = (bf16[128,2048]{1,0:T(8,128)(2,1)S(1)}, bf16[128,2048]{1,0:T(8,128)(2,1)S(1)}, u32[]{:S(2)}, u32[]{:S(2)}) collective-permute-start(bf16[128,2048]{1,0:T(8,128)(2,1)S(1)} %get-tuple-element.71.inner_ref), channel_id=1, source_target_pairs={{1,0},{2,3},{5,4},{6,7},{9,8},{10,11},{13,12},{14,15},{17,16},{18,... | collective-permute-start | bytes 1572872 | tf_op jit(solution)/shard_map/ppermute | solution.py:866
  19.9 16.5 %collective-permute-start.7 = (bf16[128,2048]{1,0:T(8,128)(2,1)S(1)}, bf16[128,2048]{1,0:T(8,128)(2,1)S(1)}, u32[]{:S(2)}, u32[]{:S(2)}) collective-permute-start(bf16[128,2048]{1,0:T(8,128)(2,1)S(1)} %get-tuple-element.72.refs_3_), channel_id=1, source_target_pairs={{1,2},{2,1},{5,6},{6,5},{9,10},{10,9},{13,14},{14,13},{17,18},{18,... | collective-permute-start | bytes 1572872 | tf_op jit(solution)/shard_map/ppermute | solution.py:866
  20.6 15.8 %collective-permute-start.6 = (bf16[128,2048]{1,0:T(8,128)(2,1)S(1)}, bf16[128,2048]{1,0:T(8,128)(2,1)S(1)}, u32[]{:S(2)}, u32[]{:S(2)}) collective-permute-start(bf16[128,2048]{1,0:T(8,128)(2,1)S(1)} %get-tuple-element.72.refs_3_), channel_id=1, source_target_pairs={{0,16},{4,12},{8,24},{12,4},{16,0},{20,28},{24,8},{28,20},{1,17},{... | collective-permute-start | bytes 1572872 | tf_op jit(solution)/shard_map/ppermute | solution.py:869
  21.0 15.5 %collective-permute-start.5 = (bf16[128,2048]{1,0:T(8,128)(2,1)S(1)}, bf16[128,2048]{1,0:T(8,128)(2,1)S(1)}, u32[]{:S(2)}, u32[]{:S(2)}) collective-permute-start(bf16[128,2048]{1,0:T(8,128)(2,1)S(1)} %get-tuple-element.72.refs_3_), channel_id=1, source_target_pairs={{0,8},{4,20},{8,0},{12,28},{16,24},{20,4},{24,16},{28,12},{1,9},{5... | collective-permute-start | bytes 1572872 | tf_op jit(solution)/shard_map/ppermute | solution.py:869
  22.2 14.6 %copy-start = (bf16[128,2048]{1,0:T(8,128)(2,1)S(1)}, bf16[128,2048]{1,0:T(8,128)(2,1)}, u32[]{:S(2)}) copy-start(bf16[128,2048]{1,0:T(8,128)(2,1)} %refs_0_.1) | copy-start | bytes 1572868
  22.3 14.5 %collective-permute-start.9 = (bf16[1024,128]{1,0:T(8,128)(2,1)S(1)}, bf16[1024,128]{1,0:T(8,128)(2,1)S(1)}, u32[]{:S(2)}, u32[]{:S(2)}) collective-permute-start(bf16[1024,128]{1,0:T(8,128)(2,1)S(1)} %get-tuple-element.75), channel_id=1, source_target_pairs={{0,8},{4,20},{8,0},{12,28},{16,24},{24,16},{1,9},{5,21},{9,1},{13,... | collective-permute-start | bytes 786440 | tf_op jit(solution)/shard_map/ppermute | solution.py:749
  37.0 6.5 %collective-permute-start.15 = (bf16[768,2048]{1,0:T(8,128)(2,1)S(1)}, bf16[768,2048]{1,0:T(8,128)(2,1)S(1)}, u32[]{:S(2)}, u32[]{:S(2)}) collective-permute-start(bf16[768,2048]{1,0:T(8,128)(2,1)S(1)} %pack.3.refs_0_), channel_id=1, source_target_pairs={{0,4},{4,0},{1,5},{5,1},{2,6},{6,2},{3,7},{7,3},{8,12},{12,8},{9,1... | collective-permute-start | bytes 9437192 | tf_op jit(solution)/shard_map/ppermute | solution.py:822
  38.2 22.1 %collective-permute-start.12 = (bf16[128,2048]{1,0:T(8,128)(2,1)S(1)}, bf16[128,2048]{1,0:T(8,128)(2,1)S(1)}, u32[]{:S(2)}, u32[]{:S(2)}) collective-permute-start(bf16[128,2048]{1,0:T(8,128)(2,1)S(1)} %choose.2.refs_1_), channel_id=1, source_target_pairs={{0,16},{4,12},{8,24},{12,4},{16,0},{20,28},{24,8},{28,20},{1,17},{... | collective-permute-start | bytes 1572872 | tf_op jit(solution)/shard_map/ppermute | solution.py:869
  38.5 21.8 %collective-permute-start.11 = (bf16[128,2048]{1,0:T(8,128)(2,1)S(1)}, bf16[128,2048]{1,0:T(8,128)(2,1)S(1)}, u32[]{:S(2)}, u32[]{:S(2)}) collective-permute-start(bf16[128,2048]{1,0:T(8,128)(2,1)S(1)} %choose.2.refs_1_), channel_id=1, source_target_pairs={{0,8},{4,20},{8,0},{12,28},{16,24},{20,4},{24,16},{28,12},{1,9},{5... | collective-permute-start | bytes 1572872 | tf_op jit(solution)/shard_map/ppermute | solution.py:869
  39.8 20.6 %collective-permute-start.10 = (bf16[128,2048]{1,0:T(8,128)(2,1)S(1)}, bf16[128,2048]{1,0:T(8,128)(2,1)S(1)}, u32[]{:S(2)}, u32[]{:S(2)}) collective-permute-start(bf16[128,2048]{1,0:T(8,128)(2,1)S(1)} %get-tuple-element.77.inner_ref), channel_id=1, source_target_pairs={{1,0},{2,3},{5,4},{6,7},{9,8},{10,11},{13,12},{14,15},{17,16},{18,... | collective-permute-start | bytes 1572872 | tf_op jit(solution)/shard_map/ppermute | solution.py:866
  41.1 19.3 %collective-permute-start.14 = (bf16[128,2048]{1,0:T(8,128)(2,1)S(1)}, bf16[128,2048]{1,0:T(8,128)(2,1)S(1)}, u32[]{:S(2)}, u32[]{:S(2)}) collective-permute-start(bf16[128,2048]{1,0:T(8,128)(2,1)S(1)} %get-tuple-element.81.refs_1_), channel_id=1, source_target_pairs={{0,16},{4,12},{8,24},{12,4},{16,0},{20,28},{24,8},{28,20},{1,17},{... | collective-permute-start | bytes 1572872 | tf_op jit(solution)/shard_map/ppermute | solution.py:872
  43.5 16.9 %collective-permute-start.13 = (bf16[1024,128]{1,0:T(8,128)(2,1)S(1)}, bf16[1024,128]{1,0:T(8,128)(2,1)S(1)}, u32[]{:S(2)}, u32[]{:S(2)}) collective-permute-start(bf16[1024,128]{1,0:T(8,128)(2,1)S(1)} %message.2), channel_id=1, source_target_pairs={{0,16},{4,12},{8,24},{12,4},{20,28},{28,20},{1,17},{5,13},{9,25},{... | collective-permute-start | bytes 786440 | tf_op jit(solution)/shard_map/ppermute | solution.py:762
  60.7 24.9 %collective-permute-start.20 = (bf16[640,2048]{1,0:T(8,128)(2,1)S(1)}, bf16[640,2048]{1,0:T(8,128)(2,1)S(1)}, u32[]{:S(2)}, u32[]{:S(2)}) collective-permute-start(bf16[640,2048]{1,0:T(8,128)(2,1)S(1)} %pack.4.refs_0_), channel_id=1, source_target_pairs={{0,4},{4,0},{1,5},{5,1},{2,6},{6,2},{3,7},{7,3},{8,12},{12,8},{9,1... | collective-permute-start | bytes 7864328 | tf_op jit(solution)/shard_map/ppermute | solution.py:822
  60.9 5.6 %collective-permute-start.21 = (f32[1024,128]{1,0:T(8,128)S(1)}, f32[1024,128]{1,0:T(8,128)S(1)}, u32[]{:S(2)}, u32[]{:S(2)}) collective-permute-start(f32[1024,128]{1,0:T(8,128)S(1)} %state.2.state_ref), channel_id=1, source_target_pairs={{0,4},{4,0},{1,5},{5,1},{2,6},{6,2},{3,7},{7,3},{8,12},{12,8},{9,1... | collective-permute-start | bytes 1572872 | tf_op jit(solution)/shard_map/ppermute | solution.py:775
  61.4 21.2 %collective-permute-start.18 = (bf16[128,2048]{1,0:T(8,128)(2,1)S(1)}, bf16[128,2048]{1,0:T(8,128)(2,1)S(1)}, u32[]{:S(2)}, u32[]{:S(2)}) collective-permute-start(bf16[128,2048]{1,0:T(8,128)(2,1)S(1)} %choose.3.refs_4_), channel_id=1, source_target_pairs={{0,16},{4,12},{8,24},{12,4},{16,0},{20,28},{24,8},{28,20},{1,17},{... | collective-permute-start | bytes 1572872 | tf_op jit(solution)/shard_map/ppermute | solution.py:869
  61.7 20.9 %collective-permute-start.17 = (bf16[128,2048]{1,0:T(8,128)(2,1)S(1)}, bf16[128,2048]{1,0:T(8,128)(2,1)S(1)}, u32[]{:S(2)}, u32[]{:S(2)}) collective-permute-start(bf16[128,2048]{1,0:T(8,128)(2,1)S(1)} %choose.3.refs_4_), channel_id=1, source_target_pairs={{0,8},{4,20},{8,0},{12,28},{16,24},{20,4},{24,16},{28,12},{1,9},{5... | collective-permute-start | bytes 1572872 | tf_op jit(solution)/shard_map/ppermute | solution.py:869
  63.9 18.7 %collective-permute-start.16 = (bf16[128,2048]{1,0:T(8,128)(2,1)S(1)}, bf16[128,2048]{1,0:T(8,128)(2,1)S(1)}, u32[]{:S(2)}, u32[]{:S(2)}) collective-permute-start(bf16[128,2048]{1,0:T(8,128)(2,1)S(1)} %get-tuple-element.89.refs_2_), channel_id=1, source_target_pairs={{0,16},{4,12},{8,24},{12,4},{16,0},{20,28},{24,8},{28,20},{1,17},{... | collective-permute-start | bytes 1572872 | tf_op jit(solution)/shard_map/ppermute | solution.py:872
  66.4 19.1 %collective-permute-start.19 = (bf16[128,2048]{1,0:T(8,128)(2,1)S(1)}, bf16[128,2048]{1,0:T(8,128)(2,1)S(1)}, u32[]{:S(2)}, u32[]{:S(2)}) collective-permute-start(bf16[128,2048]{1,0:T(8,128)(2,1)S(1)} %get-tuple-element.91.refs_0_), channel_id=1, source_target_pairs={{0,1},{1,0},{2,3},{3,2},{4,5},{5,4},{6,7},{7,6},{8,9},{9,8},{10,11... | collective-permute-start | bytes 1572872 | tf_op jit(solution)/shard_map/ppermute | solution.py:866
  85.9 6.0 %collective-permute-start.22 = (bf16[512,2048]{1,0:T(8,128)(2,1)S(1)}, bf16[512,2048]{1,0:T(8,128)(2,1)S(1)}, u32[]{:S(2)}, u32[]{:S(2)}) collective-permute-start(bf16[512,2048]{1,0:T(8,128)(2,1)S(1)} %pack.5.refs_0_), channel_id=1, source_target_pairs={{0,4},{4,0},{1,5},{5,1},{2,6},{6,2},{3,7},{7,3},{8,12},{12,8},{9,1... | collective-permute-start | bytes 6291464 | tf_op jit(solution)/shard_map/ppermute | solution.py:822
  86.7 8.3 %collective-permute-start.23 = (bf16[128,2048]{1,0:T(8,128)(2,1)S(1)}, bf16[128,2048]{1,0:T(8,128)(2,1)S(1)}, u32[]{:S(2)}, u32[]{:S(2)}) collective-permute-start(bf16[128,2048]{1,0:T(8,128)(2,1)S(1)} %get-tuple-element.101.refs_2_), channel_id=1, source_target_pairs={{0,16},{4,12},{8,24},{12,4},{16,0},{20,28},{24,8},{28,20},{1,17},{... | collective-permute-start | bytes 1572872 | tf_op jit(solution)/shard_map/ppermute | solution.py:872
  95.0 3.6 %collective-permute-start.24 = (bf16[128,2048]{1,0:T(8,128)(2,1)S(1)}, bf16[128,2048]{1,0:T(8,128)(2,1)S(1)}, u32[]{:S(2)}, u32[]{:S(2)}) collective-permute-start(bf16[128,2048]{1,0:T(8,128)(2,1)S(1)} %join.9.refs_0_), channel_id=1, source_target_pairs={{0,4},{4,0},{1,5},{5,1},{2,6},{6,2},{3,7},{7,3},{8,12},{12,8},{9,1... | collective-permute-start | bytes 1572872 | tf_op jit(solution)/shard_map/ppermute | solution.py:863
  100.4 2.0 %collective-permute-start.25 = (bf16[2048,128]{1,0:T(8,128)(2,1)S(1)}, bf16[2048,128]{1,0:T(8,128)(2,1)S(1)}, u32[]{:S(2)}, u32[]{:S(2)}) collective-permute-start(bf16[2048,128]{1,0:T(8,128)(2,1)S(1)} %get-tuple-element.118), channel_id=1, source_target_pairs={{0,4},{4,0},{1,5},{5,1},{2,6},{6,2},{3,7},{7,3},{8,12},{12,8},{9,1... | collective-permute-start | bytes 1572872 | tf_op jit(solution)/shard_map/ppermute | solution.py:739
  102.5 7.4 %collective-permute-start.26 = (bf16[1024,128]{1,0:T(8,128)(2,1)S(1)}, bf16[1024,128]{1,0:T(8,128)(2,1)S(1)}, u32[]{:S(2)}, u32[]{:S(2)}) collective-permute-start(bf16[1024,128]{1,0:T(8,128)(2,1)S(1)} %get-tuple-element.120), channel_id=1, source_target_pairs={{0,8},{8,0},{16,24},{20,4},{24,16},{28,12},{1,9},{9,1},{17,25},{21... | collective-permute-start | bytes 786440 | tf_op jit(solution)/shard_map/ppermute | solution.py:749
  109.9 8.2 %collective-permute-start.27 = (bf16[1024,128]{1,0:T(8,128)(2,1)S(1)}, bf16[1024,128]{1,0:T(8,128)(2,1)S(1)}, u32[]{:S(2)}, u32[]{:S(2)}) collective-permute-start(bf16[1024,128]{1,0:T(8,128)(2,1)S(1)} %message.3), channel_id=1, source_target_pairs={{4,12},{12,4},{16,0},{20,28},{24,8},{28,20},{5,13},{13,5},{17,1},{... | collective-permute-start | bytes 786440 | tf_op jit(solution)/shard_map/ppermute | solution.py:762
  118.2 3.4 %collective-permute-start.28 = (f32[1024,128]{1,0:T(8,128)S(1)}, f32[1024,128]{1,0:T(8,128)S(1)}, u32[]{:S(2)}, u32[]{:S(2)}) collective-permute-start(f32[1024,128]{1,0:T(8,128)S(1)} %state.3.state_ref), channel_id=1, source_target_pairs={{0,4},{4,0},{1,5},{5,1},{2,6},{6,2},{3,7},{7,3},{8,12},{12,8},{9,1... | collective-permute-start | bytes 1572872 | tf_op jit(solution)/shard_map/ppermute | solution.py:775
